TPU v7x, 512 devices: a whole 4x4x16 slice. The times are simulated.
512 devices in a mesh: dp: 64 (over z, y), tensor: 8 (over x, core).
Axes of the slice: x: 4, y: 4, z: 16, core: 2. Of those that a mesh axis runs over, the one named last changes fastest.
Arguments:
- queries: bfloat16 [1024, 16, 24, 128], P('dp', None, 'tensor'), may hold values from -160 to 160
- new_kv: bfloat16 [1024, 2, 16, 8, 128], P('dp', None, None, 'tensor'), may hold values from -6 to 6
- kv_cache: bfloat16 [12288, 2, 16, 8, 128], P('dp', None, None, 'tensor'), may hold values from -6 to 6
- page_table: int32 [1024, 12], P('dp'), may hold values from 0 to 191, as said below
- lengths: int32 [1024], P('dp'), may hold values from 128 to 192, as said below
- out_proj: bfloat16 [3072, 2560], P('tensor'), may hold values from -0.109375 to 0.109375
- residual: bfloat16 [16384, 2560], P(('dp', 'tensor')), may hold values from -60 to 60
- norm_gain: bfloat16 [2560], replicated, may hold values from 0.099609375 to 1.8984375
- score_weight: bfloat16 [2560], replicated, may hold values from -0.125 to 0.125
- fork_parent: int32 [3072], P('dp'), may hold values from 0 to 1023, as said below
Outputs:
- hidden_out: bfloat16 [16384, 2560], P(('dp', 'tensor'))
- scores: float32 [1024], P(('dp', 'tensor'))
- child_pages: bfloat16 [3072, 8, 2, 16, 8, 128], P('dp', None, None, None, 'tensor')
Inputs may be any that keep to these rules, and one draw needn't show every extreme that they name: `page_table`: the rows of one dp group use each of its 192 pages exactly once. `lengths`: some branch holds exactly 192 tokens. Among the child slots of one dp group, at most 2 have their parents in any one dp group, and that many in some pair; the parents that lie in one dp group (as fork_parent // 16) are at most 2 distinct branches over all child slots, and that many for some group.
All inputs are finite; a program needn't handle non-finite values.
Results may differ from a plain program's by a relative error of at most 0.008.
Values may be sent and summed in bfloat16 or wider, within the bound.
No kernel may reach another device: no remote copies, remote signals or barrier semaphores. Data moves between devices by JAX's collectives and lax.ppermute only.
A program may use at most 64 MiB of HBM per device.

v0:
```python
import jax
import jax.numpy as jnp
from jax import lax
from jax.sharding import PartitionSpec as P

BR_DEV = 16
CH = 16
PAGE = 16
PREFIX = 128
CAP = 2


neg_fill = -1e30


def attend(queries, new_kv, kv_cache, page_table, lengths):
    branch, steps_new, qheads, head_width = queries.shape
    kvheads = new_kv.shape[3]
    per_group = qheads // kvheads
    cache_pages = kv_cache[page_table]
    key_span = cache_pages.shape[1] * cache_pages.shape[3]
    cache_keys = cache_pages[:, :, 0].reshape(branch, key_span, kvheads, head_width)
    cache_values = cache_pages[:, :, 1].reshape(branch, key_span, kvheads, head_width)
    grouped = queries.reshape(branch, steps_new, kvheads, per_group, head_width)
    score_scale = head_width ** (-0.5)
    old_scores = (
        jnp.einsum("bckgd,bskd->bkgcs", grouped, cache_keys, preferred_element_type=jnp.float32)
        * score_scale
    )
    new_scores = (
        jnp.einsum("bckgd,btkd->bkgct", grouped, new_kv[:, 0], preferred_element_type=jnp.float32)
        * score_scale
    )
    old_mask = (jnp.arange(key_span)[None, :] < lengths[:, None])[:, None, None, None, :]
    new_mask = (jnp.arange(steps_new)[None, :] <= jnp.arange(steps_new)[:, None])[None, None, None]
    old_scores = jnp.where(old_mask, old_scores, neg_fill)
    new_scores = jnp.where(new_mask, new_scores, neg_fill)
    row_max = jnp.maximum(
        jnp.max(old_scores, axis=-1, keepdims=True), jnp.max(new_scores, axis=-1, keepdims=True)
    )
    old_probs = jnp.where(old_mask, jnp.exp(old_scores - row_max), 0.0)
    new_probs = jnp.where(new_mask, jnp.exp(new_scores - row_max), 0.0)
    denom_sum = jnp.sum(old_probs, axis=-1, keepdims=True) + jnp.sum(
        new_probs, axis=-1, keepdims=True
    )
    old_weights = (old_probs / denom_sum).astype(jnp.bfloat16)
    new_weights = (new_probs / denom_sum).astype(jnp.bfloat16)
    attended = jnp.einsum(
        "bkgcs,bskd->bckgd", old_weights, cache_values, preferred_element_type=jnp.float32
    )
    attended = attended + jnp.einsum(
        "bkgct,btkd->bckgd", new_weights, new_kv[:, 1], preferred_element_type=jnp.float32
    )
    return attended.astype(jnp.bfloat16).reshape(branch * steps_new, qheads * head_width)


def same_owner_rank(owners):
    places = jnp.arange(owners.shape[-1])
    matching = owners[..., :, None] == owners[..., None, :]
    before = places[None, :] < places[:, None]
    return jnp.sum((matching & before).astype(jnp.int32), axis=-1)


def fork_pages(listing, fork_parent, kv_cache, page_table):
    groups = lax.axis_size("dp")
    me_index = lax.axis_index("dp")
    prefix_count = PREFIX // PAGE
    my_owner = fork_parent // BR_DEV
    owners = (listing // BR_DEV).reshape(groups, -1)
    local_rows = (listing % BR_DEV).reshape(groups, -1)
    ranks = same_owner_rank(owners)
    hits = (owners == me_index)[:, :, None] & (ranks[:, :, None] == jnp.arange(CAP)[None, None, :])
    chosen = jnp.sum(jnp.where(hits, local_rows[:, :, None], 0), axis=1)
    blocks = kv_cache[page_table[chosen][..., :prefix_count]]
    arrived = lax.all_to_all(blocks, "dp", split_axis=0, concat_axis=0, tiled=True)
    my_rank = same_owner_rank(my_owner)
    return arrived[my_owner, my_rank]


def local(
    queries,
    new_kv,
    kv_cache,
    page_table,
    lengths,
    out_proj,
    residual,
    norm_gain,
    score_weight,
    fork_parent,
):
    listing = lax.all_gather(fork_parent, "dp", axis=0, tiled=True)
    attended = attend(queries, new_kv, kv_cache, page_table, lengths)
    rows_here = residual.shape[0]
    summed = lax.psum_scatter(
        jnp.dot(attended, out_proj, preferred_element_type=jnp.float32).astype(jnp.bfloat16),
        "tensor",
        scatter_dimension=0,
        tiled=True,
    ).astype(jnp.float32)
    updated = summed + residual.astype(jnp.float32)
    hidden_out = updated.astype(jnp.bfloat16)
    block_ends = updated.reshape(rows_here // CH, CH, updated.shape[1])[:, CH - 1]
    normed = (
        block_ends
        * lax.rsqrt(jnp.mean(block_ends * block_ends, axis=-1, keepdims=True) + 1e-06)
        * norm_gain.astype(jnp.float32)
    )
    scores = jax.nn.sigmoid(jnp.sum(normed * score_weight.astype(jnp.float32), axis=-1))
    child_pages = fork_pages(listing, fork_parent, kv_cache, page_table)
    return (hidden_out, scores, child_pages)


def solution(mesh):
    in_specs = (
        P("dp", None, "tensor", None),
        P("dp", None, None, "tensor", None),
        P("dp", None, None, "tensor", None),
        P("dp", None),
        P("dp"),
        P("tensor", None),
        P(("dp", "tensor"), None),
        P(),
        P(),
        P("dp"),
    )
    out_specs = (
        P(("dp", "tensor"), None),
        P(("dp", "tensor")),
        P("dp", None, None, None, "tensor", None),
    )
    return jax.shard_map(local, mesh=mesh, in_specs=in_specs, out_specs=out_specs, check_vma=False)
```

profile of v0, /device:TPU:24, one launch (start us, length us, event | category | flops | bytes accessed | tf_op | source)
XLA Modules:
  0.0 644.5 jit_solution(810497414290004629)
XLA Ops:
  7.2 1.4 dynamic-slice
  9.3 0.9 dynamic-update-slice
  10.1 288.0 %all-reduce = s32[3072]{0:T(1024)S(1)} all-reduce(s32[3072]{0:T(1024)S(1)} %dynamic-update-slice), channel_id=1, replica_groups=mesh['dp'=64,'tensor'=8] {'dp'}, use_global_device_ids=true, to_apply=%add | all-reduce | flops 3072 | bytes 24576
  298.3 0.1 copy.40
  298.6 0.5 convert_reduce_fusion
  299.1 0.1 copy.44
  299.2 0.1 reshape.199
  299.4 1.3 gather_fusion.1
  300.8 0.1 reshape.209
  300.9 11.3 %gather_fusion.2 = bf16[1024,2,16,128]{3,2,1,0:T(8,128)(2,1)} fusion(bf16[192,2,16,128]{3,2,1,0:T(8,128)(2,1)} %bitcast.114, s32[1024]{0:T(1024)S(1)} %broadcast_clamp_fusion), kind=kCustom, calls=%fused_computation.2 | custom fusion | bytes 16781312 | tf_op jit(solution)/shard_map/gather | solution.py:74
  312.2 27.0 %all-to-all-start = ((bf16[64,2,8,2,16,1,128]{6,4,3,2,1,5,0:T(8,128)(2,1)}), bf16[64,2,8,2,16,1,128]{6,4,3,2,1,5,0:T(8,128)(2,1)}, u32[]{:S(2)}, u32[]{:S(2)}) async-start(bf16[64,2,8,2,16,1,128]{6,4,3,2,1,5,0:T(8,128)(2,1)} %bitcast.116), calls=%async_computation.1 | async-start | bytes 16777216 | tf_op jit(solution)/shard_map/all_to_all | solution.py:75
  339.3 0.1 reshape.191
  339.4 2.0 gather_fusion
  341.4 0.8 iota_compare_fusion.2
  342.1 1.5 fusion.44
  343.6 1.7 fusion.42
  345.3 0.7 fusion.43
  346.0 0.2 fusion.14
  346.2 0.4 fusion.8
  346.6 0.4 fusion.9
  347.0 0.5 copy-done.5
  347.5 0.3 fusion.7
  347.8 0.1 copy.39
  347.9 1.9 convolution_convert_fusion
  349.9 0.2 convert_reduce_fusion.1
  350.1 41.6 %reduce-scatter.2.cloned.1.call-done = bf16[32,2560]{1,0:T(8,128)(2,1)} async-done(((bf16[256,2560]{1,0:T(8,128)(2,1)}), bf16[32,2560]{1,0:T(8,128)(2,1)}) %reduce-scatter.2.cloned.1.call-update) | async-done | bytes 163856 | tf_op jit(solution)/shard_map/reduce_scatter | solution.py:95
  391.8 1.6 convert_add_fusion
  393.4 0.1 fusion.26
  393.5 0.2 fusion.29
  393.7 0.5 add_divide_fusion
  394.3 237.2 %all-to-all-done = bf16[64,2,8,2,16,1,128]{6,4,3,2,1,5,0:T(8,128)(2,1)} async-done(((bf16[64,2,8,2,16,1,128]{6,4,3,2,1,5,0:T(8,128)(2,1)}), bf16[64,2,8,2,16,1,128]{6,4,3,2,1,5,0:T(8,128)(2,1)}, u32[]{:S(2)}, u32[]{:S(2)}) %all-to-all-start) | async-done | bytes 8388640 | tf_op jit(solution)/shard_map/all_to_all | solution.py:75
  631.5 6.2 gather_fusion.3
  (43 shorter events, 0.6 us)
Async XLA Ops:
  7.2 340.7 %copy-start = (bf16[384,2560]{1,0:T(8,128)(2,1)S(1)}, bf16[384,2560]{1,0:T(8,128)(2,1)}, u32[]{:S(2)}) copy-start(bf16[384,2560]{1,0:T(8,128)(2,1)} %param.15) | copy-start | bytes 5898244
  312.2 27.0 %copy-start.2 = (s32[16,12]{1,0:T(8,128)S(1)}, s32[16,12]{1,0:T(8,128)}, u32[]{:S(2)}) copy-start(s32[16,12]{1,0:T(8,128)} %param.13) | copy-start | bytes 2308
  312.2 27.1 %copy-start.1 = (bf16[192,2,16,1,128]{4,2,3,1,0:T(8,128)(2,1)S(1)}, bf16[192,2,16,1,128]{4,2,3,1,0:T(8,128)(2,1)}, u32[]{:S(2)}) copy-start(bf16[192,2,16,1,128]{4,2,3,1,0:T(8,128)(2,1)} %param.12) | copy-start | bytes 4718596
  312.2 319.3 %all-to-all-start = ((bf16[64,2,8,2,16,1,128]{6,4,3,2,1,5,0:T(8,128)(2,1)}), bf16[64,2,8,2,16,1,128]{6,4,3,2,1,5,0:T(8,128)(2,1)}, u32[]{:S(2)}, u32[]{:S(2)}) async-start(bf16[64,2,8,2,16,1,128]{6,4,3,2,1,5,0:T(8,128)(2,1)} %bitcast.116), calls=%async_computation.1 | async-start | bytes 16777216 | tf_op jit(solution)/shard_map/all_to_all | solution.py:75
  339.2 52.6 %reduce-scatter.2.cloned.1.call-start = ((), (), s32[]{:S(2)}) async-start(), calls=%async_computation.2 | async-start | bytes 1474560 | tf_op jit(solution)/shard_map/reduce_scatter | solution.py:95
  341.4 3.9 copy-start.3
  346.6 0.9 copy-start.5
  347.9 2.0 copy-start.6
  347.9 2.0 copy-start.7
  347.9 2.0 copy-start.8
  347.9 43.8 %copy-start.4 = (bf16[32,2560]{1,0:T(8,128)(2,1)S(1)}, bf16[32,2560]{1,0:T(8,128)(2,1)}, u32[]{:S(2)}) copy-start(bf16[32,2560]{1,0:T(8,128)(2,1)} %param.16) | copy-start | bytes 491524
Sparse Core Ops, SparseCore 0:
  350.0 41.7 reduce-scatter.1
where the time goes:
time: 645 us
  blocking collectives  288 us (45%)
  waiting for transfers between devices  279 us (43%)
  starting transfers between devices  27 us (4%)
  local copies, waits for them, and re-layouts  26.2 us (4%)
  between operations  15 us (2%)
    unnamed x1, blocking collectives  288 us
    all_to_all x1, waiting for transfers between devices, fork_pages(): lax.all_to_all(blocks, 'dp', split_axis=0, concat_axis=0, tiled=True)  237 us
    reduce_scatter x1, waiting for transfers between devices, local(): lax.psum_scatter(jnp.dot(attended, out_proj, preferred_element_type=jnp.f...  41.6 us
    all_to_all x1, starting transfers between devices, fork_pages(): lax.all_to_all(blocks, 'dp', split_axis=0, concat_axis=0, tiled=True)  27 us
  transfers between devices with their start and end apart: 2, of which 2 were waited for; matrix products, arithmetic and copies ran while one was open for 2% of the time, Pallas kernels for 0%

commit v1 on v0

--- a/solution.py
+++ b/solution.py
@@ -7,7 +7,6 @@
 CH = 16
 PAGE = 16
 PREFIX = 128
-CAP = 2
 
 
 neg_fill = -1e30
@@ -54,27 +53,35 @@
     return attended.astype(jnp.bfloat16).reshape(branch * steps_new, qheads * head_width)
 
 
-def same_owner_rank(owners):
-    places = jnp.arange(owners.shape[-1])
-    matching = owners[..., :, None] == owners[..., None, :]
-    before = places[None, :] < places[:, None]
-    return jnp.sum((matching & before).astype(jnp.int32), axis=-1)
+def parent_listing(fork_parent):
+    groups = lax.axis_size("dp")
+    slots = fork_parent.shape[0]
+    row = jnp.pad(fork_parent, (0, 128 - slots))
+    copies = jnp.broadcast_to(row[None, None, :], (groups, 1, 128))
+    return lax.all_to_all(copies, "dp", split_axis=0, concat_axis=0, tiled=True)[:, 0, :slots]
 
 
 def fork_pages(listing, fork_parent, kv_cache, page_table):
     groups = lax.axis_size("dp")
     me_index = lax.axis_index("dp")
     prefix_count = PREFIX // PAGE
+    flat = listing.reshape(1, -1)
+    asked = (flat // BR_DEV) == jnp.arange(groups)[:, None]
+    lowest = jnp.min(jnp.where(asked, flat % BR_DEV, BR_DEV - 1), axis=1)
+    highest = jnp.max(jnp.where(asked, flat % BR_DEV, 0), axis=1)
+    mine = jnp.arange(groups) == me_index
+    chosen = jnp.stack(
+        [jnp.sum(jnp.where(mine, lowest, 0)), jnp.sum(jnp.where(mine, highest, 0))]
+    )
+    blocks = kv_cache[page_table[chosen][..., :prefix_count]]
+    tile = blocks.shape
+    gathered = lax.all_gather(blocks.reshape(-1, tile[-1]), "dp", axis=0, tiled=True)
+    gathered = gathered.reshape((groups * 2,) + tile[1:])
     my_owner = fork_parent // BR_DEV
-    owners = (listing // BR_DEV).reshape(groups, -1)
-    local_rows = (listing % BR_DEV).reshape(groups, -1)
-    ranks = same_owner_rank(owners)
-    hits = (owners == me_index)[:, :, None] & (ranks[:, :, None] == jnp.arange(CAP)[None, None, :])
-    chosen = jnp.sum(jnp.where(hits, local_rows[:, :, None], 0), axis=1)
-    blocks = kv_cache[page_table[chosen][..., :prefix_count]]
-    arrived = lax.all_to_all(blocks, "dp", split_axis=0, concat_axis=0, tiled=True)
-    my_rank = same_owner_rank(my_owner)
-    return arrived[my_owner, my_rank]
+    hit = my_owner[:, None] == jnp.arange(groups)[None, :]
+    first = jnp.sum(jnp.where(hit, lowest[None, :], 0), axis=1)
+    second = (fork_parent % BR_DEV != first).astype(jnp.int32)
+    return gathered[my_owner * 2 + second]
 
 
 def local(
@@ -89,16 +96,15 @@
     score_weight,
     fork_parent,
 ):
-    listing = lax.all_gather(fork_parent, "dp", axis=0, tiled=True)
+    listing = parent_listing(fork_parent)
     attended = attend(queries, new_kv, kv_cache, page_table, lengths)
     rows_here = residual.shape[0]
-    summed = lax.psum_scatter(
-        jnp.dot(attended, out_proj, preferred_element_type=jnp.float32).astype(jnp.bfloat16),
-        "tensor",
-        scatter_dimension=0,
-        tiled=True,
-    ).astype(jnp.float32)
-    updated = summed + residual.astype(jnp.float32)
+    shards = lax.axis_size("tensor")
+    partial = jnp.dot(attended, out_proj, preferred_element_type=jnp.float32).astype(jnp.bfloat16)
+    terms = lax.all_to_all(
+        partial.reshape(shards, rows_here, -1), "tensor", split_axis=0, concat_axis=0, tiled=True
+    )
+    updated = jnp.sum(terms.astype(jnp.float32), axis=0) + residual.astype(jnp.float32)
     hidden_out = updated.astype(jnp.bfloat16)
     block_ends = updated.reshape(rows_here // CH, CH, updated.shape[1])[:, CH - 1]
     normed = (

time: 645 us -> 209 us (0.32)
  blocking collectives: 288 us -> 0 us
  waiting for transfers between devices: 279 us -> 143 us
  local copies, waits for them, and re-layouts: 26.2 us -> 15.1 us
    unnamed x1 -> x0, blocking collectives: 288 us -> none
    all_to_all x1 -> x2, waiting for transfers between devices: 237 us -> 31 us  [the longest x1 18.5 us: local(): lax.all_to_all(partial.reshape(shards, rows_here, -1), 'tensor', split_ax...]
    all_gather x0 -> x1, waiting for transfers between devices: none -> 112 us  [fork_pages(): lax.all_gather(blocks.reshape(-1, tile[-1]), 'dp', axis=0, tiled=True)]
    reduce_scatter x1 -> x0, waiting for transfers between devices: 41.6 us -> none  [local(): lax.psum_scatter(jnp.dot(attended, out_proj, preferred_element_type=jnp.f...]
    gather x2, local copies, waits for them, and re-layouts: 12.7 us -> 3.88 us  [fork_pages(): blocks = kv_cache[page_table[chosen][..., :prefix_count]]]
    all_to_all x1 -> x2, starting transfers between devices: 27 us -> 22.9 us  [the longest x1 18.5 us: parent_listing(): lax.all_to_all(copies, 'dp', split_axis=0, concat_axis=0, tiled=True)]
  transfers between devices with their start and end apart: 2 -> 3, of which waited for: 2 -> 3; matrix products, arithmetic and copies ran while one was open for 2% -> 5% of each run, Pallas kernels for 0% -> 0%
where the time goes in v1:
time: 209 us; the launch traced here: 206 us
  waiting for transfers between devices  143 us (68%)
  starting transfers between devices  23 us (11%)
  local copies, waits for them, and re-layouts  15.1 us (7%)
  between operations  14.3 us (7%)
  other arithmetic  5.68 us (3%)
  matrix products  4.77 us (2%)
    all_gather x1, waiting for transfers between devices, fork_pages(): lax.all_gather(blocks.reshape(-1, tile[-1]), 'dp', axis=0, tiled=True)  112 us
    all_to_all x1, starting transfers between devices, parent_listing(): lax.all_to_all(copies, 'dp', split_axis=0, concat_axis=0, tiled=True)  18.5 us
    all_to_all x1, waiting for transfers between devices, local(): lax.all_to_all(partial.reshape(shards, rows_here, -1), 'tensor', split_ax...  18.5 us
    all_to_all x1, waiting for transfers between devices, parent_listing(): lax.all_to_all(copies, 'dp', split_axis=0, concat_axis=0, tiled=True)  12.5 us
    gather x1, local copies, waits for them, and re-layouts, fork_pages(): return gathered[my_owner * 2 + second]  6.1 us
    all_to_all x1, starting transfers between devices, local(): lax.all_to_all(partial.reshape(shards, rows_here, -1), 'tensor', split_ax...  4.45 us
  transfers between devices with their start and end apart: 3, of which 3 were waited for; matrix products, arithmetic and copies ran while one was open for 5% of the time, Pallas kernels for 0%

profile of v1, /device:TPU:24, one launch (start us, length us, event | category | flops | bytes accessed | tf_op | source)
XLA Modules:
  0.0 205.8 jit_solution(5628673838706127793)
XLA Ops:
  7.2 0.8 pad.4
  8.0 0.6 broadcast_in_dim.116
  8.6 18.5 %all-to-all-start.1 = ((s32[64,1,128]{2,1,0:T(1,128)}), s32[64,1,128]{2,1,0:T(1,128)S(1)}, u32[]{:S(2)}, u32[]{:S(2)}) async-start(s32[64,1,128]{2,1,0:T(1,128)} %broadcast_in_dim.116), calls=%async_computation.1 | async-start | bytes 65536 | tf_op jit(solution)/shard_map/all_to_all | solution.py:61
  27.2 12.5 %all-to-all-done.1 = s32[64,1,128]{2,1,0:T(1,128)S(1)} async-done(((s32[64,1,128]{2,1,0:T(1,128)}), s32[64,1,128]{2,1,0:T(1,128)S(1)}, u32[]{:S(2)}, u32[]{:S(2)}) %all-to-all-start.1) | async-done | bytes 32800 | tf_op jit(solution)/shard_map/all_to_all | solution.py:61
  39.8 0.3 select_reduce_fusion.1
  40.2 0.6 fusion.31
  40.8 1.4 fusion.34
  42.2 1.3 gather_fusion.1
  43.5 2.6 %gather_fusion.2 = bf16[16,2,16,128]{3,2,1,0:T(8,128)(2,1)} fusion(bf16[192,2,16,128]{3,2,1,0:T(8,128)(2,1)} %bitcast.103, s32[1024]{0:T(1024)S(1)} %pad_clamp_fusion.1), kind=kCustom, calls=%fused_computation.2 | custom fusion | bytes 262208 | tf_op jit(solution)/shard_map/gather | solution.py:76
  46.2 0.7 compare_select_fusion
  46.9 0.1 reshape.327
  47.0 2.3 %gather_fusion = bf16[192,2,16,128]{3,2,1,0:T(8,128)(2,1)S(1)} fusion(bf16[192,2,16,128]{3,2,1,0:T(8,128)(2,1)} %bitcast.104, s32[1024]{0:T(1024)S(1)} %pad_clamp_fusion.3), kind=kCustom, calls=%fused_computation | custom fusion | bytes 3146496 | tf_op jit(solution)/shard_map/gather | solution.py:19
  49.4 1.5 fusion.40
  50.9 0.4 fusion.38
  51.3 0.7 fusion.39
  52.1 0.2 fusion.14
  52.2 0.4 fusion.8
  52.6 0.4 fusion.9
  53.0 0.5 copy-done.3
  53.5 0.3 fusion.7
  53.8 0.1 copy.35
  53.9 1.9 convolution_convert_fusion
  55.9 4.4 %all-to-all-start = ((bf16[8,32,2560]{2,1,0:T(8,128)(2,1)}), bf16[8,32,2560]{2,1,0:T(8,128)(2,1)S(1)}, u32[]{:S(2)}, u32[]{:S(2)}) async-start(bf16[8,32,2560]{2,1,0:T(8,128)(2,1)} %bitcast.100), calls=%async_computation | async-start | bytes 2621440 | tf_op jit(solution)/shard_map/all_to_all | solution.py:104
  60.4 0.2 select_reduce_fusion.2
  60.6 18.5 %all-to-all-done = bf16[8,32,2560]{2,1,0:T(8,128)(2,1)S(1)} async-done(((bf16[8,32,2560]{2,1,0:T(8,128)(2,1)}), bf16[8,32,2560]{2,1,0:T(8,128)(2,1)S(1)}, u32[]{:S(2)}, u32[]{:S(2)}) %all-to-all-start) | async-done | bytes 1310752 | tf_op jit(solution)/shard_map/all_to_all | solution.py:104
  79.1 0.2 convert_reduce_fusion
  79.3 0.7 fusion.37
  80.0 0.1 fusion.25
  80.1 0.2 fusion.28
  80.3 0.5 add_divide_fusion
  80.9 111.9 %all-gather.2.cloned.1.call-done = bf16[32768,128]{1,0:T(8,128)(2,1)} async-done(((bf16[512,128]{1,0:T(8,128)(2,1)}), bf16[32768,128]{1,0:T(8,128)(2,1)}) %all-gather.2.cloned.1.call-update) | async-done | bytes 8388624 | tf_op jit(solution)/shard_map/all_gather | solution.py:78
  192.8 6.1 %gather_fusion.3 = bf16[48,8,2,16,128]{4,3,2,1,0:T(8,128)(2,1)} fusion(bf16[128,8,2,16,128]{4,3,2,1,0:T(8,128)(2,1)} %bitcast.105, s32[1024]{0:T(1024)S(1)} %pad_clamp_fusion), kind=kCustom, calls=%fused_computation.3 | custom fusion | bytes 6291648 | tf_op jit(solution)/shard_map/gather | solution.py:84
  (36 shorter events, 0.6 us)
Async XLA Ops:
  7.2 46.8 %copy-start = (bf16[384,2560]{1,0:T(8,128)(2,1)S(1)}, bf16[384,2560]{1,0:T(8,128)(2,1)}, u32[]{:S(2)}) copy-start(bf16[384,2560]{1,0:T(8,128)(2,1)} %param.15) | copy-start | bytes 5898244
  7.2 42.1 %copy-start.6 = (s32[16]{0:T(128)S(1)}, s32[16]{0:T(128)}, u32[]{:S(2)}) copy-start(s32[16]{0:T(128)} %param.14) | copy-start | bytes 196
  8.6 31.0 %all-to-all-start.1 = ((s32[64,1,128]{2,1,0:T(1,128)}), s32[64,1,128]{2,1,0:T(1,128)S(1)}, u32[]{:S(2)}, u32[]{:S(2)}) async-start(s32[64,1,128]{2,1,0:T(1,128)} %broadcast_in_dim.116), calls=%async_computation.1 | async-start | bytes 65536 | tf_op jit(solution)/shard_map/all_to_all | solution.py:61
  27.1 165.7 %all-gather.2.cloned.1.call-start = ((), (), s32[]{:S(2)}) async-start(), calls=%async_computation.2 | async-start | bytes 8519680 | tf_op jit(solution)/shard_map/all_gather | solution.py:78
  49.3 2.0 copy-start.1
  52.6 0.9 copy-start.3
  55.8 4.5 %copy-start.4 = (bf16[2560]{0:T(1024)(128)(2,1)S(1)}, bf16[2560]{0:T(1024)(128)(2,1)}, u32[]{:S(2)}) copy-start(bf16[2560]{0:T(1024)(128)(2,1)} %param.17) | copy-start | bytes 15364
  55.8 4.5 %copy-start.5 = (bf16[2560]{0:T(1024)(128)(2,1)S(1)}, bf16[2560]{0:T(1024)(128)(2,1)}, u32[]{:S(2)}) copy-start(bf16[2560]{0:T(1024)(128)(2,1)} %param.18) | copy-start | bytes 15364
  55.8 4.5 %copy-start.7 = (s32[48]{0:T(128)S(1)}, s32[48]{0:T(128)}, u32[]{:S(2)}) copy-start(s32[48]{0:T(128)} %param.19) | copy-start | bytes 580
  55.8 23.4 %copy-start.2 = (bf16[32,2560]{1,0:T(8,128)(2,1)S(1)}, bf16[32,2560]{1,0:T(8,128)(2,1)}, u32[]{:S(2)}) copy-start(bf16[32,2560]{1,0:T(8,128)(2,1)} %param.16) | copy-start | bytes 491524
  55.9 23.2 %all-to-all-start = ((bf16[8,32,2560]{2,1,0:T(8,128)(2,1)}), bf16[8,32,2560]{2,1,0:T(8,128)(2,1)S(1)}, u32[]{:S(2)}, u32[]{:S(2)}) async-start(bf16[8,32,2560]{2,1,0:T(8,128)(2,1)} %bitcast.100), calls=%async_computation | async-start | bytes 2621440 | tf_op jit(solution)/shard_map/all_to_all | solution.py:104
Sparse Core Ops, SparseCore 0:
  46.3 146.4 all-gather.1

commit v2 on v1

--- a/solution.py
+++ b/solution.py
@@ -1,16 +1,20 @@
 import jax
 import jax.numpy as jnp
 from jax import lax
+from jax.experimental import pallas as pl
+from jax.experimental.pallas import tpu as pltpu
 from jax.sharding import PartitionSpec as P
 
 BR_DEV = 16
 CH = 16
 PAGE = 16
 PREFIX = 128
+PAGES = PREFIX // PAGE
+NZ, NY = 16, 4
+LANES = 128
 
 
 neg_fill = -1e30
-
 
 def attend(queries, new_kv, kv_cache, page_table, lengths):
     branch, steps_new, qheads, head_width = queries.shape
@@ -56,32 +60,123 @@
 def parent_listing(fork_parent):
     groups = lax.axis_size("dp")
     slots = fork_parent.shape[0]
-    row = jnp.pad(fork_parent, (0, 128 - slots))
-    copies = jnp.broadcast_to(row[None, None, :], (groups, 1, 128))
-    return lax.all_to_all(copies, "dp", split_axis=0, concat_axis=0, tiled=True)[:, 0, :slots]
+    row = jnp.pad(fork_parent, (0, LANES - slots), constant_values=-1)
+    copies = jnp.broadcast_to(row[None, None, :], (groups, 1, LANES))
+    return lax.all_to_all(copies, "dp", split_axis=0, concat_axis=0, tiled=True)[:, 0]
+
+
+def shift_z(step):
+    return [(z * NY + y, (z + step) % NZ * NY + y) for z in range(NZ) for y in range(NY)]
+
+
+def shift_y(step):
+    return [(z * NY + y, z * NY + (y + step) % NY) for z in range(NZ) for y in range(NY)]
+
+
+def pick_kernel(me_ref, listing_ref, table_ref, cache_ref, low_ref, high_ref, sems):
+    asked = listing_ref[...]
+    mine = (asked >> 4) == me_ref[0]
+    rows = asked & (BR_DEV - 1)
+    lowest = jnp.min(jnp.where(mine, rows, BR_DEV - 1))
+    highest = jnp.max(jnp.where(mine, rows, 0))
+    copies = []
+    for which, (row, out) in enumerate(((lowest, low_ref), (highest, high_ref))):
+        for page in range(PAGES):
+            copies.append(
+                pltpu.make_async_copy(
+                    cache_ref.at[table_ref[row, page]], out.at[page], sems.at[which, page]
+                )
+            )
+    for copy in copies:
+        copy.start()
+    for copy in copies:
+        copy.wait()
+
+
+def pick_pages(me_index, listing, page_table, cache):
+    block = jax.ShapeDtypeStruct((PAGES,) + cache.shape[1:], cache.dtype)
+    return pl.pallas_call(
+        pick_kernel,
+        out_shape=(block, block),
+        in_specs=[
+            pl.BlockSpec(memory_space=pltpu.SMEM),
+            pl.BlockSpec(memory_space=pltpu.VMEM),
+            pl.BlockSpec(memory_space=pltpu.SMEM),
+            pl.BlockSpec(memory_space=pl.ANY),
+        ],
+        out_specs=(pl.BlockSpec(memory_space=pl.ANY), pl.BlockSpec(memory_space=pl.ANY)),
+        scratch_shapes=[pltpu.SemaphoreType.DMA((2, PAGES))],
+    )(me_index.reshape(1), listing, page_table, cache)
+
+
+def place_kernel(array_ref, index_ref, *refs):
+    sources, out_ref, sems = refs[:-2], refs[-2], refs[-1]
+    slots = out_ref.shape[0]
+
+    @pl.loop(0, slots)
+    def _(slot):
+        for number, source in enumerate(sources):
+
+            @pl.when(array_ref[slot] == number)
+            def _():
+                pltpu.make_async_copy(
+                    source.at[index_ref[slot]], out_ref.at[slot], sems.at[slot]
+                ).start()
+
+    @pl.loop(0, slots)
+    def _(slot):
+        pltpu.make_async_copy(sources[0].at[0], out_ref.at[slot], sems.at[slot]).wait()
+
+
+def place_children(array_of, index_of, sources):
+    slots = array_of.shape[0]
+    return pl.pallas_call(
+        place_kernel,
+        out_shape=jax.ShapeDtypeStruct((slots,) + sources[0].shape[1:], sources[0].dtype),
+        in_specs=[pl.BlockSpec(memory_space=pltpu.SMEM)] * 2
+        + [pl.BlockSpec(memory_space=pl.ANY)] * len(sources),
+        out_specs=pl.BlockSpec(memory_space=pl.ANY),
+        scratch_shapes=[pltpu.SemaphoreType.DMA((slots,))],
+    )(array_of, index_of, *sources)
+
+
+def spread(block, shifts):
+    return [block] + [lax.ppermute(block, "dp", pairs) for pairs in shifts]
 
 
 def fork_pages(listing, fork_parent, kv_cache, page_table):
-    groups = lax.axis_size("dp")
     me_index = lax.axis_index("dp")
-    prefix_count = PREFIX // PAGE
-    flat = listing.reshape(1, -1)
-    asked = (flat // BR_DEV) == jnp.arange(groups)[:, None]
-    lowest = jnp.min(jnp.where(asked, flat % BR_DEV, BR_DEV - 1), axis=1)
-    highest = jnp.max(jnp.where(asked, flat % BR_DEV, 0), axis=1)
-    mine = jnp.arange(groups) == me_index
-    chosen = jnp.stack(
-        [jnp.sum(jnp.where(mine, lowest, 0)), jnp.sum(jnp.where(mine, highest, 0))]
-    )
-    blocks = kv_cache[page_table[chosen][..., :prefix_count]]
-    tile = blocks.shape
-    gathered = lax.all_gather(blocks.reshape(-1, tile[-1]), "dp", axis=0, tiled=True)
-    gathered = gathered.reshape((groups * 2,) + tile[1:])
-    my_owner = fork_parent // BR_DEV
-    hit = my_owner[:, None] == jnp.arange(groups)[None, :]
-    first = jnp.sum(jnp.where(hit, lowest[None, :], 0), axis=1)
-    second = (fork_parent % BR_DEV != first).astype(jnp.int32)
-    return gathered[my_owner * 2 + second]
+    me_z, me_y = me_index // NY, me_index % NY
+    cache = kv_cache[:, :, :, 0]
+    width = cache.shape[-1]
+    low, high = pick_pages(me_index, listing, page_table, cache)
+    rows = low.size // width
+    both = jnp.concatenate([low.reshape(rows, width), high.reshape(rows, width)])
+
+    far = spread(both, [shift_z(4), shift_z(8), shift_z(12)])
+    low_far = jnp.concatenate([part[:rows] for part in far])
+    high_far = jnp.concatenate([part[rows:] for part in far])
+    near = [shift_z(1), shift_z(2), shift_z(-1)]
+    across = [shift_y(1), shift_y(2), shift_y(3)]
+    low_column = jnp.concatenate(spread(low_far, near))
+    high_plane = jnp.concatenate(spread(high_far, across))
+    low_column, high_plane = lax.optimization_barrier((low_column, high_plane))
+    sources = spread(low_column, across) + spread(high_plane, near)
+    sources = [part.reshape((NZ,) + low.shape) for part in sources]
+
+    owner = fork_parent // BR_DEV
+    asked = listing.reshape(1, -1)
+    same = (asked // BR_DEV) == owner[:, None]
+    first = jnp.min(jnp.where(same, asked % BR_DEV, BR_DEV - 1), axis=1)
+    is_low = fork_parent % BR_DEV == first
+    apart_z = (me_z - owner // NY) % NZ
+    apart_y = (me_y - owner % NY) % NY
+    near_z = apart_z % 4
+    far_z = jnp.where(near_z == 3, apart_z + 1, apart_z) // 4 % 4
+    array_of = jnp.where(is_low, apart_y, 4 + near_z)
+    index_of = jnp.where(is_low, near_z, apart_y) * 4 + far_z
+    placed = place_children(array_of.astype(jnp.int32), index_of.astype(jnp.int32), sources)
+    return placed[:, :, :, :, None]
 
 
 def local(

time: 209 us -> 303 us (1.45)
  Pallas kernels: 0 us -> 104 us
  starting transfers between devices: 23 us -> 83.6 us
  waiting for transfers between devices: 143 us -> 83.9 us
  between operations: 14.3 us -> 1.06 us
    all_gather x1 -> x0, waiting for transfers between devices: 112 us -> none  [fork_pages(): lax.all_gather(blocks.reshape(-1, tile[-1]), 'dp', axis=0, tiled=True)]
    pallas_call x0 -> x2, Pallas kernels: none -> 104 us  [the longest x1 97.5 us: place_children(): pl.pallas_call(place_kernel, out_shape=jax.ShapeDtypeStruct((slots,) + so...]
    ppermute x0 -> x15, waiting for transfers between devices: none -> 78.7 us  [spread(): return [block] + [lax.ppermute(block, 'dp', pairs) for pairs in shifts]]
    ppermute x0 -> x15, starting transfers between devices: none -> 60.6 us  [spread(): return [block] + [lax.ppermute(block, 'dp', pairs) for pairs in shifts]]
    all_to_all x1, waiting for transfers between devices: 18.5 us -> 0.01 us  [local(): lax.all_to_all(partial.reshape(shards, rows_here, -1), 'tensor', split_ax...]
    gather x3 -> x0, local copies, waits for them, and re-layouts: 9.98 us -> none  [the longest x1 6.1 us: fork_pages(): return gathered[my_owner * 2 + second]]
    all_to_all x1, waiting for transfers between devices: 12.5 us -> 5.23 us  [parent_listing(): lax.all_to_all(copies, 'dp', split_axis=0, concat_axis=0, tiled=True)[:, 0]]
    unnamed x16 -> x27, local copies, waits for them, and re-layouts: 0.52 us -> 7.01 us
  transfers between devices with their start and end apart: 3 -> 17, of which waited for: 3 -> 6; matrix products, arithmetic and copies ran while one was open for 5% -> 7% of each run, Pallas kernels for 0% -> 0%
where the time goes in v2:
time: 303 us; the launch traced here: 300 us
  Pallas kernels  104 us (34%)
  waiting for transfers between devices  83.9 us (28%)
  starting transfers between devices  83.6 us (28%)
  local copies, waits for them, and re-layouts  14.9 us (5%)
  other arithmetic  7.04 us (2%)
  matrix products  5.57 us (2%)
    pallas_call x1, Pallas kernels, place_children(): pl.pallas_call(place_kernel, out_shape=jax.ShapeDtypeStruct((slots,) + so...  97.5 us
    ppermute x15, waiting for transfers between devices, spread(): return [block] + [lax.ppermute(block, 'dp', pairs) for pairs in shifts]  78.7 us
    ppermute x15, starting transfers between devices, spread(): return [block] + [lax.ppermute(block, 'dp', pairs) for pairs in shifts]  60.6 us
    all_to_all x1, starting transfers between devices, parent_listing(): lax.all_to_all(copies, 'dp', split_axis=0, concat_axis=0, tiled=True)[:, 0]  18.7 us
    unnamed x27, local copies, waits for them, and re-layouts  7.01 us
    pallas_call x1, Pallas kernels, pick_pages(): pl.pallas_call(pick_kernel, out_shape=(block, block), in_specs=[pl.BlockS...  6.35 us
  transfers between devices with their start and end apart: 17, of which 6 were waited for; matrix products, arithmetic and copies ran while one was open for 7% of the time, Pallas kernels for 0%

profile of v2, /device:TPU:24, one launch (start us, length us, event | category | flops | bytes accessed | tf_op | source)
XLA Modules:
  0.0 300.0 jit_solution(10195325297055535968)
XLA Ops:
  2.1 18.7 %all-to-all-start.1 = ((s32[64,1,128]{2,1,0:T(1,128)}), s32[64,1,128]{2,1,0:T(1,128)}, u32[]{:S(2)}, u32[]{:S(2)}) async-start(s32[64,1,128]{2,1,0:T(1,128)} %broadcast_in_dim.86), calls=%async_computation.1 | async-start | bytes 65536 | tf_op jit(solution)/shard_map/all_to_all | solution.py:65
  21.6 2.3 gather_fusion
  26.6 1.2 fusion.9
  27.8 5.2 %all-to-all-done.1 = s32[64,1,128]{2,1,0:T(1,128)} async-done(((s32[64,1,128]{2,1,0:T(1,128)}), s32[64,1,128]{2,1,0:T(1,128)}, u32[]{:S(2)}, u32[]{:S(2)}) %all-to-all-start.1) | async-done | bytes 32800 | tf_op jit(solution)/shard_map/all_to_all | solution.py:65
  33.0 6.4 %shard_map.121 = (bf16[8,2,16,128]{3,2,1,0:T(8,128)(2,1)}, bf16[8,2,16,128]{3,2,1,0:T(8,128)(2,1)}) custom-call(s32[1]{0:T(128)} %bitcast.26.me_ref, s32[64,128]{1,0:T(8,128)} %bitcast.27.listing_ref, s32[16,12]{1,0:T(8,128)} %table_ref.1, bf16[192,2,16,128]{3,2,1,0:T(8,128)(2,1)} %bitcast.105), custom_call_target="tpu_custom_call" | custom-call | tf_op jit(solution)/shard_map/pallas_call | solution.py:98
  40.4 3.1 %collective-permute-start = (bf16[512,128]{1,0:T(8,128)(2,1)S(1)}, bf16[512,128]{1,0:T(8,128)(2,1)S(1)}, u32[]{:S(2)}, u32[]{:S(2)}) collective-permute-start(bf16[512,128]{1,0:T(8,128)(2,1)S(1)} %pad_maximum_fusion.2), channel_id=1, source_target_pairs={{0,128},{8,136},{16,144},{24,152},{32,160},{40,168},{48,176},{56,1... | collective-permute-start | bytes 393224 | tf_op jit(solution)/shard_map/ppermute | solution.py:144
  43.4 1.3 fusion.7
  44.8 7.2 %collective-permute-start.1 = (bf16[512,128]{1,0:T(8,128)(2,1)S(1)}, bf16[512,128]{1,0:T(8,128)(2,1)S(1)}, u32[]{:S(2)}, u32[]{:S(2)}) collective-permute-start(bf16[512,128]{1,0:T(8,128)(2,1)S(1)} %pad_maximum_fusion.2), channel_id=1, source_target_pairs={{0,256},{8,264},{16,272},{24,280},{32,288},{40,296},{48,304},{56,3... | collective-permute-start | bytes 393224 | tf_op jit(solution)/shard_map/ppermute | solution.py:144
  52.0 6.5 %collective-permute-start.2 = (bf16[512,128]{1,0:T(8,128)(2,1)S(1)}, bf16[512,128]{1,0:T(8,128)(2,1)S(1)}, u32[]{:S(2)}, u32[]{:S(2)}) collective-permute-start(bf16[512,128]{1,0:T(8,128)(2,1)S(1)} %pad_maximum_fusion.2), channel_id=1, source_target_pairs={{0,384},{8,392},{16,400},{24,408},{32,416},{40,424},{48,432},{56,4... | collective-permute-start | bytes 393224 | tf_op jit(solution)/shard_map/ppermute | solution.py:144
  59.9 5.3 %collective-permute-done.1 = bf16[512,128]{1,0:T(8,128)(2,1)S(1)} collective-permute-done((bf16[512,128]{1,0:T(8,128)(2,1)S(1)}, bf16[512,128]{1,0:T(8,128)(2,1)S(1)}, u32[]{:S(2)}, u32[]{:S(2)}) %collective-permute-start.1) | collective-permute-done | bytes 131104 | tf_op jit(solution)/shard_map/ppermute | solution.py:144
  65.9 12.5 %collective-permute-done.2 = bf16[512,128]{1,0:T(8,128)(2,1)S(1)} collective-permute-done((bf16[512,128]{1,0:T(8,128)(2,1)S(1)}, bf16[512,128]{1,0:T(8,128)(2,1)S(1)}, u32[]{:S(2)}, u32[]{:S(2)}) %collective-permute-start.2) | collective-permute-done | bytes 131104 | tf_op jit(solution)/shard_map/ppermute | solution.py:144
  79.8 2.8 collective-permute-start.6
  82.6 3.9 %collective-permute-start.7 = (bf16[1024,128]{1,0:T(8,128)(2,1)}, bf16[1024,128]{1,0:T(8,128)(2,1)}, u32[]{:S(2)}, u32[]{:S(2)}) collective-permute-start(bf16[1024,128]{1,0:T(8,128)(2,1)} %pad_maximum_fusion.1), channel_id=1, source_target_pairs={{0,16},{8,24},{16,0},{24,8},{32,48},{40,56},{48,32},{56,40},{64,80... | collective-permute-start | bytes 786440 | tf_op jit(solution)/shard_map/ppermute | solution.py:144
  86.5 1.9 convolution_convert_fusion
  88.4 4.3 %all-to-all-start = ((bf16[8,32,2560]{2,1,0:T(8,128)(2,1)}), bf16[8,32,2560]{2,1,0:T(8,128)(2,1)S(1)}, u32[]{:S(2)}, u32[]{:S(2)}) async-start(bf16[8,32,2560]{2,1,0:T(8,128)(2,1)} %bitcast.107), calls=%async_computation | async-start | bytes 2621440 | tf_op jit(solution)/shard_map/all_to_all | solution.py:199
  92.7 2.7 collective-permute-start.8
  95.5 1.9 collective-permute-start.3
  97.4 2.1 collective-permute-start.4
  99.5 5.1 %collective-permute-start.5 = (bf16[1024,128]{1,0:T(8,128)(2,1)S(1)}, bf16[1024,128]{1,0:T(8,128)(2,1)S(1)}, u32[]{:S(2)}, u32[]{:S(2)}) collective-permute-start(bf16[1024,128]{1,0:T(8,128)(2,1)S(1)} %pad_maximum_fusion), channel_id=1, source_target_pairs={{0,480},{8,488},{16,496},{24,504},{32,0},{40,8},{48,16},{56,24},{6... | collective-permute-start | bytes 786440 | tf_op jit(solution)/shard_map/ppermute | solution.py:144
  104.7 1.7 constant_dynamic-update-slice_fusion.9
  106.4 1.7 constant_dynamic-update-slice_fusion.8
  108.8 4.5 %collective-permute-done.3 = bf16[1024,128]{1,0:T(8,128)(2,1)S(1)} collective-permute-done((bf16[1024,128]{1,0:T(8,128)(2,1)S(1)}, bf16[1024,128]{1,0:T(8,128)(2,1)S(1)}, u32[]{:S(2)}, u32[]{:S(2)}) %collective-permute-start.3) | collective-permute-done | bytes 262176 | tf_op jit(solution)/shard_map/ppermute | solution.py:144
  115.5 4.3 %collective-permute-start.9 = (bf16[4096,128]{1,0:T(8,128)(2,1)}, bf16[4096,128]{1,0:T(8,128)(2,1)}, u32[]{:S(2)}, u32[]{:S(2)}) collective-permute-start(bf16[4096,128]{1,0:T(8,128)(2,1)} %constant_dynamic-update-slice_fusion), channel_id=1, source_target_pairs={{0,8},{8,16},{16,24},{24,0},{32,40},{40,48},{48,56},{56,32},{64,72... | collective-permute-start | bytes 3145736 | tf_op jit(solution)/shard_map/ppermute | solution.py:144
  122.2 2.2 collective-permute-start.10
  124.5 3.0 %collective-permute-start.11 = (bf16[4096,128]{1,0:T(8,128)(2,1)}, bf16[4096,128]{1,0:T(8,128)(2,1)}, u32[]{:S(2)}, u32[]{:S(2)}) collective-permute-start(bf16[4096,128]{1,0:T(8,128)(2,1)} %constant_dynamic-update-slice_fusion), channel_id=1, source_target_pairs={{0,24},{8,0},{16,8},{24,16},{32,56},{40,32},{48,40},{56,48},{64,88... | collective-permute-start | bytes 3145736 | tf_op jit(solution)/shard_map/ppermute | solution.py:144
  127.5 7.5 %collective-permute-start.12 = (bf16[4096,128]{1,0:T(8,128)(2,1)}, bf16[4096,128]{1,0:T(8,128)(2,1)}, u32[]{:S(2)}, u32[]{:S(2)}) collective-permute-start(bf16[4096,128]{1,0:T(8,128)(2,1)} %constant_dynamic-update-slice_fusion.7), channel_id=1, source_target_pairs={{0,32},{8,40},{16,48},{24,56},{32,64},{40,72},{48,80},{56,88},{64,... | collective-permute-start | bytes 3145736 | tf_op jit(solution)/shard_map/ppermute | solution.py:144
  135.1 1.9 collective-permute-start.13
  137.2 26.8 %collective-permute-done.9 = bf16[4096,128]{1,0:T(8,128)(2,1)} collective-permute-done((bf16[4096,128]{1,0:T(8,128)(2,1)}, bf16[4096,128]{1,0:T(8,128)(2,1)}, u32[]{:S(2)}, u32[]{:S(2)}) %collective-permute-start.9) | collective-permute-done | bytes 1048608 | tf_op jit(solution)/shard_map/ppermute | solution.py:144
  164.0 6.3 %collective-permute-start.14 = (bf16[4096,128]{1,0:T(8,128)(2,1)}, bf16[4096,128]{1,0:T(8,128)(2,1)S(1)}, u32[]{:S(2)}, u32[]{:S(2)}) collective-permute-start(bf16[4096,128]{1,0:T(8,128)(2,1)} %constant_dynamic-update-slice_fusion.7), channel_id=1, source_target_pairs={{0,480},{8,488},{16,496},{24,504},{32,0},{40,8},{48,16},{56,24},{6... | collective-permute-start | bytes 3145736 | tf_op jit(solution)/shard_map/ppermute | solution.py:144
  171.9 29.5 %collective-permute-done.13 = bf16[4096,128]{1,0:T(8,128)(2,1)} collective-permute-done((bf16[4096,128]{1,0:T(8,128)(2,1)}, bf16[4096,128]{1,0:T(8,128)(2,1)}, u32[]{:S(2)}, u32[]{:S(2)}) %collective-permute-start.13) | collective-permute-done | bytes 1048608 | tf_op jit(solution)/shard_map/ppermute | solution.py:144
  201.5 1.0 copy-done.1
  202.5 97.5 %shard_map.122 = bf16[48,8,2,16,128]{4,3,2,1,0:T(8,128)(2,1)} custom-call(s32[48]{0:T(128)} %add_select_fusion.2.array_ref, s32[48]{0:T(128)} %get-tuple-element.23.index_ref, bf16[16,8,2,16,128]{4,3,2,1,0:T(8,128)(2,1)} %bitcast.30.refs_0_, bf16[16,8,2,16,128]{4,3,2,1,0:T(8,128)(2,1)} %bitcast.31.refs_1_, bf16[16,8,2,16,128]{4,3,2,1,0:T(8,128)(2,1)} %bitcast.32.refs_2_, ...), custom_call_target="tpu_custom_call" | custom-call | tf_op jit(solution)/shard_map/pallas_call | solution.py:133
  (72 shorter events, 16.5 us)
Async XLA Ops:
  0.6 85.9 %copy-start = (bf16[384,2560]{1,0:T(8,128)(2,1)S(1)}, bf16[384,2560]{1,0:T(8,128)(2,1)}, u32[]{:S(2)}) copy-start(bf16[384,2560]{1,0:T(8,128)(2,1)} %param.15) | copy-start | bytes 5898244
  2.1 31.0 %all-to-all-start.1 = ((s32[64,1,128]{2,1,0:T(1,128)}), s32[64,1,128]{2,1,0:T(1,128)}, u32[]{:S(2)}, u32[]{:S(2)}) async-start(s32[64,1,128]{2,1,0:T(1,128)} %broadcast_in_dim.86), calls=%async_computation.1 | async-start | bytes 65536 | tf_op jit(solution)/shard_map/all_to_all | solution.py:65
  23.9 0.7 copy-start.10
  23.9 0.9 copy-start.2
  24.6 1.0 copy-start.6
  39.4 19.1 %copy-start.3 = (bf16[8,2,16,128]{3,2,1,0:T(8,128)(2,1)S(1)}, bf16[8,2,16,128]{3,2,1,0:T(8,128)(2,1)}, u32[]{:S(2)}) copy-start(bf16[8,2,16,128]{3,2,1,0:T(8,128)(2,1)} %get-tuple-element.7) | copy-start | bytes 196612
  39.4 19.1 %copy-start.4 = (bf16[8,2,16,128]{3,2,1,0:T(8,128)(2,1)S(1)}, bf16[8,2,16,128]{3,2,1,0:T(8,128)(2,1)}, u32[]{:S(2)}) copy-start(bf16[8,2,16,128]{3,2,1,0:T(8,128)(2,1)} %get-tuple-element.8) | copy-start | bytes 196612
  40.4 18.9 %collective-permute-start = (bf16[512,128]{1,0:T(8,128)(2,1)S(1)}, bf16[512,128]{1,0:T(8,128)(2,1)S(1)}, u32[]{:S(2)}, u32[]{:S(2)}) collective-permute-start(bf16[512,128]{1,0:T(8,128)(2,1)S(1)} %pad_maximum_fusion.2), channel_id=1, source_target_pairs={{0,128},{8,136},{16,144},{24,152},{32,160},{40,168},{48,176},{56,1... | collective-permute-start | bytes 393224 | tf_op jit(solution)/shard_map/ppermute | solution.py:144
  44.8 20.3 %collective-permute-start.1 = (bf16[512,128]{1,0:T(8,128)(2,1)S(1)}, bf16[512,128]{1,0:T(8,128)(2,1)S(1)}, u32[]{:S(2)}, u32[]{:S(2)}) collective-permute-start(bf16[512,128]{1,0:T(8,128)(2,1)S(1)} %pad_maximum_fusion.2), channel_id=1, source_target_pairs={{0,256},{8,264},{16,272},{24,280},{32,288},{40,296},{48,304},{56,3... | collective-permute-start | bytes 393224 | tf_op jit(solution)/shard_map/ppermute | solution.py:144
  52.0 26.4 %collective-permute-start.2 = (bf16[512,128]{1,0:T(8,128)(2,1)S(1)}, bf16[512,128]{1,0:T(8,128)(2,1)S(1)}, u32[]{:S(2)}, u32[]{:S(2)}) collective-permute-start(bf16[512,128]{1,0:T(8,128)(2,1)S(1)} %pad_maximum_fusion.2), channel_id=1, source_target_pairs={{0,384},{8,392},{16,400},{24,408},{32,416},{40,424},{48,432},{56,4... | collective-permute-start | bytes 393224 | tf_op jit(solution)/shard_map/ppermute | solution.py:144
  79.8 19.7 %collective-permute-start.6 = (bf16[1024,128]{1,0:T(8,128)(2,1)}, bf16[1024,128]{1,0:T(8,128)(2,1)}, u32[]{:S(2)}, u32[]{:S(2)}) collective-permute-start(bf16[1024,128]{1,0:T(8,128)(2,1)} %pad_maximum_fusion.1), channel_id=1, source_target_pairs={{0,8},{8,16},{16,24},{24,0},{32,40},{40,48},{48,56},{56,32},{64,72... | collective-permute-start | bytes 786440 | tf_op jit(solution)/shard_map/ppermute | solution.py:144
  82.6 23.7 %collective-permute-start.7 = (bf16[1024,128]{1,0:T(8,128)(2,1)}, bf16[1024,128]{1,0:T(8,128)(2,1)}, u32[]{:S(2)}, u32[]{:S(2)}) collective-permute-start(bf16[1024,128]{1,0:T(8,128)(2,1)} %pad_maximum_fusion.1), channel_id=1, source_target_pairs={{0,16},{8,24},{16,0},{24,8},{32,48},{40,56},{48,32},{56,40},{64,80... | collective-permute-start | bytes 786440 | tf_op jit(solution)/shard_map/ppermute | solution.py:144
  88.4 48.6 %all-to-all-start = ((bf16[8,32,2560]{2,1,0:T(8,128)(2,1)}), bf16[8,32,2560]{2,1,0:T(8,128)(2,1)S(1)}, u32[]{:S(2)}, u32[]{:S(2)}) async-start(bf16[8,32,2560]{2,1,0:T(8,128)(2,1)} %bitcast.107), calls=%async_computation | async-start | bytes 2621440 | tf_op jit(solution)/shard_map/all_to_all | solution.py:199
  92.7 15.3 %collective-permute-start.8 = (bf16[1024,128]{1,0:T(8,128)(2,1)}, bf16[1024,128]{1,0:T(8,128)(2,1)S(1)}, u32[]{:S(2)}, u32[]{:S(2)}) collective-permute-start(bf16[1024,128]{1,0:T(8,128)(2,1)} %pad_maximum_fusion.1), channel_id=1, source_target_pairs={{0,24},{8,0},{16,8},{24,16},{32,56},{40,32},{48,40},{56,48},{64,88... | collective-permute-start | bytes 786440 | tf_op jit(solution)/shard_map/ppermute | solution.py:144
  95.5 17.9 %collective-permute-start.3 = (bf16[1024,128]{1,0:T(8,128)(2,1)S(1)}, bf16[1024,128]{1,0:T(8,128)(2,1)S(1)}, u32[]{:S(2)}, u32[]{:S(2)}) collective-permute-start(bf16[1024,128]{1,0:T(8,128)(2,1)S(1)} %pad_maximum_fusion), channel_id=1, source_target_pairs={{0,32},{8,40},{16,48},{24,56},{32,64},{40,72},{48,80},{56,88},{64,... | collective-permute-start | bytes 786440 | tf_op jit(solution)/shard_map/ppermute | solution.py:144
  97.4 16.7 %collective-permute-start.4 = (bf16[1024,128]{1,0:T(8,128)(2,1)S(1)}, bf16[1024,128]{1,0:T(8,128)(2,1)S(1)}, u32[]{:S(2)}, u32[]{:S(2)}) collective-permute-start(bf16[1024,128]{1,0:T(8,128)(2,1)S(1)} %pad_maximum_fusion), channel_id=1, source_target_pairs={{0,64},{8,72},{16,80},{24,88},{32,96},{40,104},{48,112},{56,120},{... | collective-permute-start | bytes 786440 | tf_op jit(solution)/shard_map/ppermute | solution.py:144
  99.5 15.3 %collective-permute-start.5 = (bf16[1024,128]{1,0:T(8,128)(2,1)S(1)}, bf16[1024,128]{1,0:T(8,128)(2,1)S(1)}, u32[]{:S(2)}, u32[]{:S(2)}) collective-permute-start(bf16[1024,128]{1,0:T(8,128)(2,1)S(1)} %pad_maximum_fusion), channel_id=1, source_target_pairs={{0,480},{8,488},{16,496},{24,504},{32,0},{40,8},{48,16},{56,24},{6... | collective-permute-start | bytes 786440 | tf_op jit(solution)/shard_map/ppermute | solution.py:144
  104.6 15.2 %copy-start.9 = (s32[48]{0:T(128)S(1)}, s32[48]{0:T(128)}, u32[]{:S(2)}) copy-start(s32[48]{0:T(128)} %param.19) | copy-start | bytes 580
  104.6 15.3 %copy-start.7 = (bf16[2560]{0:T(1024)(128)(2,1)S(1)}, bf16[2560]{0:T(1024)(128)(2,1)}, u32[]{:S(2)}) copy-start(bf16[2560]{0:T(1024)(128)(2,1)} %param.17) | copy-start | bytes 15364
  104.7 15.3 %copy-start.8 = (bf16[2560]{0:T(1024)(128)(2,1)S(1)}, bf16[2560]{0:T(1024)(128)(2,1)}, u32[]{:S(2)}) copy-start(bf16[2560]{0:T(1024)(128)(2,1)} %param.18) | copy-start | bytes 15364
  114.1 56.2 %copy-start.5 = (bf16[32,2560]{1,0:T(8,128)(2,1)S(1)}, bf16[32,2560]{1,0:T(8,128)(2,1)}, u32[]{:S(2)}) copy-start(bf16[32,2560]{1,0:T(8,128)(2,1)} %param.16) | copy-start | bytes 491524
  115.5 48.4 %collective-permute-start.9 = (bf16[4096,128]{1,0:T(8,128)(2,1)}, bf16[4096,128]{1,0:T(8,128)(2,1)}, u32[]{:S(2)}, u32[]{:S(2)}) collective-permute-start(bf16[4096,128]{1,0:T(8,128)(2,1)} %constant_dynamic-update-slice_fusion), channel_id=1, source_target_pairs={{0,8},{8,16},{16,24},{24,0},{32,40},{40,48},{48,56},{56,32},{64,72... | collective-permute-start | bytes 3145736 | tf_op jit(solution)/shard_map/ppermute | solution.py:144
  122.2 49.7 %collective-permute-start.10 = (bf16[4096,128]{1,0:T(8,128)(2,1)}, bf16[4096,128]{1,0:T(8,128)(2,1)}, u32[]{:S(2)}, u32[]{:S(2)}) collective-permute-start(bf16[4096,128]{1,0:T(8,128)(2,1)} %constant_dynamic-update-slice_fusion), channel_id=1, source_target_pairs={{0,16},{8,24},{16,0},{24,8},{32,48},{40,56},{48,32},{56,40},{64,80... | collective-permute-start | bytes 3145736 | tf_op jit(solution)/shard_map/ppermute | solution.py:144
  124.5 47.5 %collective-permute-start.11 = (bf16[4096,128]{1,0:T(8,128)(2,1)}, bf16[4096,128]{1,0:T(8,128)(2,1)}, u32[]{:S(2)}, u32[]{:S(2)}) collective-permute-start(bf16[4096,128]{1,0:T(8,128)(2,1)} %constant_dynamic-update-slice_fusion), channel_id=1, source_target_pairs={{0,24},{8,0},{16,8},{24,16},{32,56},{40,32},{48,40},{56,48},{64,88... | collective-permute-start | bytes 3145736 | tf_op jit(solution)/shard_map/ppermute | solution.py:144
  127.5 44.4 %collective-permute-start.12 = (bf16[4096,128]{1,0:T(8,128)(2,1)}, bf16[4096,128]{1,0:T(8,128)(2,1)}, u32[]{:S(2)}, u32[]{:S(2)}) collective-permute-start(bf16[4096,128]{1,0:T(8,128)(2,1)} %constant_dynamic-update-slice_fusion.7), channel_id=1, source_target_pairs={{0,32},{8,40},{16,48},{24,56},{32,64},{40,72},{48,80},{56,88},{64,... | collective-permute-start | bytes 3145736 | tf_op jit(solution)/shard_map/ppermute | solution.py:144
  135.1 66.4 %collective-permute-start.13 = (bf16[4096,128]{1,0:T(8,128)(2,1)}, bf16[4096,128]{1,0:T(8,128)(2,1)}, u32[]{:S(2)}, u32[]{:S(2)}) collective-permute-start(bf16[4096,128]{1,0:T(8,128)(2,1)} %constant_dynamic-update-slice_fusion.7), channel_id=1, source_target_pairs={{0,64},{8,72},{16,80},{24,88},{32,96},{40,104},{48,112},{56,120},{... | collective-permute-start | bytes 3145736 | tf_op jit(solution)/shard_map/ppermute | solution.py:144
  164.0 37.5 %collective-permute-start.14 = (bf16[4096,128]{1,0:T(8,128)(2,1)}, bf16[4096,128]{1,0:T(8,128)(2,1)S(1)}, u32[]{:S(2)}, u32[]{:S(2)}) collective-permute-start(bf16[4096,128]{1,0:T(8,128)(2,1)} %constant_dynamic-update-slice_fusion.7), channel_id=1, source_target_pairs={{0,480},{8,488},{16,496},{24,504},{32,0},{40,8},{48,16},{56,24},{6... | collective-permute-start | bytes 3145736 | tf_op jit(solution)/shard_map/ppermute | solution.py:144
  201.5 1.0 copy-start.1

commit v3 on v2

--- a/solution.py
+++ b/solution.py
@@ -1,3 +1,5 @@
+import functools
+
 import jax
 import jax.numpy as jnp
 from jax import lax
@@ -11,6 +13,7 @@
 PREFIX = 128
 PAGES = PREFIX // PAGE
 NZ, NY = 16, 4
+NEAR = 4
 LANES = 128
 
 
@@ -73,18 +76,46 @@
     return [(z * NY + y, z * NY + (y + step) % NY) for z in range(NZ) for y in range(NY)]
 
 
-def pick_kernel(me_ref, listing_ref, table_ref, cache_ref, low_ref, high_ref, sems):
+def groups_far():
+    return [[(near + NEAR * far) * NY + y for far in range(NZ // NEAR)] for near in range(NEAR) for y in range(NY)]
+
+
+def groups_y():
+    return [[z * NY + y for y in range(NY)] for z in range(NZ)]
+
+
+def share(block, groups):
+    copies = jnp.broadcast_to(block[None], (len(groups[0]),) + block.shape)
+    return lax.all_to_all(
+        copies, "dp", split_axis=0, concat_axis=0, tiled=True, axis_index_groups=groups
+    )
+
+
+def both_ways(block, shift):
+    up = lax.ppermute(block, "dp", shift(1))
+    down = lax.ppermute(block, "dp", shift(-1))
+    return up, down
+
+
+def forward(up, down, shift):
+    half = up.shape[0] // 2
+    up_two = lax.ppermute(up[:half], "dp", shift(1))
+    down_two = lax.ppermute(down[half:], "dp", shift(-1))
+    return up_two, down_two
+
+
+def pick_kernel(me_ref, listing_ref, table_ref, cache_ref, out_ref, sems):
     asked = listing_ref[...]
     mine = (asked >> 4) == me_ref[0]
     rows = asked & (BR_DEV - 1)
     lowest = jnp.min(jnp.where(mine, rows, BR_DEV - 1))
     highest = jnp.max(jnp.where(mine, rows, 0))
     copies = []
-    for which, (row, out) in enumerate(((lowest, low_ref), (highest, high_ref))):
+    for which, row in enumerate((lowest, highest)):
         for page in range(PAGES):
             copies.append(
                 pltpu.make_async_copy(
-                    cache_ref.at[table_ref[row, page]], out.at[page], sems.at[which, page]
+                    cache_ref.at[table_ref[row, page]], out_ref.at[which, page], sems.at[which, page]
                 )
             )
     for copy in copies:
@@ -94,88 +125,121 @@
 
 
 def pick_pages(me_index, listing, page_table, cache):
-    block = jax.ShapeDtypeStruct((PAGES,) + cache.shape[1:], cache.dtype)
     return pl.pallas_call(
         pick_kernel,
-        out_shape=(block, block),
+        out_shape=jax.ShapeDtypeStruct((2, PAGES) + cache.shape[1:], cache.dtype),
         in_specs=[
             pl.BlockSpec(memory_space=pltpu.SMEM),
             pl.BlockSpec(memory_space=pltpu.VMEM),
             pl.BlockSpec(memory_space=pltpu.SMEM),
             pl.BlockSpec(memory_space=pl.ANY),
         ],
-        out_specs=(pl.BlockSpec(memory_space=pl.ANY), pl.BlockSpec(memory_space=pl.ANY)),
+        out_specs=pl.BlockSpec(memory_space=pltpu.VMEM),
         scratch_shapes=[pltpu.SemaphoreType.DMA((2, PAGES))],
     )(me_index.reshape(1), listing, page_table, cache)
 
 
-def place_kernel(array_ref, index_ref, *refs):
-    sources, out_ref, sems = refs[:-2], refs[-2], refs[-1]
+def place_kernel(count, aliased, where_ref, *refs):
+    sources = refs[:count]
+    out_ref, held, load_sems, sems = refs[count + aliased :]
     slots = out_ref.shape[0]
+    loads, base = [], 0
+    for number, source in enumerate(sources):
+        size = source.shape[0]
+        loads.append(
+            pltpu.make_async_copy(source, held.at[pl.ds(base, size)], load_sems.at[number])
+        )
+        base += size
+    for load in loads:
+        load.start()
+    for load in loads:
+        load.wait()
 
     @pl.loop(0, slots)
     def _(slot):
-        for number, source in enumerate(sources):
-
-            @pl.when(array_ref[slot] == number)
-            def _():
-                pltpu.make_async_copy(
-                    source.at[index_ref[slot]], out_ref.at[slot], sems.at[slot]
-                ).start()
+        where = where_ref[slot]
+
+        @pl.when(where >= 0)
+        def _():
+            pltpu.make_async_copy(held.at[where], out_ref.at[slot], sems.at[slot]).start()
 
     @pl.loop(0, slots)
     def _(slot):
-        pltpu.make_async_copy(sources[0].at[0], out_ref.at[slot], sems.at[slot]).wait()
-
-
-def place_children(array_of, index_of, sources):
-    slots = array_of.shape[0]
+        @pl.when(where_ref[slot] >= 0)
+        def _():
+            pltpu.make_async_copy(held.at[0], out_ref.at[slot], sems.at[slot]).wait()
+
+
+def place_children(where, sources, earlier=None):
+    slots = where.shape[0]
+    count = len(sources)
+    blocks = sum(source.shape[0] for source in sources)
+    tile = sources[0].shape[1:]
+    given = [where] + list(sources) + ([] if earlier is None else [earlier])
     return pl.pallas_call(
-        place_kernel,
-        out_shape=jax.ShapeDtypeStruct((slots,) + sources[0].shape[1:], sources[0].dtype),
-        in_specs=[pl.BlockSpec(memory_space=pltpu.SMEM)] * 2
-        + [pl.BlockSpec(memory_space=pl.ANY)] * len(sources),
+        functools.partial(place_kernel, count, len(given) - 1 - count),
+        out_shape=jax.ShapeDtypeStruct((slots,) + tile, sources[0].dtype),
+        in_specs=[pl.BlockSpec(memory_space=pltpu.SMEM)]
+        + [pl.BlockSpec(memory_space=pl.ANY)] * (len(given) - 1),
         out_specs=pl.BlockSpec(memory_space=pl.ANY),
-        scratch_shapes=[pltpu.SemaphoreType.DMA((slots,))],
-    )(array_of, index_of, *sources)
-
-
-def spread(block, shifts):
-    return [block] + [lax.ppermute(block, "dp", pairs) for pairs in shifts]
-
-
-def fork_pages(listing, fork_parent, kv_cache, page_table):
-    me_index = lax.axis_index("dp")
-    me_z, me_y = me_index // NY, me_index % NY
-    cache = kv_cache[:, :, :, 0]
-    width = cache.shape[-1]
-    low, high = pick_pages(me_index, listing, page_table, cache)
-    rows = low.size // width
-    both = jnp.concatenate([low.reshape(rows, width), high.reshape(rows, width)])
-
-    far = spread(both, [shift_z(4), shift_z(8), shift_z(12)])
-    low_far = jnp.concatenate([part[:rows] for part in far])
-    high_far = jnp.concatenate([part[rows:] for part in far])
-    near = [shift_z(1), shift_z(2), shift_z(-1)]
-    across = [shift_y(1), shift_y(2), shift_y(3)]
-    low_column = jnp.concatenate(spread(low_far, near))
-    high_plane = jnp.concatenate(spread(high_far, across))
-    low_column, high_plane = lax.optimization_barrier((low_column, high_plane))
-    sources = spread(low_column, across) + spread(high_plane, near)
-    sources = [part.reshape((NZ,) + low.shape) for part in sources]
-
+        scratch_shapes=[
+            pltpu.VMEM((blocks,) + tile, sources[0].dtype),
+            pltpu.SemaphoreType.DMA((count,)),
+            pltpu.SemaphoreType.DMA((slots,)),
+        ],
+        input_output_aliases={} if earlier is None else {len(given) - 1: 0},
+        compiler_params=pltpu.CompilerParams(vmem_limit_bytes=24 * 2**20),
+    )(*given)
+
+
+def child_places(listing, fork_parent, me_z, me_y):
     owner = fork_parent // BR_DEV
     asked = listing.reshape(1, -1)
     same = (asked // BR_DEV) == owner[:, None]
     first = jnp.min(jnp.where(same, asked % BR_DEV, BR_DEV - 1), axis=1)
     is_low = fork_parent % BR_DEV == first
-    apart_z = (me_z - owner // NY) % NZ
-    apart_y = (me_y - owner % NY) % NY
-    near_z = apart_z % 4
-    far_z = jnp.where(near_z == 3, apart_z + 1, apart_z) // 4 % 4
-    array_of = jnp.where(is_low, apart_y, 4 + near_z)
-    index_of = jnp.where(is_low, near_z, apart_y) * 4 + far_z
-    placed = place_children(array_of.astype(jnp.int32), index_of.astype(jnp.int32), sources)
+    owner_z, owner_y = owner // NY, owner % NY
+    far = owner_z // NEAR
+    near = (me_z - owner_z) % NEAR
+    apart = (me_y - owner_y) % NY
+    step = jnp.where(is_low, apart, near)
+    inner = jnp.where(is_low, near, owner_y) * (NZ // NEAR) + far
+    place = jnp.where(step == 0, 0, jnp.where(step == 1, NZ, 2 * NZ)) + inner
+    early = jnp.where(step == 2, -1, place + jnp.where(is_low, 0, 3 * NZ))
+    late = jnp.where(step == 2, inner + jnp.where(is_low, 0, NZ), -1)
+    return early.astype(jnp.int32), late.astype(jnp.int32)
+
+
+def gather_near(listing, kv_cache, page_table):
+    me_index = lax.axis_index("dp")
+    cache = kv_cache[:, :, :, 0]
+    width = cache.shape[-1]
+    picked = pick_pages(me_index, listing, page_table, cache)
+    rows = picked[0].size // width
+
+    far = share(picked.reshape(2 * rows, width), groups_far())
+    low_far = far[:, :rows].reshape(-1, width)
+    high_far = far[:, rows:].reshape(-1, width)
+    high_plane = share(high_far, groups_y()).reshape(-1, width)
+    low_column = jnp.concatenate(
+        [low_far] + [lax.ppermute(low_far, "dp", shift_z(step)) for step in (1, 2, -1)]
+    )
+    return low_column, high_plane, picked.shape[1:]
+
+
+def fork_pages(listing, fork_parent, low_column, high_plane, tile):
+    me_index = lax.axis_index("dp")
+    me_z, me_y = me_index // NY, me_index % NY
+    early, late = child_places(listing, fork_parent, me_z, me_y)
+    low_up, low_down = both_ways(low_column, shift_y)
+    high_up, high_down = both_ways(high_plane, shift_z)
+    low_two = forward(low_up, low_down, shift_y)
+    high_two = forward(high_up, high_down, shift_z)
+    first = (low_column, low_up, low_down, high_plane, high_up, high_down)
+    placed = place_children(early, [part.reshape((-1,) + tile) for part in first])
+    placed = place_children(
+        late, [part.reshape((-1,) + tile) for part in low_two + high_two], placed
+    )
     return placed[:, :, :, :, None]
 
 
@@ -196,6 +260,8 @@
     rows_here = residual.shape[0]
     shards = lax.axis_size("tensor")
     partial = jnp.dot(attended, out_proj, preferred_element_type=jnp.float32).astype(jnp.bfloat16)
+    low_column, high_plane, tile = gather_near(listing, kv_cache, page_table)
+    low_column, high_plane, partial = lax.optimization_barrier((low_column, high_plane, partial))
     terms = lax.all_to_all(
         partial.reshape(shards, rows_here, -1), "tensor", split_axis=0, concat_axis=0, tiled=True
     )
@@ -208,7 +274,7 @@
         * norm_gain.astype(jnp.float32)
     )
     scores = jax.nn.sigmoid(jnp.sum(normed * score_weight.astype(jnp.float32), axis=-1))
-    child_pages = fork_pages(listing, fork_parent, kv_cache, page_table)
+    child_pages = fork_pages(listing, fork_parent, low_column, high_plane, tile)
     return (hidden_out, scores, child_pages)
 
 

time: 303 us -> 170 us (0.56)
  the two profiles are of different devices: /device:TPU:24 before, /device:TPU:32 now
where the time goes in v3:
time: 170 us; the launch traced here: 169 us
  starting transfers between devices  68.4 us (40%)
  waiting for transfers between devices  64.1 us (38%)
  local copies, waits for them, and re-layouts  13.8 us (8%)
  Pallas kernels  8.86 us (5%)
  other arithmetic  8.39 us (5%)
  matrix products  4.78 us (3%)
    all_to_all x2, waiting for transfers between devices, share(): lax.all_to_all(copies, 'dp', split_axis=0, concat_axis=0, tiled=True, axi...  24.7 us
    all_to_all x1, starting transfers between devices, parent_listing(): lax.all_to_all(copies, 'dp', split_axis=0, concat_axis=0, tiled=True)[:, 0]  18.4 us
    ppermute x2, waiting for transfers between devices, both_ways(): up = lax.ppermute(block, 'dp', shift(1))  15.4 us
    ppermute x3, starting transfers between devices, gather_near(): lax.ppermute(low_far, 'dp', shift_z(step))  12.2 us
    all_to_all x1, waiting for transfers between devices, parent_listing(): lax.all_to_all(copies, 'dp', split_axis=0, concat_axis=0, tiled=True)[:, 0]  12 us
    all_to_all x2, starting transfers between devices, share(): lax.all_to_all(copies, 'dp', split_axis=0, concat_axis=0, tiled=True, axi...  7.66 us
    ppermute x2, starting transfers between devices, forward(): down_two = lax.ppermute(down[half:], 'dp', shift(-1))  7.31 us
    ppermute x2, starting transfers between devices, both_ways(): down = lax.ppermute(block, 'dp', shift(-1))  6.78 us
  transfers between devices with their start and end apart: 15, of which 7 were waited for; matrix products, arithmetic and copies ran while one was open for 13% of the time, Pallas kernels for 2%

profile of v3, /device:TPU:32, one launch (start us, length us, event | category | flops | bytes accessed | tf_op | source)
XLA Modules:
  0.0 169.3 jit_solution(9808316997494178820)
XLA Ops:
  2.1 18.4 %all-to-all-start = ((s32[64,1,128]{2,1,0:T(1,128)}), s32[64,1,128]{2,1,0:T(1,128)S(1)}, u32[]{:S(2)}, u32[]{:S(2)}) async-start(s32[64,1,128]{2,1,0:T(1,128)} %broadcast_in_dim.110), calls=%async_computation | async-start | bytes 65536 | tf_op jit(solution)/shard_map/all_to_all | solution.py:68
  22.0 12.0 %all-to-all-done = s32[64,1,128]{2,1,0:T(1,128)S(1)} async-done(((s32[64,1,128]{2,1,0:T(1,128)}), s32[64,1,128]{2,1,0:T(1,128)S(1)}, u32[]{:S(2)}, u32[]{:S(2)}) %all-to-all-start) | async-done | bytes 32800 | tf_op jit(solution)/shard_map/all_to_all | solution.py:68
  34.7 2.8 %shard_map.121 = bf16[2,8,2,16,128]{4,3,2,1,0:T(8,128)(2,1)} custom-call(s32[1]{0:T(128)} %bitcast.me_ref, s32[64,128]{1,0:T(8,128)} %bitcast.132, s32[16,12]{1,0:T(8,128)} %table_ref.1, bf16[192,2,16,128]{3,2,1,0:T(8,128)(2,1)} %bitcast.118), custom_call_target="tpu_custom_call" | custom-call | tf_op jit(solution)/shard_map/pallas_call | solution.py:128
  37.4 1.8 %broadcast_in_dim.112 = bf16[4,512,128]{2,1,0:T(8,128)(2,1)} broadcast(bf16[512,128]{1,0:T(8,128)(2,1)} %bitcast.130), dimensions={1,2} | broadcast | bytes 655360 | tf_op jit(solution)/shard_map/broadcast_in_dim | solution.py:88
  39.2 4.1 %all-to-all-start.1 = ((bf16[4,512,128]{2,1,0:T(8,128)(2,1)}), bf16[4,512,128]{2,1,0:T(8,128)(2,1)}, u32[]{:S(2)}, u32[]{:S(2)}) async-start(bf16[4,512,128]{2,1,0:T(8,128)(2,1)} %broadcast_in_dim.112), calls=%async_computation.1 | async-start | bytes 1048576 | tf_op jit(solution)/shard_map/all_to_all | solution.py:89
  43.4 2.0 %gather_fusion = bf16[192,2,16,128]{3,2,1,0:T(8,128)(2,1)} fusion(bf16[192,2,16,128]{3,2,1,0:T(8,128)(2,1)S(1)} %bitcast.119, s32[1024]{0:T(1024)S(1)} %pad_clamp_fusion), kind=kCustom, calls=%fused_computation | custom fusion | bytes 3146496 | tf_op jit(solution)/shard_map/gather | solution.py:26
  45.4 1.5 fusion.47
  46.9 1.7 fusion.44
  51.2 19.2 %all-to-all-done.1 = bf16[4,512,128]{2,1,0:T(8,128)(2,1)} async-done(((bf16[4,512,128]{2,1,0:T(8,128)(2,1)}), bf16[4,512,128]{2,1,0:T(8,128)(2,1)}, u32[]{:S(2)}, u32[]{:S(2)}) %all-to-all-start.1) | async-done | bytes 524320 | tf_op jit(solution)/shard_map/all_to_all | solution.py:89
  71.4 5.7 %collective-permute-start = (bf16[1024,128]{1,0:T(8,128)(2,1)S(1)}, bf16[1024,128]{1,0:T(8,128)(2,1)}, u32[]{:S(2)}, u32[]{:S(2)}) collective-permute-start(bf16[1024,128]{1,0:T(8,128)(2,1)S(1)} %bitcast.124), channel_id=1, source_target_pairs={{0,32},{8,40},{16,48},{24,56},{32,64},{40,72},{48,80},{56,88},{64,... | collective-permute-start | bytes 786440 | tf_op jit(solution)/shard_map/ppermute | solution.py:225
  77.1 4.6 %collective-permute-start.1 = (bf16[1024,128]{1,0:T(8,128)(2,1)S(1)}, bf16[1024,128]{1,0:T(8,128)(2,1)}, u32[]{:S(2)}, u32[]{:S(2)}) collective-permute-start(bf16[1024,128]{1,0:T(8,128)(2,1)S(1)} %bitcast.125), channel_id=1, source_target_pairs={{0,64},{8,72},{16,80},{24,88},{32,96},{40,104},{48,112},{56,120},{... | collective-permute-start | bytes 786440 | tf_op jit(solution)/shard_map/ppermute | solution.py:225
  81.7 1.9 %collective-permute-start.2 = (bf16[1024,128]{1,0:T(8,128)(2,1)S(1)}, bf16[1024,128]{1,0:T(8,128)(2,1)}, u32[]{:S(2)}, u32[]{:S(2)}) collective-permute-start(bf16[1024,128]{1,0:T(8,128)(2,1)S(1)} %bitcast.126), channel_id=1, source_target_pairs={{0,480},{8,488},{16,496},{24,504},{32,0},{40,8},{48,16},{56,24},{6... | collective-permute-start | bytes 786440 | tf_op jit(solution)/shard_map/ppermute | solution.py:225
  84.7 3.5 %all-to-all-start.2 = ((bf16[4,1024,128]{2,1,0:T(8,128)(2,1)}), bf16[4,1024,128]{2,1,0:T(8,128)(2,1)S(1)}, u32[]{:S(2)}, u32[]{:S(2)}) async-start(bf16[4,1024,128]{2,1,0:T(8,128)(2,1)} %broadcast_in_dim.114), calls=%async_computation.2 | async-start | bytes 2097152 | tf_op jit(solution)/shard_map/all_to_all | solution.py:89
  88.2 1.9 %convolution_convert_fusion = bf16[256,2560]{1,0:T(8,128)(2,1)} fusion(bf16[384,2560]{1,0:T(8,128)(2,1)S(1)} %copy-done, bf16[32,8,3,128]{3,2,1,0:T(4,128)(2,1)S(1)} %bitcast.128), kind=kOutput, calls=%fused_computation.1 | convolution fusion | flops 503971840 | bytes 3473408 | tf_op jit(solution)/shard_map/dot_general | solution.py:262
  90.1 5.3 %collective-permute-done.1 = bf16[1024,128]{1,0:T(8,128)(2,1)} collective-permute-done((bf16[1024,128]{1,0:T(8,128)(2,1)S(1)}, bf16[1024,128]{1,0:T(8,128)(2,1)}, u32[]{:S(2)}, u32[]{:S(2)}) %collective-permute-start.1) | collective-permute-done | bytes 262176 | tf_op jit(solution)/shard_map/ppermute | solution.py:225
  95.5 2.1 %pad_maximum_fusion = bf16[4096,128]{1,0:T(8,128)(2,1)} fusion(bf16[1024,128]{1,0:T(8,128)(2,1)} %collective-permute-done.2, bf16[1024,128]{1,0:T(8,128)(2,1)} %collective-permute-done.1, bf16[1024,128]{1,0:T(8,128)(2,1)} %collective-permute-done, bf16[1024,128]{1,0:T(8,128)(2,1)S(1)} %bitcast.127), kind=kLoop, calls=%fused_computation.15 | loop fusion | flops 4194304 | bytes 2097152 | tf_op jit(solution)/shard_map/concatenate | solution.py:224
  97.6 5.5 %all-to-all-done.2 = bf16[4,1024,128]{2,1,0:T(8,128)(2,1)S(1)} async-done(((bf16[4,1024,128]{2,1,0:T(8,128)(2,1)}), bf16[4,1024,128]{2,1,0:T(8,128)(2,1)S(1)}, u32[]{:S(2)}, u32[]{:S(2)}) %all-to-all-start.2) | async-done | bytes 1048608 | tf_op jit(solution)/shard_map/all_to_all | solution.py:89
  103.2 4.3 %all-to-all-start.3 = ((bf16[8,32,2560]{2,1,0:T(8,128)(2,1)}), bf16[8,32,2560]{2,1,0:T(8,128)(2,1)}, u32[]{:S(2)}, u32[]{:S(2)}) async-start(bf16[8,32,2560]{2,1,0:T(8,128)(2,1)} %bitcast.121), calls=%async_computation.3 | async-start | bytes 2621440 | tf_op jit(solution)/shard_map/all_to_all | solution.py:265
  108.1 2.5 %collective-permute-start.3 = (bf16[4096,128]{1,0:T(8,128)(2,1)}, bf16[4096,128]{1,0:T(8,128)(2,1)S(1)}, u32[]{:S(2)}, u32[]{:S(2)}) collective-permute-start(bf16[4096,128]{1,0:T(8,128)(2,1)} %pad_maximum_fusion), channel_id=1, source_target_pairs={{0,8},{8,16},{16,24},{24,0},{32,40},{40,48},{48,56},{56,32},{64,72... | collective-permute-start | bytes 3145736 | tf_op jit(solution)/shard_map/ppermute | solution.py:95
  110.6 4.6 %collective-permute-start.5 = (bf16[4096,128]{1,0:T(8,128)(2,1)}, bf16[4096,128]{1,0:T(8,128)(2,1)S(1)}, u32[]{:S(2)}, u32[]{:S(2)}) collective-permute-start(bf16[4096,128]{1,0:T(8,128)(2,1)} %pad_maximum_fusion), channel_id=1, source_target_pairs={{0,24},{8,0},{16,8},{24,16},{32,56},{40,32},{48,40},{56,48},{64,88... | collective-permute-start | bytes 3145736 | tf_op jit(solution)/shard_map/ppermute | solution.py:96
  115.2 3.6 %collective-permute-start.7 = (bf16[4096,128]{1,0:T(8,128)(2,1)S(1)}, bf16[4096,128]{1,0:T(8,128)(2,1)S(1)}, u32[]{:S(2)}, u32[]{:S(2)}) collective-permute-start(bf16[4096,128]{1,0:T(8,128)(2,1)S(1)} %bitcast.108), channel_id=1, source_target_pairs={{0,32},{8,40},{16,48},{24,56},{32,64},{40,72},{48,80},{56,88},{64,... | collective-permute-start | bytes 3145736 | tf_op jit(solution)/shard_map/ppermute | solution.py:95
  118.8 2.2 %collective-permute-start.9 = (bf16[4096,128]{1,0:T(8,128)(2,1)S(1)}, bf16[4096,128]{1,0:T(8,128)(2,1)S(1)}, u32[]{:S(2)}, u32[]{:S(2)}) collective-permute-start(bf16[4096,128]{1,0:T(8,128)(2,1)S(1)} %bitcast.109), channel_id=1, source_target_pairs={{0,480},{8,488},{16,496},{24,504},{32,0},{40,8},{48,16},{56,24},{6... | collective-permute-start | bytes 3145736 | tf_op jit(solution)/shard_map/ppermute | solution.py:96
  121.6 15.4 %collective-permute-done.3 = bf16[4096,128]{1,0:T(8,128)(2,1)S(1)} collective-permute-done((bf16[4096,128]{1,0:T(8,128)(2,1)}, bf16[4096,128]{1,0:T(8,128)(2,1)S(1)}, u32[]{:S(2)}, u32[]{:S(2)}) %collective-permute-start.3) | collective-permute-done | bytes 1048608 | tf_op jit(solution)/shard_map/ppermute | solution.py:95
  137.8 2.0 %collective-permute-start.4 = (bf16[2048,128]{1,0:T(8,128)(2,1)}, bf16[2048,128]{1,0:T(8,128)(2,1)S(1)}, u32[]{:S(2)}, u32[]{:S(2)}) collective-permute-start(bf16[2048,128]{1,0:T(8,128)(2,1)} %slice.51), channel_id=1, source_target_pairs={{0,8},{8,16},{16,24},{24,0},{32,40},{40,48},{48,56},{56,32},{64,72... | collective-permute-start | bytes 1572872 | tf_op jit(solution)/shard_map/ppermute | solution.py:102
  140.7 5.1 %collective-permute-start.6 = (bf16[2048,128]{1,0:T(8,128)(2,1)}, bf16[2048,128]{1,0:T(8,128)(2,1)}, u32[]{:S(2)}, u32[]{:S(2)}) collective-permute-start(bf16[2048,128]{1,0:T(8,128)(2,1)} %slice.52), channel_id=1, source_target_pairs={{0,24},{8,0},{16,8},{24,16},{32,56},{40,32},{48,40},{56,48},{64,88... | collective-permute-start | bytes 1572872 | tf_op jit(solution)/shard_map/ppermute | solution.py:103
  146.7 3.6 %collective-permute-start.8 = (bf16[2048,128]{1,0:T(8,128)(2,1)}, bf16[2048,128]{1,0:T(8,128)(2,1)}, u32[]{:S(2)}, u32[]{:S(2)}) collective-permute-start(bf16[2048,128]{1,0:T(8,128)(2,1)} %slice.53), channel_id=1, source_target_pairs={{0,32},{8,40},{16,48},{24,56},{32,64},{40,72},{48,80},{56,88},{64,... | collective-permute-start | bytes 1572872 | tf_op jit(solution)/shard_map/ppermute | solution.py:102
  151.2 2.2 %collective-permute-start.10 = (bf16[2048,128]{1,0:T(8,128)(2,1)}, bf16[2048,128]{1,0:T(8,128)(2,1)}, u32[]{:S(2)}, u32[]{:S(2)}) collective-permute-start(bf16[2048,128]{1,0:T(8,128)(2,1)} %slice.54), channel_id=1, source_target_pairs={{0,480},{8,488},{16,496},{24,504},{32,0},{40,8},{48,16},{56,24},{6... | collective-permute-start | bytes 1572872 | tf_op jit(solution)/shard_map/ppermute | solution.py:103
  153.4 2.9 %shard_map.122.refs_4_ = bf16[48,8,2,16,128]{4,3,2,1,0:T(8,128)(2,1)} custom-call(s32[48]{0:T(128)S(1)} %get-tuple-element.21.where_ref, bf16[16,8,2,16,128]{4,3,2,1,0:T(8,128)(2,1)S(1)} %bitcast.111, bf16[16,8,2,16,128]{4,3,2,1,0:T(8,128)(2,1)S(1)} %bitcast.112, bf16[16,8,2,16,128]{4,3,2,1,0:T(8,128)(2,1)S(1)} %bitcast.113, ...), custom_call_target="tpu_custom_call" | custom-call | tf_op jit(solution)/shard_map/pallas_call | solution.py:179
  156.3 1.6 convert_reduce_fusion
  159.5 2.4 %collective-permute-done.8 = bf16[2048,128]{1,0:T(8,128)(2,1)} collective-permute-done((bf16[2048,128]{1,0:T(8,128)(2,1)}, bf16[2048,128]{1,0:T(8,128)(2,1)}, u32[]{:S(2)}, u32[]{:S(2)}) %collective-permute-start.8) | collective-permute-done | bytes 524320 | tf_op jit(solution)/shard_map/ppermute | solution.py:102
  161.9 4.2 %collective-permute-done.10 = bf16[2048,128]{1,0:T(8,128)(2,1)} collective-permute-done((bf16[2048,128]{1,0:T(8,128)(2,1)}, bf16[2048,128]{1,0:T(8,128)(2,1)}, u32[]{:S(2)}, u32[]{:S(2)}) %collective-permute-start.10) | collective-permute-done | bytes 524320 | tf_op jit(solution)/shard_map/ppermute | solution.py:103
  166.1 3.2 %shard_map.123 = bf16[48,8,2,16,128]{4,3,2,1,0:T(8,128)(2,1)} custom-call(s32[48]{0:T(128)S(1)} %compare_select_fusion.17.where_ref, bf16[8,8,2,16,128]{4,3,2,1,0:T(8,128)(2,1)S(1)} %bitcast.116, bf16[8,8,2,16,128]{4,3,2,1,0:T(8,128)(2,1)} %bitcast.33.refs_1_, bf16[8,8,2,16,128]{4,3,2,1,0:T(8,128)(2,1)} %bitcast.34.refs_2_, ...), custom_call_target="tpu_custom_call", output_to_operand_aliasing={{}: (5, {})} | custom-call | tf_op jit(solution)/shard_map/pallas_call | solution.py:179
  (66 shorter events, 14.4 us)
Async XLA Ops:
  0.6 87.6 %copy-start = (bf16[384,2560]{1,0:T(8,128)(2,1)S(1)}, bf16[384,2560]{1,0:T(8,128)(2,1)}, u32[]{:S(2)}) copy-start(bf16[384,2560]{1,0:T(8,128)(2,1)} %param.15) | copy-start | bytes 5898244
  2.1 32.0 %all-to-all-start = ((s32[64,1,128]{2,1,0:T(1,128)}), s32[64,1,128]{2,1,0:T(1,128)S(1)}, u32[]{:S(2)}, u32[]{:S(2)}) async-start(s32[64,1,128]{2,1,0:T(1,128)} %broadcast_in_dim.110), calls=%async_computation | async-start | bytes 65536 | tf_op jit(solution)/shard_map/all_to_all | solution.py:68
  34.1 0.6 copy-start.4
  34.7 8.7 %copy-start.2 = (bf16[192,2,16,1,128]{4,2,3,1,0:T(8,128)(2,1)S(1)}, bf16[192,2,16,1,128]{4,2,3,1,0:T(8,128)(2,1)}, u32[]{:S(2)}) copy-start(bf16[192,2,16,1,128]{4,2,3,1,0:T(8,128)(2,1)} %param.12) | copy-start | bytes 4718596
  39.2 31.1 %all-to-all-start.1 = ((bf16[4,512,128]{2,1,0:T(8,128)(2,1)}), bf16[4,512,128]{2,1,0:T(8,128)(2,1)}, u32[]{:S(2)}, u32[]{:S(2)}) async-start(bf16[4,512,128]{2,1,0:T(8,128)(2,1)} %broadcast_in_dim.112), calls=%async_computation.1 | async-start | bytes 1048576 | tf_op jit(solution)/shard_map/all_to_all | solution.py:89
  46.9 1.7 %copy-start.3 = (bf16[16,16,3,128]{3,1,2,0:T(8,128)(2,1)S(1)}, bf16[16,16,3,128]{3,1,2,0:T(8,128)(2,1)}, u32[]{:S(2)}) copy-start(bf16[16,16,3,128]{3,1,2,0:T(8,128)(2,1)} %param.10) | copy-start | bytes 589828
  49.8 0.9 copy-start.8
  71.4 18.7 %collective-permute-start = (bf16[1024,128]{1,0:T(8,128)(2,1)S(1)}, bf16[1024,128]{1,0:T(8,128)(2,1)}, u32[]{:S(2)}, u32[]{:S(2)}) collective-permute-start(bf16[1024,128]{1,0:T(8,128)(2,1)S(1)} %bitcast.124), channel_id=1, source_target_pairs={{0,32},{8,40},{16,48},{24,56},{32,64},{40,72},{48,80},{56,88},{64,... | collective-permute-start | bytes 786440 | tf_op jit(solution)/shard_map/ppermute | solution.py:225
  77.1 18.4 %collective-permute-start.1 = (bf16[1024,128]{1,0:T(8,128)(2,1)S(1)}, bf16[1024,128]{1,0:T(8,128)(2,1)}, u32[]{:S(2)}, u32[]{:S(2)}) collective-permute-start(bf16[1024,128]{1,0:T(8,128)(2,1)S(1)} %bitcast.125), channel_id=1, source_target_pairs={{0,64},{8,72},{16,80},{24,88},{32,96},{40,104},{48,112},{56,120},{... | collective-permute-start | bytes 786440 | tf_op jit(solution)/shard_map/ppermute | solution.py:225
  81.7 13.8 %collective-permute-start.2 = (bf16[1024,128]{1,0:T(8,128)(2,1)S(1)}, bf16[1024,128]{1,0:T(8,128)(2,1)}, u32[]{:S(2)}, u32[]{:S(2)}) collective-permute-start(bf16[1024,128]{1,0:T(8,128)(2,1)S(1)} %bitcast.126), channel_id=1, source_target_pairs={{0,480},{8,488},{16,496},{24,504},{32,0},{40,8},{48,16},{56,24},{6... | collective-permute-start | bytes 786440 | tf_op jit(solution)/shard_map/ppermute | solution.py:225
  84.7 18.5 %all-to-all-start.2 = ((bf16[4,1024,128]{2,1,0:T(8,128)(2,1)}), bf16[4,1024,128]{2,1,0:T(8,128)(2,1)S(1)}, u32[]{:S(2)}, u32[]{:S(2)}) async-start(bf16[4,1024,128]{2,1,0:T(8,128)(2,1)} %broadcast_in_dim.114), calls=%async_computation.2 | async-start | bytes 2097152 | tf_op jit(solution)/shard_map/all_to_all | solution.py:89
  97.6 9.8 %copy-start.9 = (bf16[2560]{0:T(1024)(128)(2,1)S(1)}, bf16[2560]{0:T(1024)(128)(2,1)}, u32[]{:S(2)}) copy-start(bf16[2560]{0:T(1024)(128)(2,1)} %param.17) | copy-start | bytes 15364
  97.6 9.9 %copy-start.10 = (bf16[2560]{0:T(1024)(128)(2,1)S(1)}, bf16[2560]{0:T(1024)(128)(2,1)}, u32[]{:S(2)}) copy-start(bf16[2560]{0:T(1024)(128)(2,1)} %param.18) | copy-start | bytes 15364
  97.6 23.4 %copy-start.11 = (s32[48]{0:T(128)S(1)}, s32[48]{0:T(128)}, u32[]{:S(2)}) copy-start(s32[48]{0:T(128)} %param.19) | copy-start | bytes 580
  97.6 23.4 %copy-start.5 = (s32[64,1,128]{2,1,0:T(1,128)S(1)}, s32[64,1,128]{2,1,0:T(1,128)}, u32[]{:S(2)}) copy-start(s32[64,1,128]{2,1,0:T(1,128)} %copy-done.4) | copy-start | bytes 98308
  103.2 53.1 %all-to-all-start.3 = ((bf16[8,32,2560]{2,1,0:T(8,128)(2,1)}), bf16[8,32,2560]{2,1,0:T(8,128)(2,1)}, u32[]{:S(2)}, u32[]{:S(2)}) async-start(bf16[8,32,2560]{2,1,0:T(8,128)(2,1)} %bitcast.121), calls=%async_computation.3 | async-start | bytes 2621440 | tf_op jit(solution)/shard_map/all_to_all | solution.py:265
  108.1 28.9 %collective-permute-start.3 = (bf16[4096,128]{1,0:T(8,128)(2,1)}, bf16[4096,128]{1,0:T(8,128)(2,1)S(1)}, u32[]{:S(2)}, u32[]{:S(2)}) collective-permute-start(bf16[4096,128]{1,0:T(8,128)(2,1)} %pad_maximum_fusion), channel_id=1, source_target_pairs={{0,8},{8,16},{16,24},{24,0},{32,40},{40,48},{48,56},{56,32},{64,72... | collective-permute-start | bytes 3145736 | tf_op jit(solution)/shard_map/ppermute | solution.py:95
  110.6 29.3 %collective-permute-start.5 = (bf16[4096,128]{1,0:T(8,128)(2,1)}, bf16[4096,128]{1,0:T(8,128)(2,1)S(1)}, u32[]{:S(2)}, u32[]{:S(2)}) collective-permute-start(bf16[4096,128]{1,0:T(8,128)(2,1)} %pad_maximum_fusion), channel_id=1, source_target_pairs={{0,24},{8,0},{16,8},{24,16},{32,56},{40,32},{48,40},{56,48},{64,88... | collective-permute-start | bytes 3145736 | tf_op jit(solution)/shard_map/ppermute | solution.py:96
  115.2 30.7 %collective-permute-start.7 = (bf16[4096,128]{1,0:T(8,128)(2,1)S(1)}, bf16[4096,128]{1,0:T(8,128)(2,1)S(1)}, u32[]{:S(2)}, u32[]{:S(2)}) collective-permute-start(bf16[4096,128]{1,0:T(8,128)(2,1)S(1)} %bitcast.108), channel_id=1, source_target_pairs={{0,32},{8,40},{16,48},{24,56},{32,64},{40,72},{48,80},{56,88},{64,... | collective-permute-start | bytes 3145736 | tf_op jit(solution)/shard_map/ppermute | solution.py:95
  118.8 31.5 %collective-permute-start.9 = (bf16[4096,128]{1,0:T(8,128)(2,1)S(1)}, bf16[4096,128]{1,0:T(8,128)(2,1)S(1)}, u32[]{:S(2)}, u32[]{:S(2)}) collective-permute-start(bf16[4096,128]{1,0:T(8,128)(2,1)S(1)} %bitcast.109), channel_id=1, source_target_pairs={{0,480},{8,488},{16,496},{24,504},{32,0},{40,8},{48,16},{56,24},{6... | collective-permute-start | bytes 3145736 | tf_op jit(solution)/shard_map/ppermute | solution.py:96
  137.8 15.6 %copy-start.1 = (bf16[4096,128]{1,0:T(8,128)(2,1)S(1)}, bf16[4096,128]{1,0:T(8,128)(2,1)}, u32[]{:S(2)}) copy-start(bf16[4096,128]{1,0:T(8,128)(2,1)} %pad_maximum_fusion) | copy-start | bytes 3145732
  137.8 21.7 %collective-permute-start.4 = (bf16[2048,128]{1,0:T(8,128)(2,1)}, bf16[2048,128]{1,0:T(8,128)(2,1)S(1)}, u32[]{:S(2)}, u32[]{:S(2)}) collective-permute-start(bf16[2048,128]{1,0:T(8,128)(2,1)} %slice.51), channel_id=1, source_target_pairs={{0,8},{8,16},{16,24},{24,0},{32,40},{40,48},{48,56},{56,32},{64,72... | collective-permute-start | bytes 1572872 | tf_op jit(solution)/shard_map/ppermute | solution.py:102
  140.7 18.8 %collective-permute-start.6 = (bf16[2048,128]{1,0:T(8,128)(2,1)}, bf16[2048,128]{1,0:T(8,128)(2,1)}, u32[]{:S(2)}, u32[]{:S(2)}) collective-permute-start(bf16[2048,128]{1,0:T(8,128)(2,1)} %slice.52), channel_id=1, source_target_pairs={{0,24},{8,0},{16,8},{24,16},{32,56},{40,32},{48,40},{56,48},{64,88... | collective-permute-start | bytes 1572872 | tf_op jit(solution)/shard_map/ppermute | solution.py:103
  146.7 15.2 %collective-permute-start.8 = (bf16[2048,128]{1,0:T(8,128)(2,1)}, bf16[2048,128]{1,0:T(8,128)(2,1)}, u32[]{:S(2)}, u32[]{:S(2)}) collective-permute-start(bf16[2048,128]{1,0:T(8,128)(2,1)} %slice.53), channel_id=1, source_target_pairs={{0,32},{8,40},{16,48},{24,56},{32,64},{40,72},{48,80},{56,88},{64,... | collective-permute-start | bytes 1572872 | tf_op jit(solution)/shard_map/ppermute | solution.py:102
  151.2 14.9 %collective-permute-start.10 = (bf16[2048,128]{1,0:T(8,128)(2,1)}, bf16[2048,128]{1,0:T(8,128)(2,1)}, u32[]{:S(2)}, u32[]{:S(2)}) collective-permute-start(bf16[2048,128]{1,0:T(8,128)(2,1)} %slice.54), channel_id=1, source_target_pairs={{0,480},{8,488},{16,496},{24,504},{32,0},{40,8},{48,16},{56,24},{6... | collective-permute-start | bytes 1572872 | tf_op jit(solution)/shard_map/ppermute | solution.py:103
  156.3 1.6 copy-start.6
  156.3 2.5 %copy-start.7 = (f32[2560]{0:T(1024)S(1)}, f32[2560]{0:T(1024)}, u32[]{:S(2)}) copy-start(f32[2560]{0:T(1024)} %convert_element_type.43) | copy-start | bytes 30724

commit v4 on v2

--- a/solution.py
+++ b/solution.py
@@ -1,3 +1,5 @@
+import functools
+
 import jax
 import jax.numpy as jnp
 from jax import lax
@@ -11,6 +13,8 @@
 PREFIX = 128
 PAGES = PREFIX // PAGE
 NZ, NY = 16, 4
+NEAR = 4
+FRONT = 6
 LANES = 128
 
 
@@ -69,22 +73,38 @@
     return [(z * NY + y, (z + step) % NZ * NY + y) for z in range(NZ) for y in range(NY)]
 
 
-def shift_y(step):
-    return [(z * NY + y, z * NY + (y + step) % NY) for z in range(NZ) for y in range(NY)]
-
-
-def pick_kernel(me_ref, listing_ref, table_ref, cache_ref, low_ref, high_ref, sems):
+def groups_far():
+    return [[(near + NEAR * far) * NY + y for far in range(NZ // NEAR)] for near in range(NEAR) for y in range(NY)]
+
+
+def groups_z():
+    return [[z * NY + y for z in range(NZ)] for y in range(NY)]
+
+
+def groups_y():
+    return [[z * NY + y for y in range(NY)] for z in range(NZ)]
+
+
+def share(block, groups):
+    copies = jnp.broadcast_to(block[None], (len(groups[0]),) + block.shape)
+    return lax.all_to_all(
+        copies, "dp", split_axis=0, concat_axis=0, tiled=True, axis_index_groups=groups
+    )
+
+
+def pick_kernel(me_ref, listing_ref, table_ref, cache_ref, front_ref, back_ref, sems):
     asked = listing_ref[...]
     mine = (asked >> 4) == me_ref[0]
     rows = asked & (BR_DEV - 1)
     lowest = jnp.min(jnp.where(mine, rows, BR_DEV - 1))
     highest = jnp.max(jnp.where(mine, rows, 0))
     copies = []
-    for which, (row, out) in enumerate(((lowest, low_ref), (highest, high_ref))):
+    for which, row in enumerate((lowest, highest)):
         for page in range(PAGES):
+            target = front_ref.at[which, page] if page < FRONT else back_ref.at[which, page - FRONT]
             copies.append(
                 pltpu.make_async_copy(
-                    cache_ref.at[table_ref[row, page]], out.at[page], sems.at[which, page]
+                    cache_ref.at[table_ref[row, page]], target, sems.at[which, page]
                 )
             )
     for copy in copies:
@@ -94,89 +114,85 @@
 
 
 def pick_pages(me_index, listing, page_table, cache):
-    block = jax.ShapeDtypeStruct((PAGES,) + cache.shape[1:], cache.dtype)
     return pl.pallas_call(
         pick_kernel,
-        out_shape=(block, block),
+        out_shape=tuple(
+            jax.ShapeDtypeStruct((2, pages) + cache.shape[1:], cache.dtype)
+            for pages in (FRONT, PAGES - FRONT)
+        ),
         in_specs=[
             pl.BlockSpec(memory_space=pltpu.SMEM),
             pl.BlockSpec(memory_space=pltpu.VMEM),
             pl.BlockSpec(memory_space=pltpu.SMEM),
             pl.BlockSpec(memory_space=pl.ANY),
         ],
-        out_specs=(pl.BlockSpec(memory_space=pl.ANY), pl.BlockSpec(memory_space=pl.ANY)),
+        out_specs=(pl.BlockSpec(memory_space=pltpu.VMEM),) * 2,
         scratch_shapes=[pltpu.SemaphoreType.DMA((2, PAGES))],
     )(me_index.reshape(1), listing, page_table, cache)
 
 
-def place_kernel(array_ref, index_ref, *refs):
-    sources, out_ref, sems = refs[:-2], refs[-2], refs[-1]
+def place_kernel(first_page, aliased, where_ref, source_ref, *refs):
+    out_ref, sems = refs[aliased:]
     slots = out_ref.shape[0]
+    pages = source_ref.shape[1]
+
+    def store(slot):
+        return pltpu.make_async_copy(
+            source_ref.at[where_ref[slot]], out_ref.at[slot, pl.ds(first_page, pages)], sems.at[slot]
+        )
 
     @pl.loop(0, slots)
     def _(slot):
-        for number, source in enumerate(sources):
-
-            @pl.when(array_ref[slot] == number)
-            def _():
-                pltpu.make_async_copy(
-                    source.at[index_ref[slot]], out_ref.at[slot], sems.at[slot]
-                ).start()
+        store(slot).start()
 
     @pl.loop(0, slots)
     def _(slot):
-        pltpu.make_async_copy(sources[0].at[0], out_ref.at[slot], sems.at[slot]).wait()
-
-
-def place_children(array_of, index_of, sources):
-    slots = array_of.shape[0]
+        store(slot).wait()
+
+
+def place_children(where, source, first_page, earlier=None):
+    slots = where.shape[0]
+    given = [where, source] + ([] if earlier is None else [earlier])
     return pl.pallas_call(
-        place_kernel,
-        out_shape=jax.ShapeDtypeStruct((slots,) + sources[0].shape[1:], sources[0].dtype),
-        in_specs=[pl.BlockSpec(memory_space=pltpu.SMEM)] * 2
-        + [pl.BlockSpec(memory_space=pl.ANY)] * len(sources),
+        functools.partial(place_kernel, first_page, len(given) - 2),
+        out_shape=jax.ShapeDtypeStruct((slots, PAGES) + source.shape[2:], source.dtype),
+        in_specs=[
+            pl.BlockSpec(memory_space=pltpu.SMEM),
+            pl.BlockSpec(memory_space=pltpu.VMEM),
+        ]
+        + [pl.BlockSpec(memory_space=pl.ANY)] * (len(given) - 2),
         out_specs=pl.BlockSpec(memory_space=pl.ANY),
         scratch_shapes=[pltpu.SemaphoreType.DMA((slots,))],
-    )(array_of, index_of, *sources)
-
-
-def spread(block, shifts):
-    return [block] + [lax.ppermute(block, "dp", pairs) for pairs in shifts]
-
-
-def fork_pages(listing, fork_parent, kv_cache, page_table):
-    me_index = lax.axis_index("dp")
-    me_z, me_y = me_index // NY, me_index % NY
-    cache = kv_cache[:, :, :, 0]
-    width = cache.shape[-1]
-    low, high = pick_pages(me_index, listing, page_table, cache)
-    rows = low.size // width
-    both = jnp.concatenate([low.reshape(rows, width), high.reshape(rows, width)])
-
-    far = spread(both, [shift_z(4), shift_z(8), shift_z(12)])
-    low_far = jnp.concatenate([part[:rows] for part in far])
-    high_far = jnp.concatenate([part[rows:] for part in far])
-    near = [shift_z(1), shift_z(2), shift_z(-1)]
-    across = [shift_y(1), shift_y(2), shift_y(3)]
-    low_column = jnp.concatenate(spread(low_far, near))
-    high_plane = jnp.concatenate(spread(high_far, across))
-    low_column, high_plane = lax.optimization_barrier((low_column, high_plane))
-    sources = spread(low_column, across) + spread(high_plane, near)
-    sources = [part.reshape((NZ,) + low.shape) for part in sources]
-
+        input_output_aliases={} if earlier is None else {2: 0},
+        compiler_params=pltpu.CompilerParams(vmem_limit_bytes=24 * 2**20),
+    )(*given)
+
+
+def child_places(listing, fork_parent, me_index):
     owner = fork_parent // BR_DEV
     asked = listing.reshape(1, -1)
     same = (asked // BR_DEV) == owner[:, None]
     first = jnp.min(jnp.where(same, asked % BR_DEV, BR_DEV - 1), axis=1)
-    is_low = fork_parent % BR_DEV == first
-    apart_z = (me_z - owner // NY) % NZ
-    apart_y = (me_y - owner % NY) % NY
-    near_z = apart_z % 4
-    far_z = jnp.where(near_z == 3, apart_z + 1, apart_z) // 4 % 4
-    array_of = jnp.where(is_low, apart_y, 4 + near_z)
-    index_of = jnp.where(is_low, near_z, apart_y) * 4 + far_z
-    placed = place_children(array_of.astype(jnp.int32), index_of.astype(jnp.int32), sources)
-    return placed[:, :, :, :, None]
+    which = (fork_parent % BR_DEV != first).astype(jnp.int32)
+    owner_z, owner_y = owner // NY, owner % NY
+    near = (me_index // NY - owner_z) % NEAR
+    front = owner * 2 + which
+    back = ((owner_y * NEAR + near) * (NZ // NEAR) + owner_z // NEAR) * 2 + which
+    return front, back
+
+
+def gather_parents(listing, kv_cache, page_table):
+    cache = kv_cache[:, :, :, 0]
+    width = cache.shape[-1]
+    front, back = pick_pages(lax.axis_index("dp"), listing, page_table, cache)
+    plane = share(front.reshape(-1, width), groups_y()).reshape(-1, width)
+    fronts = lax.all_gather(plane, "dp", axis=0, tiled=True, axis_index_groups=groups_z())
+    far = share(back.reshape(-1, width), groups_far()).reshape(-1, width)
+    column = jnp.concatenate(
+        [far] + [lax.ppermute(far, "dp", shift_z(step)) for step in (1, 2, -1)]
+    )
+    backs = share(column, groups_y()).reshape(-1, width)
+    return fronts.reshape((-1,) + front.shape[1:]), backs.reshape((-1,) + back.shape[1:])
 
 
 def local(
@@ -196,6 +212,8 @@
     rows_here = residual.shape[0]
     shards = lax.axis_size("tensor")
     partial = jnp.dot(attended, out_proj, preferred_element_type=jnp.float32).astype(jnp.bfloat16)
+    fronts, backs = gather_parents(listing, kv_cache, page_table)
+    backs, partial = lax.optimization_barrier((backs, partial))
     terms = lax.all_to_all(
         partial.reshape(shards, rows_here, -1), "tensor", split_axis=0, concat_axis=0, tiled=True
     )
@@ -208,7 +226,9 @@
         * norm_gain.astype(jnp.float32)
     )
     scores = jax.nn.sigmoid(jnp.sum(normed * score_weight.astype(jnp.float32), axis=-1))
-    child_pages = fork_pages(listing, fork_parent, kv_cache, page_table)
+    front_at, back_at = child_places(listing, fork_parent, lax.axis_index("dp"))
+    child_pages = place_children(back_at, backs, FRONT)
+    child_pages = place_children(front_at, fronts, 0, child_pages)[:, :, :, :, None]
     return (hidden_out, scores, child_pages)
 
 

time: 303 us -> 166 us (0.55)
  Pallas kernels: 104 us -> 8.08 us
  starting transfers between devices: 83.6 us -> 44.1 us
  waiting for transfers between devices: 83.9 us -> 63.4 us
  between operations: 1.06 us -> 14.4 us
  blocking collectives: 0 us -> 10.9 us
  other arithmetic: 7.04 us -> 3.85 us
    pallas_call x2 -> x3, Pallas kernels: 104 us -> 8.08 us  [the longest x2 5.31 us: place_children(): pl.pallas_call(functools.partial(place_kernel, first_page, len(given) - 2...]
    ppermute x15 -> x3, waiting for transfers between devices: 78.7 us -> 11.3 us  [gather_parents(): lax.ppermute(far, 'dp', shift_z(step))]
    ppermute x15 -> x3, starting transfers between devices: 60.6 us -> 10.2 us  [gather_parents(): lax.ppermute(far, 'dp', shift_z(step))]
    all_to_all x0 -> x2, waiting for transfers between devices: none -> 24.5 us  [share(): lax.all_to_all(copies, 'dp', split_axis=0, concat_axis=0, tiled=True, axi...]
    all_to_all x1, waiting for transfers between devices: 0.01 us -> 15.2 us  [local(): lax.all_to_all(partial.reshape(shards, rows_here, -1), 'tensor', split_ax...]
    all_to_all x0 -> x2, starting transfers between devices: none -> 11.2 us  [share(): lax.all_to_all(copies, 'dp', split_axis=0, concat_axis=0, tiled=True, axi...]
    all_to_all x0 -> x1, blocking collectives: none -> 10.9 us  [share(): lax.all_to_all(copies, 'dp', split_axis=0, concat_axis=0, tiled=True, axi...]
    all_to_all x1, waiting for transfers between devices: 5.23 us -> 12.5 us  [parent_listing(): lax.all_to_all(copies, 'dp', split_axis=0, concat_axis=0, tiled=True)[:, 0]]
  transfers between devices with their start and end apart: 17 -> 8, of which waited for: 6 -> 6; matrix products, arithmetic and copies ran while one was open for 7% -> 10% of each run, Pallas kernels for 0% -> 2%
where the time goes in v4:
time: 166 us; the launch traced here: 162 us
  waiting for transfers between devices  63.4 us (38%)
  starting transfers between devices  44.1 us (27%)
  between operations  14.4 us (9%)
  local copies, waits for them, and re-layouts  13.7 us (8%)
  blocking collectives  10.9 us (7%)
  Pallas kernels  8.08 us (5%)
  matrix products  3.9 us (2%)
  other arithmetic  3.85 us (2%)
    all_to_all x2, waiting for transfers between devices, share(): lax.all_to_all(copies, 'dp', split_axis=0, concat_axis=0, tiled=True, axi...  24.5 us
    all_to_all x1, starting transfers between devices, parent_listing(): lax.all_to_all(copies, 'dp', split_axis=0, concat_axis=0, tiled=True)[:, 0]  18.5 us
    all_to_all x1, waiting for transfers between devices, local(): lax.all_to_all(partial.reshape(shards, rows_here, -1), 'tensor', split_ax...  15.2 us
    all_to_all x1, waiting for transfers between devices, parent_listing(): lax.all_to_all(copies, 'dp', split_axis=0, concat_axis=0, tiled=True)[:, 0]  12.5 us
    ppermute x3, waiting for transfers between devices, gather_parents(): lax.ppermute(far, 'dp', shift_z(step))  11.3 us
    all_to_all x2, starting transfers between devices, share(): lax.all_to_all(copies, 'dp', split_axis=0, concat_axis=0, tiled=True, axi...  11.2 us
    all_to_all x1, blocking collectives, share(): lax.all_to_all(copies, 'dp', split_axis=0, concat_axis=0, tiled=True, axi...  10.9 us
    ppermute x3, starting transfers between devices, gather_parents(): lax.ppermute(far, 'dp', shift_z(step))  10.2 us
  transfers between devices with their start and end apart: 8, of which 6 were waited for; matrix products, arithmetic and copies ran while one was open for 10% of the time, Pallas kernels for 2%

profile of v4, /device:TPU:24, one launch (start us, length us, event | category | flops | bytes accessed | tf_op | source)
XLA Modules:
  0.0 162.3 jit_solution(5523423872294760738)
XLA Ops:
  7.2 0.8 pad.4
  8.0 0.6 broadcast_in_dim.98
  8.6 18.5 %all-to-all-start = ((s32[64,1,128]{2,1,0:T(1,128)}), s32[64,1,128]{2,1,0:T(1,128)S(1)}, u32[]{:S(2)}, u32[]{:S(2)}) async-start(s32[64,1,128]{2,1,0:T(1,128)} %broadcast_in_dim.98), calls=%async_computation | async-start | bytes 65536 | tf_op jit(solution)/shard_map/all_to_all | solution.py:69
  27.2 12.5 %all-to-all-done = s32[64,1,128]{2,1,0:T(1,128)S(1)} async-done(((s32[64,1,128]{2,1,0:T(1,128)}), s32[64,1,128]{2,1,0:T(1,128)S(1)}, u32[]{:S(2)}, u32[]{:S(2)}) %all-to-all-start) | async-done | bytes 32800 | tf_op jit(solution)/shard_map/all_to_all | solution.py:69
  39.6 0.6 copy-done.5
  40.2 2.8 %shard_map.121 = (bf16[2,6,2,16,128]{4,3,2,1,0:T(8,128)(2,1)}, bf16[2,2,2,16,128]{4,3,2,1,0:T(8,128)(2,1)}) custom-call(s32[1]{0:T(128)} %bitcast.me_ref, s32[64,128]{1,0:T(8,128)} %bitcast.110, s32[16,12]{1,0:T(8,128)} %table_ref.1, bf16[192,2,16,128]{3,2,1,0:T(8,128)(2,1)} %bitcast.102), custom_call_target="tpu_custom_call" | custom-call | tf_op jit(solution)/shard_map/pallas_call | solution.py:117
  43.0 0.9 broadcast_in_dim.113
  44.0 10.9 %all_to_all.25 = bf16[4,384,128]{2,1,0:T(8,128)(2,1)} all-to-all(bf16[4,384,128]{2,1,0:T(8,128)(2,1)S(1)} %broadcast_in_dim.113), channel_id=1, replica_groups={{0,8,16,24},{32,40,48,56},{64,72,80,88},{96,104,112,120},{128,136,144,1..., dimensions={0} | all-to-all | bytes 786432 | tf_op jit(solution)/shard_map/all_to_all | solution.py:90
  55.0 1.4 broadcast_in_dim.100
  56.4 3.9 %all-to-all-start.1 = ((bf16[4,128,128]{2,1,0:T(8,128)(2,1)}), bf16[4,128,128]{2,1,0:T(8,128)(2,1)}, u32[]{:S(2)}, u32[]{:S(2)}) async-start(bf16[4,128,128]{2,1,0:T(8,128)(2,1)} %broadcast_in_dim.100), calls=%async_computation.1 | async-start | bytes 262144 | tf_op jit(solution)/shard_map/all_to_all | solution.py:90
  60.4 2.0 %gather_fusion = bf16[192,2,16,128]{3,2,1,0:T(8,128)(2,1)} fusion(bf16[192,2,16,128]{3,2,1,0:T(8,128)(2,1)S(1)} %bitcast.103, s32[1024]{0:T(1024)S(1)} %pad_clamp_fusion), kind=kCustom, calls=%fused_computation | custom fusion | bytes 3146496 | tf_op jit(solution)/shard_map/gather | solution.py:27
  62.4 2.6 %fusion.37 = (bf16[16,12,1,16,1,128]{5,3,2,1,0,4:T(8,128)(2,1)S(1)}, bf16[16,12,1,16,1,128]{5,3,2,1,0,4:T(8,128)(2,1)}) fusion(bf16[16,12,2,16,1,128]{5,3,2,1,0,4:T(8,128)(2,1)} %bitcast.104), kind=kLoop, calls=%fused_computation.84 | loop fusion | bytes 3145728 | tf_op jit(solution)/shard_map/slice | solution.py:29
  65.0 9.0 %all-to-all-done.1 = bf16[4,128,128]{2,1,0:T(8,128)(2,1)} async-done(((bf16[4,128,128]{2,1,0:T(8,128)(2,1)}), bf16[4,128,128]{2,1,0:T(8,128)(2,1)}, u32[]{:S(2)}, u32[]{:S(2)}) %all-to-all-start.1) | async-done | bytes 131104 | tf_op jit(solution)/shard_map/all_to_all | solution.py:90
  73.9 2.9 %collective-permute-start.2 = (bf16[512,128]{1,0:T(8,128)(2,1)}, bf16[512,128]{1,0:T(8,128)(2,1)S(1)}, u32[]{:S(2)}, u32[]{:S(2)}) collective-permute-start(bf16[512,128]{1,0:T(8,128)(2,1)} %bitcast.4), channel_id=1, source_target_pairs={{0,480},{8,488},{16,496},{24,504},{32,0},{40,8},{48,16},{56,24},{6... | collective-permute-start | bytes 393224 | tf_op jit(solution)/shard_map/ppermute | solution.py:192
  76.9 3.8 %collective-permute-start.1 = (bf16[512,128]{1,0:T(8,128)(2,1)}, bf16[512,128]{1,0:T(8,128)(2,1)S(1)}, u32[]{:S(2)}, u32[]{:S(2)}) collective-permute-start(bf16[512,128]{1,0:T(8,128)(2,1)} %bitcast.4), channel_id=1, source_target_pairs={{0,64},{8,72},{16,80},{24,88},{32,96},{40,104},{48,112},{56,120},{... | collective-permute-start | bytes 393224 | tf_op jit(solution)/shard_map/ppermute | solution.py:192
  80.7 3.4 %collective-permute-start = (bf16[512,128]{1,0:T(8,128)(2,1)}, bf16[512,128]{1,0:T(8,128)(2,1)S(1)}, u32[]{:S(2)}, u32[]{:S(2)}) collective-permute-start(bf16[512,128]{1,0:T(8,128)(2,1)} %bitcast.4), channel_id=1, source_target_pairs={{0,32},{8,40},{16,48},{24,56},{32,64},{40,72},{48,80},{56,88},{64,... | collective-permute-start | bytes 393224 | tf_op jit(solution)/shard_map/ppermute | solution.py:192
  84.2 6.8 %collective-permute-done.1 = bf16[512,128]{1,0:T(8,128)(2,1)S(1)} collective-permute-done((bf16[512,128]{1,0:T(8,128)(2,1)}, bf16[512,128]{1,0:T(8,128)(2,1)S(1)}, u32[]{:S(2)}, u32[]{:S(2)}) %collective-permute-start.1) | collective-permute-done | bytes 131104 | tf_op jit(solution)/shard_map/ppermute | solution.py:192
  91.0 4.6 %collective-permute-done = bf16[512,128]{1,0:T(8,128)(2,1)S(1)} collective-permute-done((bf16[512,128]{1,0:T(8,128)(2,1)}, bf16[512,128]{1,0:T(8,128)(2,1)S(1)}, u32[]{:S(2)}, u32[]{:S(2)}) %collective-permute-start) | collective-permute-done | bytes 131104 | tf_op jit(solution)/shard_map/ppermute | solution.py:192
  95.5 0.9 pad_maximum_fusion
  96.5 1.6 broadcast_in_dim.101
  98.1 7.2 %all-to-all-start.2 = ((bf16[4,2048,128]{2,1,0:T(8,128)(2,1)}), bf16[4,2048,128]{2,1,0:T(8,128)(2,1)}, u32[]{:S(2)}, u32[]{:S(2)}) async-start(bf16[4,2048,128]{2,1,0:T(8,128)(2,1)} %broadcast_in_dim.101), calls=%async_computation.2 | async-start | bytes 4194304 | tf_op jit(solution)/shard_map/all_to_all | solution.py:90
  105.3 0.5 fusion.39
  105.8 0.7 fusion.38
  107.9 2.0 %convolution_convert_fusion = bf16[256,2560]{1,0:T(8,128)(2,1)} fusion(bf16[384,2560]{1,0:T(8,128)(2,1)S(1)} %copy-done, bf16[32,8,3,128]{3,2,1,0:T(4,128)(2,1)S(1)} %bitcast.107), kind=kOutput, calls=%fused_computation.1 | convolution fusion | flops 503971840 | bytes 3473408 | tf_op jit(solution)/shard_map/dot_general | solution.py:214
  109.9 15.5 %all-to-all-done.2 = bf16[4,2048,128]{2,1,0:T(8,128)(2,1)} async-done(((bf16[4,2048,128]{2,1,0:T(8,128)(2,1)}), bf16[4,2048,128]{2,1,0:T(8,128)(2,1)}, u32[]{:S(2)}, u32[]{:S(2)}) %all-to-all-start.2) | async-done | bytes 2097184 | tf_op jit(solution)/shard_map/all_to_all | solution.py:90
  125.4 4.3 %all-to-all-start.3 = ((bf16[8,32,2560]{2,1,0:T(8,128)(2,1)}), bf16[8,32,2560]{2,1,0:T(8,128)(2,1)S(1)}, u32[]{:S(2)}, u32[]{:S(2)}) async-start(bf16[8,32,2560]{2,1,0:T(8,128)(2,1)} %bitcast.28), calls=%async_computation.3 | async-start | bytes 2621440 | tf_op jit(solution)/shard_map/all_to_all | solution.py:217
  130.3 3.0 %shard_map.122.refs_0_ = bf16[48,8,2,16,128]{4,3,2,1,0:T(8,128)(2,1)} custom-call(s32[48]{0:T(128)S(1)} %get-tuple-element.23.where_ref, bf16[128,2,2,16,128]{4,3,2,1,0:T(8,128)(2,1)} %bitcast.5.source_ref), custom_call_target="tpu_custom_call" | custom-call | tf_op jit(solution)/shard_map/pallas_call | solution.py:156
  133.3 15.2 %all-to-all-done.3 = bf16[8,32,2560]{2,1,0:T(8,128)(2,1)S(1)} async-done(((bf16[8,32,2560]{2,1,0:T(8,128)(2,1)}), bf16[8,32,2560]{2,1,0:T(8,128)(2,1)S(1)}, u32[]{:S(2)}, u32[]{:S(2)}) %all-to-all-start.3) | async-done | bytes 1310752 | tf_op jit(solution)/shard_map/all_to_all | solution.py:217
  148.7 0.7 fusion.36
  149.8 0.5 add_divide_fusion
  150.3 2.8 %copy-done.1 = bf16[24576,128]{1,0:T(8,128)(2,1)S(1)} copy-done((bf16[24576,128]{1,0:T(8,128)(2,1)S(1)}, bf16[24576,128]{1,0:T(8,128)(2,1)}, u32[]{:S(2)}) %copy-start.1) | copy-done | bytes 6291480
  153.1 2.3 %shard_map.123 = bf16[48,8,2,16,128]{4,3,2,1,0:T(8,128)(2,1)} custom-call(s32[48]{0:T(128)S(1)} %multiply_add_fusion.1.where_ref, bf16[128,6,2,16,128]{4,3,2,1,0:T(8,128)(2,1)S(1)} %bitcast.100, bf16[48,8,2,16,128]{4,3,2,1,0:T(8,128)(2,1)} %shard_map.122.refs_0_), custom_call_target="tpu_custom_call", output_to_operand_aliasing={{}: (2, {})} | custom-call | tf_op jit(solution)/shard_map/pallas_call | solution.py:156
  (54 shorter events, 2.7 us)
Async XLA Ops:
  7.2 100.8 %copy-start = (bf16[384,2560]{1,0:T(8,128)(2,1)S(1)}, bf16[384,2560]{1,0:T(8,128)(2,1)}, u32[]{:S(2)}) copy-start(bf16[384,2560]{1,0:T(8,128)(2,1)} %param.15) | copy-start | bytes 5898244
  8.6 31.0 %all-to-all-start = ((s32[64,1,128]{2,1,0:T(1,128)}), s32[64,1,128]{2,1,0:T(1,128)S(1)}, u32[]{:S(2)}, u32[]{:S(2)}) async-start(s32[64,1,128]{2,1,0:T(1,128)} %broadcast_in_dim.98), calls=%async_computation | async-start | bytes 65536 | tf_op jit(solution)/shard_map/all_to_all | solution.py:69
  27.1 123.2 %all-gather.2.cloned.1.call-start = ((), (), s32[]{:S(2)}) async-start(), calls=%async_computation.5 | async-start | bytes 6684672 | tf_op jit(solution)/shard_map/all_gather | solution.py:189
  39.6 0.6 copy-start.5
  40.2 14.6 %copy-start.8 = (s32[16,12]{1,0:T(8,128)S(1)}, s32[16,12]{1,0:T(8,128)}, u32[]{:S(2)}) copy-start(s32[16,12]{1,0:T(8,128)} %table_ref.1) | copy-start | bytes 2308
  40.2 20.1 %copy-start.2 = (bf16[192,2,16,1,128]{4,2,3,1,0:T(8,128)(2,1)S(1)}, bf16[192,2,16,1,128]{4,2,3,1,0:T(8,128)(2,1)}, u32[]{:S(2)}) copy-start(bf16[192,2,16,1,128]{4,2,3,1,0:T(8,128)(2,1)} %param.12) | copy-start | bytes 4718596
  56.4 17.5 %all-to-all-start.1 = ((bf16[4,128,128]{2,1,0:T(8,128)(2,1)}), bf16[4,128,128]{2,1,0:T(8,128)(2,1)}, u32[]{:S(2)}, u32[]{:S(2)}) async-start(bf16[4,128,128]{2,1,0:T(8,128)(2,1)} %broadcast_in_dim.100), calls=%async_computation.1 | async-start | bytes 262144 | tf_op jit(solution)/shard_map/all_to_all | solution.py:90
  62.4 21.7 %copy-start.12 = (s32[16]{0:T(128)S(1)}, s32[16]{0:T(128)}, u32[]{:S(2)}) copy-start(s32[16]{0:T(128)} %param.14) | copy-start | bytes 196
  73.9 10.3 %collective-permute-start.2 = (bf16[512,128]{1,0:T(8,128)(2,1)}, bf16[512,128]{1,0:T(8,128)(2,1)S(1)}, u32[]{:S(2)}, u32[]{:S(2)}) collective-permute-start(bf16[512,128]{1,0:T(8,128)(2,1)} %bitcast.4), channel_id=1, source_target_pairs={{0,480},{8,488},{16,496},{24,504},{32,0},{40,8},{48,16},{56,24},{6... | collective-permute-start | bytes 393224 | tf_op jit(solution)/shard_map/ppermute | solution.py:192
  76.9 14.1 %collective-permute-start.1 = (bf16[512,128]{1,0:T(8,128)(2,1)}, bf16[512,128]{1,0:T(8,128)(2,1)S(1)}, u32[]{:S(2)}, u32[]{:S(2)}) collective-permute-start(bf16[512,128]{1,0:T(8,128)(2,1)} %bitcast.4), channel_id=1, source_target_pairs={{0,64},{8,72},{16,80},{24,88},{32,96},{40,104},{48,112},{56,120},{... | collective-permute-start | bytes 393224 | tf_op jit(solution)/shard_map/ppermute | solution.py:192
  80.7 14.9 %collective-permute-start = (bf16[512,128]{1,0:T(8,128)(2,1)}, bf16[512,128]{1,0:T(8,128)(2,1)S(1)}, u32[]{:S(2)}, u32[]{:S(2)}) collective-permute-start(bf16[512,128]{1,0:T(8,128)(2,1)} %bitcast.4), channel_id=1, source_target_pairs={{0,32},{8,40},{16,48},{24,56},{32,64},{40,72},{48,80},{56,88},{64,... | collective-permute-start | bytes 393224 | tf_op jit(solution)/shard_map/ppermute | solution.py:192
  98.1 7.2 %copy-start.3 = (bf16[16,16,3,128]{3,1,2,0:T(8,128)(2,1)S(1)}, bf16[16,16,3,128]{3,1,2,0:T(8,128)(2,1)}, u32[]{:S(2)}) copy-start(bf16[16,16,3,128]{3,1,2,0:T(8,128)(2,1)} %param.10) | copy-start | bytes 589828
  98.1 7.2 %copy-start.9 = (bf16[16,2,16,1,128]{4,2,3,1,0:T(8,128)(2,1)S(1)}, bf16[16,2,16,1,128]{4,2,3,1,0:T(8,128)(2,1)}, u32[]{:S(2)}) copy-start(bf16[16,2,16,1,128]{4,2,3,1,0:T(8,128)(2,1)} %param.11) | copy-start | bytes 393220
  98.1 27.4 %all-to-all-start.2 = ((bf16[4,2048,128]{2,1,0:T(8,128)(2,1)}), bf16[4,2048,128]{2,1,0:T(8,128)(2,1)}, u32[]{:S(2)}, u32[]{:S(2)}) async-start(bf16[4,2048,128]{2,1,0:T(8,128)(2,1)} %broadcast_in_dim.101), calls=%async_computation.2 | async-start | bytes 4194304 | tf_op jit(solution)/shard_map/all_to_all | solution.py:90
  105.8 1.3 copy-start.4
  109.9 19.8 %copy-start.10 = (bf16[2560]{0:T(1024)(128)(2,1)S(1)}, bf16[2560]{0:T(1024)(128)(2,1)}, u32[]{:S(2)}) copy-start(bf16[2560]{0:T(1024)(128)(2,1)} %param.17) | copy-start | bytes 15364
  109.9 19.8 %copy-start.11 = (bf16[2560]{0:T(1024)(128)(2,1)S(1)}, bf16[2560]{0:T(1024)(128)(2,1)}, u32[]{:S(2)}) copy-start(bf16[2560]{0:T(1024)(128)(2,1)} %param.18) | copy-start | bytes 15364
  109.9 19.8 %copy-start.13 = (s32[48]{0:T(128)S(1)}, s32[48]{0:T(128)}, u32[]{:S(2)}) copy-start(s32[48]{0:T(128)} %param.19) | copy-start | bytes 580
  109.9 19.9 %copy-start.6 = (s32[64,1,128]{2,1,0:T(1,128)S(1)}, s32[64,1,128]{2,1,0:T(1,128)}, u32[]{:S(2)}) copy-start(s32[64,1,128]{2,1,0:T(1,128)} %copy-done.5) | copy-start | bytes 98308
  125.4 23.0 %all-to-all-start.3 = ((bf16[8,32,2560]{2,1,0:T(8,128)(2,1)}), bf16[8,32,2560]{2,1,0:T(8,128)(2,1)S(1)}, u32[]{:S(2)}, u32[]{:S(2)}) async-start(bf16[8,32,2560]{2,1,0:T(8,128)(2,1)} %bitcast.28), calls=%async_computation.3 | async-start | bytes 2621440 | tf_op jit(solution)/shard_map/all_to_all | solution.py:217
  133.3 15.4 %copy-start.7 = (bf16[32,2560]{1,0:T(8,128)(2,1)S(1)}, bf16[32,2560]{1,0:T(8,128)(2,1)}, u32[]{:S(2)}) copy-start(bf16[32,2560]{1,0:T(8,128)(2,1)} %param.16) | copy-start | bytes 491524
  150.3 2.8 %copy-start.1 = (bf16[24576,128]{1,0:T(8,128)(2,1)S(1)}, bf16[24576,128]{1,0:T(8,128)(2,1)}, u32[]{:S(2)}) copy-start(bf16[24576,128]{1,0:T(8,128)(2,1)} %all-gather.2.cloned.1.call-done) | copy-start | bytes 18874372
Sparse Core Ops, SparseCore 0:
  55.0 87.4 all-gather.1

commit v5 on v3

--- a/solution.py
+++ b/solution.py
@@ -72,10 +72,6 @@
     return [(z * NY + y, (z + step) % NZ * NY + y) for z in range(NZ) for y in range(NY)]
 
 
-def shift_y(step):
-    return [(z * NY + y, z * NY + (y + step) % NY) for z in range(NZ) for y in range(NY)]
-
-
 def groups_far():
     return [[(near + NEAR * far) * NY + y for far in range(NZ // NEAR)] for near in range(NEAR) for y in range(NY)]
 
@@ -85,23 +81,13 @@
 
 
 def share(block, groups):
-    copies = jnp.broadcast_to(block[None], (len(groups[0]),) + block.shape)
+    return exchange(jnp.broadcast_to(block[None], (len(groups[0]),) + block.shape), groups)
+
+
+def exchange(copies, groups):
     return lax.all_to_all(
         copies, "dp", split_axis=0, concat_axis=0, tiled=True, axis_index_groups=groups
     )
-
-
-def both_ways(block, shift):
-    up = lax.ppermute(block, "dp", shift(1))
-    down = lax.ppermute(block, "dp", shift(-1))
-    return up, down
-
-
-def forward(up, down, shift):
-    half = up.shape[0] // 2
-    up_two = lax.ppermute(up[:half], "dp", shift(1))
-    down_two = lax.ppermute(down[half:], "dp", shift(-1))
-    return up_two, down_two
 
 
 def pick_kernel(me_ref, listing_ref, table_ref, cache_ref, out_ref, sems):
@@ -192,7 +178,7 @@
     )(*given)
 
 
-def child_places(listing, fork_parent, me_z, me_y):
+def child_places(listing, fork_parent, me_index):
     owner = fork_parent // BR_DEV
     asked = listing.reshape(1, -1)
     same = (asked // BR_DEV) == owner[:, None]
@@ -200,47 +186,54 @@
     is_low = fork_parent % BR_DEV == first
     owner_z, owner_y = owner // NY, owner % NY
     far = owner_z // NEAR
-    near = (me_z - owner_z) % NEAR
-    apart = (me_y - owner_y) % NY
-    step = jnp.where(is_low, apart, near)
-    inner = jnp.where(is_low, near, owner_y) * (NZ // NEAR) + far
-    place = jnp.where(step == 0, 0, jnp.where(step == 1, NZ, 2 * NZ)) + inner
-    early = jnp.where(step == 2, -1, place + jnp.where(is_low, 0, 3 * NZ))
-    late = jnp.where(step == 2, inner + jnp.where(is_low, 0, NZ), -1)
+    near = (me_index // NY - owner_z) % NEAR
+    in_plane = owner_y * (NZ // NEAR) + far
+    step = jnp.where(near == 0, 0, jnp.where(near == 1, NZ, 2 * NZ))
+    early = jnp.where(is_low | (near == 2), -1, step + in_plane)
+    in_all = (owner_y * NEAR + near) * (NZ // NEAR) + far
+    late = jnp.where(is_low, NZ + in_all, jnp.where(near == 2, in_plane, -1))
     return early.astype(jnp.int32), late.astype(jnp.int32)
 
 
-def gather_near(listing, kv_cache, page_table):
-    me_index = lax.axis_index("dp")
+def gather_far(listing, kv_cache, page_table):
     cache = kv_cache[:, :, :, 0]
     width = cache.shape[-1]
-    picked = pick_pages(me_index, listing, page_table, cache)
+    picked = pick_pages(lax.axis_index("dp"), listing, page_table, cache)
     rows = picked[0].size // width
-
-    far = share(picked.reshape(2 * rows, width), groups_far())
+    return share(picked.reshape(2 * rows, width), groups_far()), picked.shape[1:]
+
+
+def gather_near(far):
+    rows, width = far.shape[1] // 2, far.shape[2]
     low_far = far[:, :rows].reshape(-1, width)
     high_far = far[:, rows:].reshape(-1, width)
-    high_plane = share(high_far, groups_y()).reshape(-1, width)
+    copies = jnp.broadcast_to(high_far[None], (NY,) + high_far.shape)
+    low_far, copies = lax.optimization_barrier((low_far, copies))
+    high_plane = exchange(copies, groups_y()).reshape(-1, width)
     low_column = jnp.concatenate(
         [low_far] + [lax.ppermute(low_far, "dp", shift_z(step)) for step in (1, 2, -1)]
     )
-    return low_column, high_plane, picked.shape[1:]
-
-
-def fork_pages(listing, fork_parent, low_column, high_plane, tile):
-    me_index = lax.axis_index("dp")
-    me_z, me_y = me_index // NY, me_index % NY
-    early, late = child_places(listing, fork_parent, me_z, me_y)
-    low_up, low_down = both_ways(low_column, shift_y)
-    high_up, high_down = both_ways(high_plane, shift_z)
-    low_two = forward(low_up, low_down, shift_y)
-    high_two = forward(high_up, high_down, shift_z)
-    first = (low_column, low_up, low_down, high_plane, high_up, high_down)
-    placed = place_children(early, [part.reshape((-1,) + tile) for part in first])
-    placed = place_children(
-        late, [part.reshape((-1,) + tile) for part in low_two + high_two], placed
-    )
-    return placed[:, :, :, :, None]
+    return low_column, high_plane
+
+
+def gather_rest(low_column, high_plane):
+    half = high_plane.shape[0] // 2
+    low_all = share(low_column, groups_y())
+    up = lax.ppermute(high_plane, "dp", shift_z(1))
+    down = lax.ppermute(high_plane, "dp", shift_z(-1))
+    up_two = lax.ppermute(high_plane[:half], "dp", shift_z(2))
+    down_two = lax.ppermute(high_plane[half:], "dp", shift_z(-2))
+    return (high_plane, up, down), (up_two, down_two, low_all)
+
+
+def halve(held, apart):
+    shards = lax.axis_size("tensor")
+    mine = (lax.axis_index("tensor") // apart) % 2
+    pairs = held.reshape((-1, 2) + held.shape[1:])
+    keep = lax.dynamic_index_in_dim(pairs, mine, 1, keepdims=False)
+    send = lax.dynamic_index_in_dim(pairs, 1 - mine, 1, keepdims=False)
+    came = lax.ppermute(send, "tensor", [(i, i ^ apart) for i in range(shards)])
+    return keep.astype(jnp.float32) + came.astype(jnp.float32)
 
 
 def local(
@@ -255,17 +248,22 @@
     score_weight,
     fork_parent,
 ):
-    listing = parent_listing(fork_parent)
+    listing, queries = lax.optimization_barrier((parent_listing(fork_parent), queries))
     attended = attend(queries, new_kv, kv_cache, page_table, lengths)
     rows_here = residual.shape[0]
-    shards = lax.axis_size("tensor")
     partial = jnp.dot(attended, out_proj, preferred_element_type=jnp.float32).astype(jnp.bfloat16)
-    low_column, high_plane, tile = gather_near(listing, kv_cache, page_table)
-    low_column, high_plane, partial = lax.optimization_barrier((low_column, high_plane, partial))
-    terms = lax.all_to_all(
-        partial.reshape(shards, rows_here, -1), "tensor", split_axis=0, concat_axis=0, tiled=True
-    )
-    updated = jnp.sum(terms.astype(jnp.float32), axis=0) + residual.astype(jnp.float32)
+    far, tile = gather_far(listing, kv_cache, page_table)
+    held = halve(partial.reshape(lax.axis_size("tensor"), rows_here, -1), 1).astype(jnp.bfloat16)
+    far, held = lax.optimization_barrier((far, held))
+    low_column, high_plane = gather_near(far)
+    held = halve(held, 2).astype(jnp.bfloat16)
+    low_column, high_plane, held = lax.optimization_barrier((low_column, high_plane, held))
+    first, last = gather_rest(low_column, high_plane)
+    early, late = child_places(listing, fork_parent, lax.axis_index("dp"))
+    placed = place_children(early, [part.reshape((-1,) + tile) for part in first])
+    placed = place_children(late, [part.reshape((-1,) + tile) for part in last], placed)
+    child_pages = placed[:, :, :, :, None]
+    updated = halve(held, 4)[0] + residual.astype(jnp.float32)
     hidden_out = updated.astype(jnp.bfloat16)
     block_ends = updated.reshape(rows_here // CH, CH, updated.shape[1])[:, CH - 1]
     normed = (
@@ -274,7 +272,6 @@
         * norm_gain.astype(jnp.float32)
     )
     scores = jax.nn.sigmoid(jnp.sum(normed * score_weight.astype(jnp.float32), axis=-1))
-    child_pages = fork_pages(listing, fork_parent, low_column, high_plane, tile)
     return (hidden_out, scores, child_pages)
 
 

time: 170 us -> 179 us (1.053)
  the two profiles are of different devices: /device:TPU:32 before, /device:TPU:24 now
where the time goes in v5:
time: 179 us; the launch traced here: 176 us
  starting transfers between devices  70.2 us (39%)
  waiting for transfers between devices  65.8 us (37%)
  local copies, waits for them, and re-layouts  17.4 us (10%)
  Pallas kernels  9.49 us (5%)
  other arithmetic  9.12 us (5%)
  matrix products  2.74 us (2%)
    ppermute x1, waiting for transfers between devices, gather_rest(): up = lax.ppermute(high_plane, 'dp', shift_z(1))  23.7 us
    all_to_all x3, waiting for transfers between devices, exchange(): lax.all_to_all(copies, 'dp', split_axis=0, concat_axis=0, tiled=True, axi...  19.9 us
    all_to_all x1, starting transfers between devices, parent_listing(): lax.all_to_all(copies, 'dp', split_axis=0, concat_axis=0, tiled=True)[:, 0]  18.7 us
    all_to_all x3, starting transfers between devices, exchange(): lax.all_to_all(copies, 'dp', split_axis=0, concat_axis=0, tiled=True, axi...  16.8 us
    ppermute x3, starting transfers between devices, halve(): came = lax.ppermute(send, 'tensor', [(i, i ^ apart) for i in range(shards)])  10.4 us
    ppermute x1, waiting for transfers between devices, gather_rest(): down_two = lax.ppermute(high_plane[half:], 'dp', shift_z(-2))  9.37 us
    ppermute x3, starting transfers between devices, gather_near(): lax.ppermute(low_far, 'dp', shift_z(step))  9.27 us
    all_to_all x1, waiting for transfers between devices, parent_listing(): lax.all_to_all(copies, 'dp', split_axis=0, concat_axis=0, tiled=True)[:, 0]  7.45 us
  transfers between devices with their start and end apart: 14, of which 7 were waited for; matrix products, arithmetic and copies ran while one was open for 10% of the time, Pallas kernels for 1%

profile of v5, /device:TPU:24, one launch (start us, length us, event | category | flops | bytes accessed | tf_op | source)
XLA Modules:
  0.0 175.9 jit_solution(11843827320928247475)
XLA Ops:
  2.1 18.7 %all-to-all-start = ((s32[64,1,128]{2,1,0:T(1,128)}), s32[64,1,128]{2,1,0:T(1,128)}, u32[]{:S(2)}, u32[]{:S(2)}) async-start(s32[64,1,128]{2,1,0:T(1,128)} %broadcast_in_dim.110), calls=%async_computation | async-start | bytes 65536 | tf_op jit(solution)/shard_map/all_to_all | solution.py:68
  21.6 2.3 %gather_fusion = bf16[192,2,16,128]{3,2,1,0:T(8,128)(2,1)S(1)} fusion(bf16[192,2,16,128]{3,2,1,0:T(8,128)(2,1)} %bitcast.156, s32[1024]{0:T(1024)S(1)} %pad_clamp_fusion), kind=kCustom, calls=%fused_computation | custom fusion | bytes 3146496 | tf_op jit(solution)/shard_map/gather | solution.py:26
  23.9 1.6 fusion.44
  25.6 7.5 %all-to-all-done = s32[64,1,128]{2,1,0:T(1,128)} async-done(((s32[64,1,128]{2,1,0:T(1,128)}), s32[64,1,128]{2,1,0:T(1,128)}, u32[]{:S(2)}, u32[]{:S(2)}) %all-to-all-start) | async-done | bytes 32800 | tf_op jit(solution)/shard_map/all_to_all | solution.py:68
  33.1 2.8 %shard_map.121 = bf16[2,8,2,16,128]{4,3,2,1,0:T(8,128)(2,1)} custom-call(s32[1]{0:T(128)} %bitcast.me_ref, s32[64,128]{1,0:T(8,128)} %bitcast.1.listing_ref, s32[16,12]{1,0:T(8,128)} %table_ref.1, bf16[192,2,16,128]{3,2,1,0:T(8,128)(2,1)} %bitcast.157), custom_call_target="tpu_custom_call" | custom-call | tf_op jit(solution)/shard_map/pallas_call | solution.py:114
  35.8 1.8 %broadcast_in_dim.112 = bf16[4,512,128]{2,1,0:T(8,128)(2,1)} broadcast(bf16[512,128]{1,0:T(8,128)(2,1)} %bitcast.171), dimensions={1,2} | broadcast | bytes 655360 | tf_op jit(solution)/shard_map/broadcast_in_dim | solution.py:84
  37.6 4.3 %all-to-all-start.1 = ((bf16[4,512,128]{2,1,0:T(8,128)(2,1)}), bf16[4,512,128]{2,1,0:T(8,128)(2,1)}, u32[]{:S(2)}, u32[]{:S(2)}) async-start(bf16[4,512,128]{2,1,0:T(8,128)(2,1)} %broadcast_in_dim.112), calls=%async_computation.1 | async-start | bytes 1048576 | tf_op jit(solution)/shard_map/all_to_all | solution.py:88
  46.3 1.9 %collective-permute-start = (bf16[4,32,2560]{2,1,0:T(8,128)(2,1)}, bf16[4,32,2560]{2,1,0:T(8,128)(2,1)}, u32[]{:S(2)}, u32[]{:S(2)}) collective-permute-start(bf16[4,32,2560]{2,1,0:T(8,128)(2,1)} %dynamic-slice_bitcast_fusion), channel_id=1, source_target_pairs={{0,1},{1,0},{2,3},{3,2},{4,5},{5,4},{6,7},{7,6},{8,9},{9,8},{10,11... | collective-permute-start | bytes 1966088 | tf_op jit(solution)/shard_map/ppermute | solution.py:235
  49.0 1.7 collective-permute-done
  50.7 2.1 %fusion = bf16[4,32,2560]{2,1,0:T(8,128)(2,1)} fusion(bf16[4,32,2560]{2,1,0:T(8,128)(2,1)} %collective-permute-done, bf16[4,2,32,2560]{3,2,1,0:T(8,128)(2,1)S(1)} %bitcast.160, s32[]{:T(128)S(6)} %select_n.143), kind=kLoop, calls=%fused_computation.4 | loop fusion | flops 1310720 | bytes 1966084 | tf_op jit(solution)/shard_map/convert_element_type | solution.py:256
  52.8 19.8 %all-to-all-done.1 = bf16[4,512,128]{2,1,0:T(8,128)(2,1)} async-done(((bf16[4,512,128]{2,1,0:T(8,128)(2,1)}), bf16[4,512,128]{2,1,0:T(8,128)(2,1)}, u32[]{:S(2)}, u32[]{:S(2)}) %all-to-all-start.1) | async-done | bytes 524320 | tf_op jit(solution)/shard_map/all_to_all | solution.py:88
  72.6 1.1 fusion.46
  73.7 1.1 broadcast_in_dim.122
  74.8 2.5 %collective-permute-start.3 = (bf16[1024,128]{1,0:T(8,128)(2,1)S(1)}, bf16[1024,128]{1,0:T(8,128)(2,1)S(1)}, u32[]{:S(2)}, u32[]{:S(2)}) collective-permute-start(bf16[1024,128]{1,0:T(8,128)(2,1)S(1)} %bitcast.165), channel_id=1, source_target_pairs={{0,480},{8,488},{16,496},{24,504},{32,0},{40,8},{48,16},{56,24},{6... | collective-permute-start | bytes 786440 | tf_op jit(solution)/shard_map/ppermute | solution.py:214
  77.3 2.1 %collective-permute-start.2 = (bf16[1024,128]{1,0:T(8,128)(2,1)S(1)}, bf16[1024,128]{1,0:T(8,128)(2,1)}, u32[]{:S(2)}, u32[]{:S(2)}) collective-permute-start(bf16[1024,128]{1,0:T(8,128)(2,1)S(1)} %bitcast.166), channel_id=1, source_target_pairs={{0,64},{8,72},{16,80},{24,88},{32,96},{40,104},{48,112},{56,120},{... | collective-permute-start | bytes 786440 | tf_op jit(solution)/shard_map/ppermute | solution.py:214
  79.3 4.7 %collective-permute-start.1 = (bf16[1024,128]{1,0:T(8,128)(2,1)S(1)}, bf16[1024,128]{1,0:T(8,128)(2,1)}, u32[]{:S(2)}, u32[]{:S(2)}) collective-permute-start(bf16[1024,128]{1,0:T(8,128)(2,1)S(1)} %bitcast.167), channel_id=1, source_target_pairs={{0,32},{8,40},{16,48},{24,56},{32,64},{40,72},{48,80},{56,88},{64,... | collective-permute-start | bytes 786440 | tf_op jit(solution)/shard_map/ppermute | solution.py:214
  84.1 5.5 %all-to-all-start.2 = ((bf16[4,1024,128]{2,1,0:T(8,128)(2,1)}), bf16[4,1024,128]{2,1,0:T(8,128)(2,1)S(1)}, u32[]{:S(2)}, u32[]{:S(2)}) async-start(bf16[4,1024,128]{2,1,0:T(8,128)(2,1)} %broadcast_in_dim.122), calls=%async_computation.2 | async-start | bytes 2097152 | tf_op jit(solution)/shard_map/all_to_all | solution.py:88
  89.6 1.1 dynamic-slice_bitcast_fusion.1
  90.7 3.4 %collective-permute-start.4 = (bf16[2,32,2560]{2,1,0:T(8,128)(2,1)S(1)}, bf16[2,32,2560]{2,1,0:T(8,128)(2,1)S(1)}, u32[]{:S(2)}, u32[]{:S(2)}) collective-permute-start(bf16[2,32,2560]{2,1,0:T(8,128)(2,1)S(1)} %dynamic-slice_bitcast_fusion.1), channel_id=1, source_target_pairs={{0,2},{1,3},{2,0},{3,1},{4,6},{5,7},{6,4},{7,5},{8,10},{9,11},{10,... | collective-permute-start | bytes 983048 | tf_op jit(solution)/shard_map/ppermute | solution.py:235
  95.1 2.7 %collective-permute-done.1 = bf16[1024,128]{1,0:T(8,128)(2,1)} collective-permute-done((bf16[1024,128]{1,0:T(8,128)(2,1)S(1)}, bf16[1024,128]{1,0:T(8,128)(2,1)}, u32[]{:S(2)}, u32[]{:S(2)}) %collective-permute-start.1) | collective-permute-done | bytes 262176 | tf_op jit(solution)/shard_map/ppermute | solution.py:214
  97.8 2.1 %pad_maximum_fusion = bf16[4096,128]{1,0:T(8,128)(2,1)} fusion(bf16[1024,128]{1,0:T(8,128)(2,1)S(1)} %collective-permute-done.3, bf16[1024,128]{1,0:T(8,128)(2,1)} %collective-permute-done.2, bf16[1024,128]{1,0:T(8,128)(2,1)} %collective-permute-done.1, bf16[1024,128]{1,0:T(8,128)(2,1)S(1)} %bitcast.168), kind=kLoop, calls=%fused_computation.16 | loop fusion | flops 4194304 | bytes 2097152 | tf_op jit(solution)/shard_map/concatenate | solution.py:213
  100.0 3.9 %broadcast_in_dim.125 = bf16[4,4096,128]{2,1,0:T(8,128)(2,1)} broadcast(bf16[4096,128]{1,0:T(8,128)(2,1)} %pad_maximum_fusion), dimensions={1,2} | broadcast | bytes 5242880 | tf_op jit(solution)/shard_map/broadcast_in_dim | solution.py:84
  103.9 7.0 %all-to-all-start.3 = ((bf16[4,4096,128]{2,1,0:T(8,128)(2,1)}), bf16[4,4096,128]{2,1,0:T(8,128)(2,1)}, u32[]{:S(2)}, u32[]{:S(2)}) async-start(bf16[4,4096,128]{2,1,0:T(8,128)(2,1)} %broadcast_in_dim.125), calls=%async_computation.3 | async-start | bytes 8388608 | tf_op jit(solution)/shard_map/all_to_all | solution.py:88
  112.3 5.1 %collective-permute-start.5 = (bf16[1,32,2560]{2,1,0:T(8,128)(2,1)S(1)}, bf16[1,32,2560]{2,1,0:T(8,128)(2,1)S(1)}, u32[]{:S(2)}, u32[]{:S(2)}) collective-permute-start(bf16[1,32,2560]{2,1,0:T(8,128)(2,1)S(1)} %constant_dynamic-slice_fusion), channel_id=1, source_target_pairs={{0,4},{1,5},{2,6},{3,7},{4,0},{5,1},{6,2},{7,3},{8,12},{9,13},{10,... | collective-permute-start | bytes 491528 | tf_op jit(solution)/shard_map/ppermute | solution.py:235
  117.4 4.8 %collective-permute-start.8 = (bf16[4096,128]{1,0:T(8,128)(2,1)S(1)}, bf16[4096,128]{1,0:T(8,128)(2,1)S(1)}, u32[]{:S(2)}, u32[]{:S(2)}) collective-permute-start(bf16[4096,128]{1,0:T(8,128)(2,1)S(1)} %bitcast.148), channel_id=1, source_target_pairs={{0,32},{8,40},{16,48},{24,56},{32,64},{40,72},{48,80},{56,88},{64,... | collective-permute-start | bytes 3145736 | tf_op jit(solution)/shard_map/ppermute | solution.py:222
  122.2 2.3 %collective-permute-start.9 = (bf16[4096,128]{1,0:T(8,128)(2,1)S(1)}, bf16[4096,128]{1,0:T(8,128)(2,1)S(1)}, u32[]{:S(2)}, u32[]{:S(2)}) collective-permute-start(bf16[4096,128]{1,0:T(8,128)(2,1)S(1)} %bitcast.149), channel_id=1, source_target_pairs={{0,480},{8,488},{16,496},{24,504},{32,0},{40,8},{48,16},{56,24},{6... | collective-permute-start | bytes 3145736 | tf_op jit(solution)/shard_map/ppermute | solution.py:223
  124.5 4.7 %collective-permute-start.6 = (bf16[2048,128]{1,0:T(8,128)(2,1)S(1)}, bf16[2048,128]{1,0:T(8,128)(2,1)S(1)}, u32[]{:S(2)}, u32[]{:S(2)}) collective-permute-start(bf16[2048,128]{1,0:T(8,128)(2,1)S(1)} %get-tuple-element.45), channel_id=1, source_target_pairs={{0,64},{8,72},{16,80},{24,88},{32,96},{40,104},{48,112},{56,120},{... | collective-permute-start | bytes 1572872 | tf_op jit(solution)/shard_map/ppermute | solution.py:224
  129.2 3.2 %collective-permute-start.7 = (bf16[2048,128]{1,0:T(8,128)(2,1)S(1)}, bf16[2048,128]{1,0:T(8,128)(2,1)S(1)}, u32[]{:S(2)}, u32[]{:S(2)}) collective-permute-start(bf16[2048,128]{1,0:T(8,128)(2,1)S(1)} %get-tuple-element.44), channel_id=1, source_target_pairs={{0,448},{8,456},{16,464},{24,472},{32,480},{40,488},{48,496},{56,5... | collective-permute-start | bytes 1572872 | tf_op jit(solution)/shard_map/ppermute | solution.py:225
  134.1 23.7 %collective-permute-done.8 = bf16[4096,128]{1,0:T(8,128)(2,1)S(1)} collective-permute-done((bf16[4096,128]{1,0:T(8,128)(2,1)S(1)}, bf16[4096,128]{1,0:T(8,128)(2,1)S(1)}, u32[]{:S(2)}, u32[]{:S(2)}) %collective-permute-start.8) | collective-permute-done | bytes 1048608 | tf_op jit(solution)/shard_map/ppermute | solution.py:222
  157.8 2.2 %shard_map.122.refs_3_ = bf16[48,8,2,16,128]{4,3,2,1,0:T(8,128)(2,1)} custom-call(s32[48]{0:T(128)S(1)} %get-tuple-element.33.where_ref, bf16[16,8,2,16,128]{4,3,2,1,0:T(8,128)(2,1)S(1)} %bitcast.150, bf16[16,8,2,16,128]{4,3,2,1,0:T(8,128)(2,1)S(1)} %bitcast.151, bf16[16,8,2,16,128]{4,3,2,1,0:T(8,128)(2,1)S(1)} %bitcast.152), custom_call_target="tpu_custom_call" | custom-call | tf_op jit(solution)/shard_map/pallas_call | solution.py:165
  160.0 9.4 %collective-permute-done.7 = bf16[2048,128]{1,0:T(8,128)(2,1)S(1)} collective-permute-done((bf16[2048,128]{1,0:T(8,128)(2,1)S(1)}, bf16[2048,128]{1,0:T(8,128)(2,1)S(1)}, u32[]{:S(2)}, u32[]{:S(2)}) %collective-permute-start.7) | collective-permute-done | bytes 524320 | tf_op jit(solution)/shard_map/ppermute | solution.py:225
  171.3 4.5 %shard_map.123 = bf16[48,8,2,16,128]{4,3,2,1,0:T(8,128)(2,1)} custom-call(s32[48]{0:T(128)S(1)} %fusion.35.where_ref, bf16[8,8,2,16,128]{4,3,2,1,0:T(8,128)(2,1)S(1)} %bitcast.153, bf16[8,8,2,16,128]{4,3,2,1,0:T(8,128)(2,1)S(1)} %bitcast.154, bf16[64,8,2,16,128]{4,3,2,1,0:T(8,128)(2,1)} %bitcast.41.refs_2_, ...), custom_call_target="tpu_custom_call", output_to_operand_aliasing={{}: (4, {})} | custom-call | tf_op jit(solution)/shard_map/pallas_call | solution.py:165
  (74 shorter events, 13.2 us)
Async XLA Ops:
  0.6 43.9 %copy-start = (bf16[384,2560]{1,0:T(8,128)(2,1)S(1)}, bf16[384,2560]{1,0:T(8,128)(2,1)}, u32[]{:S(2)}) copy-start(bf16[384,2560]{1,0:T(8,128)(2,1)} %param.15) | copy-start | bytes 5898244
  2.1 31.0 %all-to-all-start = ((s32[64,1,128]{2,1,0:T(1,128)}), s32[64,1,128]{2,1,0:T(1,128)}, u32[]{:S(2)}, u32[]{:S(2)}) async-start(s32[64,1,128]{2,1,0:T(1,128)} %broadcast_in_dim.110), calls=%async_computation | async-start | bytes 65536 | tf_op jit(solution)/shard_map/all_to_all | solution.py:68
  23.9 1.6 copy-start.14
  33.0 8.9 %copy-start.3 = (bf16[16,12,1,16,1,128]{5,3,2,1,0,4:T(8,128)(2,1)S(1)}, bf16[16,12,1,16,1,128]{5,3,2,1,0,4:T(8,128)(2,1)}, u32[]{:S(2)}) copy-start(bf16[16,12,1,16,1,128]{5,3,2,1,0,4:T(8,128)(2,1)} %get-tuple-element.42) | copy-start | bytes 2359300
  33.0 8.9 %copy-start.7 = (bf16[16,16,3,128]{3,1,2,0:T(8,128)(2,1)S(1)}, bf16[16,16,3,128]{3,1,2,0:T(8,128)(2,1)}, u32[]{:S(2)}) copy-start(bf16[16,16,3,128]{3,1,2,0:T(8,128)(2,1)} %param.10) | copy-start | bytes 589828
  37.6 5.0 %copy-start.11 = (bf16[16,2,16,1,128]{4,2,3,1,0:T(8,128)(2,1)S(1)}, bf16[16,2,16,1,128]{4,2,3,1,0:T(8,128)(2,1)}, u32[]{:S(2)}) copy-start(bf16[16,2,16,1,128]{4,2,3,1,0:T(8,128)(2,1)} %param.11) | copy-start | bytes 393220
  37.6 35.0 %all-to-all-start.1 = ((bf16[4,512,128]{2,1,0:T(8,128)(2,1)}), bf16[4,512,128]{2,1,0:T(8,128)(2,1)}, u32[]{:S(2)}, u32[]{:S(2)}) async-start(bf16[4,512,128]{2,1,0:T(8,128)(2,1)} %broadcast_in_dim.112), calls=%async_computation.1 | async-start | bytes 1048576 | tf_op jit(solution)/shard_map/all_to_all | solution.py:88
  41.9 1.8 %copy-start.8 = (bf16[16,12,1,16,1,128]{5,3,2,1,0,4:T(8,128)(2,1)S(1)}, bf16[16,12,1,16,1,128]{5,3,2,1,0,4:T(8,128)(2,1)}, u32[]{:S(2)}) copy-start(bf16[16,12,1,16,1,128]{5,3,2,1,0,4:T(8,128)(2,1)} %get-tuple-element.43) | copy-start | bytes 2359300
  44.6 3.8 %copy-start.12 = (bf16[2560]{0:T(1024)(128)(2,1)S(1)}, bf16[2560]{0:T(1024)(128)(2,1)}, u32[]{:S(2)}) copy-start(bf16[2560]{0:T(1024)(128)(2,1)} %param.18) | copy-start | bytes 15364
  44.6 3.8 %copy-start.13 = (bf16[2560]{0:T(1024)(128)(2,1)S(1)}, bf16[2560]{0:T(1024)(128)(2,1)}, u32[]{:S(2)}) copy-start(bf16[2560]{0:T(1024)(128)(2,1)} %param.17) | copy-start | bytes 15364
  46.3 4.3 %collective-permute-start = (bf16[4,32,2560]{2,1,0:T(8,128)(2,1)}, bf16[4,32,2560]{2,1,0:T(8,128)(2,1)}, u32[]{:S(2)}, u32[]{:S(2)}) collective-permute-start(bf16[4,32,2560]{2,1,0:T(8,128)(2,1)} %dynamic-slice_bitcast_fusion), channel_id=1, source_target_pairs={{0,1},{1,0},{2,3},{3,2},{4,5},{5,4},{6,7},{7,6},{8,9},{9,8},{10,11... | collective-permute-start | bytes 1966088 | tf_op jit(solution)/shard_map/ppermute | solution.py:235
  74.8 19.3 %collective-permute-start.3 = (bf16[1024,128]{1,0:T(8,128)(2,1)S(1)}, bf16[1024,128]{1,0:T(8,128)(2,1)S(1)}, u32[]{:S(2)}, u32[]{:S(2)}) collective-permute-start(bf16[1024,128]{1,0:T(8,128)(2,1)S(1)} %bitcast.165), channel_id=1, source_target_pairs={{0,480},{8,488},{16,496},{24,504},{32,0},{40,8},{48,16},{56,24},{6... | collective-permute-start | bytes 786440 | tf_op jit(solution)/shard_map/ppermute | solution.py:214
  77.3 17.8 %collective-permute-start.2 = (bf16[1024,128]{1,0:T(8,128)(2,1)S(1)}, bf16[1024,128]{1,0:T(8,128)(2,1)}, u32[]{:S(2)}, u32[]{:S(2)}) collective-permute-start(bf16[1024,128]{1,0:T(8,128)(2,1)S(1)} %bitcast.166), channel_id=1, source_target_pairs={{0,64},{8,72},{16,80},{24,88},{32,96},{40,104},{48,112},{56,120},{... | collective-permute-start | bytes 786440 | tf_op jit(solution)/shard_map/ppermute | solution.py:214
  79.3 18.4 %collective-permute-start.1 = (bf16[1024,128]{1,0:T(8,128)(2,1)S(1)}, bf16[1024,128]{1,0:T(8,128)(2,1)}, u32[]{:S(2)}, u32[]{:S(2)}) collective-permute-start(bf16[1024,128]{1,0:T(8,128)(2,1)S(1)} %bitcast.167), channel_id=1, source_target_pairs={{0,32},{8,40},{16,48},{24,56},{32,64},{40,72},{48,80},{56,88},{64,... | collective-permute-start | bytes 786440 | tf_op jit(solution)/shard_map/ppermute | solution.py:214
  84.1 15.9 %all-to-all-start.2 = ((bf16[4,1024,128]{2,1,0:T(8,128)(2,1)}), bf16[4,1024,128]{2,1,0:T(8,128)(2,1)S(1)}, u32[]{:S(2)}, u32[]{:S(2)}) async-start(bf16[4,1024,128]{2,1,0:T(8,128)(2,1)} %broadcast_in_dim.122), calls=%async_computation.2 | async-start | bytes 2097152 | tf_op jit(solution)/shard_map/all_to_all | solution.py:88
  89.6 10.3 %copy-start.4 = (bf16[4,32,2560]{2,1,0:T(8,128)(2,1)S(1)}, bf16[4,32,2560]{2,1,0:T(8,128)(2,1)}, u32[]{:S(2)}) copy-start(bf16[4,32,2560]{2,1,0:T(8,128)(2,1)} %fusion) | copy-start | bytes 1966084
  90.7 9.2 %collective-permute-start.4 = (bf16[2,32,2560]{2,1,0:T(8,128)(2,1)S(1)}, bf16[2,32,2560]{2,1,0:T(8,128)(2,1)S(1)}, u32[]{:S(2)}, u32[]{:S(2)}) collective-permute-start(bf16[2,32,2560]{2,1,0:T(8,128)(2,1)S(1)} %dynamic-slice_bitcast_fusion.1), channel_id=1, source_target_pairs={{0,2},{1,3},{2,0},{3,1},{4,6},{5,7},{6,4},{7,5},{8,10},{9,11},{10,... | collective-permute-start | bytes 983048 | tf_op jit(solution)/shard_map/ppermute | solution.py:235
  100.0 12.2 %copy-start.5 = (bf16[2,32,2560]{2,1,0:T(8,128)(2,1)}, bf16[2,32,2560]{2,1,0:T(8,128)(2,1)S(1)}, u32[]{:S(2)}) copy-start(bf16[2,32,2560]{2,1,0:T(8,128)(2,1)S(1)} %fusion.9) | copy-start | bytes 983044
  103.9 7.0 %copy-start.15 = (s32[48]{0:T(128)S(1)}, s32[48]{0:T(128)}, u32[]{:S(2)}) copy-start(s32[48]{0:T(128)} %param.19) | copy-start | bytes 580
  103.9 66.4 %all-to-all-start.3 = ((bf16[4,4096,128]{2,1,0:T(8,128)(2,1)}), bf16[4,4096,128]{2,1,0:T(8,128)(2,1)}, u32[]{:S(2)}, u32[]{:S(2)}) async-start(bf16[4,4096,128]{2,1,0:T(8,128)(2,1)} %broadcast_in_dim.125), calls=%async_computation.3 | async-start | bytes 8388608 | tf_op jit(solution)/shard_map/all_to_all | solution.py:88
  110.9 21.6 %copy-start.9 = (bf16[32,2560]{1,0:T(8,128)(2,1)S(1)}, bf16[32,2560]{1,0:T(8,128)(2,1)}, u32[]{:S(2)}) copy-start(bf16[32,2560]{1,0:T(8,128)(2,1)} %param.16) | copy-start | bytes 491524
  112.2 20.2 %copy-start.6 = (bf16[2,32,2560]{2,1,0:T(8,128)(2,1)S(1)}, bf16[2,32,2560]{2,1,0:T(8,128)(2,1)}, u32[]{:S(2)}) copy-start(bf16[2,32,2560]{2,1,0:T(8,128)(2,1)} %copy-done.5) | copy-start | bytes 983044
  112.2 21.1 %copy-start.10 = (f32[2560]{0:T(1024)S(1)}, f32[2560]{0:T(1024)}, u32[]{:S(2)}) copy-start(f32[2560]{0:T(1024)} %convert_element_type.80) | copy-start | bytes 30724
  112.3 20.2 %collective-permute-start.5 = (bf16[1,32,2560]{2,1,0:T(8,128)(2,1)S(1)}, bf16[1,32,2560]{2,1,0:T(8,128)(2,1)S(1)}, u32[]{:S(2)}, u32[]{:S(2)}) collective-permute-start(bf16[1,32,2560]{2,1,0:T(8,128)(2,1)S(1)} %constant_dynamic-slice_fusion), channel_id=1, source_target_pairs={{0,4},{1,5},{2,6},{3,7},{4,0},{5,1},{6,2},{7,3},{8,12},{9,13},{10,... | collective-permute-start | bytes 491528 | tf_op jit(solution)/shard_map/ppermute | solution.py:235
  117.4 40.4 %collective-permute-start.8 = (bf16[4096,128]{1,0:T(8,128)(2,1)S(1)}, bf16[4096,128]{1,0:T(8,128)(2,1)S(1)}, u32[]{:S(2)}, u32[]{:S(2)}) collective-permute-start(bf16[4096,128]{1,0:T(8,128)(2,1)S(1)} %bitcast.148), channel_id=1, source_target_pairs={{0,32},{8,40},{16,48},{24,56},{32,64},{40,72},{48,80},{56,88},{64,... | collective-permute-start | bytes 3145736 | tf_op jit(solution)/shard_map/ppermute | solution.py:222
  122.2 35.6 %collective-permute-start.9 = (bf16[4096,128]{1,0:T(8,128)(2,1)S(1)}, bf16[4096,128]{1,0:T(8,128)(2,1)S(1)}, u32[]{:S(2)}, u32[]{:S(2)}) collective-permute-start(bf16[4096,128]{1,0:T(8,128)(2,1)S(1)} %bitcast.149), channel_id=1, source_target_pairs={{0,480},{8,488},{16,496},{24,504},{32,0},{40,8},{48,16},{56,24},{6... | collective-permute-start | bytes 3145736 | tf_op jit(solution)/shard_map/ppermute | solution.py:223
  124.5 35.6 %collective-permute-start.6 = (bf16[2048,128]{1,0:T(8,128)(2,1)S(1)}, bf16[2048,128]{1,0:T(8,128)(2,1)S(1)}, u32[]{:S(2)}, u32[]{:S(2)}) collective-permute-start(bf16[2048,128]{1,0:T(8,128)(2,1)S(1)} %get-tuple-element.45), channel_id=1, source_target_pairs={{0,64},{8,72},{16,80},{24,88},{32,96},{40,104},{48,112},{56,120},{... | collective-permute-start | bytes 1572872 | tf_op jit(solution)/shard_map/ppermute | solution.py:224
  129.2 40.2 %collective-permute-start.7 = (bf16[2048,128]{1,0:T(8,128)(2,1)S(1)}, bf16[2048,128]{1,0:T(8,128)(2,1)S(1)}, u32[]{:S(2)}, u32[]{:S(2)}) collective-permute-start(bf16[2048,128]{1,0:T(8,128)(2,1)S(1)} %get-tuple-element.44), channel_id=1, source_target_pairs={{0,448},{8,456},{16,464},{24,472},{32,480},{40,488},{48,496},{56,5... | collective-permute-start | bytes 1572872 | tf_op jit(solution)/shard_map/ppermute | solution.py:225
  169.4 0.9 copy-start.1
  170.3 1.0 copy-start.2

commit v6 on v4

--- a/solution.py
+++ b/solution.py
@@ -181,18 +181,32 @@
     return front, back
 
 
-def gather_parents(listing, kv_cache, page_table):
-    cache = kv_cache[:, :, :, 0]
-    width = cache.shape[-1]
-    front, back = pick_pages(lax.axis_index("dp"), listing, page_table, cache)
+def gather_fronts(front):
+    width = front.shape[-1]
     plane = share(front.reshape(-1, width), groups_y()).reshape(-1, width)
     fronts = lax.all_gather(plane, "dp", axis=0, tiled=True, axis_index_groups=groups_z())
-    far = share(back.reshape(-1, width), groups_far()).reshape(-1, width)
-    column = jnp.concatenate(
+    return fronts.reshape((-1,) + front.shape[1:])
+
+
+def gather_backs_far(back):
+    width = back.shape[-1]
+    return share(back.reshape(-1, width), groups_far()).reshape(-1, width)
+
+
+def gather_backs_near(far):
+    return jnp.concatenate(
         [far] + [lax.ppermute(far, "dp", shift_z(step)) for step in (1, 2, -1)]
     )
-    backs = share(column, groups_y()).reshape(-1, width)
-    return fronts.reshape((-1,) + front.shape[1:]), backs.reshape((-1,) + back.shape[1:])
+
+
+def halve(held, apart):
+    shards = lax.axis_size("tensor")
+    mine = (lax.axis_index("tensor") // apart) % 2
+    pairs = held.reshape((-1, 2) + held.shape[1:])
+    keep = lax.dynamic_index_in_dim(pairs, mine, 1, keepdims=False)
+    send = lax.dynamic_index_in_dim(pairs, 1 - mine, 1, keepdims=False)
+    came = lax.ppermute(send, "tensor", [(i, i ^ apart) for i in range(shards)])
+    return keep.astype(jnp.float32) + came.astype(jnp.float32)
 
 
 def local(
@@ -207,17 +221,19 @@
     score_weight,
     fork_parent,
 ):
-    listing = parent_listing(fork_parent)
+    listing, queries = lax.optimization_barrier((parent_listing(fork_parent), queries))
+    cache = kv_cache[:, :, :, 0]
+    front, back = pick_pages(lax.axis_index("dp"), listing, page_table, cache)
+    fronts = gather_fronts(front)
     attended = attend(queries, new_kv, kv_cache, page_table, lengths)
     rows_here = residual.shape[0]
-    shards = lax.axis_size("tensor")
     partial = jnp.dot(attended, out_proj, preferred_element_type=jnp.float32).astype(jnp.bfloat16)
-    fronts, backs = gather_parents(listing, kv_cache, page_table)
-    backs, partial = lax.optimization_barrier((backs, partial))
-    terms = lax.all_to_all(
-        partial.reshape(shards, rows_here, -1), "tensor", split_axis=0, concat_axis=0, tiled=True
-    )
-    updated = jnp.sum(terms.astype(jnp.float32), axis=0) + residual.astype(jnp.float32)
+    far, partial = lax.optimization_barrier((gather_backs_far(back), partial))
+    held = halve(partial.reshape(lax.axis_size("tensor"), rows_here, -1), 1).astype(jnp.bfloat16)
+    column, held = lax.optimization_barrier((gather_backs_near(far), held))
+    backs = share(column, groups_y()).reshape((-1,) + back.shape[1:])
+    held = halve(held, 2).astype(jnp.bfloat16)
+    updated = halve(held, 4)[0] + residual.astype(jnp.float32)
     hidden_out = updated.astype(jnp.bfloat16)
     block_ends = updated.reshape(rows_here // CH, CH, updated.shape[1])[:, CH - 1]
     normed = (

time: 166 us -> 163 us (0.982)
  waiting for transfers between devices: 63.4 us -> 56.7 us
  starting transfers between devices: 44.1 us -> 48.1 us
  other arithmetic: 3.85 us -> 6.33 us
    all_to_all x1 -> x0, waiting for transfers between devices: 15.2 us -> none  [local(): lax.all_to_all(partial.reshape(shards, rows_here, -1), 'tensor', split_ax...]
    ppermute x3 -> x6, starting transfers between devices: 10.2 us -> 19.6 us  [the longest x3 9.94 us: halve(): came = lax.ppermute(send, 'tensor', [(i, i ^ apart) for i in range(shards)])]
    ppermute x3 -> x6, waiting for transfers between devices: 11.3 us -> 17.9 us  [the longest x3 13.6 us: gather_backs_near(): lax.ppermute(far, 'dp', shift_z(step))]
    all_to_all x1 -> x0, starting transfers between devices: 4.27 us -> none  [local(): lax.all_to_all(partial.reshape(shards, rows_here, -1), 'tensor', split_ax...]
    all_to_all x2, waiting for transfers between devices: 24.5 us -> 26.3 us  [share(): lax.all_to_all(copies, 'dp', split_axis=0, concat_axis=0, tiled=True, axi...]
    unnamed x28 -> x30, local copies, waits for them, and re-layouts: 3.45 us -> 3.44 us
  transfers between devices with their start and end apart: 8 -> 10, of which waited for: 6 -> 7; matrix products, arithmetic and copies ran while one was open for 10% -> 10% of each run, Pallas kernels for 2% -> 2%
where the time goes in v6:
time: 163 us; the launch traced here: 161 us
  waiting for transfers between devices  56.7 us (35%)
  starting transfers between devices  48.1 us (30%)
  between operations  14.5 us (9%)
  local copies, waits for them, and re-layouts  13.6 us (8%)
  blocking collectives  10.9 us (7%)
  Pallas kernels  8.07 us (5%)
  other arithmetic  6.33 us (4%)
  matrix products  2.74 us (2%)
    all_to_all x2, waiting for transfers between devices, share(): lax.all_to_all(copies, 'dp', split_axis=0, concat_axis=0, tiled=True, axi...  26.3 us
    all_to_all x1, starting transfers between devices, parent_listing(): lax.all_to_all(copies, 'dp', split_axis=0, concat_axis=0, tiled=True)[:, 0]  18.5 us
    ppermute x3, waiting for transfers between devices, gather_backs_near(): lax.ppermute(far, 'dp', shift_z(step))  13.6 us
    all_to_all x1, waiting for transfers between devices, parent_listing(): lax.all_to_all(copies, 'dp', split_axis=0, concat_axis=0, tiled=True)[:, 0]  12.5 us
    all_to_all x1, blocking collectives, share(): lax.all_to_all(copies, 'dp', split_axis=0, concat_axis=0, tiled=True, axi...  10.9 us
    all_to_all x2, starting transfers between devices, share(): lax.all_to_all(copies, 'dp', split_axis=0, concat_axis=0, tiled=True, axi...  10 us
    ppermute x3, starting transfers between devices, halve(): came = lax.ppermute(send, 'tensor', [(i, i ^ apart) for i in range(shards)])  9.94 us
    ppermute x3, starting transfers between devices, gather_backs_near(): lax.ppermute(far, 'dp', shift_z(step))  9.65 us
  transfers between devices with their start and end apart: 10, of which 7 were waited for; matrix products, arithmetic and copies ran while one was open for 10% of the time, Pallas kernels for 2%

profile of v6, /device:TPU:24, one launch (start us, length us, event | category | flops | bytes accessed | tf_op | source)
XLA Modules:
  0.0 160.9 jit_solution(15249793021161646748)
XLA Ops:
  7.2 0.8 pad.4
  8.6 18.5 %all-to-all-start = ((s32[64,1,128]{2,1,0:T(1,128)}), s32[64,1,128]{2,1,0:T(1,128)S(1)}, u32[]{:S(2)}, u32[]{:S(2)}) async-start(s32[64,1,128]{2,1,0:T(1,128)} %broadcast_in_dim.98), calls=%async_computation | async-start | bytes 65536 | tf_op jit(solution)/shard_map/all_to_all | solution.py:69
  27.2 12.5 %all-to-all-done = s32[64,1,128]{2,1,0:T(1,128)S(1)} async-done(((s32[64,1,128]{2,1,0:T(1,128)}), s32[64,1,128]{2,1,0:T(1,128)S(1)}, u32[]{:S(2)}, u32[]{:S(2)}) %all-to-all-start) | async-done | bytes 32800 | tf_op jit(solution)/shard_map/all_to_all | solution.py:69
  40.2 2.8 %shard_map.121 = (bf16[2,6,2,16,128]{4,3,2,1,0:T(8,128)(2,1)}, bf16[2,2,2,16,128]{4,3,2,1,0:T(8,128)(2,1)}) custom-call(s32[1]{0:T(128)} %bitcast.me_ref, s32[64,128]{1,0:T(8,128)} %bitcast.161, s32[16,12]{1,0:T(8,128)} %table_ref.1, bf16[192,2,16,128]{3,2,1,0:T(8,128)(2,1)} %bitcast.145), custom_call_target="tpu_custom_call" | custom-call | tf_op jit(solution)/shard_map/pallas_call | solution.py:117
  43.0 0.9 broadcast_in_dim.112
  44.0 10.9 %all_to_all.20 = bf16[4,384,128]{2,1,0:T(8,128)(2,1)} all-to-all(bf16[4,384,128]{2,1,0:T(8,128)(2,1)S(1)} %broadcast_in_dim.112), channel_id=1, replica_groups={{0,8,16,24},{32,40,48,56},{64,72,80,88},{96,104,112,120},{128,136,144,1..., dimensions={0} | all-to-all | bytes 786432 | tf_op jit(solution)/shard_map/all_to_all | solution.py:90
  55.6 0.7 convert_element_type.83
  56.3 1.3 convert_element_type.84
  58.3 2.0 %gather_fusion = bf16[192,2,16,128]{3,2,1,0:T(8,128)(2,1)} fusion(bf16[192,2,16,128]{3,2,1,0:T(8,128)(2,1)S(1)} %bitcast.146, s32[1024]{0:T(1024)S(1)} %pad_clamp_fusion), kind=kCustom, calls=%fused_computation | custom fusion | bytes 3146496 | tf_op jit(solution)/shard_map/gather | solution.py:27
  60.3 0.7 iota_compare_fusion
  61.1 2.6 %fusion.40 = (bf16[16,12,1,16,1,128]{5,3,2,1,0,4:T(8,128)(2,1)S(1)}, bf16[16,12,1,16,1,128]{5,3,2,1,0,4:T(8,128)(2,1)}) fusion(bf16[16,12,2,16,1,128]{5,3,2,1,0,4:T(8,128)(2,1)} %bitcast.147), kind=kLoop, calls=%fused_computation.92 | loop fusion | bytes 3145728 | tf_op jit(solution)/shard_map/slice | solution.py:29
  64.3 3.3 %all-to-all-start.1 = ((bf16[4,128,128]{2,1,0:T(8,128)(2,1)}), bf16[4,128,128]{2,1,0:T(8,128)(2,1)S(1)}, u32[]{:S(2)}, u32[]{:S(2)}) async-start(bf16[4,128,128]{2,1,0:T(8,128)(2,1)} %broadcast_in_dim.100), calls=%async_computation.1 | async-start | bytes 262144 | tf_op jit(solution)/shard_map/all_to_all | solution.py:90
  68.2 0.7 fusion.41
  70.3 0.8 convolution_convert_fusion
  71.2 12.5 %all-to-all-done.1 = bf16[4,128,128]{2,1,0:T(8,128)(2,1)S(1)} async-done(((bf16[4,128,128]{2,1,0:T(8,128)(2,1)}), bf16[4,128,128]{2,1,0:T(8,128)(2,1)S(1)}, u32[]{:S(2)}, u32[]{:S(2)}) %all-to-all-start.1) | async-done | bytes 131104 | tf_op jit(solution)/shard_map/all_to_all | solution.py:90
  83.7 1.9 %collective-permute-start.3 = (bf16[4,32,2560]{2,1,0:T(8,128)(2,1)S(1)}, bf16[4,32,2560]{2,1,0:T(8,128)(2,1)S(1)}, u32[]{:S(2)}, u32[]{:S(2)}) collective-permute-start(bf16[4,32,2560]{2,1,0:T(8,128)(2,1)S(1)} %dynamic-slice_bitcast_fusion), channel_id=1, source_target_pairs={{0,1},{1,0},{2,3},{3,2},{4,5},{5,4},{6,7},{7,6},{8,9},{9,8},{10,11... | collective-permute-start | bytes 1966088 | tf_op jit(solution)/shard_map/ppermute | solution.py:208
  85.7 1.9 %collective-permute-start.2 = (bf16[512,128]{1,0:T(8,128)(2,1)S(1)}, bf16[512,128]{1,0:T(8,128)(2,1)S(1)}, u32[]{:S(2)}, u32[]{:S(2)}) collective-permute-start(bf16[512,128]{1,0:T(8,128)(2,1)S(1)} %bitcast.156), channel_id=1, source_target_pairs={{0,480},{8,488},{16,496},{24,504},{32,0},{40,8},{48,16},{56,24},{6... | collective-permute-start | bytes 393224 | tf_op jit(solution)/shard_map/ppermute | solution.py:198
  87.6 5.1 %collective-permute-start.1 = (bf16[512,128]{1,0:T(8,128)(2,1)S(1)}, bf16[512,128]{1,0:T(8,128)(2,1)S(1)}, u32[]{:S(2)}, u32[]{:S(2)}) collective-permute-start(bf16[512,128]{1,0:T(8,128)(2,1)S(1)} %bitcast.157), channel_id=1, source_target_pairs={{0,64},{8,72},{16,80},{24,88},{32,96},{40,104},{48,112},{56,120},{... | collective-permute-start | bytes 393224 | tf_op jit(solution)/shard_map/ppermute | solution.py:198
  92.7 2.6 %collective-permute-start = (bf16[512,128]{1,0:T(8,128)(2,1)S(1)}, bf16[512,128]{1,0:T(8,128)(2,1)S(1)}, u32[]{:S(2)}, u32[]{:S(2)}) collective-permute-start(bf16[512,128]{1,0:T(8,128)(2,1)S(1)} %bitcast.158), channel_id=1, source_target_pairs={{0,32},{8,40},{16,48},{24,56},{32,64},{40,72},{48,80},{56,88},{64,... | collective-permute-start | bytes 393224 | tf_op jit(solution)/shard_map/ppermute | solution.py:198
  95.4 0.8 collective-permute-done.2
  96.2 6.7 %collective-permute-done.1 = bf16[512,128]{1,0:T(8,128)(2,1)S(1)} collective-permute-done((bf16[512,128]{1,0:T(8,128)(2,1)S(1)}, bf16[512,128]{1,0:T(8,128)(2,1)S(1)}, u32[]{:S(2)}, u32[]{:S(2)}) %collective-permute-start.1) | collective-permute-done | bytes 131104 | tf_op jit(solution)/shard_map/ppermute | solution.py:198
  102.9 6.1 %collective-permute-done = bf16[512,128]{1,0:T(8,128)(2,1)S(1)} collective-permute-done((bf16[512,128]{1,0:T(8,128)(2,1)S(1)}, bf16[512,128]{1,0:T(8,128)(2,1)S(1)}, u32[]{:S(2)}, u32[]{:S(2)}) %collective-permute-start) | collective-permute-done | bytes 131104 | tf_op jit(solution)/shard_map/ppermute | solution.py:198
  109.3 3.4 %collective-permute-start.4 = (bf16[2,32,2560]{2,1,0:T(8,128)(2,1)S(1)}, bf16[2,32,2560]{2,1,0:T(8,128)(2,1)S(1)}, u32[]{:S(2)}, u32[]{:S(2)}) collective-permute-start(bf16[2,32,2560]{2,1,0:T(8,128)(2,1)S(1)} %dynamic-slice_bitcast_fusion.1), channel_id=1, source_target_pairs={{0,2},{1,3},{2,0},{3,1},{4,6},{5,7},{6,4},{7,5},{8,10},{9,11},{10,... | collective-permute-start | bytes 983048 | tf_op jit(solution)/shard_map/ppermute | solution.py:208
  113.2 1.6 broadcast_in_dim.113
  114.8 6.7 %all-to-all-start.3 = ((bf16[4,2048,128]{2,1,0:T(8,128)(2,1)}), bf16[4,2048,128]{2,1,0:T(8,128)(2,1)}, u32[]{:S(2)}, u32[]{:S(2)}) async-start(bf16[4,2048,128]{2,1,0:T(8,128)(2,1)} %broadcast_in_dim.113), calls=%async_computation.3 | async-start | bytes 4194304 | tf_op jit(solution)/shard_map/all_to_all | solution.py:90
  121.6 4.6 %collective-permute-start.5 = (bf16[1,32,2560]{2,1,0:T(8,128)(2,1)S(1)}, bf16[1,32,2560]{2,1,0:T(8,128)(2,1)S(1)}, u32[]{:S(2)}, u32[]{:S(2)}) collective-permute-start(bf16[1,32,2560]{2,1,0:T(8,128)(2,1)S(1)} %constant_dynamic-slice_fusion), channel_id=1, source_target_pairs={{0,4},{1,5},{2,6},{3,7},{4,0},{5,1},{6,2},{7,3},{8,12},{9,13},{10,... | collective-permute-start | bytes 491528 | tf_op jit(solution)/shard_map/ppermute | solution.py:208
  126.2 4.3 %collective-permute-done.5 = bf16[1,32,2560]{2,1,0:T(8,128)(2,1)S(1)} collective-permute-done((bf16[1,32,2560]{2,1,0:T(8,128)(2,1)S(1)}, bf16[1,32,2560]{2,1,0:T(8,128)(2,1)S(1)}, u32[]{:S(2)}, u32[]{:S(2)}) %collective-permute-start.5) | collective-permute-done | bytes 163872 | tf_op jit(solution)/shard_map/ppermute | solution.py:208
  130.5 0.7 fusion.39
  132.1 13.8 %all-to-all-done.3 = bf16[4,2048,128]{2,1,0:T(8,128)(2,1)} async-done(((bf16[4,2048,128]{2,1,0:T(8,128)(2,1)}), bf16[4,2048,128]{2,1,0:T(8,128)(2,1)}, u32[]{:S(2)}, u32[]{:S(2)}) %all-to-all-start.3) | async-done | bytes 2097184 | tf_op jit(solution)/shard_map/all_to_all | solution.py:90
  145.9 3.0 %shard_map.122.refs_0_ = bf16[48,8,2,16,128]{4,3,2,1,0:T(8,128)(2,1)} custom-call(s32[48]{0:T(128)S(1)} %get-tuple-element.31.where_ref, bf16[128,2,2,16,128]{4,3,2,1,0:T(8,128)(2,1)} %bitcast.40.source_ref), custom_call_target="tpu_custom_call" | custom-call | tf_op jit(solution)/shard_map/pallas_call | solution.py:156
  148.9 2.8 %copy-done.1 = bf16[24576,128]{1,0:T(8,128)(2,1)S(1)} copy-done((bf16[24576,128]{1,0:T(8,128)(2,1)S(1)}, bf16[24576,128]{1,0:T(8,128)(2,1)}, u32[]{:S(2)}) %copy-start.1) | copy-done | bytes 6291480
  151.7 2.3 %shard_map.123 = bf16[48,8,2,16,128]{4,3,2,1,0:T(8,128)(2,1)} custom-call(s32[48]{0:T(128)S(1)} %multiply_add_fusion.1.where_ref, bf16[128,6,2,16,128]{4,3,2,1,0:T(8,128)(2,1)S(1)} %bitcast.143, bf16[48,8,2,16,128]{4,3,2,1,0:T(8,128)(2,1)} %shard_map.122.refs_0_), custom_call_target="tpu_custom_call", output_to_operand_aliasing={{}: (2, {})} | custom-call | tf_op jit(solution)/shard_map/pallas_call | solution.py:156
  (64 shorter events, 7.0 us)
Async XLA Ops:
  7.2 63.1 %copy-start = (bf16[384,2560]{1,0:T(8,128)(2,1)S(1)}, bf16[384,2560]{1,0:T(8,128)(2,1)}, u32[]{:S(2)}) copy-start(bf16[384,2560]{1,0:T(8,128)(2,1)} %param.15) | copy-start | bytes 5898244
  8.6 31.0 %all-to-all-start = ((s32[64,1,128]{2,1,0:T(1,128)}), s32[64,1,128]{2,1,0:T(1,128)S(1)}, u32[]{:S(2)}, u32[]{:S(2)}) async-start(s32[64,1,128]{2,1,0:T(1,128)} %broadcast_in_dim.98), calls=%async_computation | async-start | bytes 65536 | tf_op jit(solution)/shard_map/all_to_all | solution.py:69
  27.1 121.8 %all-gather.2.cloned.1.call-start = ((), (), s32[]{:S(2)}) async-start(), calls=%async_computation.4 | async-start | bytes 6684672 | tf_op jit(solution)/shard_map/all_gather | solution.py:187
  39.6 0.6 copy-start.7
  40.2 14.7 %copy-start.11 = (s32[16,12]{1,0:T(8,128)S(1)}, s32[16,12]{1,0:T(8,128)}, u32[]{:S(2)}) copy-start(s32[16,12]{1,0:T(8,128)} %table_ref.1) | copy-start | bytes 2308
  40.2 18.1 %copy-start.2 = (bf16[192,2,16,1,128]{4,2,3,1,0:T(8,128)(2,1)S(1)}, bf16[192,2,16,1,128]{4,2,3,1,0:T(8,128)(2,1)}, u32[]{:S(2)}) copy-start(bf16[192,2,16,1,128]{4,2,3,1,0:T(8,128)(2,1)} %param.12) | copy-start | bytes 4718596
  61.0 2.6 %copy-start.12 = (bf16[2,2,2,16,128]{4,3,2,1,0:T(8,128)(2,1)S(1)}, bf16[2,2,2,16,128]{4,3,2,1,0:T(8,128)(2,1)}, u32[]{:S(2)}) copy-start(bf16[2,2,2,16,128]{4,3,2,1,0:T(8,128)(2,1)} %get-tuple-element.12) | copy-start | bytes 98308
  61.0 6.6 %copy-start.5 = (bf16[16,16,3,128]{3,1,2,0:T(8,128)(2,1)S(1)}, bf16[16,16,3,128]{3,1,2,0:T(8,128)(2,1)}, u32[]{:S(2)}) copy-start(bf16[16,16,3,128]{3,1,2,0:T(8,128)(2,1)} %param.10) | copy-start | bytes 589828
  61.0 6.6 %copy-start.13 = (bf16[16,2,16,1,128]{4,2,3,1,0:T(8,128)(2,1)S(1)}, bf16[16,2,16,1,128]{4,2,3,1,0:T(8,128)(2,1)}, u32[]{:S(2)}) copy-start(bf16[16,2,16,1,128]{4,2,3,1,0:T(8,128)(2,1)} %param.11) | copy-start | bytes 393220
  64.3 19.3 %all-to-all-start.1 = ((bf16[4,128,128]{2,1,0:T(8,128)(2,1)}), bf16[4,128,128]{2,1,0:T(8,128)(2,1)S(1)}, u32[]{:S(2)}, u32[]{:S(2)}) async-start(bf16[4,128,128]{2,1,0:T(8,128)(2,1)} %broadcast_in_dim.100), calls=%async_computation.1 | async-start | bytes 262144 | tf_op jit(solution)/shard_map/all_to_all | solution.py:90
  68.2 1.3 copy-start.6
  70.3 15.3 %copy-start.14 = (s32[48]{0:T(128)S(1)}, s32[48]{0:T(128)}, u32[]{:S(2)}) copy-start(s32[48]{0:T(128)} %param.19) | copy-start | bytes 580
  70.3 25.0 %copy-start.8 = (s32[64,1,128]{2,1,0:T(1,128)S(1)}, s32[64,1,128]{2,1,0:T(1,128)}, u32[]{:S(2)}) copy-start(s32[64,1,128]{2,1,0:T(1,128)} %copy-done.7) | copy-start | bytes 98308
  83.7 25.3 %collective-permute-start.3 = (bf16[4,32,2560]{2,1,0:T(8,128)(2,1)S(1)}, bf16[4,32,2560]{2,1,0:T(8,128)(2,1)S(1)}, u32[]{:S(2)}, u32[]{:S(2)}) collective-permute-start(bf16[4,32,2560]{2,1,0:T(8,128)(2,1)S(1)} %dynamic-slice_bitcast_fusion), channel_id=1, source_target_pairs={{0,1},{1,0},{2,3},{3,2},{4,5},{5,4},{6,7},{7,6},{8,9},{9,8},{10,11... | collective-permute-start | bytes 1966088 | tf_op jit(solution)/shard_map/ppermute | solution.py:208
  85.7 10.5 %collective-permute-start.2 = (bf16[512,128]{1,0:T(8,128)(2,1)S(1)}, bf16[512,128]{1,0:T(8,128)(2,1)S(1)}, u32[]{:S(2)}, u32[]{:S(2)}) collective-permute-start(bf16[512,128]{1,0:T(8,128)(2,1)S(1)} %bitcast.156), channel_id=1, source_target_pairs={{0,480},{8,488},{16,496},{24,504},{32,0},{40,8},{48,16},{56,24},{6... | collective-permute-start | bytes 393224 | tf_op jit(solution)/shard_map/ppermute | solution.py:198
  87.6 15.3 %collective-permute-start.1 = (bf16[512,128]{1,0:T(8,128)(2,1)S(1)}, bf16[512,128]{1,0:T(8,128)(2,1)S(1)}, u32[]{:S(2)}, u32[]{:S(2)}) collective-permute-start(bf16[512,128]{1,0:T(8,128)(2,1)S(1)} %bitcast.157), channel_id=1, source_target_pairs={{0,64},{8,72},{16,80},{24,88},{32,96},{40,104},{48,112},{56,120},{... | collective-permute-start | bytes 393224 | tf_op jit(solution)/shard_map/ppermute | solution.py:198
  92.7 16.3 %collective-permute-start = (bf16[512,128]{1,0:T(8,128)(2,1)S(1)}, bf16[512,128]{1,0:T(8,128)(2,1)S(1)}, u32[]{:S(2)}, u32[]{:S(2)}) collective-permute-start(bf16[512,128]{1,0:T(8,128)(2,1)S(1)} %bitcast.158), channel_id=1, source_target_pairs={{0,32},{8,40},{16,48},{24,56},{32,64},{40,72},{48,80},{56,88},{64,... | collective-permute-start | bytes 393224 | tf_op jit(solution)/shard_map/ppermute | solution.py:198
  109.2 3.5 %copy-start.3 = (bf16[4,32,2560]{2,1,0:T(8,128)(2,1)}, bf16[4,32,2560]{2,1,0:T(8,128)(2,1)S(1)}, u32[]{:S(2)}) copy-start(bf16[4,32,2560]{2,1,0:T(8,128)(2,1)S(1)} %fusion) | copy-start | bytes 1966084
  109.3 12.2 %collective-permute-start.4 = (bf16[2,32,2560]{2,1,0:T(8,128)(2,1)S(1)}, bf16[2,32,2560]{2,1,0:T(8,128)(2,1)S(1)}, u32[]{:S(2)}, u32[]{:S(2)}) collective-permute-start(bf16[2,32,2560]{2,1,0:T(8,128)(2,1)S(1)} %dynamic-slice_bitcast_fusion.1), channel_id=1, source_target_pairs={{0,2},{1,3},{2,0},{3,1},{4,6},{5,7},{6,4},{7,5},{8,10},{9,11},{10,... | collective-permute-start | bytes 983048 | tf_op jit(solution)/shard_map/ppermute | solution.py:208
  114.8 6.7 %copy-start.4 = (bf16[4,32,2560]{2,1,0:T(8,128)(2,1)S(1)}, bf16[4,32,2560]{2,1,0:T(8,128)(2,1)}, u32[]{:S(2)}) copy-start(bf16[4,32,2560]{2,1,0:T(8,128)(2,1)} %copy-done.3) | copy-start | bytes 1966084
  114.8 15.7 %copy-start.9 = (bf16[32,2560]{1,0:T(8,128)(2,1)S(1)}, bf16[32,2560]{1,0:T(8,128)(2,1)}, u32[]{:S(2)}) copy-start(bf16[32,2560]{1,0:T(8,128)(2,1)} %param.16) | copy-start | bytes 491524
  114.8 31.2 %all-to-all-start.3 = ((bf16[4,2048,128]{2,1,0:T(8,128)(2,1)}), bf16[4,2048,128]{2,1,0:T(8,128)(2,1)}, u32[]{:S(2)}, u32[]{:S(2)}) async-start(bf16[4,2048,128]{2,1,0:T(8,128)(2,1)} %broadcast_in_dim.113), calls=%async_computation.3 | async-start | bytes 4194304 | tf_op jit(solution)/shard_map/all_to_all | solution.py:90
  121.5 9.9 %copy-start.10 = (f32[2560]{0:T(1024)S(1)}, f32[2560]{0:T(1024)}, u32[]{:S(2)}) copy-start(f32[2560]{0:T(1024)} %convert_element_type.84) | copy-start | bytes 30724
  121.6 8.9 %collective-permute-start.5 = (bf16[1,32,2560]{2,1,0:T(8,128)(2,1)S(1)}, bf16[1,32,2560]{2,1,0:T(8,128)(2,1)S(1)}, u32[]{:S(2)}, u32[]{:S(2)}) collective-permute-start(bf16[1,32,2560]{2,1,0:T(8,128)(2,1)S(1)} %constant_dynamic-slice_fusion), channel_id=1, source_target_pairs={{0,4},{1,5},{2,6},{3,7},{4,0},{5,1},{6,2},{7,3},{8,12},{9,13},{10,... | collective-permute-start | bytes 491528 | tf_op jit(solution)/shard_map/ppermute | solution.py:208
  148.9 2.8 %copy-start.1 = (bf16[24576,128]{1,0:T(8,128)(2,1)S(1)}, bf16[24576,128]{1,0:T(8,128)(2,1)}, u32[]{:S(2)}) copy-start(bf16[24576,128]{1,0:T(8,128)(2,1)} %all-gather.2.cloned.1.call-done) | copy-start | bytes 18874372
Sparse Core Ops, SparseCore 0:
  55.0 91.2 all-gather.1

commit v7 on v6

--- a/solution.py
+++ b/solution.py
@@ -14,20 +14,24 @@
 PAGES = PREFIX // PAGE
 NZ, NY = 16, 4
 NEAR = 4
-FRONT = 6
+FRONT = 5
 LANES = 128
 
 
 neg_fill = -1e30
 
-def attend(queries, new_kv, kv_cache, page_table, lengths):
+def cached(kv_cache, page_table):
+    pages = kv_cache[page_table]
+    branch, count, _, page, kvheads, head_width = pages.shape
+    flat = (branch, count * page, kvheads, head_width)
+    return pages[:, :, 0].reshape(flat), pages[:, :, 1].reshape(flat)
+
+
+def attend(queries, new_kv, cache_keys, cache_values, lengths):
     branch, steps_new, qheads, head_width = queries.shape
     kvheads = new_kv.shape[3]
     per_group = qheads // kvheads
-    cache_pages = kv_cache[page_table]
-    key_span = cache_pages.shape[1] * cache_pages.shape[3]
-    cache_keys = cache_pages[:, :, 0].reshape(branch, key_span, kvheads, head_width)
-    cache_values = cache_pages[:, :, 1].reshape(branch, key_span, kvheads, head_width)
+    key_span = cache_keys.shape[1]
     grouped = queries.reshape(branch, steps_new, kvheads, per_group, head_width)
     score_scale = head_width ** (-0.5)
     old_scores = (
@@ -221,11 +225,14 @@
     score_weight,
     fork_parent,
 ):
-    listing, queries = lax.optimization_barrier((parent_listing(fork_parent), queries))
+    keys, values = cached(kv_cache, page_table)
+    listing, queries, keys, values = lax.optimization_barrier(
+        (parent_listing(fork_parent), queries, keys, values)
+    )
     cache = kv_cache[:, :, :, 0]
     front, back = pick_pages(lax.axis_index("dp"), listing, page_table, cache)
     fronts = gather_fronts(front)
-    attended = attend(queries, new_kv, kv_cache, page_table, lengths)
+    attended = attend(queries, new_kv, keys, values, lengths)
     rows_here = residual.shape[0]
     partial = jnp.dot(attended, out_proj, preferred_element_type=jnp.float32).astype(jnp.bfloat16)
     far, partial = lax.optimization_barrier((gather_backs_far(back), partial))

time: 163 us -> 177 us (1.086)
  waiting for transfers between devices: 56.7 us -> 70.7 us
    all_to_all x2, waiting for transfers between devices: 26.3 us -> 38.1 us  [share(): lax.all_to_all(copies, 'dp', split_axis=0, concat_axis=0, tiled=True, axi...]
    ppermute x3, waiting for transfers between devices: 13.6 us -> 21.1 us  [gather_backs_near(): lax.ppermute(far, 'dp', shift_z(step))]
    all_to_all x1, waiting for transfers between devices: 12.5 us -> 7.46 us  [parent_listing(): lax.all_to_all(copies, 'dp', split_axis=0, concat_axis=0, tiled=True)[:, 0]]
where the time goes in v7:
time: 177 us; the launch traced here: 175 us
  waiting for transfers between devices  70.7 us (40%)
  starting transfers between devices  48.6 us (27%)
  between operations  14.6 us (8%)
  local copies, waits for them, and re-layouts  13.6 us (8%)
  blocking collectives  10.7 us (6%)
  Pallas kernels  8.29 us (5%)
  other arithmetic  5.6 us (3%)
  matrix products  2.74 us (2%)
    all_to_all x2, waiting for transfers between devices, share(): lax.all_to_all(copies, 'dp', split_axis=0, concat_axis=0, tiled=True, axi...  38.1 us
    ppermute x3, waiting for transfers between devices, gather_backs_near(): lax.ppermute(far, 'dp', shift_z(step))  21.1 us
    all_to_all x1, starting transfers between devices, parent_listing(): lax.all_to_all(copies, 'dp', split_axis=0, concat_axis=0, tiled=True)[:, 0]  18.7 us
    all_to_all x2, starting transfers between devices, share(): lax.all_to_all(copies, 'dp', split_axis=0, concat_axis=0, tiled=True, axi...  11.3 us
    all_to_all x1, blocking collectives, share(): lax.all_to_all(copies, 'dp', split_axis=0, concat_axis=0, tiled=True, axi...  10.7 us
    ppermute x3, starting transfers between devices, halve(): came = lax.ppermute(send, 'tensor', [(i, i ^ apart) for i in range(shards)])  9.99 us
    ppermute x3, starting transfers between devices, gather_backs_near(): lax.ppermute(far, 'dp', shift_z(step))  8.51 us
    all_to_all x1, waiting for transfers between devices, parent_listing(): lax.all_to_all(copies, 'dp', split_axis=0, concat_axis=0, tiled=True)[:, 0]  7.46 us
  transfers between devices with their start and end apart: 10, of which 7 were waited for; matrix products, arithmetic and copies ran while one was open for 10% of the time, Pallas kernels for 2%

profile of v7, /device:TPU:24, one launch (start us, length us, event | category | flops | bytes accessed | tf_op | source)
XLA Modules:
  0.0 174.8 jit_solution(3262884576386338615)
XLA Ops:
  7.2 0.8 pad.4
  8.6 18.7 %all-to-all-start = ((s32[64,1,128]{2,1,0:T(1,128)}), s32[64,1,128]{2,1,0:T(1,128)}, u32[]{:S(2)}, u32[]{:S(2)}) async-start(s32[64,1,128]{2,1,0:T(1,128)} %broadcast_in_dim.98), calls=%async_computation | async-start | bytes 65536 | tf_op jit(solution)/shard_map/all_to_all | solution.py:73
  28.2 2.3 %gather_fusion = bf16[192,2,16,128]{3,2,1,0:T(8,128)(2,1)S(1)} fusion(bf16[192,2,16,128]{3,2,1,0:T(8,128)(2,1)} %bitcast.149, s32[1024]{0:T(1024)S(1)} %pad_clamp_fusion), kind=kCustom, calls=%fused_computation | custom fusion | bytes 3146496 | tf_op jit(solution)/shard_map/gather | solution.py:24
  30.5 1.6 fusion.42
  32.1 7.5 %all-to-all-done = s32[64,1,128]{2,1,0:T(1,128)} async-done(((s32[64,1,128]{2,1,0:T(1,128)}), s32[64,1,128]{2,1,0:T(1,128)}, u32[]{:S(2)}, u32[]{:S(2)}) %all-to-all-start) | async-done | bytes 32800 | tf_op jit(solution)/shard_map/all_to_all | solution.py:73
  39.6 2.8 %shard_map.121 = (bf16[2,5,2,16,128]{4,3,2,1,0:T(8,128)(2,1)}, bf16[2,3,2,16,128]{4,3,2,1,0:T(8,128)(2,1)}) custom-call(s32[1]{0:T(128)} %bitcast.me_ref, s32[64,128]{1,0:T(8,128)} %bitcast.1.listing_ref, s32[16,12]{1,0:T(8,128)} %table_ref.1, bf16[192,2,16,128]{3,2,1,0:T(8,128)(2,1)} %bitcast.150), custom_call_target="tpu_custom_call" | custom-call | tf_op jit(solution)/shard_map/pallas_call | solution.py:121
  42.4 1.0 broadcast_in_dim.112
  43.4 10.7 %all_to_all.20 = bf16[4,320,128]{2,1,0:T(8,128)(2,1)} all-to-all(bf16[4,320,128]{2,1,0:T(8,128)(2,1)S(1)} %broadcast_in_dim.112), channel_id=1, replica_groups={{0,8,16,24},{32,40,48,56},{64,72,80,88},{96,104,112,120},{128,136,144,1..., dimensions={0} | all-to-all | bytes 655360 | tf_op jit(solution)/shard_map/all_to_all | solution.py:94
  54.2 1.5 broadcast_in_dim.101
  55.7 3.4 %all-to-all-start.1 = ((bf16[4,192,128]{2,1,0:T(8,128)(2,1)}), bf16[4,192,128]{2,1,0:T(8,128)(2,1)S(1)}, u32[]{:S(2)}, u32[]{:S(2)}) async-start(bf16[4,192,128]{2,1,0:T(8,128)(2,1)} %broadcast_in_dim.101), calls=%async_computation.1 | async-start | bytes 393216 | tf_op jit(solution)/shard_map/all_to_all | solution.py:94
  61.8 0.8 convolution_convert_fusion
  62.6 13.1 %all-to-all-done.1 = bf16[4,192,128]{2,1,0:T(8,128)(2,1)S(1)} async-done(((bf16[4,192,128]{2,1,0:T(8,128)(2,1)}), bf16[4,192,128]{2,1,0:T(8,128)(2,1)S(1)}, u32[]{:S(2)}, u32[]{:S(2)}) %all-to-all-start.1) | async-done | bytes 196640 | tf_op jit(solution)/shard_map/all_to_all | solution.py:94
  75.7 0.9 dynamic-slice_bitcast_fusion
  76.6 1.9 %collective-permute-start.3 = (bf16[4,32,2560]{2,1,0:T(8,128)(2,1)}, bf16[4,32,2560]{2,1,0:T(8,128)(2,1)}, u32[]{:S(2)}, u32[]{:S(2)}) collective-permute-start(bf16[4,32,2560]{2,1,0:T(8,128)(2,1)} %dynamic-slice_bitcast_fusion), channel_id=1, source_target_pairs={{0,1},{1,0},{2,3},{3,2},{4,5},{5,4},{6,7},{7,6},{8,9},{9,8},{10,11... | collective-permute-start | bytes 1966088 | tf_op jit(solution)/shard_map/ppermute | solution.py:212
  78.7 3.4 %collective-permute-start.2 = (bf16[768,128]{1,0:T(8,128)(2,1)S(1)}, bf16[768,128]{1,0:T(8,128)(2,1)S(1)}, u32[]{:S(2)}, u32[]{:S(2)}) collective-permute-start(bf16[768,128]{1,0:T(8,128)(2,1)S(1)} %bitcast.159), channel_id=1, source_target_pairs={{0,480},{8,488},{16,496},{24,504},{32,0},{40,8},{48,16},{56,24},{6... | collective-permute-start | bytes 589832 | tf_op jit(solution)/shard_map/ppermute | solution.py:202
  82.1 1.9 %collective-permute-start.1 = (bf16[768,128]{1,0:T(8,128)(2,1)S(1)}, bf16[768,128]{1,0:T(8,128)(2,1)S(1)}, u32[]{:S(2)}, u32[]{:S(2)}) collective-permute-start(bf16[768,128]{1,0:T(8,128)(2,1)S(1)} %bitcast.160), channel_id=1, source_target_pairs={{0,64},{8,72},{16,80},{24,88},{32,96},{40,104},{48,112},{56,120},{... | collective-permute-start | bytes 589832 | tf_op jit(solution)/shard_map/ppermute | solution.py:202
  84.0 3.2 %collective-permute-start = (bf16[768,128]{1,0:T(8,128)(2,1)S(1)}, bf16[768,128]{1,0:T(8,128)(2,1)S(1)}, u32[]{:S(2)}, u32[]{:S(2)}) collective-permute-start(bf16[768,128]{1,0:T(8,128)(2,1)S(1)} %bitcast.161), channel_id=1, source_target_pairs={{0,32},{8,40},{16,48},{24,56},{32,64},{40,72},{48,80},{56,88},{64,... | collective-permute-start | bytes 589832 | tf_op jit(solution)/shard_map/ppermute | solution.py:202
  87.2 0.8 add_select_fusion.1
  88.0 4.0 %collective-permute-done.2 = bf16[768,128]{1,0:T(8,128)(2,1)S(1)} collective-permute-done((bf16[768,128]{1,0:T(8,128)(2,1)S(1)}, bf16[768,128]{1,0:T(8,128)(2,1)S(1)}, u32[]{:S(2)}, u32[]{:S(2)}) %collective-permute-start.2) | collective-permute-done | bytes 196640 | tf_op jit(solution)/shard_map/ppermute | solution.py:202
  92.0 9.5 %collective-permute-done.1 = bf16[768,128]{1,0:T(8,128)(2,1)S(1)} collective-permute-done((bf16[768,128]{1,0:T(8,128)(2,1)S(1)}, bf16[768,128]{1,0:T(8,128)(2,1)S(1)}, u32[]{:S(2)}, u32[]{:S(2)}) %collective-permute-start.1) | collective-permute-done | bytes 196640 | tf_op jit(solution)/shard_map/ppermute | solution.py:202
  101.5 7.6 %collective-permute-done = bf16[768,128]{1,0:T(8,128)(2,1)S(1)} collective-permute-done((bf16[768,128]{1,0:T(8,128)(2,1)S(1)}, bf16[768,128]{1,0:T(8,128)(2,1)S(1)}, u32[]{:S(2)}, u32[]{:S(2)}) %collective-permute-start) | collective-permute-done | bytes 196640 | tf_op jit(solution)/shard_map/ppermute | solution.py:202
  109.2 1.2 fusion
  110.5 3.4 %collective-permute-start.4 = (bf16[2,32,2560]{2,1,0:T(8,128)(2,1)S(1)}, bf16[2,32,2560]{2,1,0:T(8,128)(2,1)S(1)}, u32[]{:S(2)}, u32[]{:S(2)}) collective-permute-start(bf16[2,32,2560]{2,1,0:T(8,128)(2,1)S(1)} %dynamic-slice_bitcast_fusion.1), channel_id=1, source_target_pairs={{0,2},{1,3},{2,0},{3,1},{4,6},{5,7},{6,4},{7,5},{8,10},{9,11},{10,... | collective-permute-start | bytes 983048 | tf_op jit(solution)/shard_map/ppermute | solution.py:212
  114.4 2.1 %broadcast_in_dim.113 = bf16[4,3072,128]{2,1,0:T(8,128)(2,1)} broadcast(bf16[3072,128]{1,0:T(8,128)(2,1)S(1)} %pad_maximum_fusion), dimensions={1,2} | broadcast | bytes 3932160 | tf_op jit(solution)/shard_map/broadcast_in_dim | solution.py:93
  116.4 8.0 %all-to-all-start.3 = ((bf16[4,3072,128]{2,1,0:T(8,128)(2,1)}), bf16[4,3072,128]{2,1,0:T(8,128)(2,1)}, u32[]{:S(2)}, u32[]{:S(2)}) async-start(bf16[4,3072,128]{2,1,0:T(8,128)(2,1)} %broadcast_in_dim.113), calls=%async_computation.3 | async-start | bytes 6291456 | tf_op jit(solution)/shard_map/all_to_all | solution.py:94
  124.5 4.7 %collective-permute-start.5 = (bf16[1,32,2560]{2,1,0:T(8,128)(2,1)S(1)}, bf16[1,32,2560]{2,1,0:T(8,128)(2,1)S(1)}, u32[]{:S(2)}, u32[]{:S(2)}) collective-permute-start(bf16[1,32,2560]{2,1,0:T(8,128)(2,1)S(1)} %constant_dynamic-slice_fusion), channel_id=1, source_target_pairs={{0,4},{1,5},{2,6},{3,7},{4,0},{5,1},{6,2},{7,3},{8,12},{9,13},{10,... | collective-permute-start | bytes 491528 | tf_op jit(solution)/shard_map/ppermute | solution.py:212
  129.2 4.0 %collective-permute-done.5 = bf16[1,32,2560]{2,1,0:T(8,128)(2,1)S(1)} collective-permute-done((bf16[1,32,2560]{2,1,0:T(8,128)(2,1)S(1)}, bf16[1,32,2560]{2,1,0:T(8,128)(2,1)S(1)}, u32[]{:S(2)}, u32[]{:S(2)}) %collective-permute-start.5) | collective-permute-done | bytes 163872 | tf_op jit(solution)/shard_map/ppermute | solution.py:212
  133.2 0.7 fusion.41
  134.9 25.0 %all-to-all-done.3 = bf16[4,3072,128]{2,1,0:T(8,128)(2,1)} async-done(((bf16[4,3072,128]{2,1,0:T(8,128)(2,1)}), bf16[4,3072,128]{2,1,0:T(8,128)(2,1)}, u32[]{:S(2)}, u32[]{:S(2)}) %all-to-all-start.3) | async-done | bytes 3145760 | tf_op jit(solution)/shard_map/all_to_all | solution.py:94
  159.9 3.3 %shard_map.122.refs_0_ = bf16[48,8,2,16,128]{4,3,2,1,0:T(8,128)(2,1)} custom-call(s32[48]{0:T(128)S(1)} %get-tuple-element.35.where_ref, bf16[128,3,2,16,128]{4,3,2,1,0:T(8,128)(2,1)} %bitcast.42.source_ref), custom_call_target="tpu_custom_call" | custom-call | tf_op jit(solution)/shard_map/pallas_call | solution.py:160
  163.3 2.5 %copy-done.1 = bf16[20480,128]{1,0:T(8,128)(2,1)S(1)} copy-done((bf16[20480,128]{1,0:T(8,128)(2,1)S(1)}, bf16[20480,128]{1,0:T(8,128)(2,1)}, u32[]{:S(2)}) %copy-start.1) | copy-done | bytes 5242904
  165.7 2.2 %shard_map.123 = bf16[48,8,2,16,128]{4,3,2,1,0:T(8,128)(2,1)} custom-call(s32[48]{0:T(128)S(1)} %multiply_add_fusion.1.where_ref, bf16[128,5,2,16,128]{4,3,2,1,0:T(8,128)(2,1)S(1)} %bitcast.147, bf16[48,8,2,16,128]{4,3,2,1,0:T(8,128)(2,1)} %shard_map.122.refs_0_), custom_call_target="tpu_custom_call", output_to_operand_aliasing={{}: (2, {})} | custom-call | tf_op jit(solution)/shard_map/pallas_call | solution.py:160
  (60 shorter events, 5.8 us)
Async XLA Ops:
  7.2 54.6 %copy-start = (bf16[384,2560]{1,0:T(8,128)(2,1)S(1)}, bf16[384,2560]{1,0:T(8,128)(2,1)}, u32[]{:S(2)}) copy-start(bf16[384,2560]{1,0:T(8,128)(2,1)} %param.15) | copy-start | bytes 5898244
  8.6 31.0 %all-to-all-start = ((s32[64,1,128]{2,1,0:T(1,128)}), s32[64,1,128]{2,1,0:T(1,128)}, u32[]{:S(2)}, u32[]{:S(2)}) async-start(s32[64,1,128]{2,1,0:T(1,128)} %broadcast_in_dim.98), calls=%async_computation | async-start | bytes 65536 | tf_op jit(solution)/shard_map/all_to_all | solution.py:73
  27.3 135.9 %all-gather.2.cloned.1.call-start = ((), (), s32[]{:S(2)}) async-start(), calls=%async_computation.4 | async-start | bytes 5570560 | tf_op jit(solution)/shard_map/all_gather | solution.py:191
  32.1 22.0 %copy-start.11 = (s32[16]{0:T(128)S(1)}, s32[16]{0:T(128)}, u32[]{:S(2)}) copy-start(s32[16]{0:T(128)} %param.14) | copy-start | bytes 196
  39.6 19.5 %copy-start.5 = (bf16[16,16,3,128]{3,1,2,0:T(8,128)(2,1)S(1)}, bf16[16,16,3,128]{3,1,2,0:T(8,128)(2,1)}, u32[]{:S(2)}) copy-start(bf16[16,16,3,128]{3,1,2,0:T(8,128)(2,1)} %param.10) | copy-start | bytes 589828
  39.6 19.5 %copy-start.8 = (bf16[16,2,16,1,128]{4,2,3,1,0:T(8,128)(2,1)S(1)}, bf16[16,2,16,1,128]{4,2,3,1,0:T(8,128)(2,1)}, u32[]{:S(2)}) copy-start(bf16[16,2,16,1,128]{4,2,3,1,0:T(8,128)(2,1)} %param.11) | copy-start | bytes 393220
  42.4 17.2 %copy-start.2 = (bf16[16,12,1,16,1,128]{5,3,2,1,0,4:T(8,128)(2,1)S(1)}, bf16[16,12,1,16,1,128]{5,3,2,1,0,4:T(8,128)(2,1)}, u32[]{:S(2)}) copy-start(bf16[16,12,1,16,1,128]{5,3,2,1,0,4:T(8,128)(2,1)} %get-tuple-element.40) | copy-start | bytes 2359300
  55.7 20.0 %all-to-all-start.1 = ((bf16[4,192,128]{2,1,0:T(8,128)(2,1)}), bf16[4,192,128]{2,1,0:T(8,128)(2,1)S(1)}, u32[]{:S(2)}, u32[]{:S(2)}) async-start(bf16[4,192,128]{2,1,0:T(8,128)(2,1)} %broadcast_in_dim.101), calls=%async_computation.1 | async-start | bytes 393216 | tf_op jit(solution)/shard_map/all_to_all | solution.py:94
  59.6 1.3 copy-start.6
  61.7 16.8 %copy-start.12 = (s32[48]{0:T(128)S(1)}, s32[48]{0:T(128)}, u32[]{:S(2)}) copy-start(s32[48]{0:T(128)} %param.19) | copy-start | bytes 580
  61.7 16.9 %copy-start.9 = (bf16[2560]{0:T(1024)(128)(2,1)S(1)}, bf16[2560]{0:T(1024)(128)(2,1)}, u32[]{:S(2)}) copy-start(bf16[2560]{0:T(1024)(128)(2,1)} %param.17) | copy-start | bytes 15364
  61.8 16.9 %copy-start.10 = (bf16[2560]{0:T(1024)(128)(2,1)S(1)}, bf16[2560]{0:T(1024)(128)(2,1)}, u32[]{:S(2)}) copy-start(bf16[2560]{0:T(1024)(128)(2,1)} %param.18) | copy-start | bytes 15364
  76.6 32.6 %collective-permute-start.3 = (bf16[4,32,2560]{2,1,0:T(8,128)(2,1)}, bf16[4,32,2560]{2,1,0:T(8,128)(2,1)}, u32[]{:S(2)}, u32[]{:S(2)}) collective-permute-start(bf16[4,32,2560]{2,1,0:T(8,128)(2,1)} %dynamic-slice_bitcast_fusion), channel_id=1, source_target_pairs={{0,1},{1,0},{2,3},{3,2},{4,5},{5,4},{6,7},{7,6},{8,9},{9,8},{10,11... | collective-permute-start | bytes 1966088 | tf_op jit(solution)/shard_map/ppermute | solution.py:212
  78.7 13.3 %collective-permute-start.2 = (bf16[768,128]{1,0:T(8,128)(2,1)S(1)}, bf16[768,128]{1,0:T(8,128)(2,1)S(1)}, u32[]{:S(2)}, u32[]{:S(2)}) collective-permute-start(bf16[768,128]{1,0:T(8,128)(2,1)S(1)} %bitcast.159), channel_id=1, source_target_pairs={{0,480},{8,488},{16,496},{24,504},{32,0},{40,8},{48,16},{56,24},{6... | collective-permute-start | bytes 589832 | tf_op jit(solution)/shard_map/ppermute | solution.py:202
  82.1 19.5 %collective-permute-start.1 = (bf16[768,128]{1,0:T(8,128)(2,1)S(1)}, bf16[768,128]{1,0:T(8,128)(2,1)S(1)}, u32[]{:S(2)}, u32[]{:S(2)}) collective-permute-start(bf16[768,128]{1,0:T(8,128)(2,1)S(1)} %bitcast.160), channel_id=1, source_target_pairs={{0,64},{8,72},{16,80},{24,88},{32,96},{40,104},{48,112},{56,120},{... | collective-permute-start | bytes 589832 | tf_op jit(solution)/shard_map/ppermute | solution.py:202
  84.0 25.1 %collective-permute-start = (bf16[768,128]{1,0:T(8,128)(2,1)S(1)}, bf16[768,128]{1,0:T(8,128)(2,1)S(1)}, u32[]{:S(2)}, u32[]{:S(2)}) collective-permute-start(bf16[768,128]{1,0:T(8,128)(2,1)S(1)} %bitcast.161), channel_id=1, source_target_pairs={{0,32},{8,40},{16,48},{24,56},{32,64},{40,72},{48,80},{56,88},{64,... | collective-permute-start | bytes 589832 | tf_op jit(solution)/shard_map/ppermute | solution.py:202
  110.4 3.5 %copy-start.3 = (bf16[4,32,2560]{2,1,0:T(8,128)(2,1)}, bf16[4,32,2560]{2,1,0:T(8,128)(2,1)S(1)}, u32[]{:S(2)}) copy-start(bf16[4,32,2560]{2,1,0:T(8,128)(2,1)S(1)} %fusion) | copy-start | bytes 1966084
  110.5 13.9 %collective-permute-start.4 = (bf16[2,32,2560]{2,1,0:T(8,128)(2,1)S(1)}, bf16[2,32,2560]{2,1,0:T(8,128)(2,1)S(1)}, u32[]{:S(2)}, u32[]{:S(2)}) collective-permute-start(bf16[2,32,2560]{2,1,0:T(8,128)(2,1)S(1)} %dynamic-slice_bitcast_fusion.1), channel_id=1, source_target_pairs={{0,2},{1,3},{2,0},{3,1},{4,6},{5,7},{6,4},{7,5},{8,10},{9,11},{10,... | collective-permute-start | bytes 983048 | tf_op jit(solution)/shard_map/ppermute | solution.py:212
  116.4 8.0 %copy-start.4 = (bf16[4,32,2560]{2,1,0:T(8,128)(2,1)S(1)}, bf16[4,32,2560]{2,1,0:T(8,128)(2,1)}, u32[]{:S(2)}) copy-start(bf16[4,32,2560]{2,1,0:T(8,128)(2,1)} %copy-done.3) | copy-start | bytes 1966084
  116.4 16.8 %copy-start.7 = (bf16[32,2560]{1,0:T(8,128)(2,1)S(1)}, bf16[32,2560]{1,0:T(8,128)(2,1)}, u32[]{:S(2)}) copy-start(bf16[32,2560]{1,0:T(8,128)(2,1)} %param.16) | copy-start | bytes 491524
  116.4 43.5 %all-to-all-start.3 = ((bf16[4,3072,128]{2,1,0:T(8,128)(2,1)}), bf16[4,3072,128]{2,1,0:T(8,128)(2,1)}, u32[]{:S(2)}, u32[]{:S(2)}) async-start(bf16[4,3072,128]{2,1,0:T(8,128)(2,1)} %broadcast_in_dim.113), calls=%async_computation.3 | async-start | bytes 6291456 | tf_op jit(solution)/shard_map/all_to_all | solution.py:94
  124.5 8.7 %collective-permute-start.5 = (bf16[1,32,2560]{2,1,0:T(8,128)(2,1)S(1)}, bf16[1,32,2560]{2,1,0:T(8,128)(2,1)S(1)}, u32[]{:S(2)}, u32[]{:S(2)}) collective-permute-start(bf16[1,32,2560]{2,1,0:T(8,128)(2,1)S(1)} %constant_dynamic-slice_fusion), channel_id=1, source_target_pairs={{0,4},{1,5},{2,6},{3,7},{4,0},{5,1},{6,2},{7,3},{8,12},{9,13},{10,... | collective-permute-start | bytes 491528 | tf_op jit(solution)/shard_map/ppermute | solution.py:212
  163.2 2.5 %copy-start.1 = (bf16[20480,128]{1,0:T(8,128)(2,1)S(1)}, bf16[20480,128]{1,0:T(8,128)(2,1)}, u32[]{:S(2)}) copy-start(bf16[20480,128]{1,0:T(8,128)(2,1)} %all-gather.2.cloned.1.call-done) | copy-start | bytes 15728644
Sparse Core Ops, SparseCore 0:
  54.2 87.5 all-gather.1

commit v8 on v5

--- a/solution.py
+++ b/solution.py
@@ -19,14 +19,18 @@
 
 neg_fill = -1e30
 
-def attend(queries, new_kv, kv_cache, page_table, lengths):
+def cached(kv_cache, page_table):
+    pages = kv_cache[page_table]
+    branch, count, _, page, kvheads, head_width = pages.shape
+    flat = (branch, count * page, kvheads, head_width)
+    return pages[:, :, 0].reshape(flat), pages[:, :, 1].reshape(flat)
+
+
+def attend(queries, new_kv, cache_keys, cache_values, lengths):
     branch, steps_new, qheads, head_width = queries.shape
     kvheads = new_kv.shape[3]
     per_group = qheads // kvheads
-    cache_pages = kv_cache[page_table]
-    key_span = cache_pages.shape[1] * cache_pages.shape[3]
-    cache_keys = cache_pages[:, :, 0].reshape(branch, key_span, kvheads, head_width)
-    cache_values = cache_pages[:, :, 1].reshape(branch, key_span, kvheads, head_width)
+    key_span = cache_keys.shape[1]
     grouped = queries.reshape(branch, steps_new, kvheads, per_group, head_width)
     score_scale = head_width ** (-0.5)
     old_scores = (
@@ -91,6 +95,7 @@
 
 
 def pick_kernel(me_ref, listing_ref, table_ref, cache_ref, out_ref, sems):
+    copies_wanted = out_ref.shape[0]
     asked = listing_ref[...]
     mine = (asked >> 4) == me_ref[0]
     rows = asked & (BR_DEV - 1)
@@ -101,19 +106,21 @@
         for page in range(PAGES):
             copies.append(
                 pltpu.make_async_copy(
-                    cache_ref.at[table_ref[row, page]], out_ref.at[which, page], sems.at[which, page]
+                    cache_ref.at[table_ref[row, page]], out_ref.at[0, which, page], sems.at[which, page]
                 )
             )
     for copy in copies:
         copy.start()
     for copy in copies:
         copy.wait()
-
-
-def pick_pages(me_index, listing, page_table, cache):
+    for number in range(1, copies_wanted):
+        out_ref[number] = out_ref[0]
+
+
+def pick_pages(me_index, listing, page_table, cache, copies):
     return pl.pallas_call(
         pick_kernel,
-        out_shape=jax.ShapeDtypeStruct((2, PAGES) + cache.shape[1:], cache.dtype),
+        out_shape=jax.ShapeDtypeStruct((copies, 2, PAGES) + cache.shape[1:], cache.dtype),
         in_specs=[
             pl.BlockSpec(memory_space=pltpu.SMEM),
             pl.BlockSpec(memory_space=pltpu.VMEM),
@@ -195,34 +202,29 @@
     return early.astype(jnp.int32), late.astype(jnp.int32)
 
 
-def gather_far(listing, kv_cache, page_table):
-    cache = kv_cache[:, :, :, 0]
-    width = cache.shape[-1]
-    picked = pick_pages(lax.axis_index("dp"), listing, page_table, cache)
-    rows = picked[0].size // width
-    return share(picked.reshape(2 * rows, width), groups_far()), picked.shape[1:]
+def gather_far(picked):
+    groups = groups_far()
+    return exchange(picked.reshape(len(groups[0]), -1, picked.shape[-1]), groups)
 
 
 def gather_near(far):
     rows, width = far.shape[1] // 2, far.shape[2]
     low_far = far[:, :rows].reshape(-1, width)
     high_far = far[:, rows:].reshape(-1, width)
-    copies = jnp.broadcast_to(high_far[None], (NY,) + high_far.shape)
-    low_far, copies = lax.optimization_barrier((low_far, copies))
-    high_plane = exchange(copies, groups_y()).reshape(-1, width)
+    high_plane = share(high_far, groups_y()).reshape(-1, width)
     low_column = jnp.concatenate(
         [low_far] + [lax.ppermute(low_far, "dp", shift_z(step)) for step in (1, 2, -1)]
     )
-    return low_column, high_plane
-
-
-def gather_rest(low_column, high_plane):
+    return jnp.broadcast_to(low_column[None], (NY,) + low_column.shape), high_plane
+
+
+def gather_rest(low_copies, high_plane):
     half = high_plane.shape[0] // 2
-    low_all = share(low_column, groups_y())
+    low_all = exchange(low_copies, groups_y())
     up = lax.ppermute(high_plane, "dp", shift_z(1))
     down = lax.ppermute(high_plane, "dp", shift_z(-1))
-    up_two = lax.ppermute(high_plane[:half], "dp", shift_z(2))
-    down_two = lax.ppermute(high_plane[half:], "dp", shift_z(-2))
+    up_two = lax.ppermute(up[:half], "dp", shift_z(1))
+    down_two = lax.ppermute(down[half:], "dp", shift_z(-1))
     return (high_plane, up, down), (up_two, down_two, low_all)
 
 
@@ -248,22 +250,26 @@
     score_weight,
     fork_parent,
 ):
-    listing, queries = lax.optimization_barrier((parent_listing(fork_parent), queries))
-    attended = attend(queries, new_kv, kv_cache, page_table, lengths)
+    keys, values = cached(kv_cache, page_table)
+    listing, keys, values = lax.optimization_barrier((parent_listing(fork_parent), keys, values))
+    cache = kv_cache[:, :, :, 0]
+    picked = pick_pages(lax.axis_index("dp"), listing, page_table, cache, NZ // NEAR)
+    tile = picked.shape[2:]
+    picked, queries = lax.optimization_barrier((picked, queries))
+    attended = attend(queries, new_kv, keys, values, lengths)
     rows_here = residual.shape[0]
     partial = jnp.dot(attended, out_proj, preferred_element_type=jnp.float32).astype(jnp.bfloat16)
-    far, tile = gather_far(listing, kv_cache, page_table)
-    held = halve(partial.reshape(lax.axis_size("tensor"), rows_here, -1), 1).astype(jnp.bfloat16)
-    far, held = lax.optimization_barrier((far, held))
-    low_column, high_plane = gather_near(far)
-    held = halve(held, 2).astype(jnp.bfloat16)
-    low_column, high_plane, held = lax.optimization_barrier((low_column, high_plane, held))
-    first, last = gather_rest(low_column, high_plane)
+    held = partial.reshape(lax.axis_size("tensor"), rows_here, -1)
+    held = halve(held, 1).astype(jnp.bfloat16)
+    far, held = lax.optimization_barrier((gather_far(picked), held))
+    held = halve(halve(held, 2).astype(jnp.bfloat16), 4)
+    low_copies, high_plane, held = lax.optimization_barrier(gather_near(far) + (held,))
+    first, last = gather_rest(low_copies, high_plane)
     early, late = child_places(listing, fork_parent, lax.axis_index("dp"))
     placed = place_children(early, [part.reshape((-1,) + tile) for part in first])
     placed = place_children(late, [part.reshape((-1,) + tile) for part in last], placed)
     child_pages = placed[:, :, :, :, None]
-    updated = halve(held, 4)[0] + residual.astype(jnp.float32)
+    updated = held[0] + residual.astype(jnp.float32)
     hidden_out = updated.astype(jnp.bfloat16)
     block_ends = updated.reshape(rows_here // CH, CH, updated.shape[1])[:, CH - 1]
     normed = (

time: 179 us -> 169 us (0.944)
  waiting for transfers between devices: 65.8 us -> 58.5 us
  starting transfers between devices: 70.2 us -> 67.6 us
    ppermute x1, waiting for transfers between devices: 23.7 us -> 0.01 us  [gather_rest(): up = lax.ppermute(high_plane, 'dp', shift_z(1))]
    ppermute x1, waiting for transfers between devices: 0.01 us -> 17.9 us  [gather_rest(): down = lax.ppermute(high_plane, 'dp', shift_z(-1))]
    broadcast_in_dim x2 -> x1, local copies, waits for them, and re-layouts: 5.67 us -> 1.11 us  [share(): jnp.broadcast_to(block[None], (len(groups[0]),) + block.shape)]
    broadcast_in_dim x2, local copies, waits for them, and re-layouts: 1.19 us -> 3.84 us  [the longest x1 3.75 us: gather_near(): jnp.broadcast_to(low_column[None], (NY,) + low_column.shape)]
    ppermute x2, starting transfers between devices: 7.95 us -> 5.84 us  [the longest x1 3.41 us: gather_rest(): down_two = lax.ppermute(down[half:], 'dp', shift_z(-1))]
    ppermute x3, waiting for transfers between devices: 3.67 us -> 1.68 us  [gather_near(): lax.ppermute(low_far, 'dp', shift_z(step))]
  transfers between devices with their start and end apart: 14 -> 14, of which waited for: 7 -> 9; matrix products, arithmetic and copies ran while one was open for 10% -> 12% of each run, Pallas kernels for 1% -> 1%
where the time goes in v8:
time: 169 us; the launch traced here: 166 us
  starting transfers between devices  67.6 us (40%)
  waiting for transfers between devices  58.5 us (35%)
  local copies, waits for them, and re-layouts  16.1 us (10%)
  other arithmetic  10.1 us (6%)
  Pallas kernels  9.69 us (6%)
  matrix products  2.74 us (2%)
    all_to_all x3, waiting for transfers between devices, exchange(): lax.all_to_all(copies, 'dp', split_axis=0, concat_axis=0, tiled=True, axi...  20.7 us
    all_to_all x1, starting transfers between devices, parent_listing(): lax.all_to_all(copies, 'dp', split_axis=0, concat_axis=0, tiled=True)[:, 0]  18.7 us
    ppermute x1, waiting for transfers between devices, gather_rest(): down = lax.ppermute(high_plane, 'dp', shift_z(-1))  17.9 us
    all_to_all x3, starting transfers between devices, exchange(): lax.all_to_all(copies, 'dp', split_axis=0, concat_axis=0, tiled=True, axi...  15.9 us
    ppermute x3, starting transfers between devices, halve(): came = lax.ppermute(send, 'tensor', [(i, i ^ apart) for i in range(shards)])  9.94 us
    ppermute x3, starting transfers between devices, gather_near(): lax.ppermute(low_far, 'dp', shift_z(step))  9.42 us
    all_to_all x1, waiting for transfers between devices, parent_listing(): lax.all_to_all(copies, 'dp', split_axis=0, concat_axis=0, tiled=True)[:, 0]  7.45 us
    pallas_call x2, Pallas kernels, place_children(): pl.pallas_call(functools.partial(place_kernel, count, len(given) - 1 - co...  6.72 us
  transfers between devices with their start and end apart: 14, of which 9 were waited for; matrix products, arithmetic and copies ran while one was open for 12% of the time, Pallas kernels for 1%

profile of v8, /device:TPU:24, one launch (start us, length us, event | category | flops | bytes accessed | tf_op | source)
XLA Modules:
  0.0 165.8 jit_solution(6090411916382180897)
XLA Ops:
  2.1 18.7 %all-to-all-start = ((s32[64,1,128]{2,1,0:T(1,128)}), s32[64,1,128]{2,1,0:T(1,128)}, u32[]{:S(2)}, u32[]{:S(2)}) async-start(s32[64,1,128]{2,1,0:T(1,128)} %broadcast_in_dim.103), calls=%async_computation | async-start | bytes 65536 | tf_op jit(solution)/shard_map/all_to_all | solution.py:72
  21.6 2.3 %gather_fusion = bf16[192,2,16,128]{3,2,1,0:T(8,128)(2,1)S(1)} fusion(bf16[192,2,16,128]{3,2,1,0:T(8,128)(2,1)} %bitcast.159, s32[1024]{0:T(1024)S(1)} %pad_clamp_fusion), kind=kCustom, calls=%fused_computation | custom fusion | bytes 3146496 | tf_op jit(solution)/shard_map/gather | solution.py:23
  23.9 1.6 fusion.46
  25.6 7.4 %all-to-all-done = s32[64,1,128]{2,1,0:T(1,128)} async-done(((s32[64,1,128]{2,1,0:T(1,128)}), s32[64,1,128]{2,1,0:T(1,128)}, u32[]{:S(2)}, u32[]{:S(2)}) %all-to-all-start) | async-done | bytes 32800 | tf_op jit(solution)/shard_map/all_to_all | solution.py:72
  33.1 3.0 %shard_map.121 = bf16[4,2,8,2,16,128]{5,4,3,2,1,0:T(8,128)(2,1)} custom-call(s32[1]{0:T(128)} %bitcast.me_ref, s32[64,128]{1,0:T(8,128)} %bitcast.1.listing_ref, s32[16,12]{1,0:T(8,128)} %table_ref.1, bf16[192,2,16,128]{3,2,1,0:T(8,128)(2,1)} %bitcast.160), custom_call_target="tpu_custom_call" | custom-call | tf_op jit(solution)/shard_map/pallas_call | solution.py:121
  36.0 4.3 %all-to-all-start.1 = ((bf16[4,512,128]{2,1,0:T(8,128)(2,1)}), bf16[4,512,128]{2,1,0:T(8,128)(2,1)}, u32[]{:S(2)}, u32[]{:S(2)}) async-start(bf16[4,512,128]{2,1,0:T(8,128)(2,1)} %bitcast.167), calls=%async_computation.1 | async-start | bytes 1048576 | tf_op jit(solution)/shard_map/all_to_all | solution.py:92
  44.7 1.9 %collective-permute-start = (bf16[4,32,2560]{2,1,0:T(8,128)(2,1)}, bf16[4,32,2560]{2,1,0:T(8,128)(2,1)}, u32[]{:S(2)}, u32[]{:S(2)}) collective-permute-start(bf16[4,32,2560]{2,1,0:T(8,128)(2,1)} %dynamic-slice_bitcast_fusion), channel_id=1, source_target_pairs={{0,1},{1,0},{2,3},{3,2},{4,5},{5,4},{6,7},{7,6},{8,9},{9,8},{10,11... | collective-permute-start | bytes 1966088 | tf_op jit(solution)/shard_map/ppermute | solution.py:237
  46.7 2.4 %collective-permute-done = bf16[4,32,2560]{2,1,0:T(8,128)(2,1)} collective-permute-done((bf16[4,32,2560]{2,1,0:T(8,128)(2,1)}, bf16[4,32,2560]{2,1,0:T(8,128)(2,1)}, u32[]{:S(2)}, u32[]{:S(2)}) %collective-permute-start) | collective-permute-done | bytes 655392 | tf_op jit(solution)/shard_map/ppermute | solution.py:237
  49.0 2.1 %fusion = bf16[4,32,2560]{2,1,0:T(8,128)(2,1)} fusion(bf16[4,32,2560]{2,1,0:T(8,128)(2,1)} %collective-permute-done, bf16[4,2,32,2560]{3,2,1,0:T(8,128)(2,1)S(1)} %bitcast.163, s32[]{:T(128)S(6)} %select_n.143), kind=kLoop, calls=%fused_computation.4 | loop fusion | flops 1310720 | bytes 1966084 | tf_op jit(solution)/shard_map/convert_element_type | solution.py:263
  51.1 19.8 %all-to-all-done.1 = bf16[4,512,128]{2,1,0:T(8,128)(2,1)} async-done(((bf16[4,512,128]{2,1,0:T(8,128)(2,1)}), bf16[4,512,128]{2,1,0:T(8,128)(2,1)}, u32[]{:S(2)}, u32[]{:S(2)}) %all-to-all-start.1) | async-done | bytes 524320 | tf_op jit(solution)/shard_map/all_to_all | solution.py:92
  70.9 1.7 %dynamic-slice_bitcast_fusion.1 = bf16[2,32,2560]{2,1,0:T(8,128)(2,1)} fusion(bf16[2,2,32,2560]{3,2,1,0:T(8,128)(2,1)} %bitcast.165, s32[]{:T(128)S(6)} %select_n.148), kind=kLoop, calls=%fused_computation.34 | loop fusion | bytes 655364 | tf_op jit(solution)/shard_map/jit(dynamic_index_in_dim)/squeeze | solution.py:236
  72.6 3.4 %collective-permute-start.4 = (bf16[2,32,2560]{2,1,0:T(8,128)(2,1)}, bf16[2,32,2560]{2,1,0:T(8,128)(2,1)}, u32[]{:S(2)}, u32[]{:S(2)}) collective-permute-start(bf16[2,32,2560]{2,1,0:T(8,128)(2,1)} %dynamic-slice_bitcast_fusion.1), channel_id=1, source_target_pairs={{0,2},{1,3},{2,0},{3,1},{4,6},{5,7},{6,4},{7,5},{8,10},{9,11},{10,... | collective-permute-start | bytes 983048 | tf_op jit(solution)/shard_map/ppermute | solution.py:237
  77.2 2.5 %collective-permute-start.3 = (bf16[1024,128]{1,0:T(8,128)(2,1)S(1)}, bf16[1024,128]{1,0:T(8,128)(2,1)S(1)}, u32[]{:S(2)}, u32[]{:S(2)}) collective-permute-start(bf16[1024,128]{1,0:T(8,128)(2,1)S(1)} %bitcast.169), channel_id=1, source_target_pairs={{0,480},{8,488},{16,496},{24,504},{32,0},{40,8},{48,16},{56,24},{6... | collective-permute-start | bytes 786440 | tf_op jit(solution)/shard_map/ppermute | solution.py:216
  79.6 1.9 %collective-permute-start.2 = (bf16[1024,128]{1,0:T(8,128)(2,1)S(1)}, bf16[1024,128]{1,0:T(8,128)(2,1)}, u32[]{:S(2)}, u32[]{:S(2)}) collective-permute-start(bf16[1024,128]{1,0:T(8,128)(2,1)S(1)} %bitcast.170), channel_id=1, source_target_pairs={{0,64},{8,72},{16,80},{24,88},{32,96},{40,104},{48,112},{56,120},{... | collective-permute-start | bytes 786440 | tf_op jit(solution)/shard_map/ppermute | solution.py:216
  81.6 5.0 %collective-permute-start.1 = (bf16[1024,128]{1,0:T(8,128)(2,1)S(1)}, bf16[1024,128]{1,0:T(8,128)(2,1)}, u32[]{:S(2)}, u32[]{:S(2)}) collective-permute-start(bf16[1024,128]{1,0:T(8,128)(2,1)S(1)} %bitcast.171), channel_id=1, source_target_pairs={{0,32},{8,40},{16,48},{24,56},{32,64},{40,72},{48,80},{56,88},{64,... | collective-permute-start | bytes 786440 | tf_op jit(solution)/shard_map/ppermute | solution.py:216
  86.6 1.1 broadcast_in_dim.114
  87.7 4.8 %all-to-all-start.2 = ((bf16[4,1024,128]{2,1,0:T(8,128)(2,1)}), bf16[4,1024,128]{2,1,0:T(8,128)(2,1)S(1)}, u32[]{:S(2)}, u32[]{:S(2)}) async-start(bf16[4,1024,128]{2,1,0:T(8,128)(2,1)} %broadcast_in_dim.114), calls=%async_computation.2 | async-start | bytes 2097152 | tf_op jit(solution)/shard_map/all_to_all | solution.py:92
  92.5 1.1 fusion.12
  93.7 4.6 %collective-permute-start.5 = (bf16[1,32,2560]{2,1,0:T(8,128)(2,1)S(1)}, bf16[1,32,2560]{2,1,0:T(8,128)(2,1)S(1)}, u32[]{:S(2)}, u32[]{:S(2)}) collective-permute-start(bf16[1,32,2560]{2,1,0:T(8,128)(2,1)S(1)} %constant_dynamic-slice_fusion), channel_id=1, source_target_pairs={{0,4},{1,5},{2,6},{3,7},{4,0},{5,1},{6,2},{7,3},{8,12},{9,13},{10,... | collective-permute-start | bytes 491528 | tf_op jit(solution)/shard_map/ppermute | solution.py:237
  98.4 1.7 %collective-permute-done.1 = bf16[1024,128]{1,0:T(8,128)(2,1)} collective-permute-done((bf16[1024,128]{1,0:T(8,128)(2,1)S(1)}, bf16[1024,128]{1,0:T(8,128)(2,1)}, u32[]{:S(2)}, u32[]{:S(2)}) %collective-permute-start.1) | collective-permute-done | bytes 262176 | tf_op jit(solution)/shard_map/ppermute | solution.py:216
  100.0 2.1 %pad_maximum_fusion = bf16[4096,128]{1,0:T(8,128)(2,1)} fusion(bf16[1024,128]{1,0:T(8,128)(2,1)S(1)} %collective-permute-done.3, bf16[1024,128]{1,0:T(8,128)(2,1)} %collective-permute-done.2, bf16[1024,128]{1,0:T(8,128)(2,1)} %collective-permute-done.1, bf16[1024,128]{1,0:T(8,128)(2,1)S(1)} %bitcast.172), kind=kLoop, calls=%fused_computation.16 | loop fusion | flops 4194304 | bytes 2097152 | tf_op jit(solution)/shard_map/concatenate | solution.py:215
  102.5 3.8 %broadcast_in_dim.112 = bf16[4,4096,128]{2,1,0:T(8,128)(2,1)} broadcast(bf16[4096,128]{1,0:T(8,128)(2,1)} %pad_maximum_fusion), dimensions={1,2} | broadcast | bytes 5242880 | tf_op jit(solution)/shard_map/broadcast_in_dim | solution.py:218
  106.2 6.9 %all-to-all-start.3 = ((bf16[4,4096,128]{2,1,0:T(8,128)(2,1)}), bf16[4,4096,128]{2,1,0:T(8,128)(2,1)}, u32[]{:S(2)}, u32[]{:S(2)}) async-start(bf16[4,4096,128]{2,1,0:T(8,128)(2,1)} %broadcast_in_dim.112), calls=%async_computation.3 | async-start | bytes 8388608 | tf_op jit(solution)/shard_map/all_to_all | solution.py:92
  114.9 4.1 %collective-permute-start.8 = (bf16[4096,128]{1,0:T(8,128)(2,1)S(1)}, bf16[4096,128]{1,0:T(8,128)(2,1)S(1)}, u32[]{:S(2)}, u32[]{:S(2)}) collective-permute-start(bf16[4096,128]{1,0:T(8,128)(2,1)S(1)} %bitcast.151), channel_id=1, source_target_pairs={{0,480},{8,488},{16,496},{24,504},{32,0},{40,8},{48,16},{56,24},{6... | collective-permute-start | bytes 3145736 | tf_op jit(solution)/shard_map/ppermute | solution.py:225
  119.0 3.7 %collective-permute-start.6 = (bf16[4096,128]{1,0:T(8,128)(2,1)S(1)}, bf16[4096,128]{1,0:T(8,128)(2,1)S(1)}, u32[]{:S(2)}, u32[]{:S(2)}) collective-permute-start(bf16[4096,128]{1,0:T(8,128)(2,1)S(1)} %bitcast.152), channel_id=1, source_target_pairs={{0,32},{8,40},{16,48},{24,56},{32,64},{40,72},{48,80},{56,88},{64,... | collective-permute-start | bytes 3145736 | tf_op jit(solution)/shard_map/ppermute | solution.py:224
  123.6 17.9 %collective-permute-done.8 = bf16[4096,128]{1,0:T(8,128)(2,1)S(1)} collective-permute-done((bf16[4096,128]{1,0:T(8,128)(2,1)S(1)}, bf16[4096,128]{1,0:T(8,128)(2,1)S(1)}, u32[]{:S(2)}, u32[]{:S(2)}) %collective-permute-start.8) | collective-permute-done | bytes 1048608 | tf_op jit(solution)/shard_map/ppermute | solution.py:225
  141.5 3.4 %collective-permute-start.9 = (bf16[2048,128]{1,0:T(8,128)(2,1)S(1)}, bf16[2048,128]{1,0:T(8,128)(2,1)S(1)}, u32[]{:S(2)}, u32[]{:S(2)}) collective-permute-start(bf16[2048,128]{1,0:T(8,128)(2,1)S(1)} %slice.42), channel_id=1, source_target_pairs={{0,480},{8,488},{16,496},{24,504},{32,0},{40,8},{48,16},{56,24},{6... | collective-permute-start | bytes 1572872 | tf_op jit(solution)/shard_map/ppermute | solution.py:227
  145.0 2.4 %collective-permute-start.7 = (bf16[2048,128]{1,0:T(8,128)(2,1)S(1)}, bf16[2048,128]{1,0:T(8,128)(2,1)S(1)}, u32[]{:S(2)}, u32[]{:S(2)}) collective-permute-start(bf16[2048,128]{1,0:T(8,128)(2,1)S(1)} %slice.41), channel_id=1, source_target_pairs={{0,32},{8,40},{16,48},{24,56},{32,64},{40,72},{48,80},{56,88},{64,... | collective-permute-start | bytes 1572872 | tf_op jit(solution)/shard_map/ppermute | solution.py:226
  148.2 2.2 %shard_map.122.refs_3_ = bf16[48,8,2,16,128]{4,3,2,1,0:T(8,128)(2,1)} custom-call(s32[48]{0:T(128)S(1)} %get-tuple-element.35.where_ref, bf16[16,8,2,16,128]{4,3,2,1,0:T(8,128)(2,1)S(1)} %bitcast.153, bf16[16,8,2,16,128]{4,3,2,1,0:T(8,128)(2,1)S(1)} %bitcast.155, bf16[16,8,2,16,128]{4,3,2,1,0:T(8,128)(2,1)S(1)} %bitcast.154), custom_call_target="tpu_custom_call" | custom-call | tf_op jit(solution)/shard_map/pallas_call | solution.py:172
  150.3 3.7 %collective-permute-done.9 = bf16[2048,128]{1,0:T(8,128)(2,1)S(1)} collective-permute-done((bf16[2048,128]{1,0:T(8,128)(2,1)S(1)}, bf16[2048,128]{1,0:T(8,128)(2,1)S(1)}, u32[]{:S(2)}, u32[]{:S(2)}) %collective-permute-start.9) | collective-permute-done | bytes 524320 | tf_op jit(solution)/shard_map/ppermute | solution.py:227
  154.1 4.3 %collective-permute-done.7 = bf16[2048,128]{1,0:T(8,128)(2,1)S(1)} collective-permute-done((bf16[2048,128]{1,0:T(8,128)(2,1)S(1)}, bf16[2048,128]{1,0:T(8,128)(2,1)S(1)}, u32[]{:S(2)}, u32[]{:S(2)}) %collective-permute-start.7) | collective-permute-done | bytes 524320 | tf_op jit(solution)/shard_map/ppermute | solution.py:226
  161.3 4.6 %shard_map.123 = bf16[48,8,2,16,128]{4,3,2,1,0:T(8,128)(2,1)} custom-call(s32[48]{0:T(128)S(1)} %fusion.37.where_ref, bf16[8,8,2,16,128]{4,3,2,1,0:T(8,128)(2,1)S(1)} %bitcast.157, bf16[8,8,2,16,128]{4,3,2,1,0:T(8,128)(2,1)S(1)} %bitcast.156, bf16[64,8,2,16,128]{4,3,2,1,0:T(8,128)(2,1)} %bitcast.43.refs_2_, ...), custom_call_target="tpu_custom_call", output_to_operand_aliasing={{}: (4, {})} | custom-call | tf_op jit(solution)/shard_map/pallas_call | solution.py:172
  (69 shorter events, 14.4 us)
Async XLA Ops:
  0.6 42.3 %copy-start = (bf16[384,2560]{1,0:T(8,128)(2,1)S(1)}, bf16[384,2560]{1,0:T(8,128)(2,1)}, u32[]{:S(2)}) copy-start(bf16[384,2560]{1,0:T(8,128)(2,1)} %param.15) | copy-start | bytes 5898244
  2.1 31.0 %all-to-all-start = ((s32[64,1,128]{2,1,0:T(1,128)}), s32[64,1,128]{2,1,0:T(1,128)}, u32[]{:S(2)}, u32[]{:S(2)}) async-start(s32[64,1,128]{2,1,0:T(1,128)} %broadcast_in_dim.103), calls=%async_computation | async-start | bytes 65536 | tf_op jit(solution)/shard_map/all_to_all | solution.py:72
  23.9 1.6 copy-start.11
  33.0 7.3 %copy-start.3 = (bf16[16,12,1,16,1,128]{5,3,2,1,0,4:T(8,128)(2,1)S(1)}, bf16[16,12,1,16,1,128]{5,3,2,1,0,4:T(8,128)(2,1)}, u32[]{:S(2)}) copy-start(bf16[16,12,1,16,1,128]{5,3,2,1,0,4:T(8,128)(2,1)} %get-tuple-element.45) | copy-start | bytes 2359300
  33.0 7.3 %copy-start.4 = (bf16[16,16,3,128]{3,1,2,0:T(8,128)(2,1)S(1)}, bf16[16,16,3,128]{3,1,2,0:T(8,128)(2,1)}, u32[]{:S(2)}) copy-start(bf16[16,16,3,128]{3,1,2,0:T(8,128)(2,1)} %param.10) | copy-start | bytes 589828
  36.0 5.0 %copy-start.8 = (bf16[16,2,16,1,128]{4,2,3,1,0:T(8,128)(2,1)S(1)}, bf16[16,2,16,1,128]{4,2,3,1,0:T(8,128)(2,1)}, u32[]{:S(2)}) copy-start(bf16[16,2,16,1,128]{4,2,3,1,0:T(8,128)(2,1)} %param.11) | copy-start | bytes 393220
  36.0 34.9 %all-to-all-start.1 = ((bf16[4,512,128]{2,1,0:T(8,128)(2,1)}), bf16[4,512,128]{2,1,0:T(8,128)(2,1)}, u32[]{:S(2)}, u32[]{:S(2)}) async-start(bf16[4,512,128]{2,1,0:T(8,128)(2,1)} %bitcast.167), calls=%async_computation.1 | async-start | bytes 1048576 | tf_op jit(solution)/shard_map/all_to_all | solution.py:92
  40.3 1.8 %copy-start.5 = (bf16[16,12,1,16,1,128]{5,3,2,1,0,4:T(8,128)(2,1)S(1)}, bf16[16,12,1,16,1,128]{5,3,2,1,0,4:T(8,128)(2,1)}, u32[]{:S(2)}) copy-start(bf16[16,12,1,16,1,128]{5,3,2,1,0,4:T(8,128)(2,1)} %get-tuple-element.44) | copy-start | bytes 2359300
  44.7 4.3 %collective-permute-start = (bf16[4,32,2560]{2,1,0:T(8,128)(2,1)}, bf16[4,32,2560]{2,1,0:T(8,128)(2,1)}, u32[]{:S(2)}, u32[]{:S(2)}) collective-permute-start(bf16[4,32,2560]{2,1,0:T(8,128)(2,1)} %dynamic-slice_bitcast_fusion), channel_id=1, source_target_pairs={{0,1},{1,0},{2,3},{3,2},{4,5},{5,4},{6,7},{7,6},{8,9},{9,8},{10,11... | collective-permute-start | bytes 1966088 | tf_op jit(solution)/shard_map/ppermute | solution.py:237
  72.6 19.9 %collective-permute-start.4 = (bf16[2,32,2560]{2,1,0:T(8,128)(2,1)}, bf16[2,32,2560]{2,1,0:T(8,128)(2,1)}, u32[]{:S(2)}, u32[]{:S(2)}) collective-permute-start(bf16[2,32,2560]{2,1,0:T(8,128)(2,1)} %dynamic-slice_bitcast_fusion.1), channel_id=1, source_target_pairs={{0,2},{1,3},{2,0},{3,1},{4,6},{5,7},{6,4},{7,5},{8,10},{9,11},{10,... | collective-permute-start | bytes 983048 | tf_op jit(solution)/shard_map/ppermute | solution.py:237
  77.2 21.2 %collective-permute-start.3 = (bf16[1024,128]{1,0:T(8,128)(2,1)S(1)}, bf16[1024,128]{1,0:T(8,128)(2,1)S(1)}, u32[]{:S(2)}, u32[]{:S(2)}) collective-permute-start(bf16[1024,128]{1,0:T(8,128)(2,1)S(1)} %bitcast.169), channel_id=1, source_target_pairs={{0,480},{8,488},{16,496},{24,504},{32,0},{40,8},{48,16},{56,24},{6... | collective-permute-start | bytes 786440 | tf_op jit(solution)/shard_map/ppermute | solution.py:216
  79.6 18.7 %collective-permute-start.2 = (bf16[1024,128]{1,0:T(8,128)(2,1)S(1)}, bf16[1024,128]{1,0:T(8,128)(2,1)}, u32[]{:S(2)}, u32[]{:S(2)}) collective-permute-start(bf16[1024,128]{1,0:T(8,128)(2,1)S(1)} %bitcast.170), channel_id=1, source_target_pairs={{0,64},{8,72},{16,80},{24,88},{32,96},{40,104},{48,112},{56,120},{... | collective-permute-start | bytes 786440 | tf_op jit(solution)/shard_map/ppermute | solution.py:216
  81.6 18.4 %collective-permute-start.1 = (bf16[1024,128]{1,0:T(8,128)(2,1)S(1)}, bf16[1024,128]{1,0:T(8,128)(2,1)}, u32[]{:S(2)}, u32[]{:S(2)}) collective-permute-start(bf16[1024,128]{1,0:T(8,128)(2,1)S(1)} %bitcast.171), channel_id=1, source_target_pairs={{0,32},{8,40},{16,48},{24,56},{32,64},{40,72},{48,80},{56,88},{64,... | collective-permute-start | bytes 786440 | tf_op jit(solution)/shard_map/ppermute | solution.py:216
  87.7 14.7 %all-to-all-start.2 = ((bf16[4,1024,128]{2,1,0:T(8,128)(2,1)}), bf16[4,1024,128]{2,1,0:T(8,128)(2,1)S(1)}, u32[]{:S(2)}, u32[]{:S(2)}) async-start(bf16[4,1024,128]{2,1,0:T(8,128)(2,1)} %broadcast_in_dim.114), calls=%async_computation.2 | async-start | bytes 2097152 | tf_op jit(solution)/shard_map/all_to_all | solution.py:92
  93.7 8.7 %collective-permute-start.5 = (bf16[1,32,2560]{2,1,0:T(8,128)(2,1)S(1)}, bf16[1,32,2560]{2,1,0:T(8,128)(2,1)S(1)}, u32[]{:S(2)}, u32[]{:S(2)}) collective-permute-start(bf16[1,32,2560]{2,1,0:T(8,128)(2,1)S(1)} %constant_dynamic-slice_fusion), channel_id=1, source_target_pairs={{0,4},{1,5},{2,6},{3,7},{4,0},{5,1},{6,2},{7,3},{8,12},{9,13},{10,... | collective-permute-start | bytes 491528 | tf_op jit(solution)/shard_map/ppermute | solution.py:237
  106.2 6.9 %copy-start.9 = (bf16[2560]{0:T(1024)(128)(2,1)S(1)}, bf16[2560]{0:T(1024)(128)(2,1)}, u32[]{:S(2)}) copy-start(bf16[2560]{0:T(1024)(128)(2,1)} %param.17) | copy-start | bytes 15364
  106.2 6.9 %copy-start.10 = (bf16[2560]{0:T(1024)(128)(2,1)S(1)}, bf16[2560]{0:T(1024)(128)(2,1)}, u32[]{:S(2)}) copy-start(bf16[2560]{0:T(1024)(128)(2,1)} %param.18) | copy-start | bytes 15364
  106.2 7.5 %copy-start.12 = (s32[48]{0:T(128)S(1)}, s32[48]{0:T(128)}, u32[]{:S(2)}) copy-start(s32[48]{0:T(128)} %param.19) | copy-start | bytes 580
  106.2 16.5 %copy-start.6 = (bf16[32,2560]{1,0:T(8,128)(2,1)S(1)}, bf16[32,2560]{1,0:T(8,128)(2,1)}, u32[]{:S(2)}) copy-start(bf16[32,2560]{1,0:T(8,128)(2,1)} %param.16) | copy-start | bytes 491524
  106.2 54.0 %all-to-all-start.3 = ((bf16[4,4096,128]{2,1,0:T(8,128)(2,1)}), bf16[4,4096,128]{2,1,0:T(8,128)(2,1)}, u32[]{:S(2)}, u32[]{:S(2)}) async-start(bf16[4,4096,128]{2,1,0:T(8,128)(2,1)} %broadcast_in_dim.112), calls=%async_computation.3 | async-start | bytes 8388608 | tf_op jit(solution)/shard_map/all_to_all | solution.py:92
  114.9 26.5 %collective-permute-start.8 = (bf16[4096,128]{1,0:T(8,128)(2,1)S(1)}, bf16[4096,128]{1,0:T(8,128)(2,1)S(1)}, u32[]{:S(2)}, u32[]{:S(2)}) collective-permute-start(bf16[4096,128]{1,0:T(8,128)(2,1)S(1)} %bitcast.151), channel_id=1, source_target_pairs={{0,480},{8,488},{16,496},{24,504},{32,0},{40,8},{48,16},{56,24},{6... | collective-permute-start | bytes 3145736 | tf_op jit(solution)/shard_map/ppermute | solution.py:225
  119.0 25.9 %collective-permute-start.6 = (bf16[4096,128]{1,0:T(8,128)(2,1)S(1)}, bf16[4096,128]{1,0:T(8,128)(2,1)S(1)}, u32[]{:S(2)}, u32[]{:S(2)}) collective-permute-start(bf16[4096,128]{1,0:T(8,128)(2,1)S(1)} %bitcast.152), channel_id=1, source_target_pairs={{0,32},{8,40},{16,48},{24,56},{32,64},{40,72},{48,80},{56,88},{64,... | collective-permute-start | bytes 3145736 | tf_op jit(solution)/shard_map/ppermute | solution.py:224
  122.7 24.7 %copy-start.7 = (f32[2560]{0:T(1024)S(1)}, f32[2560]{0:T(1024)}, u32[]{:S(2)}) copy-start(f32[2560]{0:T(1024)} %convert_element_type.81) | copy-start | bytes 30724
  141.5 12.6 %collective-permute-start.9 = (bf16[2048,128]{1,0:T(8,128)(2,1)S(1)}, bf16[2048,128]{1,0:T(8,128)(2,1)S(1)}, u32[]{:S(2)}, u32[]{:S(2)}) collective-permute-start(bf16[2048,128]{1,0:T(8,128)(2,1)S(1)} %slice.42), channel_id=1, source_target_pairs={{0,480},{8,488},{16,496},{24,504},{32,0},{40,8},{48,16},{56,24},{6... | collective-permute-start | bytes 1572872 | tf_op jit(solution)/shard_map/ppermute | solution.py:227
  145.0 13.5 %collective-permute-start.7 = (bf16[2048,128]{1,0:T(8,128)(2,1)S(1)}, bf16[2048,128]{1,0:T(8,128)(2,1)S(1)}, u32[]{:S(2)}, u32[]{:S(2)}) collective-permute-start(bf16[2048,128]{1,0:T(8,128)(2,1)S(1)} %slice.41), channel_id=1, source_target_pairs={{0,32},{8,40},{16,48},{24,56},{32,64},{40,72},{48,80},{56,88},{64,... | collective-permute-start | bytes 1572872 | tf_op jit(solution)/shard_map/ppermute | solution.py:226
  158.4 0.8 copy-start.1
  160.2 1.0 copy-start.2

commit v9 on v7

--- a/solution.py
+++ b/solution.py
@@ -14,7 +14,7 @@
 PAGES = PREFIX // PAGE
 NZ, NY = 16, 4
 NEAR = 4
-FRONT = 5
+FRONT = 6
 LANES = 128
 
 
@@ -90,7 +90,10 @@
 
 
 def share(block, groups):
-    copies = jnp.broadcast_to(block[None], (len(groups[0]),) + block.shape)
+    return exchange(jnp.broadcast_to(block[None], (len(groups[0]),) + block.shape), groups)
+
+
+def exchange(copies, groups):
     return lax.all_to_all(
         copies, "dp", split_axis=0, concat_axis=0, tiled=True, axis_index_groups=groups
     )
@@ -105,24 +108,27 @@
     copies = []
     for which, row in enumerate((lowest, highest)):
         for page in range(PAGES):
-            target = front_ref.at[which, page] if page < FRONT else back_ref.at[which, page - FRONT]
+            part, at = (front_ref, page) if page < FRONT else (back_ref, page - FRONT)
             copies.append(
                 pltpu.make_async_copy(
-                    cache_ref.at[table_ref[row, page]], target, sems.at[which, page]
+                    cache_ref.at[table_ref[row, page]], part.at[0, which, at], sems.at[which, page]
                 )
             )
     for copy in copies:
         copy.start()
     for copy in copies:
         copy.wait()
+    for part in (front_ref, back_ref):
+        for number in range(1, part.shape[0]):
+            part[number] = part[0]
 
 
 def pick_pages(me_index, listing, page_table, cache):
     return pl.pallas_call(
         pick_kernel,
         out_shape=tuple(
-            jax.ShapeDtypeStruct((2, pages) + cache.shape[1:], cache.dtype)
-            for pages in (FRONT, PAGES - FRONT)
+            jax.ShapeDtypeStruct((copies, 2, pages) + cache.shape[1:], cache.dtype)
+            for copies, pages in ((NY, FRONT), (NZ // NEAR, PAGES - FRONT))
         ),
         in_specs=[
             pl.BlockSpec(memory_space=pltpu.SMEM),
@@ -136,17 +142,26 @@
 
 
 def place_kernel(first_page, aliased, where_ref, source_ref, *refs):
-    out_ref, sems = refs[aliased:]
-    slots = out_ref.shape[0]
-    pages = source_ref.shape[1]
+    out_ref, held, load_sems, sems = refs[aliased:]
+    slots, pages = held.shape[:2]
+
+    def load(slot):
+        return pltpu.make_async_copy(
+            source_ref.at[where_ref[slot]], held.at[slot], load_sems.at[slot]
+        )
 
     def store(slot):
         return pltpu.make_async_copy(
-            source_ref.at[where_ref[slot]], out_ref.at[slot, pl.ds(first_page, pages)], sems.at[slot]
+            held.at[slot], out_ref.at[slot, pl.ds(first_page, pages)], sems.at[slot]
         )
 
     @pl.loop(0, slots)
     def _(slot):
+        load(slot).start()
+
+    @pl.loop(0, slots)
+    def _(slot):
+        load(slot).wait()
         store(slot).start()
 
     @pl.loop(0, slots)
@@ -162,13 +177,17 @@
         out_shape=jax.ShapeDtypeStruct((slots, PAGES) + source.shape[2:], source.dtype),
         in_specs=[
             pl.BlockSpec(memory_space=pltpu.SMEM),
-            pl.BlockSpec(memory_space=pltpu.VMEM),
+            pl.BlockSpec(memory_space=pltpu.HBM),
         ]
         + [pl.BlockSpec(memory_space=pl.ANY)] * (len(given) - 2),
         out_specs=pl.BlockSpec(memory_space=pl.ANY),
-        scratch_shapes=[pltpu.SemaphoreType.DMA((slots,))],
+        scratch_shapes=[
+            pltpu.VMEM((slots,) + source.shape[1:], source.dtype),
+            pltpu.SemaphoreType.DMA((slots,)),
+            pltpu.SemaphoreType.DMA((slots,)),
+        ],
         input_output_aliases={} if earlier is None else {2: 0},
-        compiler_params=pltpu.CompilerParams(vmem_limit_bytes=24 * 2**20),
+        compiler_params=pltpu.CompilerParams(vmem_limit_bytes=58 * 2**20),
     )(*given)
 
 
@@ -187,14 +206,14 @@
 
 def gather_fronts(front):
     width = front.shape[-1]
-    plane = share(front.reshape(-1, width), groups_y()).reshape(-1, width)
+    plane = exchange(front.reshape(NY, -1, width), groups_y()).reshape(-1, width)
     fronts = lax.all_gather(plane, "dp", axis=0, tiled=True, axis_index_groups=groups_z())
-    return fronts.reshape((-1,) + front.shape[1:])
+    return fronts.reshape((-1,) + front.shape[2:])
 
 
 def gather_backs_far(back):
     width = back.shape[-1]
-    return share(back.reshape(-1, width), groups_far()).reshape(-1, width)
+    return exchange(back.reshape(NZ // NEAR, -1, width), groups_far()).reshape(-1, width)
 
 
 def gather_backs_near(far):
@@ -238,7 +257,7 @@
     far, partial = lax.optimization_barrier((gather_backs_far(back), partial))
     held = halve(partial.reshape(lax.axis_size("tensor"), rows_here, -1), 1).astype(jnp.bfloat16)
     column, held = lax.optimization_barrier((gather_backs_near(far), held))
-    backs = share(column, groups_y()).reshape((-1,) + back.shape[1:])
+    backs = share(column, groups_y()).reshape((-1,) + back.shape[2:])
     held = halve(held, 2).astype(jnp.bfloat16)
     updated = halve(held, 4)[0] + residual.astype(jnp.float32)
     hidden_out = updated.astype(jnp.bfloat16)

time: 177 us -> 155 us (0.88)
  waiting for transfers between devices: 70.7 us -> 49.8 us
  local copies, waits for them, and re-layouts: 13.6 us -> 8.18 us
  Pallas kernels: 8.29 us -> 10.1 us
    all_to_all x2, waiting for transfers between devices: 38.1 us -> 24.1 us  [exchange(): lax.all_to_all(copies, 'dp', split_axis=0, concat_axis=0, tiled=True, axi...]
    ppermute x3, waiting for transfers between devices: 21.1 us -> 12.3 us  [gather_backs_near(): lax.ppermute(far, 'dp', shift_z(step))]
    broadcast_in_dim x3 -> x1, local copies, waits for them, and re-layouts: 4.57 us -> 1.59 us  [share(): jnp.broadcast_to(block[None], (len(groups[0]),) + block.shape)]
    all_gather x1, waiting for transfers between devices: 0.02 us -> 2.2 us  [gather_fronts(): lax.all_gather(plane, 'dp', axis=0, tiled=True, axis_index_groups=groups_...]
  transfers between devices with their start and end apart: 10 -> 10, of which waited for: 7 -> 7; matrix products, arithmetic and copies ran while one was open for 10% -> 9% of each run, Pallas kernels for 2% -> 2%
where the time goes in v9:
time: 155 us; the launch traced here: 152 us
  waiting for transfers between devices  49.8 us (32%)
  starting transfers between devices  49.1 us (32%)
  between operations  14.5 us (9%)
  blocking collectives  12.1 us (8%)
  Pallas kernels  10.1 us (7%)
  local copies, waits for them, and re-layouts  8.18 us (5%)
  other arithmetic  5.62 us (4%)
  matrix products  2.74 us (2%)
    all_to_all x2, waiting for transfers between devices, exchange(): lax.all_to_all(copies, 'dp', split_axis=0, concat_axis=0, tiled=True, axi...  24.1 us
    all_to_all x1, starting transfers between devices, parent_listing(): lax.all_to_all(copies, 'dp', split_axis=0, concat_axis=0, tiled=True)[:, 0]  18.7 us
    ppermute x3, waiting for transfers between devices, gather_backs_near(): lax.ppermute(far, 'dp', shift_z(step))  12.3 us
    all_to_all x1, blocking collectives, exchange(): lax.all_to_all(copies, 'dp', split_axis=0, concat_axis=0, tiled=True, axi...  12.1 us
    ppermute x3, starting transfers between devices, gather_backs_near(): lax.ppermute(far, 'dp', shift_z(step))  10.2 us
    all_to_all x2, starting transfers between devices, exchange(): lax.all_to_all(copies, 'dp', split_axis=0, concat_axis=0, tiled=True, axi...  10.1 us
    ppermute x3, starting transfers between devices, halve(): came = lax.ppermute(send, 'tensor', [(i, i ^ apart) for i in range(shards)])  9.98 us
    all_to_all x1, waiting for transfers between devices, parent_listing(): lax.all_to_all(copies, 'dp', split_axis=0, concat_axis=0, tiled=True)[:, 0]  7.64 us
  transfers between devices with their start and end apart: 10, of which 7 were waited for; matrix products, arithmetic and copies ran while one was open for 9% of the time, Pallas kernels for 2%

profile of v9, /device:TPU:24, one launch (start us, length us, event | category | flops | bytes accessed | tf_op | source)
XLA Modules:
  0.0 152.2 jit_solution(9542736843906247017)
XLA Ops:
  7.2 0.8 pad.4
  8.0 0.6 broadcast_in_dim.84
  8.6 18.7 %all-to-all-start = ((s32[64,1,128]{2,1,0:T(1,128)}), s32[64,1,128]{2,1,0:T(1,128)}, u32[]{:S(2)}, u32[]{:S(2)}) async-start(s32[64,1,128]{2,1,0:T(1,128)} %broadcast_in_dim.84), calls=%async_computation | async-start | bytes 65536 | tf_op jit(solution)/shard_map/all_to_all | solution.py:73
  27.4 0.7 compare_select_fusion
  28.2 2.3 %gather_fusion = bf16[192,2,16,128]{3,2,1,0:T(8,128)(2,1)S(1)} fusion(bf16[192,2,16,128]{3,2,1,0:T(8,128)(2,1)} %bitcast.149, s32[1024]{0:T(1024)S(1)} %pad_clamp_fusion), kind=kCustom, calls=%fused_computation | custom fusion | bytes 3146496 | tf_op jit(solution)/shard_map/gather | solution.py:24
  30.5 1.6 %fusion.42 = (bf16[16,12,1,16,1,128]{5,3,2,1,0,4:T(8,128)(2,1)}, bf16[16,12,1,16,1,128]{5,3,2,1,0,4:T(8,128)(2,1)}) fusion(bf16[16,12,2,16,1,128]{5,3,2,1,0,4:T(8,128)(2,1)S(1)} %bitcast.151), kind=kLoop, calls=%fused_computation.94 | loop fusion | bytes 3145728 | tf_op jit(solution)/shard_map/slice | solution.py:27
  32.1 7.6 %all-to-all-done = s32[64,1,128]{2,1,0:T(1,128)} async-done(((s32[64,1,128]{2,1,0:T(1,128)}), s32[64,1,128]{2,1,0:T(1,128)}, u32[]{:S(2)}, u32[]{:S(2)}) %all-to-all-start) | async-done | bytes 32800 | tf_op jit(solution)/shard_map/all_to_all | solution.py:73
  39.7 3.0 %shard_map.121 = (bf16[4,2,6,2,16,128]{5,4,3,2,1,0:T(8,128)(2,1)}, bf16[4,2,2,2,16,128]{5,4,3,2,1,0:T(8,128)(2,1)}) custom-call(s32[1]{0:T(128)} %bitcast.me_ref, s32[64,128]{1,0:T(8,128)} %bitcast.1.listing_ref, s32[16,12]{1,0:T(8,128)} %table_ref.1, bf16[192,2,16,128]{3,2,1,0:T(8,128)(2,1)} %bitcast.150), custom_call_target="tpu_custom_call" | custom-call | tf_op jit(solution)/shard_map/pallas_call | solution.py:127
  42.7 12.1 %all_to_all.20 = bf16[4,384,128]{2,1,0:T(8,128)(2,1)} all-to-all(bf16[4,384,128]{2,1,0:T(8,128)(2,1)} %bitcast.164), channel_id=1, replica_groups={{0,8,16,24},{32,40,48,56},{64,72,80,88},{96,104,112,120},{128,136,144,1..., dimensions={0} | all-to-all | bytes 786432 | tf_op jit(solution)/shard_map/all_to_all | solution.py:97
  55.1 3.3 %all-to-all-start.1 = ((bf16[4,128,128]{2,1,0:T(8,128)(2,1)}), bf16[4,128,128]{2,1,0:T(8,128)(2,1)S(1)}, u32[]{:S(2)}, u32[]{:S(2)}) async-start(bf16[4,128,128]{2,1,0:T(8,128)(2,1)} %bitcast.166), calls=%async_computation.1 | async-start | bytes 262144 | tf_op jit(solution)/shard_map/all_to_all | solution.py:97
  59.0 0.7 fusion.43
  61.1 0.8 convolution_convert_fusion
  62.0 10.4 %all-to-all-done.1 = bf16[4,128,128]{2,1,0:T(8,128)(2,1)S(1)} async-done(((bf16[4,128,128]{2,1,0:T(8,128)(2,1)}), bf16[4,128,128]{2,1,0:T(8,128)(2,1)S(1)}, u32[]{:S(2)}, u32[]{:S(2)}) %all-to-all-start.1) | async-done | bytes 131104 | tf_op jit(solution)/shard_map/all_to_all | solution.py:97
  72.4 1.9 %collective-permute-start.3 = (bf16[4,32,2560]{2,1,0:T(8,128)(2,1)S(1)}, bf16[4,32,2560]{2,1,0:T(8,128)(2,1)S(1)}, u32[]{:S(2)}, u32[]{:S(2)}) collective-permute-start(bf16[4,32,2560]{2,1,0:T(8,128)(2,1)S(1)} %dynamic-slice_bitcast_fusion), channel_id=1, source_target_pairs={{0,1},{1,0},{2,3},{3,2},{4,5},{5,4},{6,7},{7,6},{8,9},{9,8},{10,11... | collective-permute-start | bytes 1966088 | tf_op jit(solution)/shard_map/ppermute | solution.py:231
  74.4 1.9 %collective-permute-start.2 = (bf16[512,128]{1,0:T(8,128)(2,1)S(1)}, bf16[512,128]{1,0:T(8,128)(2,1)S(1)}, u32[]{:S(2)}, u32[]{:S(2)}) collective-permute-start(bf16[512,128]{1,0:T(8,128)(2,1)S(1)} %bitcast.160), channel_id=1, source_target_pairs={{0,480},{8,488},{16,496},{24,504},{32,0},{40,8},{48,16},{56,24},{6... | collective-permute-start | bytes 393224 | tf_op jit(solution)/shard_map/ppermute | solution.py:221
  76.3 4.4 %collective-permute-start.1 = (bf16[512,128]{1,0:T(8,128)(2,1)S(1)}, bf16[512,128]{1,0:T(8,128)(2,1)S(1)}, u32[]{:S(2)}, u32[]{:S(2)}) collective-permute-start(bf16[512,128]{1,0:T(8,128)(2,1)S(1)} %bitcast.161), channel_id=1, source_target_pairs={{0,64},{8,72},{16,80},{24,88},{32,96},{40,104},{48,112},{56,120},{... | collective-permute-start | bytes 393224 | tf_op jit(solution)/shard_map/ppermute | solution.py:221
  80.7 3.9 %collective-permute-start = (bf16[512,128]{1,0:T(8,128)(2,1)S(1)}, bf16[512,128]{1,0:T(8,128)(2,1)S(1)}, u32[]{:S(2)}, u32[]{:S(2)}) collective-permute-start(bf16[512,128]{1,0:T(8,128)(2,1)S(1)} %bitcast.162), channel_id=1, source_target_pairs={{0,32},{8,40},{16,48},{24,56},{32,64},{40,72},{48,80},{56,88},{64,... | collective-permute-start | bytes 393224 | tf_op jit(solution)/shard_map/ppermute | solution.py:221
  84.6 0.8 add_select_fusion.1
  85.4 6.1 %collective-permute-done.1 = bf16[512,128]{1,0:T(8,128)(2,1)S(1)} collective-permute-done((bf16[512,128]{1,0:T(8,128)(2,1)S(1)}, bf16[512,128]{1,0:T(8,128)(2,1)S(1)}, u32[]{:S(2)}, u32[]{:S(2)}) %collective-permute-start.1) | collective-permute-done | bytes 131104 | tf_op jit(solution)/shard_map/ppermute | solution.py:221
  91.5 6.3 %collective-permute-done = bf16[512,128]{1,0:T(8,128)(2,1)S(1)} collective-permute-done((bf16[512,128]{1,0:T(8,128)(2,1)S(1)}, bf16[512,128]{1,0:T(8,128)(2,1)S(1)}, u32[]{:S(2)}, u32[]{:S(2)}) %collective-permute-start) | collective-permute-done | bytes 131104 | tf_op jit(solution)/shard_map/ppermute | solution.py:221
  98.0 0.9 copy-done.2
  98.9 3.4 %collective-permute-start.4 = (bf16[2,32,2560]{2,1,0:T(8,128)(2,1)S(1)}, bf16[2,32,2560]{2,1,0:T(8,128)(2,1)S(1)}, u32[]{:S(2)}, u32[]{:S(2)}) collective-permute-start(bf16[2,32,2560]{2,1,0:T(8,128)(2,1)S(1)} %dynamic-slice_bitcast_fusion.1), channel_id=1, source_target_pairs={{0,2},{1,3},{2,0},{3,1},{4,6},{5,7},{6,4},{7,5},{8,10},{9,11},{10,... | collective-permute-start | bytes 983048 | tf_op jit(solution)/shard_map/ppermute | solution.py:231
  102.7 0.6 multiply_add_fusion
  103.3 1.6 %broadcast_in_dim.95 = bf16[4,2048,128]{2,1,0:T(8,128)(2,1)} broadcast(bf16[2048,128]{1,0:T(8,128)(2,1)S(1)} %pad_maximum_fusion), dimensions={1,2} | broadcast | bytes 2621440 | tf_op jit(solution)/shard_map/broadcast_in_dim | solution.py:93
  104.9 6.8 %all-to-all-start.3 = ((bf16[4,2048,128]{2,1,0:T(8,128)(2,1)}), bf16[4,2048,128]{2,1,0:T(8,128)(2,1)}, u32[]{:S(2)}, u32[]{:S(2)}) async-start(bf16[4,2048,128]{2,1,0:T(8,128)(2,1)} %broadcast_in_dim.95), calls=%async_computation.3 | async-start | bytes 4194304 | tf_op jit(solution)/shard_map/all_to_all | solution.py:97
  111.9 4.6 %collective-permute-start.5 = (bf16[1,32,2560]{2,1,0:T(8,128)(2,1)S(1)}, bf16[1,32,2560]{2,1,0:T(8,128)(2,1)S(1)}, u32[]{:S(2)}, u32[]{:S(2)}) collective-permute-start(bf16[1,32,2560]{2,1,0:T(8,128)(2,1)S(1)} %constant_dynamic-slice_fusion), channel_id=1, source_target_pairs={{0,4},{1,5},{2,6},{3,7},{4,0},{5,1},{6,2},{7,3},{8,12},{9,13},{10,... | collective-permute-start | bytes 491528 | tf_op jit(solution)/shard_map/ppermute | solution.py:231
  117.1 3.5 %collective-permute-done.5 = bf16[1,32,2560]{2,1,0:T(8,128)(2,1)S(1)} collective-permute-done((bf16[1,32,2560]{2,1,0:T(8,128)(2,1)S(1)}, bf16[1,32,2560]{2,1,0:T(8,128)(2,1)S(1)}, u32[]{:S(2)}, u32[]{:S(2)}) %collective-permute-start.5) | collective-permute-done | bytes 163872 | tf_op jit(solution)/shard_map/ppermute | solution.py:231
  120.6 0.7 fusion.41
  122.2 13.7 %all-to-all-done.3 = bf16[4,2048,128]{2,1,0:T(8,128)(2,1)} async-done(((bf16[4,2048,128]{2,1,0:T(8,128)(2,1)}), bf16[4,2048,128]{2,1,0:T(8,128)(2,1)}, u32[]{:S(2)}, u32[]{:S(2)}) %all-to-all-start.3) | async-done | bytes 2097184 | tf_op jit(solution)/shard_map/all_to_all | solution.py:97
  136.0 3.3 %shard_map.122.refs_0_ = bf16[48,8,2,16,128]{4,3,2,1,0:T(8,128)(2,1)} custom-call(s32[48]{0:T(128)} %get-tuple-element.35.where_ref, bf16[128,2,2,16,128]{4,3,2,1,0:T(8,128)(2,1)} %bitcast.42.source_ref), custom_call_target="tpu_custom_call" | custom-call | tf_op jit(solution)/shard_map/pallas_call | solution.py:175
  139.3 2.2 %all-gather.2.cloned.1.call-done = bf16[24576,128]{1,0:T(8,128)(2,1)} async-done(((bf16[1536,128]{1,0:T(8,128)(2,1)}), bf16[24576,128]{1,0:T(8,128)(2,1)}) %all-gather.2.cloned.1.call-update) | async-done | bytes 6291472 | tf_op jit(solution)/shard_map/all_gather | solution.py:210
  141.5 3.8 %shard_map.123 = bf16[48,8,2,16,128]{4,3,2,1,0:T(8,128)(2,1)} custom-call(s32[48]{0:T(128)} %multiply_add_fusion.1.where_ref, bf16[128,6,2,16,128]{4,3,2,1,0:T(8,128)(2,1)} %bitcast.148, bf16[48,8,2,16,128]{4,3,2,1,0:T(8,128)(2,1)} %shard_map.122.refs_0_), custom_call_target="tpu_custom_call", output_to_operand_aliasing={{}: (2, {})} | custom-call | tf_op jit(solution)/shard_map/pallas_call | solution.py:175
  (56 shorter events, 4.4 us)
Async XLA Ops:
  7.2 54.0 %copy-start = (bf16[384,2560]{1,0:T(8,128)(2,1)S(1)}, bf16[384,2560]{1,0:T(8,128)(2,1)}, u32[]{:S(2)}) copy-start(bf16[384,2560]{1,0:T(8,128)(2,1)} %param.15) | copy-start | bytes 5898244
  8.6 31.1 %all-to-all-start = ((s32[64,1,128]{2,1,0:T(1,128)}), s32[64,1,128]{2,1,0:T(1,128)}, u32[]{:S(2)}, u32[]{:S(2)}) async-start(s32[64,1,128]{2,1,0:T(1,128)} %broadcast_in_dim.84), calls=%async_computation | async-start | bytes 65536 | tf_op jit(solution)/shard_map/all_to_all | solution.py:73
  27.3 114.2 %all-gather.2.cloned.1.call-start = ((), (), s32[]{:S(2)}) async-start(), calls=%async_computation.4 | async-start | bytes 6684672 | tf_op jit(solution)/shard_map/all_gather | solution.py:210
  32.1 22.9 %copy-start.8 = (bf16[2560]{0:T(1024)(128)(2,1)S(1)}, bf16[2560]{0:T(1024)(128)(2,1)}, u32[]{:S(2)}) copy-start(bf16[2560]{0:T(1024)(128)(2,1)} %param.17) | copy-start | bytes 15364
  32.1 22.9 %copy-start.9 = (bf16[2560]{0:T(1024)(128)(2,1)S(1)}, bf16[2560]{0:T(1024)(128)(2,1)}, u32[]{:S(2)}) copy-start(bf16[2560]{0:T(1024)(128)(2,1)} %param.18) | copy-start | bytes 15364
  32.1 23.0 %copy-start.10 = (s32[16]{0:T(128)S(1)}, s32[16]{0:T(128)}, u32[]{:S(2)}) copy-start(s32[16]{0:T(128)} %param.14) | copy-start | bytes 196
  39.7 18.7 %copy-start.4 = (bf16[16,16,3,128]{3,1,2,0:T(8,128)(2,1)S(1)}, bf16[16,16,3,128]{3,1,2,0:T(8,128)(2,1)}, u32[]{:S(2)}) copy-start(bf16[16,16,3,128]{3,1,2,0:T(8,128)(2,1)} %param.10) | copy-start | bytes 589828
  39.7 18.8 %copy-start.7 = (bf16[16,2,16,1,128]{4,2,3,1,0:T(8,128)(2,1)S(1)}, bf16[16,2,16,1,128]{4,2,3,1,0:T(8,128)(2,1)}, u32[]{:S(2)}) copy-start(bf16[16,2,16,1,128]{4,2,3,1,0:T(8,128)(2,1)} %param.11) | copy-start | bytes 393220
  42.7 16.3 %copy-start.1 = (bf16[16,12,1,16,1,128]{5,3,2,1,0,4:T(8,128)(2,1)S(1)}, bf16[16,12,1,16,1,128]{5,3,2,1,0,4:T(8,128)(2,1)}, u32[]{:S(2)}) copy-start(bf16[16,12,1,16,1,128]{5,3,2,1,0,4:T(8,128)(2,1)} %get-tuple-element.40) | copy-start | bytes 2359300
  55.1 17.2 %all-to-all-start.1 = ((bf16[4,128,128]{2,1,0:T(8,128)(2,1)}), bf16[4,128,128]{2,1,0:T(8,128)(2,1)S(1)}, u32[]{:S(2)}, u32[]{:S(2)}) async-start(bf16[4,128,128]{2,1,0:T(8,128)(2,1)} %bitcast.166), calls=%async_computation.1 | async-start | bytes 262144 | tf_op jit(solution)/shard_map/all_to_all | solution.py:97
  59.0 1.3 copy-start.5
  61.1 13.2 %copy-start.11 = (s32[48]{0:T(128)S(1)}, s32[48]{0:T(128)}, u32[]{:S(2)}) copy-start(s32[48]{0:T(128)} %param.19) | copy-start | bytes 580
  72.4 25.4 %collective-permute-start.3 = (bf16[4,32,2560]{2,1,0:T(8,128)(2,1)S(1)}, bf16[4,32,2560]{2,1,0:T(8,128)(2,1)S(1)}, u32[]{:S(2)}, u32[]{:S(2)}) collective-permute-start(bf16[4,32,2560]{2,1,0:T(8,128)(2,1)S(1)} %dynamic-slice_bitcast_fusion), channel_id=1, source_target_pairs={{0,1},{1,0},{2,3},{3,2},{4,5},{5,4},{6,7},{7,6},{8,9},{9,8},{10,11... | collective-permute-start | bytes 1966088 | tf_op jit(solution)/shard_map/ppermute | solution.py:231
  74.4 11.1 %collective-permute-start.2 = (bf16[512,128]{1,0:T(8,128)(2,1)S(1)}, bf16[512,128]{1,0:T(8,128)(2,1)S(1)}, u32[]{:S(2)}, u32[]{:S(2)}) collective-permute-start(bf16[512,128]{1,0:T(8,128)(2,1)S(1)} %bitcast.160), channel_id=1, source_target_pairs={{0,480},{8,488},{16,496},{24,504},{32,0},{40,8},{48,16},{56,24},{6... | collective-permute-start | bytes 393224 | tf_op jit(solution)/shard_map/ppermute | solution.py:221
  76.3 15.2 %collective-permute-start.1 = (bf16[512,128]{1,0:T(8,128)(2,1)S(1)}, bf16[512,128]{1,0:T(8,128)(2,1)S(1)}, u32[]{:S(2)}, u32[]{:S(2)}) collective-permute-start(bf16[512,128]{1,0:T(8,128)(2,1)S(1)} %bitcast.161), channel_id=1, source_target_pairs={{0,64},{8,72},{16,80},{24,88},{32,96},{40,104},{48,112},{56,120},{... | collective-permute-start | bytes 393224 | tf_op jit(solution)/shard_map/ppermute | solution.py:221
  80.7 17.1 %collective-permute-start = (bf16[512,128]{1,0:T(8,128)(2,1)S(1)}, bf16[512,128]{1,0:T(8,128)(2,1)S(1)}, u32[]{:S(2)}, u32[]{:S(2)}) collective-permute-start(bf16[512,128]{1,0:T(8,128)(2,1)S(1)} %bitcast.162), channel_id=1, source_target_pairs={{0,32},{8,40},{16,48},{24,56},{32,64},{40,72},{48,80},{56,88},{64,... | collective-permute-start | bytes 393224 | tf_op jit(solution)/shard_map/ppermute | solution.py:221
  98.0 0.9 copy-start.2
  98.9 12.9 %collective-permute-start.4 = (bf16[2,32,2560]{2,1,0:T(8,128)(2,1)S(1)}, bf16[2,32,2560]{2,1,0:T(8,128)(2,1)S(1)}, u32[]{:S(2)}, u32[]{:S(2)}) collective-permute-start(bf16[2,32,2560]{2,1,0:T(8,128)(2,1)S(1)} %dynamic-slice_bitcast_fusion.1), channel_id=1, source_target_pairs={{0,2},{1,3},{2,0},{3,1},{4,6},{5,7},{6,4},{7,5},{8,10},{9,11},{10,... | collective-permute-start | bytes 983048 | tf_op jit(solution)/shard_map/ppermute | solution.py:231
  104.9 6.8 %copy-start.3 = (bf16[4,32,2560]{2,1,0:T(8,128)(2,1)S(1)}, bf16[4,32,2560]{2,1,0:T(8,128)(2,1)}, u32[]{:S(2)}) copy-start(bf16[4,32,2560]{2,1,0:T(8,128)(2,1)} %copy-done.2) | copy-start | bytes 1966084
  104.9 15.7 %copy-start.6 = (bf16[32,2560]{1,0:T(8,128)(2,1)S(1)}, bf16[32,2560]{1,0:T(8,128)(2,1)}, u32[]{:S(2)}) copy-start(bf16[32,2560]{1,0:T(8,128)(2,1)} %param.16) | copy-start | bytes 491524
  104.9 31.0 %all-to-all-start.3 = ((bf16[4,2048,128]{2,1,0:T(8,128)(2,1)}), bf16[4,2048,128]{2,1,0:T(8,128)(2,1)}, u32[]{:S(2)}, u32[]{:S(2)}) async-start(bf16[4,2048,128]{2,1,0:T(8,128)(2,1)} %broadcast_in_dim.95), calls=%async_computation.3 | async-start | bytes 4194304 | tf_op jit(solution)/shard_map/all_to_all | solution.py:97
  111.9 8.7 %collective-permute-start.5 = (bf16[1,32,2560]{2,1,0:T(8,128)(2,1)S(1)}, bf16[1,32,2560]{2,1,0:T(8,128)(2,1)S(1)}, u32[]{:S(2)}, u32[]{:S(2)}) collective-permute-start(bf16[1,32,2560]{2,1,0:T(8,128)(2,1)S(1)} %constant_dynamic-slice_fusion), channel_id=1, source_target_pairs={{0,4},{1,5},{2,6},{3,7},{4,0},{5,1},{6,2},{7,3},{8,12},{9,13},{10,... | collective-permute-start | bytes 491528 | tf_op jit(solution)/shard_map/ppermute | solution.py:231
Sparse Core Ops, SparseCore 0:
  55.0 86.4 all-gather.1

commit v10 on v9

--- a/solution.py
+++ b/solution.py
@@ -15,7 +15,6 @@
 NZ, NY = 16, 4
 NEAR = 4
 FRONT = 6
-LANES = 128
 
 
 neg_fill = -1e30
@@ -67,9 +66,7 @@
 
 def parent_listing(fork_parent):
     groups = lax.axis_size("dp")
-    slots = fork_parent.shape[0]
-    row = jnp.pad(fork_parent, (0, LANES - slots), constant_values=-1)
-    copies = jnp.broadcast_to(row[None, None, :], (groups, 1, LANES))
+    copies = jnp.broadcast_to(fork_parent[None, None, :], (groups, 1, fork_parent.shape[0]))
     return lax.all_to_all(copies, "dp", split_axis=0, concat_axis=0, tiled=True)[:, 0]
 
 
@@ -155,17 +152,12 @@
             held.at[slot], out_ref.at[slot, pl.ds(first_page, pages)], sems.at[slot]
         )
 
-    @pl.loop(0, slots)
-    def _(slot):
+    for slot in range(slots):
         load(slot).start()
-
-    @pl.loop(0, slots)
-    def _(slot):
+    for slot in range(slots):
         load(slot).wait()
         store(slot).start()
-
-    @pl.loop(0, slots)
-    def _(slot):
+    for slot in range(slots):
         store(slot).wait()
 
 

time: 155 us -> 155 us (level)
  local copies, waits for them, and re-layouts: 8.18 us -> 9.84 us
    all_gather x1, waiting for transfers between devices: 2.2 us -> 0.02 us  [gather_fronts(): lax.all_gather(plane, 'dp', axis=0, tiled=True, axis_index_groups=groups_...]
  transfers between devices with their start and end apart: 10 -> 10, of which waited for: 7 -> 7; matrix products, arithmetic and copies ran while one was open for 9% -> 10% of each run, Pallas kernels for 2% -> 2%
where the time goes in v10:
time: 155 us; the launch traced here: 153 us
  waiting for transfers between devices  48.9 us (32%)
  starting transfers between devices  48.7 us (31%)
  between operations  14.5 us (9%)
  blocking collectives  12.1 us (8%)
  Pallas kernels  9.93 us (6%)
  local copies, waits for them, and re-layouts  9.84 us (6%)
  other arithmetic  5.77 us (4%)
  matrix products  2.73 us (2%)
    all_to_all x2, waiting for transfers between devices, exchange(): lax.all_to_all(copies, 'dp', split_axis=0, concat_axis=0, tiled=True, axi...  24.2 us
    all_to_all x1, starting transfers between devices, parent_listing(): lax.all_to_all(copies, 'dp', split_axis=0, concat_axis=0, tiled=True)[:, 0]  18.7 us
    ppermute x3, waiting for transfers between devices, gather_backs_near(): lax.ppermute(far, 'dp', shift_z(step))  13.2 us
    all_to_all x1, blocking collectives, exchange(): lax.all_to_all(copies, 'dp', split_axis=0, concat_axis=0, tiled=True, axi...  12.1 us
    ppermute x3, starting transfers between devices, gather_backs_near(): lax.ppermute(far, 'dp', shift_z(step))  10.2 us
    ppermute x3, starting transfers between devices, halve(): came = lax.ppermute(send, 'tensor', [(i, i ^ apart) for i in range(shards)])  9.98 us
    all_to_all x2, starting transfers between devices, exchange(): lax.all_to_all(copies, 'dp', split_axis=0, concat_axis=0, tiled=True, axi...  9.76 us
    all_to_all x1, waiting for transfers between devices, parent_listing(): lax.all_to_all(copies, 'dp', split_axis=0, concat_axis=0, tiled=True)[:, 0]  7.64 us
  transfers between devices with their start and end apart: 10, of which 7 were waited for; matrix products, arithmetic and copies ran while one was open for 10% of the time, Pallas kernels for 2%

profile of v10, /device:TPU:24, one launch (start us, length us, event | category | flops | bytes accessed | tf_op | source)
XLA Modules:
  0.0 152.5 jit_solution(6733231693462436101)
XLA Ops:
  7.2 1.4 broadcast_in_dim.84
  8.6 18.7 %all-to-all-start = ((s32[64,1,48]{2,1,0:T(1,128)}), s32[64,1,48]{2,1,0:T(1,128)}, u32[]{:S(2)}, u32[]{:S(2)}) async-start(s32[64,1,48]{2,1,0:T(1,128)} %broadcast_in_dim.84), calls=%async_computation | async-start | bytes 65536 | tf_op jit(solution)/shard_map/all_to_all | solution.py:70
  27.4 0.7 compare_select_fusion
  28.2 2.3 %gather_fusion = bf16[192,2,16,128]{3,2,1,0:T(8,128)(2,1)S(1)} fusion(bf16[192,2,16,128]{3,2,1,0:T(8,128)(2,1)} %bitcast.123, s32[1024]{0:T(1024)S(1)} %pad_clamp_fusion), kind=kCustom, calls=%fused_computation | custom fusion | bytes 3146496 | tf_op jit(solution)/shard_map/gather | solution.py:23
  30.5 1.6 %fusion.41 = (bf16[16,12,1,16,1,128]{5,3,2,1,0,4:T(8,128)(2,1)}, bf16[16,12,1,16,1,128]{5,3,2,1,0,4:T(8,128)(2,1)}) fusion(bf16[16,12,2,16,1,128]{5,3,2,1,0,4:T(8,128)(2,1)S(1)} %bitcast.125), kind=kLoop, calls=%fused_computation.92 | loop fusion | bytes 3145728 | tf_op jit(solution)/shard_map/slice | solution.py:26
  32.1 7.6 %all-to-all-done = s32[64,1,48]{2,1,0:T(1,128)} async-done(((s32[64,1,48]{2,1,0:T(1,128)}), s32[64,1,48]{2,1,0:T(1,128)}, u32[]{:S(2)}, u32[]{:S(2)}) %all-to-all-start) | async-done | bytes 12320 | tf_op jit(solution)/shard_map/all_to_all | solution.py:70
  39.7 3.0 %shard_map.121 = (bf16[4,2,6,2,16,128]{5,4,3,2,1,0:T(8,128)(2,1)}, bf16[4,2,2,2,16,128]{5,4,3,2,1,0:T(8,128)(2,1)}) custom-call(s32[1]{0:T(128)} %bitcast.me_ref, s32[64,48]{1,0:T(8,128)} %bitcast.1.listing_ref, s32[16,12]{1,0:T(8,128)} %table_ref.1, bf16[192,2,16,128]{3,2,1,0:T(8,128)(2,1)} %bitcast.124), custom_call_target="tpu_custom_call" | custom-call | tf_op jit(solution)/shard_map/pallas_call | solution.py:124
  42.7 12.1 %all_to_all.20 = bf16[4,384,128]{2,1,0:T(8,128)(2,1)} all-to-all(bf16[4,384,128]{2,1,0:T(8,128)(2,1)} %bitcast.138), channel_id=1, replica_groups={{0,8,16,24},{32,40,48,56},{64,72,80,88},{96,104,112,120},{128,136,144,1..., dimensions={0} | all-to-all | bytes 786432 | tf_op jit(solution)/shard_map/all_to_all | solution.py:94
  55.1 3.3 %all-to-all-start.1 = ((bf16[4,128,128]{2,1,0:T(8,128)(2,1)}), bf16[4,128,128]{2,1,0:T(8,128)(2,1)S(1)}, u32[]{:S(2)}, u32[]{:S(2)}) async-start(bf16[4,128,128]{2,1,0:T(8,128)(2,1)} %bitcast.140), calls=%async_computation.1 | async-start | bytes 262144 | tf_op jit(solution)/shard_map/all_to_all | solution.py:94
  59.0 0.7 fusion.42
  61.1 0.8 convolution_convert_fusion
  62.0 10.4 %all-to-all-done.1 = bf16[4,128,128]{2,1,0:T(8,128)(2,1)S(1)} async-done(((bf16[4,128,128]{2,1,0:T(8,128)(2,1)}), bf16[4,128,128]{2,1,0:T(8,128)(2,1)S(1)}, u32[]{:S(2)}, u32[]{:S(2)}) %all-to-all-start.1) | async-done | bytes 131104 | tf_op jit(solution)/shard_map/all_to_all | solution.py:94
  72.3 0.9 dynamic-slice_bitcast_fusion
  73.2 1.9 %collective-permute-start.3 = (bf16[4,32,2560]{2,1,0:T(8,128)(2,1)}, bf16[4,32,2560]{2,1,0:T(8,128)(2,1)}, u32[]{:S(2)}, u32[]{:S(2)}) collective-permute-start(bf16[4,32,2560]{2,1,0:T(8,128)(2,1)} %dynamic-slice_bitcast_fusion), channel_id=1, source_target_pairs={{0,1},{1,0},{2,3},{3,2},{4,5},{5,4},{6,7},{7,6},{8,9},{9,8},{10,11... | collective-permute-start | bytes 1966088 | tf_op jit(solution)/shard_map/ppermute | solution.py:223
  75.2 0.8 reshape.266
  76.0 1.9 %collective-permute-start.2 = (bf16[512,128]{1,0:T(8,128)(2,1)S(1)}, bf16[512,128]{1,0:T(8,128)(2,1)S(1)}, u32[]{:S(2)}, u32[]{:S(2)}) collective-permute-start(bf16[512,128]{1,0:T(8,128)(2,1)S(1)} %bitcast.134), channel_id=1, source_target_pairs={{0,480},{8,488},{16,496},{24,504},{32,0},{40,8},{48,16},{56,24},{6... | collective-permute-start | bytes 393224 | tf_op jit(solution)/shard_map/ppermute | solution.py:213
  77.9 4.4 %collective-permute-start.1 = (bf16[512,128]{1,0:T(8,128)(2,1)S(1)}, bf16[512,128]{1,0:T(8,128)(2,1)S(1)}, u32[]{:S(2)}, u32[]{:S(2)}) collective-permute-start(bf16[512,128]{1,0:T(8,128)(2,1)S(1)} %bitcast.135), channel_id=1, source_target_pairs={{0,64},{8,72},{16,80},{24,88},{32,96},{40,104},{48,112},{56,120},{... | collective-permute-start | bytes 393224 | tf_op jit(solution)/shard_map/ppermute | solution.py:213
  82.3 3.9 %collective-permute-start = (bf16[512,128]{1,0:T(8,128)(2,1)S(1)}, bf16[512,128]{1,0:T(8,128)(2,1)S(1)}, u32[]{:S(2)}, u32[]{:S(2)}) collective-permute-start(bf16[512,128]{1,0:T(8,128)(2,1)S(1)} %bitcast.136), channel_id=1, source_target_pairs={{0,32},{8,40},{16,48},{24,56},{32,64},{40,72},{48,80},{56,88},{64,... | collective-permute-start | bytes 393224 | tf_op jit(solution)/shard_map/ppermute | solution.py:213
  86.9 6.3 %collective-permute-done.1 = bf16[512,128]{1,0:T(8,128)(2,1)S(1)} collective-permute-done((bf16[512,128]{1,0:T(8,128)(2,1)S(1)}, bf16[512,128]{1,0:T(8,128)(2,1)S(1)}, u32[]{:S(2)}, u32[]{:S(2)}) %collective-permute-start.1) | collective-permute-done | bytes 131104 | tf_op jit(solution)/shard_map/ppermute | solution.py:213
  93.1 6.4 %collective-permute-done = bf16[512,128]{1,0:T(8,128)(2,1)S(1)} collective-permute-done((bf16[512,128]{1,0:T(8,128)(2,1)S(1)}, bf16[512,128]{1,0:T(8,128)(2,1)S(1)}, u32[]{:S(2)}, u32[]{:S(2)}) %collective-permute-start) | collective-permute-done | bytes 131104 | tf_op jit(solution)/shard_map/ppermute | solution.py:213
  99.6 1.2 fusion
  100.8 0.9 copy-done.2
  101.7 3.4 %collective-permute-start.4 = (bf16[2,32,2560]{2,1,0:T(8,128)(2,1)S(1)}, bf16[2,32,2560]{2,1,0:T(8,128)(2,1)S(1)}, u32[]{:S(2)}, u32[]{:S(2)}) collective-permute-start(bf16[2,32,2560]{2,1,0:T(8,128)(2,1)S(1)} %dynamic-slice_bitcast_fusion.1), channel_id=1, source_target_pairs={{0,2},{1,3},{2,0},{3,1},{4,6},{5,7},{6,4},{7,5},{8,10},{9,11},{10,... | collective-permute-start | bytes 983048 | tf_op jit(solution)/shard_map/ppermute | solution.py:223
  105.4 0.6 multiply_add_fusion
  106.0 1.6 %broadcast_in_dim.95 = bf16[4,2048,128]{2,1,0:T(8,128)(2,1)} broadcast(bf16[2048,128]{1,0:T(8,128)(2,1)S(1)} %pad_maximum_fusion), dimensions={1,2} | broadcast | bytes 2621440 | tf_op jit(solution)/shard_map/broadcast_in_dim | solution.py:90
  107.6 6.4 %all-to-all-start.3 = ((bf16[4,2048,128]{2,1,0:T(8,128)(2,1)}), bf16[4,2048,128]{2,1,0:T(8,128)(2,1)}, u32[]{:S(2)}, u32[]{:S(2)}) async-start(bf16[4,2048,128]{2,1,0:T(8,128)(2,1)} %broadcast_in_dim.95), calls=%async_computation.3 | async-start | bytes 4194304 | tf_op jit(solution)/shard_map/all_to_all | solution.py:94
  114.2 4.7 %collective-permute-start.5 = (bf16[1,32,2560]{2,1,0:T(8,128)(2,1)S(1)}, bf16[1,32,2560]{2,1,0:T(8,128)(2,1)S(1)}, u32[]{:S(2)}, u32[]{:S(2)}) collective-permute-start(bf16[1,32,2560]{2,1,0:T(8,128)(2,1)S(1)} %constant_dynamic-slice_fusion), channel_id=1, source_target_pairs={{0,4},{1,5},{2,6},{3,7},{4,0},{5,1},{6,2},{7,3},{8,12},{9,13},{10,... | collective-permute-start | bytes 491528 | tf_op jit(solution)/shard_map/ppermute | solution.py:223
  119.4 3.8 %collective-permute-done.5 = bf16[1,32,2560]{2,1,0:T(8,128)(2,1)S(1)} collective-permute-done((bf16[1,32,2560]{2,1,0:T(8,128)(2,1)S(1)}, bf16[1,32,2560]{2,1,0:T(8,128)(2,1)S(1)}, u32[]{:S(2)}, u32[]{:S(2)}) %collective-permute-start.5) | collective-permute-done | bytes 163872 | tf_op jit(solution)/shard_map/ppermute | solution.py:223
  123.2 0.7 fusion.40
  124.8 13.8 %all-to-all-done.3 = bf16[4,2048,128]{2,1,0:T(8,128)(2,1)} async-done(((bf16[4,2048,128]{2,1,0:T(8,128)(2,1)}), bf16[4,2048,128]{2,1,0:T(8,128)(2,1)}, u32[]{:S(2)}, u32[]{:S(2)}) %all-to-all-start.3) | async-done | bytes 2097184 | tf_op jit(solution)/shard_map/all_to_all | solution.py:94
  138.7 3.2 %shard_map.122.refs_0_ = bf16[48,8,2,16,128]{4,3,2,1,0:T(8,128)(2,1)} custom-call(s32[48]{0:T(128)} %get-tuple-element.35.where_ref, bf16[128,2,2,16,128]{4,3,2,1,0:T(8,128)(2,1)} %bitcast.41.source_ref), custom_call_target="tpu_custom_call" | custom-call | tf_op jit(solution)/shard_map/pallas_call | solution.py:167
  141.9 3.8 %shard_map.123 = bf16[48,8,2,16,128]{4,3,2,1,0:T(8,128)(2,1)} custom-call(s32[48]{0:T(128)} %multiply_add_fusion.1.where_ref, bf16[128,6,2,16,128]{4,3,2,1,0:T(8,128)(2,1)} %bitcast.122, bf16[48,8,2,16,128]{4,3,2,1,0:T(8,128)(2,1)} %shard_map.122.refs_0_), custom_call_target="tpu_custom_call", output_to_operand_aliasing={{}: (2, {})} | custom-call | tf_op jit(solution)/shard_map/pallas_call | solution.py:167
  (56 shorter events, 4.7 us)
Async XLA Ops:
  7.2 53.9 %copy-start = (bf16[384,2560]{1,0:T(8,128)(2,1)S(1)}, bf16[384,2560]{1,0:T(8,128)(2,1)}, u32[]{:S(2)}) copy-start(bf16[384,2560]{1,0:T(8,128)(2,1)} %param.15) | copy-start | bytes 5898244
  8.6 31.1 %all-to-all-start = ((s32[64,1,48]{2,1,0:T(1,128)}), s32[64,1,48]{2,1,0:T(1,128)}, u32[]{:S(2)}, u32[]{:S(2)}) async-start(s32[64,1,48]{2,1,0:T(1,128)} %broadcast_in_dim.84), calls=%async_computation | async-start | bytes 65536 | tf_op jit(solution)/shard_map/all_to_all | solution.py:70
  27.3 114.6 %all-gather.2.cloned.1.call-start = ((), (), s32[]{:S(2)}) async-start(), calls=%async_computation.4 | async-start | bytes 6684672 | tf_op jit(solution)/shard_map/all_gather | solution.py:202
  32.1 22.9 %copy-start.8 = (bf16[2560]{0:T(1024)(128)(2,1)S(1)}, bf16[2560]{0:T(1024)(128)(2,1)}, u32[]{:S(2)}) copy-start(bf16[2560]{0:T(1024)(128)(2,1)} %param.17) | copy-start | bytes 15364
  32.1 22.9 %copy-start.9 = (bf16[2560]{0:T(1024)(128)(2,1)S(1)}, bf16[2560]{0:T(1024)(128)(2,1)}, u32[]{:S(2)}) copy-start(bf16[2560]{0:T(1024)(128)(2,1)} %param.18) | copy-start | bytes 15364
  32.1 23.0 %copy-start.11 = (s32[16]{0:T(128)S(1)}, s32[16]{0:T(128)}, u32[]{:S(2)}) copy-start(s32[16]{0:T(128)} %param.14) | copy-start | bytes 196
  39.7 18.7 %copy-start.4 = (bf16[16,16,3,128]{3,1,2,0:T(8,128)(2,1)S(1)}, bf16[16,16,3,128]{3,1,2,0:T(8,128)(2,1)}, u32[]{:S(2)}) copy-start(bf16[16,16,3,128]{3,1,2,0:T(8,128)(2,1)} %param.10) | copy-start | bytes 589828
  39.7 18.8 %copy-start.7 = (bf16[16,2,16,1,128]{4,2,3,1,0:T(8,128)(2,1)S(1)}, bf16[16,2,16,1,128]{4,2,3,1,0:T(8,128)(2,1)}, u32[]{:S(2)}) copy-start(bf16[16,2,16,1,128]{4,2,3,1,0:T(8,128)(2,1)} %param.11) | copy-start | bytes 393220
  42.7 16.3 %copy-start.1 = (bf16[16,12,1,16,1,128]{5,3,2,1,0,4:T(8,128)(2,1)S(1)}, bf16[16,12,1,16,1,128]{5,3,2,1,0,4:T(8,128)(2,1)}, u32[]{:S(2)}) copy-start(bf16[16,12,1,16,1,128]{5,3,2,1,0,4:T(8,128)(2,1)} %get-tuple-element.40) | copy-start | bytes 2359300
  55.1 17.2 %all-to-all-start.1 = ((bf16[4,128,128]{2,1,0:T(8,128)(2,1)}), bf16[4,128,128]{2,1,0:T(8,128)(2,1)S(1)}, u32[]{:S(2)}, u32[]{:S(2)}) async-start(bf16[4,128,128]{2,1,0:T(8,128)(2,1)} %bitcast.140), calls=%async_computation.1 | async-start | bytes 262144 | tf_op jit(solution)/shard_map/all_to_all | solution.py:94
  59.0 1.3 copy-start.5
  61.1 14.0 %copy-start.10 = (s32[48]{0:T(128)S(1)}, s32[48]{0:T(128)}, u32[]{:S(2)}) copy-start(s32[48]{0:T(128)} %param.19) | copy-start | bytes 580
  73.2 26.3 %collective-permute-start.3 = (bf16[4,32,2560]{2,1,0:T(8,128)(2,1)}, bf16[4,32,2560]{2,1,0:T(8,128)(2,1)}, u32[]{:S(2)}, u32[]{:S(2)}) collective-permute-start(bf16[4,32,2560]{2,1,0:T(8,128)(2,1)} %dynamic-slice_bitcast_fusion), channel_id=1, source_target_pairs={{0,1},{1,0},{2,3},{3,2},{4,5},{5,4},{6,7},{7,6},{8,9},{9,8},{10,11... | collective-permute-start | bytes 1966088 | tf_op jit(solution)/shard_map/ppermute | solution.py:223
  76.0 10.8 %collective-permute-start.2 = (bf16[512,128]{1,0:T(8,128)(2,1)S(1)}, bf16[512,128]{1,0:T(8,128)(2,1)S(1)}, u32[]{:S(2)}, u32[]{:S(2)}) collective-permute-start(bf16[512,128]{1,0:T(8,128)(2,1)S(1)} %bitcast.134), channel_id=1, source_target_pairs={{0,480},{8,488},{16,496},{24,504},{32,0},{40,8},{48,16},{56,24},{6... | collective-permute-start | bytes 393224 | tf_op jit(solution)/shard_map/ppermute | solution.py:213
  77.9 15.2 %collective-permute-start.1 = (bf16[512,128]{1,0:T(8,128)(2,1)S(1)}, bf16[512,128]{1,0:T(8,128)(2,1)S(1)}, u32[]{:S(2)}, u32[]{:S(2)}) collective-permute-start(bf16[512,128]{1,0:T(8,128)(2,1)S(1)} %bitcast.135), channel_id=1, source_target_pairs={{0,64},{8,72},{16,80},{24,88},{32,96},{40,104},{48,112},{56,120},{... | collective-permute-start | bytes 393224 | tf_op jit(solution)/shard_map/ppermute | solution.py:213
  82.3 17.2 %collective-permute-start = (bf16[512,128]{1,0:T(8,128)(2,1)S(1)}, bf16[512,128]{1,0:T(8,128)(2,1)S(1)}, u32[]{:S(2)}, u32[]{:S(2)}) collective-permute-start(bf16[512,128]{1,0:T(8,128)(2,1)S(1)} %bitcast.136), channel_id=1, source_target_pairs={{0,32},{8,40},{16,48},{24,56},{32,64},{40,72},{48,80},{56,88},{64,... | collective-permute-start | bytes 393224 | tf_op jit(solution)/shard_map/ppermute | solution.py:213
  100.8 0.9 copy-start.2
  101.7 12.3 %collective-permute-start.4 = (bf16[2,32,2560]{2,1,0:T(8,128)(2,1)S(1)}, bf16[2,32,2560]{2,1,0:T(8,128)(2,1)S(1)}, u32[]{:S(2)}, u32[]{:S(2)}) collective-permute-start(bf16[2,32,2560]{2,1,0:T(8,128)(2,1)S(1)} %dynamic-slice_bitcast_fusion.1), channel_id=1, source_target_pairs={{0,2},{1,3},{2,0},{3,1},{4,6},{5,7},{6,4},{7,5},{8,10},{9,11},{10,... | collective-permute-start | bytes 983048 | tf_op jit(solution)/shard_map/ppermute | solution.py:223
  107.6 6.4 %copy-start.3 = (bf16[4,32,2560]{2,1,0:T(8,128)(2,1)S(1)}, bf16[4,32,2560]{2,1,0:T(8,128)(2,1)}, u32[]{:S(2)}) copy-start(bf16[4,32,2560]{2,1,0:T(8,128)(2,1)} %copy-done.2) | copy-start | bytes 1966084
  107.6 15.6 %copy-start.6 = (bf16[32,2560]{1,0:T(8,128)(2,1)S(1)}, bf16[32,2560]{1,0:T(8,128)(2,1)}, u32[]{:S(2)}) copy-start(bf16[32,2560]{1,0:T(8,128)(2,1)} %param.16) | copy-start | bytes 491524
  107.6 31.1 %all-to-all-start.3 = ((bf16[4,2048,128]{2,1,0:T(8,128)(2,1)}), bf16[4,2048,128]{2,1,0:T(8,128)(2,1)}, u32[]{:S(2)}, u32[]{:S(2)}) async-start(bf16[4,2048,128]{2,1,0:T(8,128)(2,1)} %broadcast_in_dim.95), calls=%async_computation.3 | async-start | bytes 4194304 | tf_op jit(solution)/shard_map/all_to_all | solution.py:94
  114.2 9.0 %collective-permute-start.5 = (bf16[1,32,2560]{2,1,0:T(8,128)(2,1)S(1)}, bf16[1,32,2560]{2,1,0:T(8,128)(2,1)S(1)}, u32[]{:S(2)}, u32[]{:S(2)}) collective-permute-start(bf16[1,32,2560]{2,1,0:T(8,128)(2,1)S(1)} %constant_dynamic-slice_fusion), channel_id=1, source_target_pairs={{0,4},{1,5},{2,6},{3,7},{4,0},{5,1},{6,2},{7,3},{8,12},{9,13},{10,... | collective-permute-start | bytes 491528 | tf_op jit(solution)/shard_map/ppermute | solution.py:223
Sparse Core Ops, SparseCore 0:
  55.0 86.3 all-gather.1

commit v11 on v9

--- a/solution.py
+++ b/solution.py
@@ -204,11 +204,14 @@
     return front, back
 
 
-def gather_fronts(front):
-    width = front.shape[-1]
-    plane = exchange(front.reshape(NY, -1, width), groups_y()).reshape(-1, width)
+def gather_plane(front):
+    return exchange(front.reshape(NY, -1, front.shape[-1]), groups_y())
+
+
+def gather_fronts(plane, tile):
+    plane = plane.reshape(-1, plane.shape[-1])
     fronts = lax.all_gather(plane, "dp", axis=0, tiled=True, axis_index_groups=groups_z())
-    return fronts.reshape((-1,) + front.shape[2:])
+    return fronts.reshape((-1,) + tile)
 
 
 def gather_backs_far(back):
@@ -217,9 +220,9 @@
 
 
 def gather_backs_near(far):
-    return jnp.concatenate(
-        [far] + [lax.ppermute(far, "dp", shift_z(step)) for step in (1, 2, -1)]
-    )
+    half = far.shape[0] // 2
+    sent = ((far, 1), (far[:half], 2), (far[half:], -2), (far, -1))
+    return jnp.concatenate([far] + [lax.ppermute(x, "dp", shift_z(step)) for x, step in sent])
 
 
 def halve(held, apart):
@@ -245,20 +248,20 @@
     fork_parent,
 ):
     keys, values = cached(kv_cache, page_table)
-    listing, queries, keys, values = lax.optimization_barrier(
-        (parent_listing(fork_parent), queries, keys, values)
-    )
+    listing, keys, values = lax.optimization_barrier((parent_listing(fork_parent), keys, values))
     cache = kv_cache[:, :, :, 0]
     front, back = pick_pages(lax.axis_index("dp"), listing, page_table, cache)
-    fronts = gather_fronts(front)
+    front, back, queries = lax.optimization_barrier((front, back, queries))
     attended = attend(queries, new_kv, keys, values, lengths)
     rows_here = residual.shape[0]
     partial = jnp.dot(attended, out_proj, preferred_element_type=jnp.float32).astype(jnp.bfloat16)
-    far, partial = lax.optimization_barrier((gather_backs_far(back), partial))
-    held = halve(partial.reshape(lax.axis_size("tensor"), rows_here, -1), 1).astype(jnp.bfloat16)
-    column, held = lax.optimization_barrier((gather_backs_near(far), held))
-    backs = share(column, groups_y()).reshape((-1,) + back.shape[2:])
+    plane, partial = lax.optimization_barrier((gather_plane(front), partial))
+    fronts = gather_fronts(plane, front.shape[2:])
+    held = partial.reshape(lax.axis_size("tensor"), rows_here, -1)
+    held = halve(held, 1).astype(jnp.bfloat16)
+    far, held = lax.optimization_barrier((gather_backs_far(back), held))
     held = halve(held, 2).astype(jnp.bfloat16)
+    backs = share(gather_backs_near(far), groups_y()).reshape((-1,) + back.shape[2:])
     updated = halve(held, 4)[0] + residual.astype(jnp.float32)
     hidden_out = updated.astype(jnp.bfloat16)
     block_ends = updated.reshape(rows_here // CH, CH, updated.shape[1])[:, CH - 1]

time: 155 us -> 156 us (level)
  blocking collectives: 12.1 us -> 0 us
  starting transfers between devices: 49.1 us -> 59 us
  other arithmetic: 5.62 us -> 7.51 us
    all_to_all x1 -> x0, blocking collectives: 12.1 us -> none  [exchange(): lax.all_to_all(copies, 'dp', split_axis=0, concat_axis=0, tiled=True, axi...]
    ppermute x3 -> x4, waiting for transfers between devices: 12.3 us -> 1.21 us  [gather_backs_near(): lax.ppermute(x, 'dp', shift_z(step))]
    all_gather x1, waiting for transfers between devices: 2.2 us -> 10.6 us  [gather_fronts(): lax.all_gather(plane, 'dp', axis=0, tiled=True, axis_index_groups=groups_...]
    all_to_all x2 -> x3, starting transfers between devices: 10.1 us -> 17.4 us  [exchange(): lax.all_to_all(copies, 'dp', split_axis=0, concat_axis=0, tiled=True, axi...]
    all_to_all x2 -> x3, waiting for transfers between devices: 24.1 us -> 27.9 us  [exchange(): lax.all_to_all(copies, 'dp', split_axis=0, concat_axis=0, tiled=True, axi...]
    ppermute x3 -> x4, starting transfers between devices: 10.2 us -> 12.6 us  [gather_backs_near(): lax.ppermute(x, 'dp', shift_z(step))]
    convert_element_type x1, other arithmetic: 0.16 us -> 2.15 us  [local(): held = halve(held, 1).astype(jnp.bfloat16)]
    squeeze x3, local copies, waits for them, and re-layouts: 0.09 us -> 1.91 us  [halve(): send = lax.dynamic_index_in_dim(pairs, 1 - mine, 1, keepdims=False)]
  transfers between devices with their start and end apart: 10 -> 12, of which waited for: 7 -> 7; matrix products, arithmetic and copies ran while one was open for 9% -> 12% of each run, Pallas kernels for 2% -> 2%
where the time goes in v11:
time: 156 us; the launch traced here: 154 us
  starting transfers between devices  59 us (38%)
  waiting for transfers between devices  50.6 us (32%)
  between operations  14.6 us (9%)
  Pallas kernels  10.1 us (6%)
  local copies, waits for them, and re-layouts  9.23 us (6%)
  other arithmetic  7.51 us (5%)
  matrix products  2.74 us (2%)
    all_to_all x3, waiting for transfers between devices, exchange(): lax.all_to_all(copies, 'dp', split_axis=0, concat_axis=0, tiled=True, axi...  27.9 us
    all_to_all x1, starting transfers between devices, parent_listing(): lax.all_to_all(copies, 'dp', split_axis=0, concat_axis=0, tiled=True)[:, 0]  18.7 us
    all_to_all x3, starting transfers between devices, exchange(): lax.all_to_all(copies, 'dp', split_axis=0, concat_axis=0, tiled=True, axi...  17.4 us
    ppermute x4, starting transfers between devices, gather_backs_near(): lax.ppermute(x, 'dp', shift_z(step))  12.6 us
    all_gather x1, waiting for transfers between devices, gather_fronts(): lax.all_gather(plane, 'dp', axis=0, tiled=True, axis_index_groups=groups_...  10.6 us
    ppermute x3, starting transfers between devices, halve(): came = lax.ppermute(send, 'tensor', [(i, i ^ apart) for i in range(shards)])  10.3 us
    all_to_all x1, waiting for transfers between devices, parent_listing(): lax.all_to_all(copies, 'dp', split_axis=0, concat_axis=0, tiled=True)[:, 0]  7.59 us
    pallas_call x2, Pallas kernels, place_children(): pl.pallas_call(functools.partial(place_kernel, first_page, len(given) - 2...  7.12 us
  transfers between devices with their start and end apart: 12, of which 7 were waited for; matrix products, arithmetic and copies ran while one was open for 12% of the time, Pallas kernels for 2%

profile of v11, /device:TPU:24, one launch (start us, length us, event | category | flops | bytes accessed | tf_op | source)
XLA Modules:
  0.0 153.7 jit_solution(7638259618048828962)
XLA Ops:
  7.2 0.8 pad.4
  8.6 18.7 %all-to-all-start = ((s32[64,1,128]{2,1,0:T(1,128)}), s32[64,1,128]{2,1,0:T(1,128)}, u32[]{:S(2)}, u32[]{:S(2)}) async-start(s32[64,1,128]{2,1,0:T(1,128)} %broadcast_in_dim.84), calls=%async_computation | async-start | bytes 65536 | tf_op jit(solution)/shard_map/all_to_all | solution.py:73
  27.3 0.7 compare_select_fusion
  28.1 2.3 %gather_fusion = bf16[192,2,16,128]{3,2,1,0:T(8,128)(2,1)S(1)} fusion(bf16[192,2,16,128]{3,2,1,0:T(8,128)(2,1)} %bitcast.149, s32[1024]{0:T(1024)S(1)} %pad_clamp_fusion), kind=kCustom, calls=%fused_computation | custom fusion | bytes 3146496 | tf_op jit(solution)/shard_map/gather | solution.py:24
  30.4 1.6 %fusion.42 = (bf16[16,12,1,16,1,128]{5,3,2,1,0,4:T(8,128)(2,1)}, bf16[16,12,1,16,1,128]{5,3,2,1,0,4:T(8,128)(2,1)}) fusion(bf16[16,12,2,16,1,128]{5,3,2,1,0,4:T(8,128)(2,1)S(1)} %bitcast.151), kind=kLoop, calls=%fused_computation.98 | loop fusion | bytes 3145728 | tf_op jit(solution)/shard_map/slice | solution.py:27
  32.1 7.6 %all-to-all-done = s32[64,1,128]{2,1,0:T(1,128)} async-done(((s32[64,1,128]{2,1,0:T(1,128)}), s32[64,1,128]{2,1,0:T(1,128)}, u32[]{:S(2)}, u32[]{:S(2)}) %all-to-all-start) | async-done | bytes 32800 | tf_op jit(solution)/shard_map/all_to_all | solution.py:73
  39.7 3.0 %shard_map.121 = (bf16[4,2,6,2,16,128]{5,4,3,2,1,0:T(8,128)(2,1)}, bf16[4,2,2,2,16,128]{5,4,3,2,1,0:T(8,128)(2,1)}) custom-call(s32[1]{0:T(128)} %bitcast.me_ref, s32[64,128]{1,0:T(8,128)} %bitcast.1.listing_ref, s32[16,12]{1,0:T(8,128)} %table_ref.1, bf16[192,2,16,128]{3,2,1,0:T(8,128)(2,1)} %bitcast.150), custom_call_target="tpu_custom_call" | custom-call | tf_op jit(solution)/shard_map/pallas_call | solution.py:127
  42.7 6.6 %all-to-all-start.2 = ((bf16[4,384,128]{2,1,0:T(8,128)(2,1)}), bf16[4,384,128]{2,1,0:T(8,128)(2,1)}, u32[]{:S(2)}, u32[]{:S(2)}) async-start(bf16[4,384,128]{2,1,0:T(8,128)(2,1)} %bitcast.163), calls=%async_computation.2 | async-start | bytes 786432 | tf_op jit(solution)/shard_map/all_to_all | solution.py:97
  51.9 0.8 convolution_convert_fusion
  52.8 1.9 %all-to-all-done.2 = bf16[4,384,128]{2,1,0:T(8,128)(2,1)} async-done(((bf16[4,384,128]{2,1,0:T(8,128)(2,1)}), bf16[4,384,128]{2,1,0:T(8,128)(2,1)}, u32[]{:S(2)}, u32[]{:S(2)}) %all-to-all-start.2) | async-done | bytes 393248 | tf_op jit(solution)/shard_map/all_to_all | solution.py:97
  54.7 0.9 dynamic-slice_bitcast_fusion
  55.6 1.9 %collective-permute-start = (bf16[4,32,2560]{2,1,0:T(8,128)(2,1)}, bf16[4,32,2560]{2,1,0:T(8,128)(2,1)}, u32[]{:S(2)}, u32[]{:S(2)}) collective-permute-start(bf16[4,32,2560]{2,1,0:T(8,128)(2,1)} %dynamic-slice_bitcast_fusion), channel_id=1, source_target_pairs={{0,1},{1,0},{2,3},{3,2},{4,5},{5,4},{6,7},{7,6},{8,9},{9,8},{10,11... | collective-permute-start | bytes 1966088 | tf_op jit(solution)/shard_map/ppermute | solution.py:234
  57.7 3.3 %all-to-all-start.1 = ((bf16[4,128,128]{2,1,0:T(8,128)(2,1)}), bf16[4,128,128]{2,1,0:T(8,128)(2,1)S(1)}, u32[]{:S(2)}, u32[]{:S(2)}) async-start(bf16[4,128,128]{2,1,0:T(8,128)(2,1)} %bitcast.6), calls=%async_computation.1 | async-start | bytes 262144 | tf_op jit(solution)/shard_map/all_to_all | solution.py:97
  61.1 0.8 add_select_fusion.1
  62.9 2.2 %fusion = bf16[4,32,2560]{2,1,0:T(8,128)(2,1)} fusion(bf16[4,32,2560]{2,1,0:T(8,128)(2,1)} %collective-permute-done, bf16[4,2,32,2560]{3,2,1,0:T(8,128)(2,1)S(1)} %bitcast.153, s32[]{:T(128)S(6)} %select_n.124), kind=kLoop, calls=%fused_computation.4 | loop fusion | flops 1310720 | bytes 1966084 | tf_op jit(solution)/shard_map/convert_element_type | solution.py:261
  65.1 13.2 %all-to-all-done.1 = bf16[4,128,128]{2,1,0:T(8,128)(2,1)S(1)} async-done(((bf16[4,128,128]{2,1,0:T(8,128)(2,1)}), bf16[4,128,128]{2,1,0:T(8,128)(2,1)S(1)}, u32[]{:S(2)}, u32[]{:S(2)}) %all-to-all-start.1) | async-done | bytes 131104 | tf_op jit(solution)/shard_map/all_to_all | solution.py:97
  78.2 1.9 %collective-permute-start.6 = (bf16[512,128]{1,0:T(8,128)(2,1)S(1)}, bf16[512,128]{1,0:T(8,128)(2,1)S(1)}, u32[]{:S(2)}, u32[]{:S(2)}) collective-permute-start(bf16[512,128]{1,0:T(8,128)(2,1)S(1)} %bitcast.157), channel_id=1, source_target_pairs={{0,480},{8,488},{16,496},{24,504},{32,0},{40,8},{48,16},{56,24},{6... | collective-permute-start | bytes 393224 | tf_op jit(solution)/shard_map/ppermute | solution.py:225
  80.2 4.0 %collective-permute-start.3 = (bf16[512,128]{1,0:T(8,128)(2,1)S(1)}, bf16[512,128]{1,0:T(8,128)(2,1)S(1)}, u32[]{:S(2)}, u32[]{:S(2)}) collective-permute-start(bf16[512,128]{1,0:T(8,128)(2,1)S(1)} %bitcast.158), channel_id=1, source_target_pairs={{0,32},{8,40},{16,48},{24,56},{32,64},{40,72},{48,80},{56,88},{64,... | collective-permute-start | bytes 393224 | tf_op jit(solution)/shard_map/ppermute | solution.py:225
  84.2 2.6 %collective-permute-start.5 = (bf16[256,128]{1,0:T(8,128)(2,1)S(1)}, bf16[256,128]{1,0:T(8,128)(2,1)S(1)}, u32[]{:S(2)}, u32[]{:S(2)}) collective-permute-start(bf16[256,128]{1,0:T(8,128)(2,1)S(1)} %get-tuple-element.45), channel_id=1, source_target_pairs={{0,448},{8,456},{16,464},{24,472},{32,480},{40,488},{48,496},{56,5... | collective-permute-start | bytes 196616 | tf_op jit(solution)/shard_map/ppermute | solution.py:225
  86.7 4.2 %collective-permute-start.4 = (bf16[256,128]{1,0:T(8,128)(2,1)S(1)}, bf16[256,128]{1,0:T(8,128)(2,1)S(1)}, u32[]{:S(2)}, u32[]{:S(2)}) collective-permute-start(bf16[256,128]{1,0:T(8,128)(2,1)S(1)} %get-tuple-element.46), channel_id=1, source_target_pairs={{0,64},{8,72},{16,80},{24,88},{32,96},{40,104},{48,112},{56,120},{... | collective-permute-start | bytes 196616 | tf_op jit(solution)/shard_map/ppermute | solution.py:225
  90.9 1.0 dynamic-slice_bitcast_fusion.1
  91.9 3.4 %collective-permute-start.1 = (bf16[2,32,2560]{2,1,0:T(8,128)(2,1)S(1)}, bf16[2,32,2560]{2,1,0:T(8,128)(2,1)S(1)}, u32[]{:S(2)}, u32[]{:S(2)}) collective-permute-start(bf16[2,32,2560]{2,1,0:T(8,128)(2,1)S(1)} %dynamic-slice_bitcast_fusion.1), channel_id=1, source_target_pairs={{0,2},{1,3},{2,0},{3,1},{4,6},{5,7},{6,4},{7,5},{8,10},{9,11},{10,... | collective-permute-start | bytes 983048 | tf_op jit(solution)/shard_map/ppermute | solution.py:234
  95.5 1.2 collective-permute-done.4
  96.7 1.6 %broadcast_in_dim.95 = bf16[4,2048,128]{2,1,0:T(8,128)(2,1)} broadcast(bf16[2048,128]{1,0:T(8,128)(2,1)S(1)} %constant_dynamic-update-slice_fusion), dimensions={1,2} | broadcast | bytes 2621440 | tf_op jit(solution)/shard_map/broadcast_in_dim | solution.py:93
  98.3 7.5 %all-to-all-start.3 = ((bf16[4,2048,128]{2,1,0:T(8,128)(2,1)}), bf16[4,2048,128]{2,1,0:T(8,128)(2,1)}, u32[]{:S(2)}, u32[]{:S(2)}) async-start(bf16[4,2048,128]{2,1,0:T(8,128)(2,1)} %broadcast_in_dim.95), calls=%async_computation.3 | async-start | bytes 4194304 | tf_op jit(solution)/shard_map/all_to_all | solution.py:97
  106.0 4.9 %collective-permute-start.2 = (bf16[1,32,2560]{2,1,0:T(8,128)(2,1)S(1)}, bf16[1,32,2560]{2,1,0:T(8,128)(2,1)S(1)}, u32[]{:S(2)}, u32[]{:S(2)}) collective-permute-start(bf16[1,32,2560]{2,1,0:T(8,128)(2,1)S(1)} %constant_dynamic-slice_fusion), channel_id=1, source_target_pairs={{0,4},{1,5},{2,6},{3,7},{4,0},{5,1},{6,2},{7,3},{8,12},{9,13},{10,... | collective-permute-start | bytes 491528 | tf_op jit(solution)/shard_map/ppermute | solution.py:234
  111.4 3.3 %collective-permute-done.2 = bf16[1,32,2560]{2,1,0:T(8,128)(2,1)S(1)} collective-permute-done((bf16[1,32,2560]{2,1,0:T(8,128)(2,1)S(1)}, bf16[1,32,2560]{2,1,0:T(8,128)(2,1)S(1)}, u32[]{:S(2)}, u32[]{:S(2)}) %collective-permute-start.2) | collective-permute-done | bytes 163872 | tf_op jit(solution)/shard_map/ppermute | solution.py:234
  114.7 0.7 fusion.41
  116.3 12.9 %all-to-all-done.3 = bf16[4,2048,128]{2,1,0:T(8,128)(2,1)} async-done(((bf16[4,2048,128]{2,1,0:T(8,128)(2,1)}), bf16[4,2048,128]{2,1,0:T(8,128)(2,1)}, u32[]{:S(2)}, u32[]{:S(2)}) %all-to-all-start.3) | async-done | bytes 2097184 | tf_op jit(solution)/shard_map/all_to_all | solution.py:97
  129.2 3.3 %shard_map.122.refs_0_ = bf16[48,8,2,16,128]{4,3,2,1,0:T(8,128)(2,1)} custom-call(s32[48]{0:T(128)} %get-tuple-element.39.where_ref, bf16[128,2,2,16,128]{4,3,2,1,0:T(8,128)(2,1)} %bitcast.42.source_ref), custom_call_target="tpu_custom_call" | custom-call | tf_op jit(solution)/shard_map/pallas_call | solution.py:175
  132.5 10.6 %all-gather.2.cloned.1.call-done = bf16[24576,128]{1,0:T(8,128)(2,1)} async-done(((bf16[1536,128]{1,0:T(8,128)(2,1)}), bf16[24576,128]{1,0:T(8,128)(2,1)}) %all-gather.2.cloned.1.call-update) | async-done | bytes 6291472 | tf_op jit(solution)/shard_map/all_gather | solution.py:213
  143.1 3.8 %shard_map.123 = bf16[48,8,2,16,128]{4,3,2,1,0:T(8,128)(2,1)} custom-call(s32[48]{0:T(128)} %multiply_add_fusion.1.where_ref, bf16[128,6,2,16,128]{4,3,2,1,0:T(8,128)(2,1)} %bitcast.148, bf16[48,8,2,16,128]{4,3,2,1,0:T(8,128)(2,1)} %shard_map.122.refs_0_), custom_call_target="tpu_custom_call", output_to_operand_aliasing={{}: (2, {})} | custom-call | tf_op jit(solution)/shard_map/pallas_call | solution.py:175
  (62 shorter events, 6.1 us)
Async XLA Ops:
  7.2 44.7 %copy-start = (bf16[384,2560]{1,0:T(8,128)(2,1)S(1)}, bf16[384,2560]{1,0:T(8,128)(2,1)}, u32[]{:S(2)}) copy-start(bf16[384,2560]{1,0:T(8,128)(2,1)} %param.15) | copy-start | bytes 5898244
  8.6 31.1 %all-to-all-start = ((s32[64,1,128]{2,1,0:T(1,128)}), s32[64,1,128]{2,1,0:T(1,128)}, u32[]{:S(2)}, u32[]{:S(2)}) async-start(s32[64,1,128]{2,1,0:T(1,128)} %broadcast_in_dim.84), calls=%async_computation | async-start | bytes 65536 | tf_op jit(solution)/shard_map/all_to_all | solution.py:73
  30.4 1.6 %copy-start.9 = (s32[16]{0:T(128)S(1)}, s32[16]{0:T(128)}, u32[]{:S(2)}) copy-start(s32[16]{0:T(128)} %param.14) | copy-start | bytes 196
  32.1 17.2 %copy-start.1 = (bf16[16,12,1,16,1,128]{5,3,2,1,0,4:T(8,128)(2,1)S(1)}, bf16[16,12,1,16,1,128]{5,3,2,1,0,4:T(8,128)(2,1)}, u32[]{:S(2)}) copy-start(bf16[16,12,1,16,1,128]{5,3,2,1,0,4:T(8,128)(2,1)} %get-tuple-element.44) | copy-start | bytes 2359300
  32.1 17.2 %copy-start.3 = (bf16[16,16,3,128]{3,1,2,0:T(8,128)(2,1)S(1)}, bf16[16,16,3,128]{3,1,2,0:T(8,128)(2,1)}, u32[]{:S(2)}) copy-start(bf16[16,16,3,128]{3,1,2,0:T(8,128)(2,1)} %param.10) | copy-start | bytes 589828
  42.7 7.3 %copy-start.6 = (bf16[16,2,16,1,128]{4,2,3,1,0:T(8,128)(2,1)S(1)}, bf16[16,2,16,1,128]{4,2,3,1,0:T(8,128)(2,1)}, u32[]{:S(2)}) copy-start(bf16[16,2,16,1,128]{4,2,3,1,0:T(8,128)(2,1)} %param.11) | copy-start | bytes 393220
  42.7 12.0 %all-to-all-start.2 = ((bf16[4,384,128]{2,1,0:T(8,128)(2,1)}), bf16[4,384,128]{2,1,0:T(8,128)(2,1)}, u32[]{:S(2)}, u32[]{:S(2)}) async-start(bf16[4,384,128]{2,1,0:T(8,128)(2,1)} %bitcast.163), calls=%async_computation.2 | async-start | bytes 786432 | tf_op jit(solution)/shard_map/all_to_all | solution.py:97
  49.3 93.8 %all-gather.2.cloned.1.call-start = ((), (), s32[]{:S(2)}) async-start(), calls=%async_computation.4 | async-start | bytes 6684672 | tf_op jit(solution)/shard_map/all_gather | solution.py:213
  49.3 1.8 %copy-start.4 = (bf16[16,12,1,16,1,128]{5,3,2,1,0,4:T(8,128)(2,1)S(1)}, bf16[16,12,1,16,1,128]{5,3,2,1,0,4:T(8,128)(2,1)}, u32[]{:S(2)}) copy-start(bf16[16,12,1,16,1,128]{5,3,2,1,0,4:T(8,128)(2,1)} %get-tuple-element.43) | copy-start | bytes 2359300
  52.8 4.8 %copy-start.10 = (s32[48]{0:T(128)S(1)}, s32[48]{0:T(128)}, u32[]{:S(2)}) copy-start(s32[48]{0:T(128)} %param.19) | copy-start | bytes 580
  52.8 4.9 %copy-start.7 = (bf16[2560]{0:T(1024)(128)(2,1)S(1)}, bf16[2560]{0:T(1024)(128)(2,1)}, u32[]{:S(2)}) copy-start(bf16[2560]{0:T(1024)(128)(2,1)} %param.17) | copy-start | bytes 15364
  52.8 4.9 %copy-start.8 = (bf16[2560]{0:T(1024)(128)(2,1)S(1)}, bf16[2560]{0:T(1024)(128)(2,1)}, u32[]{:S(2)}) copy-start(bf16[2560]{0:T(1024)(128)(2,1)} %param.18) | copy-start | bytes 15364
  55.6 7.3 %collective-permute-start = (bf16[4,32,2560]{2,1,0:T(8,128)(2,1)}, bf16[4,32,2560]{2,1,0:T(8,128)(2,1)}, u32[]{:S(2)}, u32[]{:S(2)}) collective-permute-start(bf16[4,32,2560]{2,1,0:T(8,128)(2,1)} %dynamic-slice_bitcast_fusion), channel_id=1, source_target_pairs={{0,1},{1,0},{2,3},{3,2},{4,5},{5,4},{6,7},{7,6},{8,9},{9,8},{10,11... | collective-permute-start | bytes 1966088 | tf_op jit(solution)/shard_map/ppermute | solution.py:234
  57.7 20.5 %all-to-all-start.1 = ((bf16[4,128,128]{2,1,0:T(8,128)(2,1)}), bf16[4,128,128]{2,1,0:T(8,128)(2,1)S(1)}, u32[]{:S(2)}, u32[]{:S(2)}) async-start(bf16[4,128,128]{2,1,0:T(8,128)(2,1)} %bitcast.6), calls=%async_computation.1 | async-start | bytes 262144 | tf_op jit(solution)/shard_map/all_to_all | solution.py:97
  78.2 18.5 %collective-permute-start.6 = (bf16[512,128]{1,0:T(8,128)(2,1)S(1)}, bf16[512,128]{1,0:T(8,128)(2,1)S(1)}, u32[]{:S(2)}, u32[]{:S(2)}) collective-permute-start(bf16[512,128]{1,0:T(8,128)(2,1)S(1)} %bitcast.157), channel_id=1, source_target_pairs={{0,480},{8,488},{16,496},{24,504},{32,0},{40,8},{48,16},{56,24},{6... | collective-permute-start | bytes 393224 | tf_op jit(solution)/shard_map/ppermute | solution.py:225
  80.2 15.3 %collective-permute-start.3 = (bf16[512,128]{1,0:T(8,128)(2,1)S(1)}, bf16[512,128]{1,0:T(8,128)(2,1)S(1)}, u32[]{:S(2)}, u32[]{:S(2)}) collective-permute-start(bf16[512,128]{1,0:T(8,128)(2,1)S(1)} %bitcast.158), channel_id=1, source_target_pairs={{0,32},{8,40},{16,48},{24,56},{32,64},{40,72},{48,80},{56,88},{64,... | collective-permute-start | bytes 393224 | tf_op jit(solution)/shard_map/ppermute | solution.py:225
  84.2 12.5 %collective-permute-start.5 = (bf16[256,128]{1,0:T(8,128)(2,1)S(1)}, bf16[256,128]{1,0:T(8,128)(2,1)S(1)}, u32[]{:S(2)}, u32[]{:S(2)}) collective-permute-start(bf16[256,128]{1,0:T(8,128)(2,1)S(1)} %get-tuple-element.45), channel_id=1, source_target_pairs={{0,448},{8,456},{16,464},{24,472},{32,480},{40,488},{48,496},{56,5... | collective-permute-start | bytes 196616 | tf_op jit(solution)/shard_map/ppermute | solution.py:225
  86.7 9.9 %collective-permute-start.4 = (bf16[256,128]{1,0:T(8,128)(2,1)S(1)}, bf16[256,128]{1,0:T(8,128)(2,1)S(1)}, u32[]{:S(2)}, u32[]{:S(2)}) collective-permute-start(bf16[256,128]{1,0:T(8,128)(2,1)S(1)} %get-tuple-element.46), channel_id=1, source_target_pairs={{0,64},{8,72},{16,80},{24,88},{32,96},{40,104},{48,112},{56,120},{... | collective-permute-start | bytes 196616 | tf_op jit(solution)/shard_map/ppermute | solution.py:225
  91.9 13.9 %collective-permute-start.1 = (bf16[2,32,2560]{2,1,0:T(8,128)(2,1)S(1)}, bf16[2,32,2560]{2,1,0:T(8,128)(2,1)S(1)}, u32[]{:S(2)}, u32[]{:S(2)}) collective-permute-start(bf16[2,32,2560]{2,1,0:T(8,128)(2,1)S(1)} %dynamic-slice_bitcast_fusion.1), channel_id=1, source_target_pairs={{0,2},{1,3},{2,0},{3,1},{4,6},{5,7},{6,4},{7,5},{8,10},{9,11},{10,... | collective-permute-start | bytes 983048 | tf_op jit(solution)/shard_map/ppermute | solution.py:234
  98.3 7.5 %copy-start.2 = (bf16[4,32,2560]{2,1,0:T(8,128)(2,1)S(1)}, bf16[4,32,2560]{2,1,0:T(8,128)(2,1)}, u32[]{:S(2)}) copy-start(bf16[4,32,2560]{2,1,0:T(8,128)(2,1)} %fusion) | copy-start | bytes 1966084
  98.3 16.3 %copy-start.5 = (bf16[32,2560]{1,0:T(8,128)(2,1)S(1)}, bf16[32,2560]{1,0:T(8,128)(2,1)}, u32[]{:S(2)}) copy-start(bf16[32,2560]{1,0:T(8,128)(2,1)} %param.16) | copy-start | bytes 491524
  98.3 30.8 %all-to-all-start.3 = ((bf16[4,2048,128]{2,1,0:T(8,128)(2,1)}), bf16[4,2048,128]{2,1,0:T(8,128)(2,1)}, u32[]{:S(2)}, u32[]{:S(2)}) async-start(bf16[4,2048,128]{2,1,0:T(8,128)(2,1)} %broadcast_in_dim.95), calls=%async_computation.3 | async-start | bytes 4194304 | tf_op jit(solution)/shard_map/all_to_all | solution.py:97
  106.0 8.7 %collective-permute-start.2 = (bf16[1,32,2560]{2,1,0:T(8,128)(2,1)S(1)}, bf16[1,32,2560]{2,1,0:T(8,128)(2,1)S(1)}, u32[]{:S(2)}, u32[]{:S(2)}) collective-permute-start(bf16[1,32,2560]{2,1,0:T(8,128)(2,1)S(1)} %constant_dynamic-slice_fusion), channel_id=1, source_target_pairs={{0,4},{1,5},{2,6},{3,7},{4,0},{5,1},{6,2},{7,3},{8,12},{9,13},{10,... | collective-permute-start | bytes 491528 | tf_op jit(solution)/shard_map/ppermute | solution.py:234
Sparse Core Ops, SparseCore 0:
  54.8 88.1 all-gather.1

commit v12 on v11

--- a/solution.py
+++ b/solution.py
@@ -14,7 +14,9 @@
 PAGES = PREFIX // PAGE
 NZ, NY = 16, 4
 NEAR = 4
-FRONT = 6
+FRONT = (6, 5)
+FRONT_AT = (0, FRONT[0])
+BACK_AT = (0, PAGES - FRONT[0])
 LANES = 128
 
 
@@ -108,10 +110,13 @@
     copies = []
     for which, row in enumerate((lowest, highest)):
         for page in range(PAGES):
-            part, at = (front_ref, page) if page < FRONT else (back_ref, page - FRONT)
+            if page < FRONT[which]:
+                target = front_ref.at[0, FRONT_AT[which] + page]
+            else:
+                target = back_ref.at[0, BACK_AT[which] + page - FRONT[which]]
             copies.append(
                 pltpu.make_async_copy(
-                    cache_ref.at[table_ref[row, page]], part.at[0, which, at], sems.at[which, page]
+                    cache_ref.at[table_ref[row, page]], target, sems.at[which, page]
                 )
             )
     for copy in copies:
@@ -127,8 +132,8 @@
     return pl.pallas_call(
         pick_kernel,
         out_shape=tuple(
-            jax.ShapeDtypeStruct((copies, 2, pages) + cache.shape[1:], cache.dtype)
-            for copies, pages in ((NY, FRONT), (NZ // NEAR, PAGES - FRONT))
+            jax.ShapeDtypeStruct((copies, pages) + cache.shape[1:], cache.dtype)
+            for copies, pages in ((NY, sum(FRONT)), (NZ // NEAR, 2 * PAGES - sum(FRONT)))
         ),
         in_specs=[
             pl.BlockSpec(memory_space=pltpu.SMEM),
@@ -141,39 +146,44 @@
     )(me_index.reshape(1), listing, page_table, cache)
 
 
-def place_kernel(first_page, aliased, where_ref, source_ref, *refs):
+def place_kernel(spans, aliased, where_ref, source_ref, *refs):
     out_ref, held, load_sems, sems = refs[aliased:]
-    slots, pages = held.shape[:2]
-
-    def load(slot):
+    slots = held.shape[0]
+
+    def load(slot, span):
+        first, pages, _ = span
+        block = source_ref.at[where_ref[slot] >> 1, pl.ds(first, pages)]
+        return pltpu.make_async_copy(block, held.at[slot, pl.ds(0, pages)], load_sems.at[slot])
+
+    def store(slot, span):
+        _, pages, target = span
         return pltpu.make_async_copy(
-            source_ref.at[where_ref[slot]], held.at[slot], load_sems.at[slot]
+            held.at[slot, pl.ds(0, pages)], out_ref.at[slot, pl.ds(target, pages)], sems.at[slot]
         )
 
-    def store(slot):
-        return pltpu.make_async_copy(
-            held.at[slot], out_ref.at[slot, pl.ds(first_page, pages)], sems.at[slot]
-        )
-
-    @pl.loop(0, slots)
-    def _(slot):
-        load(slot).start()
-
-    @pl.loop(0, slots)
-    def _(slot):
-        load(slot).wait()
-        store(slot).start()
-
-    @pl.loop(0, slots)
-    def _(slot):
-        store(slot).wait()
-
-
-def place_children(where, source, first_page, earlier=None):
+    def each_slot(step):
+        @pl.loop(0, slots)
+        def _(slot):
+            for which, span in enumerate(spans):
+
+                @pl.when((where_ref[slot] & 1) == which)
+                def _():
+                    step(slot, span)
+
+    def pass_on(slot, span):
+        load(slot, span).wait()
+        store(slot, span).start()
+
+    each_slot(lambda slot, span: load(slot, span).start())
+    each_slot(pass_on)
+    each_slot(lambda slot, span: store(slot, span).wait())
+
+
+def place_children(where, source, spans, earlier=None):
     slots = where.shape[0]
     given = [where, source] + ([] if earlier is None else [earlier])
     return pl.pallas_call(
-        functools.partial(place_kernel, first_page, len(given) - 2),
+        functools.partial(place_kernel, spans, len(given) - 2),
         out_shape=jax.ShapeDtypeStruct((slots, PAGES) + source.shape[2:], source.dtype),
         in_specs=[
             pl.BlockSpec(memory_space=pltpu.SMEM),
@@ -182,7 +192,7 @@
         + [pl.BlockSpec(memory_space=pl.ANY)] * (len(given) - 2),
         out_specs=pl.BlockSpec(memory_space=pl.ANY),
         scratch_shapes=[
-            pltpu.VMEM((slots,) + source.shape[1:], source.dtype),
+            pltpu.VMEM((slots, max(span[1] for span in spans)) + source.shape[2:], source.dtype),
             pltpu.SemaphoreType.DMA((slots,)),
             pltpu.SemaphoreType.DMA((slots,)),
         ],
@@ -256,12 +266,12 @@
     rows_here = residual.shape[0]
     partial = jnp.dot(attended, out_proj, preferred_element_type=jnp.float32).astype(jnp.bfloat16)
     plane, partial = lax.optimization_barrier((gather_plane(front), partial))
-    fronts = gather_fronts(plane, front.shape[2:])
+    fronts = gather_fronts(plane, front.shape[1:])
     held = partial.reshape(lax.axis_size("tensor"), rows_here, -1)
     held = halve(held, 1).astype(jnp.bfloat16)
     far, held = lax.optimization_barrier((gather_backs_far(back), held))
     held = halve(held, 2).astype(jnp.bfloat16)
-    backs = share(gather_backs_near(far), groups_y()).reshape((-1,) + back.shape[2:])
+    backs = share(gather_backs_near(far), groups_y()).reshape((-1,) + back.shape[1:])
     updated = halve(held, 4)[0] + residual.astype(jnp.float32)
     hidden_out = updated.astype(jnp.bfloat16)
     block_ends = updated.reshape(rows_here // CH, CH, updated.shape[1])[:, CH - 1]
@@ -272,8 +282,10 @@
     )
     scores = jax.nn.sigmoid(jnp.sum(normed * score_weight.astype(jnp.float32), axis=-1))
     front_at, back_at = child_places(listing, fork_parent, lax.axis_index("dp"))
-    child_pages = place_children(back_at, backs, FRONT)
-    child_pages = place_children(front_at, fronts, 0, child_pages)[:, :, :, :, None]
+    front_spans = [(FRONT_AT[which], FRONT[which], 0) for which in range(2)]
+    back_spans = [(BACK_AT[which], PAGES - FRONT[which], FRONT[which]) for which in range(2)]
+    child_pages = place_children(back_at, backs, back_spans)
+    child_pages = place_children(front_at, fronts, front_spans, child_pages)[:, :, :, :, None]
     return (hidden_out, scores, child_pages)
 
 

time: 156 us -> 156 us (level)
  waiting for transfers between devices: 50.6 us -> 48.1 us
    all_gather x1, waiting for transfers between devices: 10.6 us -> 1.13 us  [gather_fronts(): lax.all_gather(plane, 'dp', axis=0, tiled=True, axis_index_groups=groups_...]
    all_to_all x3, waiting for transfers between devices: 27.9 us -> 34.9 us  [exchange(): lax.all_to_all(copies, 'dp', split_axis=0, concat_axis=0, tiled=True, axi...]
where the time goes in v12:
time: 156 us; the launch traced here: 153 us
  starting transfers between devices  60.1 us (39%)
  waiting for transfers between devices  48.1 us (31%)
  between operations  14.6 us (9%)
  Pallas kernels  10.6 us (7%)
  local copies, waits for them, and re-layouts  9.48 us (6%)
  other arithmetic  7.49 us (5%)
  matrix products  2.74 us (2%)
    all_to_all x3, waiting for transfers between devices, exchange(): lax.all_to_all(copies, 'dp', split_axis=0, concat_axis=0, tiled=True, axi...  34.9 us
    all_to_all x1, starting transfers between devices, parent_listing(): lax.all_to_all(copies, 'dp', split_axis=0, concat_axis=0, tiled=True)[:, 0]  18.7 us
    all_to_all x3, starting transfers between devices, exchange(): lax.all_to_all(copies, 'dp', split_axis=0, concat_axis=0, tiled=True, axi...  18.3 us
    ppermute x4, starting transfers between devices, gather_backs_near(): lax.ppermute(x, 'dp', shift_z(step))  13 us
    ppermute x3, starting transfers between devices, halve(): came = lax.ppermute(send, 'tensor', [(i, i ^ apart) for i in range(shards)])  10.1 us
    pallas_call x2, Pallas kernels, place_children(): pl.pallas_call(functools.partial(place_kernel, spans, len(given) - 2), ou...  7.69 us
    all_to_all x1, waiting for transfers between devices, parent_listing(): lax.all_to_all(copies, 'dp', split_axis=0, concat_axis=0, tiled=True)[:, 0]  7.43 us
    ppermute x3, waiting for transfers between devices, halve(): came = lax.ppermute(send, 'tensor', [(i, i ^ apart) for i in range(shards)])  3.37 us
  transfers between devices with their start and end apart: 12, of which 7 were waited for; matrix products, arithmetic and copies ran while one was open for 12% of the time, Pallas kernels for 2%

profile of v12, /device:TPU:24, one launch (start us, length us, event | category | flops | bytes accessed | tf_op | source)
XLA Modules:
  0.0 153.1 jit_solution(12281452370691868484)
XLA Ops:
  7.2 0.8 pad.4
  8.6 18.7 %all-to-all-start = ((s32[64,1,128]{2,1,0:T(1,128)}), s32[64,1,128]{2,1,0:T(1,128)}, u32[]{:S(2)}, u32[]{:S(2)}) async-start(s32[64,1,128]{2,1,0:T(1,128)} %broadcast_in_dim.84), calls=%async_computation | async-start | bytes 65536 | tf_op jit(solution)/shard_map/all_to_all | solution.py:75
  28.1 2.3 %gather_fusion = bf16[192,2,16,128]{3,2,1,0:T(8,128)(2,1)S(1)} fusion(bf16[192,2,16,128]{3,2,1,0:T(8,128)(2,1)} %bitcast.148, s32[1024]{0:T(1024)S(1)} %pad_clamp_fusion), kind=kCustom, calls=%fused_computation | custom fusion | bytes 3146496 | tf_op jit(solution)/shard_map/gather | solution.py:26
  30.4 1.6 %fusion.42 = (bf16[16,12,1,16,1,128]{5,3,2,1,0,4:T(8,128)(2,1)}, bf16[16,12,1,16,1,128]{5,3,2,1,0,4:T(8,128)(2,1)}) fusion(bf16[16,12,2,16,1,128]{5,3,2,1,0,4:T(8,128)(2,1)S(1)} %bitcast.150), kind=kLoop, calls=%fused_computation.98 | loop fusion | bytes 3145728 | tf_op jit(solution)/shard_map/slice | solution.py:29
  32.1 7.4 %all-to-all-done = s32[64,1,128]{2,1,0:T(1,128)} async-done(((s32[64,1,128]{2,1,0:T(1,128)}), s32[64,1,128]{2,1,0:T(1,128)}, u32[]{:S(2)}, u32[]{:S(2)}) %all-to-all-start) | async-done | bytes 32800 | tf_op jit(solution)/shard_map/all_to_all | solution.py:75
  39.6 2.9 %shard_map.121 = (bf16[4,11,2,16,128]{4,3,2,1,0:T(8,128)(2,1)}, bf16[4,5,2,16,128]{4,3,2,1,0:T(8,128)(2,1)}) custom-call(s32[1]{0:T(128)} %bitcast.me_ref, s32[64,128]{1,0:T(8,128)} %bitcast.1.listing_ref, s32[16,12]{1,0:T(8,128)} %table_ref.1, bf16[192,2,16,128]{3,2,1,0:T(8,128)(2,1)} %bitcast.149), custom_call_target="tpu_custom_call" | custom-call | tf_op jit(solution)/shard_map/pallas_call | solution.py:132
  42.5 6.9 %all-to-all-start.2 = ((bf16[4,352,128]{2,1,0:T(8,128)(2,1)}), bf16[4,352,128]{2,1,0:T(8,128)(2,1)}, u32[]{:S(2)}, u32[]{:S(2)}) async-start(bf16[4,352,128]{2,1,0:T(8,128)(2,1)} %bitcast.164), calls=%async_computation.2 | async-start | bytes 720896 | tf_op jit(solution)/shard_map/all_to_all | solution.py:99
  49.4 0.7 fusion.44
  52.0 0.8 convolution_convert_fusion
  52.9 1.7 %all-to-all-done.2 = bf16[4,352,128]{2,1,0:T(8,128)(2,1)} async-done(((bf16[4,352,128]{2,1,0:T(8,128)(2,1)}), bf16[4,352,128]{2,1,0:T(8,128)(2,1)}, u32[]{:S(2)}, u32[]{:S(2)}) %all-to-all-start.2) | async-done | bytes 360480 | tf_op jit(solution)/shard_map/all_to_all | solution.py:99
  54.7 0.9 dynamic-slice_bitcast_fusion
  55.6 1.9 %collective-permute-start = (bf16[4,32,2560]{2,1,0:T(8,128)(2,1)}, bf16[4,32,2560]{2,1,0:T(8,128)(2,1)}, u32[]{:S(2)}, u32[]{:S(2)}) collective-permute-start(bf16[4,32,2560]{2,1,0:T(8,128)(2,1)} %dynamic-slice_bitcast_fusion), channel_id=1, source_target_pairs={{0,1},{1,0},{2,3},{3,2},{4,5},{5,4},{6,7},{7,6},{8,9},{9,8},{10,11... | collective-permute-start | bytes 1966088 | tf_op jit(solution)/shard_map/ppermute | solution.py:244
  57.7 3.4 %all-to-all-start.1 = ((bf16[4,160,128]{2,1,0:T(8,128)(2,1)}), bf16[4,160,128]{2,1,0:T(8,128)(2,1)S(1)}, u32[]{:S(2)}, u32[]{:S(2)}) async-start(bf16[4,160,128]{2,1,0:T(8,128)(2,1)} %bitcast.165), calls=%async_computation.1 | async-start | bytes 327680 | tf_op jit(solution)/shard_map/all_to_all | solution.py:99
  61.1 0.8 add_select_fusion.1
  62.8 2.2 %fusion = bf16[4,32,2560]{2,1,0:T(8,128)(2,1)} fusion(bf16[4,32,2560]{2,1,0:T(8,128)(2,1)} %collective-permute-done, bf16[4,2,32,2560]{3,2,1,0:T(8,128)(2,1)S(1)} %bitcast.153, s32[]{:T(128)S(6)} %select_n.124), kind=kLoop, calls=%fused_computation.4 | loop fusion | flops 1310720 | bytes 1966084 | tf_op jit(solution)/shard_map/convert_element_type | solution.py:271
  65.0 14.9 %all-to-all-done.1 = bf16[4,160,128]{2,1,0:T(8,128)(2,1)S(1)} async-done(((bf16[4,160,128]{2,1,0:T(8,128)(2,1)}), bf16[4,160,128]{2,1,0:T(8,128)(2,1)S(1)}, u32[]{:S(2)}, u32[]{:S(2)}) %all-to-all-start.1) | async-done | bytes 163872 | tf_op jit(solution)/shard_map/all_to_all | solution.py:99
  79.9 1.9 %collective-permute-start.6 = (bf16[640,128]{1,0:T(8,128)(2,1)S(1)}, bf16[640,128]{1,0:T(8,128)(2,1)S(1)}, u32[]{:S(2)}, u32[]{:S(2)}) collective-permute-start(bf16[640,128]{1,0:T(8,128)(2,1)S(1)} %bitcast.157), channel_id=1, source_target_pairs={{0,480},{8,488},{16,496},{24,504},{32,0},{40,8},{48,16},{56,24},{6... | collective-permute-start | bytes 491528 | tf_op jit(solution)/shard_map/ppermute | solution.py:235
  81.9 4.3 %collective-permute-start.3 = (bf16[640,128]{1,0:T(8,128)(2,1)S(1)}, bf16[640,128]{1,0:T(8,128)(2,1)S(1)}, u32[]{:S(2)}, u32[]{:S(2)}) collective-permute-start(bf16[640,128]{1,0:T(8,128)(2,1)S(1)} %bitcast.158), channel_id=1, source_target_pairs={{0,32},{8,40},{16,48},{24,56},{32,64},{40,72},{48,80},{56,88},{64,... | collective-permute-start | bytes 491528 | tf_op jit(solution)/shard_map/ppermute | solution.py:235
  86.2 2.0 %collective-permute-start.5 = (bf16[320,128]{1,0:T(8,128)(2,1)S(1)}, bf16[320,128]{1,0:T(8,128)(2,1)S(1)}, u32[]{:S(2)}, u32[]{:S(2)}) collective-permute-start(bf16[320,128]{1,0:T(8,128)(2,1)S(1)} %get-tuple-element.45), channel_id=1, source_target_pairs={{0,448},{8,456},{16,464},{24,472},{32,480},{40,488},{48,496},{56,5... | collective-permute-start | bytes 245768 | tf_op jit(solution)/shard_map/ppermute | solution.py:235
  88.2 4.8 %collective-permute-start.4 = (bf16[320,128]{1,0:T(8,128)(2,1)S(1)}, bf16[320,128]{1,0:T(8,128)(2,1)S(1)}, u32[]{:S(2)}, u32[]{:S(2)}) collective-permute-start(bf16[320,128]{1,0:T(8,128)(2,1)S(1)} %get-tuple-element.46), channel_id=1, source_target_pairs={{0,64},{8,72},{16,80},{24,88},{32,96},{40,104},{48,112},{56,120},{... | collective-permute-start | bytes 245768 | tf_op jit(solution)/shard_map/ppermute | solution.py:235
  93.0 1.0 dynamic-slice_bitcast_fusion.1
  94.0 3.4 %collective-permute-start.1 = (bf16[2,32,2560]{2,1,0:T(8,128)(2,1)S(1)}, bf16[2,32,2560]{2,1,0:T(8,128)(2,1)S(1)}, u32[]{:S(2)}, u32[]{:S(2)}) collective-permute-start(bf16[2,32,2560]{2,1,0:T(8,128)(2,1)S(1)} %dynamic-slice_bitcast_fusion.1), channel_id=1, source_target_pairs={{0,2},{1,3},{2,0},{3,1},{4,6},{5,7},{6,4},{7,5},{8,10},{9,11},{10,... | collective-permute-start | bytes 983048 | tf_op jit(solution)/shard_map/ppermute | solution.py:244
  97.5 1.2 collective-permute-done.4
  98.7 1.8 %broadcast_in_dim.95 = bf16[4,2560,128]{2,1,0:T(8,128)(2,1)} broadcast(bf16[2560,128]{1,0:T(8,128)(2,1)S(1)} %constant_dynamic-update-slice_fusion), dimensions={1,2} | broadcast | bytes 3276800 | tf_op jit(solution)/shard_map/broadcast_in_dim | solution.py:95
  100.6 8.1 %all-to-all-start.3 = ((bf16[4,2560,128]{2,1,0:T(8,128)(2,1)}), bf16[4,2560,128]{2,1,0:T(8,128)(2,1)}, u32[]{:S(2)}, u32[]{:S(2)}) async-start(bf16[4,2560,128]{2,1,0:T(8,128)(2,1)} %broadcast_in_dim.95), calls=%async_computation.3 | async-start | bytes 5242880 | tf_op jit(solution)/shard_map/all_to_all | solution.py:99
  108.8 4.8 %collective-permute-start.2 = (bf16[1,32,2560]{2,1,0:T(8,128)(2,1)S(1)}, bf16[1,32,2560]{2,1,0:T(8,128)(2,1)S(1)}, u32[]{:S(2)}, u32[]{:S(2)}) collective-permute-start(bf16[1,32,2560]{2,1,0:T(8,128)(2,1)S(1)} %constant_dynamic-slice_fusion), channel_id=1, source_target_pairs={{0,4},{1,5},{2,6},{3,7},{4,0},{5,1},{6,2},{7,3},{8,12},{9,13},{10,... | collective-permute-start | bytes 491528 | tf_op jit(solution)/shard_map/ppermute | solution.py:244
  114.1 3.4 %collective-permute-done.2 = bf16[1,32,2560]{2,1,0:T(8,128)(2,1)S(1)} collective-permute-done((bf16[1,32,2560]{2,1,0:T(8,128)(2,1)S(1)}, bf16[1,32,2560]{2,1,0:T(8,128)(2,1)S(1)}, u32[]{:S(2)}, u32[]{:S(2)}) %collective-permute-start.2) | collective-permute-done | bytes 163872 | tf_op jit(solution)/shard_map/ppermute | solution.py:244
  117.5 0.7 fusion.41
  119.1 18.3 %all-to-all-done.3 = bf16[4,2560,128]{2,1,0:T(8,128)(2,1)} async-done(((bf16[4,2560,128]{2,1,0:T(8,128)(2,1)}), bf16[4,2560,128]{2,1,0:T(8,128)(2,1)}, u32[]{:S(2)}, u32[]{:S(2)}) %all-to-all-start.3) | async-done | bytes 2621472 | tf_op jit(solution)/shard_map/all_to_all | solution.py:99
  137.4 3.8 %shard_map.122.refs_0_ = bf16[48,8,2,16,128]{4,3,2,1,0:T(8,128)(2,1)} custom-call(s32[48]{0:T(128)} %get-tuple-element.39.where_ref, bf16[64,5,2,16,128]{4,3,2,1,0:T(8,128)(2,1)} %bitcast.42.source_ref), custom_call_target="tpu_custom_call" | custom-call | tf_op jit(solution)/shard_map/pallas_call | solution.py:185
  141.2 1.1 all-gather.2.cloned.1.call-done
  142.3 3.9 %shard_map.123 = bf16[48,8,2,16,128]{4,3,2,1,0:T(8,128)(2,1)} custom-call(s32[48]{0:T(128)} %multiply_add_fusion.1.where_ref, bf16[64,11,2,16,128]{4,3,2,1,0:T(8,128)(2,1)} %bitcast.151, bf16[48,8,2,16,128]{4,3,2,1,0:T(8,128)(2,1)} %shard_map.122.refs_0_), custom_call_target="tpu_custom_call", output_to_operand_aliasing={{}: (2, {})} | custom-call | tf_op jit(solution)/shard_map/pallas_call | solution.py:185
  (62 shorter events, 6.1 us)
Async XLA Ops:
  7.2 44.9 %copy-start = (bf16[384,2560]{1,0:T(8,128)(2,1)S(1)}, bf16[384,2560]{1,0:T(8,128)(2,1)}, u32[]{:S(2)}) copy-start(bf16[384,2560]{1,0:T(8,128)(2,1)} %param.15) | copy-start | bytes 5898244
  8.6 31.0 %all-to-all-start = ((s32[64,1,128]{2,1,0:T(1,128)}), s32[64,1,128]{2,1,0:T(1,128)}, u32[]{:S(2)}, u32[]{:S(2)}) async-start(s32[64,1,128]{2,1,0:T(1,128)} %broadcast_in_dim.84), calls=%async_computation | async-start | bytes 65536 | tf_op jit(solution)/shard_map/all_to_all | solution.py:75
  30.4 1.6 %copy-start.9 = (s32[16]{0:T(128)S(1)}, s32[16]{0:T(128)}, u32[]{:S(2)}) copy-start(s32[16]{0:T(128)} %param.14) | copy-start | bytes 196
  32.1 17.4 %copy-start.1 = (bf16[16,12,1,16,1,128]{5,3,2,1,0,4:T(8,128)(2,1)S(1)}, bf16[16,12,1,16,1,128]{5,3,2,1,0,4:T(8,128)(2,1)}, u32[]{:S(2)}) copy-start(bf16[16,12,1,16,1,128]{5,3,2,1,0,4:T(8,128)(2,1)} %get-tuple-element.44) | copy-start | bytes 2359300
  32.1 17.4 %copy-start.3 = (bf16[16,16,3,128]{3,1,2,0:T(8,128)(2,1)S(1)}, bf16[16,16,3,128]{3,1,2,0:T(8,128)(2,1)}, u32[]{:S(2)}) copy-start(bf16[16,16,3,128]{3,1,2,0:T(8,128)(2,1)} %param.10) | copy-start | bytes 589828
  42.5 7.6 %copy-start.6 = (bf16[16,2,16,1,128]{4,2,3,1,0:T(8,128)(2,1)S(1)}, bf16[16,2,16,1,128]{4,2,3,1,0:T(8,128)(2,1)}, u32[]{:S(2)}) copy-start(bf16[16,2,16,1,128]{4,2,3,1,0:T(8,128)(2,1)} %param.11) | copy-start | bytes 393220
  42.5 12.1 %all-to-all-start.2 = ((bf16[4,352,128]{2,1,0:T(8,128)(2,1)}), bf16[4,352,128]{2,1,0:T(8,128)(2,1)}, u32[]{:S(2)}, u32[]{:S(2)}) async-start(bf16[4,352,128]{2,1,0:T(8,128)(2,1)} %bitcast.164), calls=%async_computation.2 | async-start | bytes 720896 | tf_op jit(solution)/shard_map/all_to_all | solution.py:99
  49.4 92.9 %all-gather.2.cloned.1.call-start = ((), (), s32[]{:S(2)}) async-start(), calls=%async_computation.4 | async-start | bytes 6127616 | tf_op jit(solution)/shard_map/all_gather | solution.py:223
  49.4 1.8 %copy-start.4 = (bf16[16,12,1,16,1,128]{5,3,2,1,0,4:T(8,128)(2,1)S(1)}, bf16[16,12,1,16,1,128]{5,3,2,1,0,4:T(8,128)(2,1)}, u32[]{:S(2)}) copy-start(bf16[16,12,1,16,1,128]{5,3,2,1,0,4:T(8,128)(2,1)} %get-tuple-element.43) | copy-start | bytes 2359300
  52.9 4.6 %copy-start.10 = (s32[48]{0:T(128)S(1)}, s32[48]{0:T(128)}, u32[]{:S(2)}) copy-start(s32[48]{0:T(128)} %param.19) | copy-start | bytes 580
  52.9 4.7 %copy-start.7 = (bf16[2560]{0:T(1024)(128)(2,1)S(1)}, bf16[2560]{0:T(1024)(128)(2,1)}, u32[]{:S(2)}) copy-start(bf16[2560]{0:T(1024)(128)(2,1)} %param.17) | copy-start | bytes 15364
  52.9 4.7 %copy-start.8 = (bf16[2560]{0:T(1024)(128)(2,1)S(1)}, bf16[2560]{0:T(1024)(128)(2,1)}, u32[]{:S(2)}) copy-start(bf16[2560]{0:T(1024)(128)(2,1)} %param.18) | copy-start | bytes 15364
  55.6 7.3 %collective-permute-start = (bf16[4,32,2560]{2,1,0:T(8,128)(2,1)}, bf16[4,32,2560]{2,1,0:T(8,128)(2,1)}, u32[]{:S(2)}, u32[]{:S(2)}) collective-permute-start(bf16[4,32,2560]{2,1,0:T(8,128)(2,1)} %dynamic-slice_bitcast_fusion), channel_id=1, source_target_pairs={{0,1},{1,0},{2,3},{3,2},{4,5},{5,4},{6,7},{7,6},{8,9},{9,8},{10,11... | collective-permute-start | bytes 1966088 | tf_op jit(solution)/shard_map/ppermute | solution.py:244
  57.7 22.3 %all-to-all-start.1 = ((bf16[4,160,128]{2,1,0:T(8,128)(2,1)}), bf16[4,160,128]{2,1,0:T(8,128)(2,1)S(1)}, u32[]{:S(2)}, u32[]{:S(2)}) async-start(bf16[4,160,128]{2,1,0:T(8,128)(2,1)} %bitcast.165), calls=%async_computation.1 | async-start | bytes 327680 | tf_op jit(solution)/shard_map/all_to_all | solution.py:99
  79.9 18.8 %collective-permute-start.6 = (bf16[640,128]{1,0:T(8,128)(2,1)S(1)}, bf16[640,128]{1,0:T(8,128)(2,1)S(1)}, u32[]{:S(2)}, u32[]{:S(2)}) collective-permute-start(bf16[640,128]{1,0:T(8,128)(2,1)S(1)} %bitcast.157), channel_id=1, source_target_pairs={{0,480},{8,488},{16,496},{24,504},{32,0},{40,8},{48,16},{56,24},{6... | collective-permute-start | bytes 491528 | tf_op jit(solution)/shard_map/ppermute | solution.py:235
  81.9 15.6 %collective-permute-start.3 = (bf16[640,128]{1,0:T(8,128)(2,1)S(1)}, bf16[640,128]{1,0:T(8,128)(2,1)S(1)}, u32[]{:S(2)}, u32[]{:S(2)}) collective-permute-start(bf16[640,128]{1,0:T(8,128)(2,1)S(1)} %bitcast.158), channel_id=1, source_target_pairs={{0,32},{8,40},{16,48},{24,56},{32,64},{40,72},{48,80},{56,88},{64,... | collective-permute-start | bytes 491528 | tf_op jit(solution)/shard_map/ppermute | solution.py:235
  86.2 12.5 %collective-permute-start.5 = (bf16[320,128]{1,0:T(8,128)(2,1)S(1)}, bf16[320,128]{1,0:T(8,128)(2,1)S(1)}, u32[]{:S(2)}, u32[]{:S(2)}) collective-permute-start(bf16[320,128]{1,0:T(8,128)(2,1)S(1)} %get-tuple-element.45), channel_id=1, source_target_pairs={{0,448},{8,456},{16,464},{24,472},{32,480},{40,488},{48,496},{56,5... | collective-permute-start | bytes 245768 | tf_op jit(solution)/shard_map/ppermute | solution.py:235
  88.2 10.5 %collective-permute-start.4 = (bf16[320,128]{1,0:T(8,128)(2,1)S(1)}, bf16[320,128]{1,0:T(8,128)(2,1)S(1)}, u32[]{:S(2)}, u32[]{:S(2)}) collective-permute-start(bf16[320,128]{1,0:T(8,128)(2,1)S(1)} %get-tuple-element.46), channel_id=1, source_target_pairs={{0,64},{8,72},{16,80},{24,88},{32,96},{40,104},{48,112},{56,120},{... | collective-permute-start | bytes 245768 | tf_op jit(solution)/shard_map/ppermute | solution.py:235
  94.0 14.7 %collective-permute-start.1 = (bf16[2,32,2560]{2,1,0:T(8,128)(2,1)S(1)}, bf16[2,32,2560]{2,1,0:T(8,128)(2,1)S(1)}, u32[]{:S(2)}, u32[]{:S(2)}) collective-permute-start(bf16[2,32,2560]{2,1,0:T(8,128)(2,1)S(1)} %dynamic-slice_bitcast_fusion.1), channel_id=1, source_target_pairs={{0,2},{1,3},{2,0},{3,1},{4,6},{5,7},{6,4},{7,5},{8,10},{9,11},{10,... | collective-permute-start | bytes 983048 | tf_op jit(solution)/shard_map/ppermute | solution.py:244
  100.6 8.1 %copy-start.2 = (bf16[4,32,2560]{2,1,0:T(8,128)(2,1)S(1)}, bf16[4,32,2560]{2,1,0:T(8,128)(2,1)}, u32[]{:S(2)}) copy-start(bf16[4,32,2560]{2,1,0:T(8,128)(2,1)} %fusion) | copy-start | bytes 1966084
  100.6 16.9 %copy-start.5 = (bf16[32,2560]{1,0:T(8,128)(2,1)S(1)}, bf16[32,2560]{1,0:T(8,128)(2,1)}, u32[]{:S(2)}) copy-start(bf16[32,2560]{1,0:T(8,128)(2,1)} %param.16) | copy-start | bytes 491524
  100.6 36.8 %all-to-all-start.3 = ((bf16[4,2560,128]{2,1,0:T(8,128)(2,1)}), bf16[4,2560,128]{2,1,0:T(8,128)(2,1)}, u32[]{:S(2)}, u32[]{:S(2)}) async-start(bf16[4,2560,128]{2,1,0:T(8,128)(2,1)} %broadcast_in_dim.95), calls=%async_computation.3 | async-start | bytes 5242880 | tf_op jit(solution)/shard_map/all_to_all | solution.py:99
  108.8 8.7 %collective-permute-start.2 = (bf16[1,32,2560]{2,1,0:T(8,128)(2,1)S(1)}, bf16[1,32,2560]{2,1,0:T(8,128)(2,1)S(1)}, u32[]{:S(2)}, u32[]{:S(2)}) collective-permute-start(bf16[1,32,2560]{2,1,0:T(8,128)(2,1)S(1)} %constant_dynamic-slice_fusion), channel_id=1, source_target_pairs={{0,4},{1,5},{2,6},{3,7},{4,0},{5,1},{6,2},{7,3},{8,12},{9,13},{10,... | collective-permute-start | bytes 491528 | tf_op jit(solution)/shard_map/ppermute | solution.py:244
Sparse Core Ops, SparseCore 0:
  54.8 87.4 all-gather.1

commit v13 on v9

--- a/solution.py
+++ b/solution.py
@@ -99,28 +99,18 @@
     )
 
 
-def pick_kernel(me_ref, listing_ref, table_ref, cache_ref, front_ref, back_ref, sems):
+def pick_kernel(me_ref, listing_ref, table_ref, cache_ref, front_ref, back_ref):
     asked = listing_ref[...]
     mine = (asked >> 4) == me_ref[0]
     rows = asked & (BR_DEV - 1)
     lowest = jnp.min(jnp.where(mine, rows, BR_DEV - 1))
     highest = jnp.max(jnp.where(mine, rows, 0))
-    copies = []
     for which, row in enumerate((lowest, highest)):
         for page in range(PAGES):
             part, at = (front_ref, page) if page < FRONT else (back_ref, page - FRONT)
-            copies.append(
-                pltpu.make_async_copy(
-                    cache_ref.at[table_ref[row, page]], part.at[0, which, at], sems.at[which, page]
-                )
-            )
-    for copy in copies:
-        copy.start()
-    for copy in copies:
-        copy.wait()
-    for part in (front_ref, back_ref):
-        for number in range(1, part.shape[0]):
-            part[number] = part[0]
+            block = cache_ref[table_ref[row, page]]
+            for number in range(part.shape[0]):
+                part[number, which, at] = block
 
 
 def pick_pages(me_index, listing, page_table, cache):
@@ -134,10 +124,10 @@
             pl.BlockSpec(memory_space=pltpu.SMEM),
             pl.BlockSpec(memory_space=pltpu.VMEM),
             pl.BlockSpec(memory_space=pltpu.SMEM),
-            pl.BlockSpec(memory_space=pl.ANY),
+            pl.BlockSpec(memory_space=pltpu.VMEM),
         ],
         out_specs=(pl.BlockSpec(memory_space=pltpu.VMEM),) * 2,
-        scratch_shapes=[pltpu.SemaphoreType.DMA((2, PAGES))],
+        compiler_params=pltpu.CompilerParams(vmem_limit_bytes=16 * 2**20),
     )(me_index.reshape(1), listing, page_table, cache)
 
 

time: 155 us -> 155 us (level)
  waiting for transfers between devices: 49.8 us -> 47.2 us
  local copies, waits for them, and re-layouts: 8.18 us -> 10.6 us
  starting transfers between devices: 49.1 us -> 51.5 us
  Pallas kernels: 10.1 us -> 8.17 us
    all_to_all x2, starting transfers between devices: 10.1 us -> 13.3 us  [exchange(): lax.all_to_all(copies, 'dp', split_axis=0, concat_axis=0, tiled=True, axi...]
    all_to_all x1, waiting for transfers between devices: 7.64 us -> 5.25 us  [parent_listing(): lax.all_to_all(copies, 'dp', split_axis=0, concat_axis=0, tiled=True)[:, 0]]
    pallas_call x1, Pallas kernels: 2.95 us -> 1.04 us  [pick_pages(): pl.pallas_call(pick_kernel, out_shape=tuple((jax.ShapeDtypeStruct((copies...]
  transfers between devices with their start and end apart: 10 -> 10, of which waited for: 7 -> 8; matrix products, arithmetic and copies ran while one was open for 9% -> 12% of each run, Pallas kernels for 2% -> 2%
where the time goes in v13:
time: 155 us; the launch traced here: 152 us
  starting transfers between devices  51.5 us (33%)
  waiting for transfers between devices  47.2 us (30%)
  between operations  14.4 us (9%)
  blocking collectives  10.9 us (7%)
  local copies, waits for them, and re-layouts  10.6 us (7%)
  Pallas kernels  8.17 us (5%)
  other arithmetic  6.87 us (4%)
  matrix products  2.73 us (2%)
    all_to_all x2, waiting for transfers between devices, exchange(): lax.all_to_all(copies, 'dp', split_axis=0, concat_axis=0, tiled=True, axi...  23.6 us
    all_to_all x1, starting transfers between devices, parent_listing(): lax.all_to_all(copies, 'dp', split_axis=0, concat_axis=0, tiled=True)[:, 0]  18.7 us
    all_to_all x2, starting transfers between devices, exchange(): lax.all_to_all(copies, 'dp', split_axis=0, concat_axis=0, tiled=True, axi...  13.3 us
    ppermute x3, waiting for transfers between devices, gather_backs_near(): lax.ppermute(far, 'dp', shift_z(step))  13.1 us
    all_to_all x1, blocking collectives, exchange(): lax.all_to_all(copies, 'dp', split_axis=0, concat_axis=0, tiled=True, axi...  10.9 us
    ppermute x3, starting transfers between devices, halve(): came = lax.ppermute(send, 'tensor', [(i, i ^ apart) for i in range(shards)])  9.97 us
    ppermute x3, starting transfers between devices, gather_backs_near(): lax.ppermute(far, 'dp', shift_z(step))  9.45 us
    pallas_call x2, Pallas kernels, place_children(): pl.pallas_call(functools.partial(place_kernel, first_page, len(given) - 2...  7.12 us
  transfers between devices with their start and end apart: 10, of which 8 were waited for; matrix products, arithmetic and copies ran while one was open for 12% of the time, Pallas kernels for 2%

profile of v13, /device:TPU:24, one launch (start us, length us, event | category | flops | bytes accessed | tf_op | source)
XLA Modules:
  0.0 152.4 jit_solution(27206085977045025)
XLA Ops:
  7.2 0.8 pad.4
  8.6 18.7 %all-to-all-start = ((s32[64,1,128]{2,1,0:T(1,128)}), s32[64,1,128]{2,1,0:T(1,128)}, u32[]{:S(2)}, u32[]{:S(2)}) async-start(s32[64,1,128]{2,1,0:T(1,128)} %broadcast_in_dim.84), calls=%async_computation | async-start | bytes 65536 | tf_op jit(solution)/shard_map/all_to_all | solution.py:73
  27.4 0.7 compare_select_fusion
  28.2 3.4 %gather_fusion = bf16[192,2,16,128]{3,2,1,0:T(8,128)(2,1)} fusion(bf16[192,2,16,128]{3,2,1,0:T(8,128)(2,1)} %bitcast.147, s32[1024]{0:T(1024)S(1)} %pad_clamp_fusion), kind=kCustom, calls=%fused_computation | custom fusion | bytes 3146496 | tf_op jit(solution)/shard_map/gather | solution.py:24
  31.6 2.9 %fusion.42 = (bf16[16,12,1,16,1,128]{5,3,2,1,0,4:T(8,128)(2,1)}, bf16[16,12,1,16,1,128]{5,3,2,1,0,4:T(8,128)(2,1)}) fusion(bf16[16,12,2,16,1,128]{5,3,2,1,0,4:T(8,128)(2,1)} %bitcast.153), kind=kLoop, calls=%fused_computation.94 | loop fusion | bytes 3145728 | tf_op jit(solution)/shard_map/slice | solution.py:27
  34.5 5.2 %all-to-all-done = s32[64,1,128]{2,1,0:T(1,128)} async-done(((s32[64,1,128]{2,1,0:T(1,128)}), s32[64,1,128]{2,1,0:T(1,128)}, u32[]{:S(2)}, u32[]{:S(2)}) %all-to-all-start) | async-done | bytes 32800 | tf_op jit(solution)/shard_map/all_to_all | solution.py:73
  39.7 1.0 shard_map.121
  40.8 10.9 %all_to_all.20 = bf16[4,384,128]{2,1,0:T(8,128)(2,1)} all-to-all(bf16[4,384,128]{2,1,0:T(8,128)(2,1)S(1)} %bitcast.149), channel_id=1, replica_groups={{0,8,16,24},{32,40,48,56},{64,72,80,88},{96,104,112,120},{128,136,144,1..., dimensions={0} | all-to-all | bytes 786432 | tf_op jit(solution)/shard_map/all_to_all | solution.py:97
  51.8 0.7 convert_element_type.84
  52.6 0.7 iota_compare_fusion
  53.3 5.7 %all-to-all-start.1 = ((bf16[4,128,128]{2,1,0:T(8,128)(2,1)}), bf16[4,128,128]{2,1,0:T(8,128)(2,1)S(1)}, u32[]{:S(2)}, u32[]{:S(2)}) async-start(bf16[4,128,128]{2,1,0:T(8,128)(2,1)} %bitcast.150), calls=%async_computation.1 | async-start | bytes 262144 | tf_op jit(solution)/shard_map/all_to_all | solution.py:97
  59.6 0.7 fusion.43
  61.7 0.8 convolution_convert_fusion
  62.5 9.8 %all-to-all-done.1 = bf16[4,128,128]{2,1,0:T(8,128)(2,1)S(1)} async-done(((bf16[4,128,128]{2,1,0:T(8,128)(2,1)}), bf16[4,128,128]{2,1,0:T(8,128)(2,1)S(1)}, u32[]{:S(2)}, u32[]{:S(2)}) %all-to-all-start.1) | async-done | bytes 131104 | tf_op jit(solution)/shard_map/all_to_all | solution.py:97
  72.3 1.9 %collective-permute-start.3 = (bf16[4,32,2560]{2,1,0:T(8,128)(2,1)S(1)}, bf16[4,32,2560]{2,1,0:T(8,128)(2,1)S(1)}, u32[]{:S(2)}, u32[]{:S(2)}) collective-permute-start(bf16[4,32,2560]{2,1,0:T(8,128)(2,1)S(1)} %dynamic-slice_bitcast_fusion), channel_id=1, source_target_pairs={{0,1},{1,0},{2,3},{3,2},{4,5},{5,4},{6,7},{7,6},{8,9},{9,8},{10,11... | collective-permute-start | bytes 1966088 | tf_op jit(solution)/shard_map/ppermute | solution.py:221
  74.3 1.9 %collective-permute-start.2 = (bf16[512,128]{1,0:T(8,128)(2,1)S(1)}, bf16[512,128]{1,0:T(8,128)(2,1)S(1)}, u32[]{:S(2)}, u32[]{:S(2)}) collective-permute-start(bf16[512,128]{1,0:T(8,128)(2,1)S(1)} %bitcast.162), channel_id=1, source_target_pairs={{0,480},{8,488},{16,496},{24,504},{32,0},{40,8},{48,16},{56,24},{6... | collective-permute-start | bytes 393224 | tf_op jit(solution)/shard_map/ppermute | solution.py:211
  76.2 5.0 %collective-permute-start.1 = (bf16[512,128]{1,0:T(8,128)(2,1)S(1)}, bf16[512,128]{1,0:T(8,128)(2,1)S(1)}, u32[]{:S(2)}, u32[]{:S(2)}) collective-permute-start(bf16[512,128]{1,0:T(8,128)(2,1)S(1)} %bitcast.163), channel_id=1, source_target_pairs={{0,64},{8,72},{16,80},{24,88},{32,96},{40,104},{48,112},{56,120},{... | collective-permute-start | bytes 393224 | tf_op jit(solution)/shard_map/ppermute | solution.py:211
  81.3 2.5 %collective-permute-start = (bf16[512,128]{1,0:T(8,128)(2,1)S(1)}, bf16[512,128]{1,0:T(8,128)(2,1)S(1)}, u32[]{:S(2)}, u32[]{:S(2)}) collective-permute-start(bf16[512,128]{1,0:T(8,128)(2,1)S(1)} %bitcast.164), channel_id=1, source_target_pairs={{0,32},{8,40},{16,48},{24,56},{32,64},{40,72},{48,80},{56,88},{64,... | collective-permute-start | bytes 393224 | tf_op jit(solution)/shard_map/ppermute | solution.py:211
  83.7 0.8 add_select_fusion.1
  84.9 6.3 %collective-permute-done.1 = bf16[512,128]{1,0:T(8,128)(2,1)S(1)} collective-permute-done((bf16[512,128]{1,0:T(8,128)(2,1)S(1)}, bf16[512,128]{1,0:T(8,128)(2,1)S(1)}, u32[]{:S(2)}, u32[]{:S(2)}) %collective-permute-start.1) | collective-permute-done | bytes 131104 | tf_op jit(solution)/shard_map/ppermute | solution.py:211
  91.2 6.4 %collective-permute-done = bf16[512,128]{1,0:T(8,128)(2,1)S(1)} collective-permute-done((bf16[512,128]{1,0:T(8,128)(2,1)S(1)}, bf16[512,128]{1,0:T(8,128)(2,1)S(1)}, u32[]{:S(2)}, u32[]{:S(2)}) %collective-permute-start) | collective-permute-done | bytes 131104 | tf_op jit(solution)/shard_map/ppermute | solution.py:211
  97.9 0.9 copy-done.5
  98.8 3.4 %collective-permute-start.4 = (bf16[2,32,2560]{2,1,0:T(8,128)(2,1)S(1)}, bf16[2,32,2560]{2,1,0:T(8,128)(2,1)S(1)}, u32[]{:S(2)}, u32[]{:S(2)}) collective-permute-start(bf16[2,32,2560]{2,1,0:T(8,128)(2,1)S(1)} %dynamic-slice_bitcast_fusion.1), channel_id=1, source_target_pairs={{0,2},{1,3},{2,0},{3,1},{4,6},{5,7},{6,4},{7,5},{8,10},{9,11},{10,... | collective-permute-start | bytes 983048 | tf_op jit(solution)/shard_map/ppermute | solution.py:221
  103.2 1.6 %broadcast_in_dim.95 = bf16[4,2048,128]{2,1,0:T(8,128)(2,1)} broadcast(bf16[2048,128]{1,0:T(8,128)(2,1)S(1)} %pad_maximum_fusion), dimensions={1,2} | broadcast | bytes 2621440 | tf_op jit(solution)/shard_map/broadcast_in_dim | solution.py:93
  104.8 7.6 %all-to-all-start.3 = ((bf16[4,2048,128]{2,1,0:T(8,128)(2,1)}), bf16[4,2048,128]{2,1,0:T(8,128)(2,1)}, u32[]{:S(2)}, u32[]{:S(2)}) async-start(bf16[4,2048,128]{2,1,0:T(8,128)(2,1)} %broadcast_in_dim.95), calls=%async_computation.3 | async-start | bytes 4194304 | tf_op jit(solution)/shard_map/all_to_all | solution.py:97
  112.5 4.6 %collective-permute-start.5 = (bf16[1,32,2560]{2,1,0:T(8,128)(2,1)S(1)}, bf16[1,32,2560]{2,1,0:T(8,128)(2,1)S(1)}, u32[]{:S(2)}, u32[]{:S(2)}) collective-permute-start(bf16[1,32,2560]{2,1,0:T(8,128)(2,1)S(1)} %constant_dynamic-slice_fusion), channel_id=1, source_target_pairs={{0,4},{1,5},{2,6},{3,7},{4,0},{5,1},{6,2},{7,3},{8,12},{9,13},{10,... | collective-permute-start | bytes 491528 | tf_op jit(solution)/shard_map/ppermute | solution.py:221
  117.7 4.0 %collective-permute-done.5 = bf16[1,32,2560]{2,1,0:T(8,128)(2,1)S(1)} collective-permute-done((bf16[1,32,2560]{2,1,0:T(8,128)(2,1)S(1)}, bf16[1,32,2560]{2,1,0:T(8,128)(2,1)S(1)}, u32[]{:S(2)}, u32[]{:S(2)}) %collective-permute-start.5) | collective-permute-done | bytes 163872 | tf_op jit(solution)/shard_map/ppermute | solution.py:221
  121.7 0.7 fusion.41
  123.3 13.8 %all-to-all-done.3 = bf16[4,2048,128]{2,1,0:T(8,128)(2,1)} async-done(((bf16[4,2048,128]{2,1,0:T(8,128)(2,1)}), bf16[4,2048,128]{2,1,0:T(8,128)(2,1)}, u32[]{:S(2)}, u32[]{:S(2)}) %all-to-all-start.3) | async-done | bytes 2097184 | tf_op jit(solution)/shard_map/all_to_all | solution.py:97
  137.1 3.3 %shard_map.122.refs_0_ = bf16[48,8,2,16,128]{4,3,2,1,0:T(8,128)(2,1)} custom-call(s32[48]{0:T(128)} %get-tuple-element.35.where_ref, bf16[128,2,2,16,128]{4,3,2,1,0:T(8,128)(2,1)} %bitcast.42.source_ref), custom_call_target="tpu_custom_call" | custom-call | tf_op jit(solution)/shard_map/pallas_call | solution.py:165
  140.5 1.2 all-gather.2.cloned.1.call-done
  141.7 3.8 %shard_map.123 = bf16[48,8,2,16,128]{4,3,2,1,0:T(8,128)(2,1)} custom-call(s32[48]{0:T(128)} %multiply_add_fusion.1.where_ref, bf16[128,6,2,16,128]{4,3,2,1,0:T(8,128)(2,1)} %bitcast.152, bf16[48,8,2,16,128]{4,3,2,1,0:T(8,128)(2,1)} %shard_map.122.refs_0_), custom_call_target="tpu_custom_call", output_to_operand_aliasing={{}: (2, {})} | custom-call | tf_op jit(solution)/shard_map/pallas_call | solution.py:165
  (58 shorter events, 5.9 us)
Async XLA Ops:
  7.2 54.5 %copy-start = (bf16[384,2560]{1,0:T(8,128)(2,1)S(1)}, bf16[384,2560]{1,0:T(8,128)(2,1)}, u32[]{:S(2)}) copy-start(bf16[384,2560]{1,0:T(8,128)(2,1)} %param.15) | copy-start | bytes 5898244
  8.6 31.1 %all-to-all-start = ((s32[64,1,128]{2,1,0:T(1,128)}), s32[64,1,128]{2,1,0:T(1,128)}, u32[]{:S(2)}, u32[]{:S(2)}) async-start(s32[64,1,128]{2,1,0:T(1,128)} %broadcast_in_dim.84), calls=%async_computation | async-start | bytes 65536 | tf_op jit(solution)/shard_map/all_to_all | solution.py:73
  27.3 114.4 %all-gather.2.cloned.1.call-start = ((), (), s32[]{:S(2)}) async-start(), calls=%async_computation.4 | async-start | bytes 6684672 | tf_op jit(solution)/shard_map/all_gather | solution.py:200
  31.6 8.2 %copy-start.1 = (bf16[192,2,16,1,128]{4,2,3,1,0:T(8,128)(2,1)S(1)}, bf16[192,2,16,1,128]{4,2,3,1,0:T(8,128)(2,1)}, u32[]{:S(2)}) copy-start(bf16[192,2,16,1,128]{4,2,3,1,0:T(8,128)(2,1)} %param.12) | copy-start | bytes 4718596
  31.6 8.2 %copy-start.3 = (s32[16,12]{1,0:T(8,128)S(1)}, s32[16,12]{1,0:T(8,128)}, u32[]{:S(2)}) copy-start(s32[16,12]{1,0:T(8,128)} %table_ref.1) | copy-start | bytes 2308
  34.5 17.3 %copy-start.11 = (bf16[2560]{0:T(1024)(128)(2,1)S(1)}, bf16[2560]{0:T(1024)(128)(2,1)}, u32[]{:S(2)}) copy-start(bf16[2560]{0:T(1024)(128)(2,1)} %param.17) | copy-start | bytes 15364
  40.8 10.9 %copy-start.2 = (bf16[4,2,2,2,16,128]{5,4,3,2,1,0:T(8,128)(2,1)}, bf16[4,2,2,2,16,128]{5,4,3,2,1,0:T(8,128)(2,1)S(1)}, u32[]{:S(2)}) copy-start(bf16[4,2,2,2,16,128]{5,4,3,2,1,0:T(8,128)(2,1)S(1)} %get-tuple-element.14) | copy-start | bytes 393220
  40.8 18.2 %copy-start.7 = (bf16[16,16,3,128]{3,1,2,0:T(8,128)(2,1)S(1)}, bf16[16,16,3,128]{3,1,2,0:T(8,128)(2,1)}, u32[]{:S(2)}) copy-start(bf16[16,16,3,128]{3,1,2,0:T(8,128)(2,1)} %param.10) | copy-start | bytes 589828
  40.8 18.2 %copy-start.10 = (bf16[16,2,16,1,128]{4,2,3,1,0:T(8,128)(2,1)S(1)}, bf16[16,2,16,1,128]{4,2,3,1,0:T(8,128)(2,1)}, u32[]{:S(2)}) copy-start(bf16[16,2,16,1,128]{4,2,3,1,0:T(8,128)(2,1)} %param.11) | copy-start | bytes 393220
  40.8 18.7 %copy-start.4 = (bf16[16,12,1,16,1,128]{5,3,2,1,0,4:T(8,128)(2,1)S(1)}, bf16[16,12,1,16,1,128]{5,3,2,1,0,4:T(8,128)(2,1)}, u32[]{:S(2)}) copy-start(bf16[16,12,1,16,1,128]{5,3,2,1,0,4:T(8,128)(2,1)} %get-tuple-element.40) | copy-start | bytes 2359300
  53.3 19.0 %all-to-all-start.1 = ((bf16[4,128,128]{2,1,0:T(8,128)(2,1)}), bf16[4,128,128]{2,1,0:T(8,128)(2,1)S(1)}, u32[]{:S(2)}, u32[]{:S(2)}) async-start(bf16[4,128,128]{2,1,0:T(8,128)(2,1)} %bitcast.150), calls=%async_computation.1 | async-start | bytes 262144 | tf_op jit(solution)/shard_map/all_to_all | solution.py:97
  59.5 1.3 copy-start.8
  61.6 12.6 %copy-start.12 = (s32[48]{0:T(128)S(1)}, s32[48]{0:T(128)}, u32[]{:S(2)}) copy-start(s32[48]{0:T(128)} %param.19) | copy-start | bytes 580
  72.3 25.4 %collective-permute-start.3 = (bf16[4,32,2560]{2,1,0:T(8,128)(2,1)S(1)}, bf16[4,32,2560]{2,1,0:T(8,128)(2,1)S(1)}, u32[]{:S(2)}, u32[]{:S(2)}) collective-permute-start(bf16[4,32,2560]{2,1,0:T(8,128)(2,1)S(1)} %dynamic-slice_bitcast_fusion), channel_id=1, source_target_pairs={{0,1},{1,0},{2,3},{3,2},{4,5},{5,4},{6,7},{7,6},{8,9},{9,8},{10,11... | collective-permute-start | bytes 1966088 | tf_op jit(solution)/shard_map/ppermute | solution.py:221
  74.3 10.6 %collective-permute-start.2 = (bf16[512,128]{1,0:T(8,128)(2,1)S(1)}, bf16[512,128]{1,0:T(8,128)(2,1)S(1)}, u32[]{:S(2)}, u32[]{:S(2)}) collective-permute-start(bf16[512,128]{1,0:T(8,128)(2,1)S(1)} %bitcast.162), channel_id=1, source_target_pairs={{0,480},{8,488},{16,496},{24,504},{32,0},{40,8},{48,16},{56,24},{6... | collective-permute-start | bytes 393224 | tf_op jit(solution)/shard_map/ppermute | solution.py:211
  76.2 15.0 %collective-permute-start.1 = (bf16[512,128]{1,0:T(8,128)(2,1)S(1)}, bf16[512,128]{1,0:T(8,128)(2,1)S(1)}, u32[]{:S(2)}, u32[]{:S(2)}) collective-permute-start(bf16[512,128]{1,0:T(8,128)(2,1)S(1)} %bitcast.163), channel_id=1, source_target_pairs={{0,64},{8,72},{16,80},{24,88},{32,96},{40,104},{48,112},{56,120},{... | collective-permute-start | bytes 393224 | tf_op jit(solution)/shard_map/ppermute | solution.py:211
  81.3 16.4 %collective-permute-start = (bf16[512,128]{1,0:T(8,128)(2,1)S(1)}, bf16[512,128]{1,0:T(8,128)(2,1)S(1)}, u32[]{:S(2)}, u32[]{:S(2)}) collective-permute-start(bf16[512,128]{1,0:T(8,128)(2,1)S(1)} %bitcast.164), channel_id=1, source_target_pairs={{0,32},{8,40},{16,48},{24,56},{32,64},{40,72},{48,80},{56,88},{64,... | collective-permute-start | bytes 393224 | tf_op jit(solution)/shard_map/ppermute | solution.py:211
  97.8 0.9 copy-start.5
  98.8 13.6 %collective-permute-start.4 = (bf16[2,32,2560]{2,1,0:T(8,128)(2,1)S(1)}, bf16[2,32,2560]{2,1,0:T(8,128)(2,1)S(1)}, u32[]{:S(2)}, u32[]{:S(2)}) collective-permute-start(bf16[2,32,2560]{2,1,0:T(8,128)(2,1)S(1)} %dynamic-slice_bitcast_fusion.1), channel_id=1, source_target_pairs={{0,2},{1,3},{2,0},{3,1},{4,6},{5,7},{6,4},{7,5},{8,10},{9,11},{10,... | collective-permute-start | bytes 983048 | tf_op jit(solution)/shard_map/ppermute | solution.py:221
  104.8 7.6 %copy-start.6 = (bf16[4,32,2560]{2,1,0:T(8,128)(2,1)S(1)}, bf16[4,32,2560]{2,1,0:T(8,128)(2,1)}, u32[]{:S(2)}) copy-start(bf16[4,32,2560]{2,1,0:T(8,128)(2,1)} %copy-done.5) | copy-start | bytes 1966084
  104.8 16.9 %copy-start.9 = (bf16[32,2560]{1,0:T(8,128)(2,1)S(1)}, bf16[32,2560]{1,0:T(8,128)(2,1)}, u32[]{:S(2)}) copy-start(bf16[32,2560]{1,0:T(8,128)(2,1)} %param.16) | copy-start | bytes 491524
  104.8 32.4 %all-to-all-start.3 = ((bf16[4,2048,128]{2,1,0:T(8,128)(2,1)}), bf16[4,2048,128]{2,1,0:T(8,128)(2,1)}, u32[]{:S(2)}, u32[]{:S(2)}) async-start(bf16[4,2048,128]{2,1,0:T(8,128)(2,1)} %broadcast_in_dim.95), calls=%async_computation.3 | async-start | bytes 4194304 | tf_op jit(solution)/shard_map/all_to_all | solution.py:97
  112.5 9.2 %collective-permute-start.5 = (bf16[1,32,2560]{2,1,0:T(8,128)(2,1)S(1)}, bf16[1,32,2560]{2,1,0:T(8,128)(2,1)S(1)}, u32[]{:S(2)}, u32[]{:S(2)}) collective-permute-start(bf16[1,32,2560]{2,1,0:T(8,128)(2,1)S(1)} %constant_dynamic-slice_fusion), channel_id=1, source_target_pairs={{0,4},{1,5},{2,6},{3,7},{4,0},{5,1},{6,2},{7,3},{8,12},{9,13},{10,... | collective-permute-start | bytes 491528 | tf_op jit(solution)/shard_map/ppermute | solution.py:221
Sparse Core Ops, SparseCore 0:
  51.9 89.7 all-gather.1
